TPU v7x, 512 devices: a whole 4x8x8 slice. The times are simulated.
512 devices in a mesh: sec: 4 (over y_lo, core), row: 128 (over z, x, y_hi).
Axes of the slice: x: 4, y: 8 (y_hi: 4, y_lo: 2; y = y_hi * 2 + y_lo), z: 8, core: 2. Of those that a mesh axis runs over, the one named last changes fastest.
Arguments:
- images: bfloat16 [4, 8192, 1088], P('sec', 'row'), may hold values from -12 to 12
- initial: float32 [4, 2, 128, 16], P('sec', None, 'row'), may hold values from -6 to 6
- offsets: int32 [4, 2, 128, 16], P('sec', None, 'row'), may hold values from -4 to 4
- stiffness: float32 [8, 2], replicated, may hold values from 0.1 to 0.8
- plan: int32 [3], replicated, may hold values from 0 to 7
Outputs:
- flow_field: float32 [4, 2, 128, 16], P('sec', None, 'row')
- moving: float32 [4, 2, 128, 16], P('sec', None, 'row')
All inputs are finite; a program needn't handle non-finite values.
Results may differ from a plain program's by a relative error of at most 0.0003.
Values may be sent and summed in bfloat16 or wider, within the bound.
No kernel may reach another device: no remote copies, remote signals or barrier semaphores. Data moves between devices by JAX's collectives and lax.ppermute only.
A program may use at most 64 MiB of HBM per device.

v0:
```python
import math

import jax
import jax.numpy as jnp
from jax import lax
from jax.sharding import PartitionSpec as P

PATCH = 128
STRIDE = 64
SWEEPS = 3


step_size = 0.2
floor_ratio = 0.2


def shifted(block, axis, distance):
    devices = range(lax.axis_size(axis))
    route = [(i - distance, i) for i in devices if i - distance in devices]
    return lax.ppermute(block, axis, route)


def extended_2(shard, sides, width):
    for axis, dim in sides:
        devices, length = (lax.axis_size(axis), shard.shape[dim])
        up = [(i, (i + 1) % devices) for i in range(devices - 1)]
        down = [(j, i) for i, j in up]
        last = lax.slice_in_dim(shard, length - width, length, axis=dim)
        initial = lax.slice_in_dim(shard, 0, width, axis=dim)
        before = lax.ppermute(last, axis, up)
        after = lax.ppermute(initial, axis, down)
        shard = jnp.concatenate([before, shard, after], axis=dim)
    return shard


def dft_tables(length):
    freq = jnp.arange(length, dtype=jnp.int32)
    phase = freq[:, None] * freq[None, :] % length
    folded = jnp.minimum(phase, length - phase)
    angle = folded.astype(jnp.float32) * (2.0 * math.pi / length)
    upper = (phase * 2 > length).astype(jnp.float32)
    middle = (folded * 2 == length).astype(jnp.float32)
    sine = jnp.sin(angle) * (1.0 - 2.0 * upper) * (1.0 - middle)
    return jnp.concatenate([jnp.cos(angle), -sine], axis=0).astype(jnp.bfloat16)


def cut_patches(extended, height, across, stride, length):
    blocks_per = length // stride
    tiling = extended.reshape(height + blocks_per - 1, stride, across + blocks_per - 1, stride)
    pieces = [
        tiling[i : i + height, :, j : j + across, :]
        for i in range(blocks_per)
        for j in range(blocks_per)
    ]
    stacked = jnp.stack(pieces).reshape(blocks_per, blocks_per, height, stride, across, stride)
    return stacked.transpose(2, 4, 0, 3, 1, 5).reshape(height * across, length, length)


def spectra(patches, tables):
    length = patches.shape[-1]
    number = patches.shape[0]
    segmented = jnp.dot(
        patches.reshape(number * length, length), tables.T, preferred_element_type=jnp.float32
    )
    segmented = segmented.reshape(number, length, 2 * length).astype(jnp.bfloat16)
    product = jnp.einsum("ky,nyl->nkl", tables, segmented, preferred_element_type=jnp.float32)
    real_part = product[:, :length, :length] - product[:, length:, length:]
    imag_part = product[:, :length, length:] + product[:, length:, :length]
    return jnp.concatenate([real_part, imag_part], axis=-1).astype(jnp.bfloat16)


def spectrum_norms(spec):
    length = spec.shape[1]
    energy = jnp.sum(jnp.square(spec.astype(jnp.float32)), axis=(1, 2))
    return jnp.sqrt(energy / (length * length) + 1e-06)


def correlate(spec_lower, spec_upper, norm_lower, norm_upper, shift_y, shift_x):
    length = spec_lower.shape[1]
    lower_f = spec_lower.astype(jnp.float32)
    upper_f = spec_upper.astype(jnp.float32)
    low_re = lower_f[..., :length]
    low_im = lower_f[..., length:]
    up_re = upper_f[..., :length]
    up_im = upper_f[..., length:]
    cross_re = low_re * up_re + low_im * up_im
    cross_im = low_re * up_im - low_im * up_re
    modulus = jnp.sqrt(cross_re * cross_re + cross_im * cross_im)
    divisor = modulus + (floor_ratio * norm_lower * norm_upper)[:, None, None]
    white_re = cross_re / divisor
    white_im = cross_im / divisor
    freq = jnp.arange(length, dtype=jnp.int32)
    beside_all = jnp.arange(3, dtype=jnp.int32) - 1

    def twiddle(shift):
        lagged = shift[:, None] + beside_all[None, :]
        phase = freq[None, :, None] * lagged[:, None, :] % length
        angle = phase.astype(jnp.float32) * (2.0 * math.pi / length)
        return (jnp.cos(angle), jnp.sin(angle))

    cos_x, sin_x = twiddle(shift_x)
    cos_y, sin_y = twiddle(shift_y)
    highest = lax.Precision.HIGHEST
    part_re = jnp.einsum("nkl,nli->nki", white_re, cos_x, precision=highest) - jnp.einsum(
        "nkl,nli->nki", white_im, sin_x, precision=highest
    )
    part_im = jnp.einsum("nkl,nli->nki", white_re, sin_x, precision=highest) + jnp.einsum(
        "nkl,nli->nki", white_im, cos_x, precision=highest
    )
    values = jnp.einsum("nkj,nki->nji", cos_y, part_re, precision=highest) - jnp.einsum(
        "nkj,nki->nji", sin_y, part_im, precision=highest
    )
    values = values / (length * length)
    grad_y = 0.5 * (values[:, 2, 1] - values[:, 0, 1])
    curve_y = 2.0 * values[:, 1, 1] - values[:, 0, 1] - values[:, 2, 1]
    grad_x = 0.5 * (values[:, 1, 2] - values[:, 1, 0])
    curve_x = 2.0 * values[:, 1, 1] - values[:, 1, 0] - values[:, 1, 2]
    flow_y = shift_y.astype(jnp.float32) + grad_y / (1.0 + jnp.abs(curve_y))
    flow_x = shift_x.astype(jnp.float32) + grad_x / (1.0 + jnp.abs(curve_x))
    return (flow_y, flow_x)


def per_device(images, initial, offsets, stiffness, plan):
    height = offsets.shape[2]
    across = offsets.shape[3]
    below_rows = shifted(images, "row", -1)
    extended = jnp.concatenate([images, below_rows], axis=1)[0]
    tables = dft_tables(PATCH)
    own_patches = cut_patches(extended, height, across, STRIDE, PATCH)
    own_spec = spectra(own_patches, tables)
    own_norm = spectrum_norms(own_spec)
    next_ext = shifted(extended, "sec", -1)
    next_spec = spectra(cut_patches(next_ext, height, across, STRIDE, PATCH), tables)
    next_norm = spectrum_norms(next_spec)
    sec_here = lax.axis_index("sec")
    valid_up = (sec_here < lax.axis_size("sec") - 1).astype(jnp.float32)
    patch_count = own_spec.shape[0]
    groups = 4
    per_group = patch_count // groups

    def one_group(pieces):
        return correlate(pieces[0], pieces[1], pieces[2], pieces[3], pieces[4], pieces[5])

    grouped = (
        own_spec.reshape(groups, per_group, PATCH, 2 * PATCH),
        next_spec.reshape(groups, per_group, PATCH, 2 * PATCH),
        own_norm.reshape(groups, per_group),
        next_norm.reshape(groups, per_group),
        offsets[0, 0].reshape(groups, per_group),
        offsets[0, 1].reshape(groups, per_group),
    )
    flow_y, flow_x = lax.map(one_group, grouped)
    flow_field = (
        jnp.stack([flow_y.reshape(height, across), flow_x.reshape(height, across)], axis=0)
        * valid_up
    )[None]
    global_rows = lax.axis_index("row") * height + jnp.arange(height, dtype=jnp.int32)
    col_ids = jnp.arange(across, dtype=jnp.int32)
    has_up = (global_rows > 0).astype(jnp.float32)[:, None]
    has_down = (global_rows < lax.axis_size("row") * height - 1).astype(jnp.float32)[:, None]
    has_left = (col_ids > 0).astype(jnp.float32)[None, :]
    has_right = (col_ids < across - 1).astype(jnp.float32)[None, :]
    level_ids = jnp.arange(stiffness.shape[0], dtype=jnp.int32)
    moving = initial
    for sweep_no in range(SWEEPS):
        picks = (level_ids == plan[sweep_no]).astype(jnp.float32)
        spring = jnp.sum(stiffness[:, 0] * picks)
        tether = jnp.sum(stiffness[:, 1] * picks)
        framed = extended_2(moving, (("row", 2),), 1)
        row_above = framed[:, :, :-2]
        row_below = framed[:, :, 2:]
        col_left = jnp.pad(moving[..., :-1], ((0, 0), (0, 0), (0, 0), (1, 0)))
        col_right = jnp.pad(moving[..., 1:], ((0, 0), (0, 0), (0, 0), (0, 1)))
        laplace = (
            (row_above - moving) * has_up
            + (row_below - moving) * has_down
            + (col_left - moving) * has_left
            + (col_right - moving) * has_right
        )
        above_sec = shifted(moving, "sec", -1)
        residual = (above_sec - moving - flow_field) * valid_up
        below_res = shifted(residual, "sec", 1)
        moving = moving + step_size * (spring * laplace + tether * (residual - below_res))
    return (flow_field, moving)


def solution(mesh):
    return jax.shard_map(
        per_device,
        mesh=mesh,
        in_specs=(
            P("sec", "row", None),
            P("sec", None, "row", None),
            P("sec", None, "row", None),
            P(),
            P(),
        ),
        out_specs=(P("sec", None, "row", None), P("sec", None, "row", None)),
        check_vma=False,
    )
```

profile of v0, /device:TPU:254, one launch (start us, length us, event | category | flops | bytes accessed | tf_op | source)
XLA Modules:
  0.0 121.8 jit_solution(7784021692376291411)
XLA Ops:
  0.6 2.7 %collective-permute-start.4 = (f32[1,2,1,16]{3,2,1,0:T(1,128)}, f32[1,2,1,16]{3,2,1,0:T(1,128)}, u32[]{:S(2)}, u32[]{:S(2)}) collective-permute-start(f32[1,2,1,16]{3,2,1,0:T(1,128)} %param.8), channel_id=1, source_target_pairs={{128,0},{256,128},{384,256},{129,1},{257,129},{385,257},{130,2},{2... | collective-permute-start | bytes 392 | tf_op jit(solution)/shard_map/ppermute | solution.py:20
  3.3 4.8 %collective-permute-start.2 = (f32[1,2,1,16]{3,2,1,0:T(1,128)}, f32[1,2,1,16]{3,2,1,0:T(1,128)}, u32[]{:S(2)}, u32[]{:S(2)}) collective-permute-start(f32[1,2,1,16]{3,2,1,0:T(1,128)} %param.8), channel_id=1, source_target_pairs={{0,1},{1,2},{2,3},{3,4},{4,5},{5,6},{6,7},{7,8},{8,9},{9,10},{10,1... | collective-permute-start | bytes 392 | tf_op jit(solution)/shard_map/ppermute | solution.py:30
  8.2 1.9 %collective-permute-start.3 = (f32[1,2,1,16]{3,2,1,0:T(1,128)}, f32[1,2,1,16]{3,2,1,0:T(1,128)}, u32[]{:S(2)}, u32[]{:S(2)}) collective-permute-start(f32[1,2,1,16]{3,2,1,0:T(1,128)} %param.8), channel_id=1, source_target_pairs={{1,0},{2,1},{3,2},{4,3},{5,4},{6,5},{7,6},{8,7},{9,8},{10,9},{11,1... | collective-permute-start | bytes 392 | tf_op jit(solution)/shard_map/ppermute | solution.py:31
  10.1 5.2 %collective-permute-start = (bf16[1,64,1088]{2,1,0:T(8,128)(2,1)}, bf16[1,64,1088]{2,1,0:T(8,128)(2,1)S(1)}, u32[]{:S(2)}, u32[]{:S(2)}) collective-permute-start(bf16[1,64,1088]{2,1,0:T(8,128)(2,1)} %param.7), channel_id=1, source_target_pairs={{1,0},{2,1},{3,2},{4,3},{5,4},{6,5},{7,6},{8,7},{9,8},{10,9},{11,1... | collective-permute-start | bytes 417800 | tf_op jit(solution)/shard_map/ppermute | solution.py:20
  19.8 3.3 %fusion.72 = (f32[]{:T(128)}, f32[]{:T(128)}, f32[]{:T(128)}, f32[]{:T(128)}, f32[]{:T(128)}, /*index=5*/f32[]{:T(128)}) fusion(s32[]{:T(128)} %bitcast.31, f32[8,2]{0,1:T(2,128)} %param.10, s32[]{:T(128)} %bitcast.30, s32[]{:T(128)} %bitcast.27), kind=kLoop, calls=%fused_computation.141 | loop fusion | flops 114 | bytes 100 | tf_op jit(solution)/shard_map/reduce_sum | solution.py:167
  24.2 4.1 %collective-permute-done = bf16[1,64,1088]{2,1,0:T(8,128)(2,1)S(1)} collective-permute-done((bf16[1,64,1088]{2,1,0:T(8,128)(2,1)}, bf16[1,64,1088]{2,1,0:T(8,128)(2,1)S(1)}, u32[]{:S(2)}, u32[]{:S(2)}) %collective-permute-start) | collective-permute-done | bytes 139296 | tf_op jit(solution)/shard_map/ppermute | solution.py:20
  30.6 2.4 %fusion.79 = (bf16[1,64,16,64]{1,0,3,2:T(2,128)(2,1)S(1)}, bf16[1,64,16,64]{1,0,3,2:T(2,128)(2,1)S(1)}, bf16[1,64,16,64]{1,0,3,2:T(2,128)(2,1)S(1)}, bf16[1,64,16,64]{1,0,3,2:T(2,128)(2,1)S(1)}) fusion(bf16[2,64,17,64]{1,0,3,2:T(2,128)(2,1)S(1)} %reshape_squeeze.10), kind=kLoop, calls=%fused_computation.150 | loop fusion | bytes 1048576 | tf_op jit(solution)/shard_map/slice | solution.py:51
  36.6 3.2 %convolution_bitcast_fusion.1 = f32[16,256,256]{1,2,0:T(8,128)} fusion(bf16[16,128,128]{2,1,0:T(8,128)(2,1)S(1)} %dot_general.52, bf16[128,128]{1,0:T(8,128)(2,1)S(1)} %get-tuple-element.185, bf16[128,128]{1,0:T(8,128)(2,1)S(1)} %get-tuple-element.186), kind=kOutput, calls=%fused_computation.87 | convolution fusion | flops 403439616 | bytes 4784128 | tf_op jit(solution)/shard_map/ky,nyl->nkl/dot_general | solution.py:66
  39.9 2.6 %fusion.63 = (bf16[16,128,128]{1,2,0:T(8,128)(2,1)S(1)}, bf16[16,128,128]{1,2,0:T(8,128)(2,1)S(1)}) fusion(f32[16,256,256]{1,2,0:T(8,128)} %convolution_bitcast_fusion.1), kind=kLoop, calls=%fused_computation.99 | loop fusion | flops 1048576 | bytes 5242880 | tf_op jit(solution)/shard_map/convert.13
  44.1 3.0 %fusion.78 = (bf16[1,64,16,64]{1,0,3,2:T(2,128)(2,1)}, bf16[1,64,16,64]{1,0,3,2:T(2,128)(2,1)S(1)}, bf16[1,64,16,64]{1,0,3,2:T(2,128)(2,1)S(1)}, bf16[1,64,16,64]{1,0,3,2:T(2,128)(2,1)S(1)}) fusion(bf16[2,64,17,64]{1,0,3,2:T(2,128)(2,1)S(1)} %reshape.337), kind=kLoop, calls=%fused_computation.149 | loop fusion | bytes 1048576 | tf_op jit(solution)/shard_map/slice | solution.py:51
  51.6 3.2 %convolution_bitcast_fusion = f32[16,256,256]{1,2,0:T(8,128)} fusion(bf16[16,128,128]{2,1,0:T(8,128)(2,1)S(1)} %dot_general.55, bf16[128,128]{1,0:T(8,128)(2,1)S(1)} %get-tuple-element.185, bf16[128,128]{1,0:T(8,128)(2,1)S(1)} %get-tuple-element.186), kind=kOutput, calls=%fused_computation.86 | convolution fusion | flops 403439616 | bytes 4784128 | tf_op jit(solution)/shard_map/ky,nyl->nkl/dot_general | solution.py:66
  54.8 2.6 %fusion.61 = (bf16[16,128,128]{1,2,0:T(8,128)(2,1)S(1)}, bf16[16,128,128]{1,2,0:T(8,128)(2,1)S(1)}) fusion(f32[16,256,256]{1,2,0:T(8,128)} %convolution_bitcast_fusion), kind=kLoop, calls=%fused_computation.95 | loop fusion | flops 1048576 | bytes 5242880 | tf_op jit(solution)/shard_map/convert.9
  58.6 16.0 %while.14 = (s32[]{:T(128)}, f32[4,4]{1,0:T(4,128)S(1)}, f32[4,4]{1,0:T(4,128)S(1)}, s32[4,4]{1,0:T(4,128)S(1)}, bf16[4,4,128,256]{3,2,1,0:T(8,128)(2,1)S(1)}, /...) while((s32[]{:T(128)}, f32[4,4]{1,0:T(4,128)S(1)}, ...), condition=%wide.region_3.4_spmd, body=%wide.region_2.3_spmd.sunk | while | flops 10990777 | bytes 5293549 | solution.py:152
  75.5 2.4 %collective-permute-start.5 = (f32[1,2,1,16]{3,2,1,0:T(1,128)S(1)}, f32[1,2,1,16]{3,2,1,0:T(1,128)S(1)}, u32[]{:S(2)}, u32[]{:S(2)}) collective-permute-start(f32[1,2,1,16]{3,2,1,0:T(1,128)S(1)} %get-tuple-element.154), channel_id=1, source_target_pairs={{0,128},{128,256},{256,384},{1,129},{129,257},{257,385},{2,130},{1... | collective-permute-start | bytes 392 | tf_op jit(solution)/shard_map/ppermute | solution.py:20
  77.9 2.4 %collective-permute-done.5 = f32[1,2,1,16]{3,2,1,0:T(1,128)S(1)} collective-permute-done((f32[1,2,1,16]{3,2,1,0:T(1,128)S(1)}, f32[1,2,1,16]{3,2,1,0:T(1,128)S(1)}, u32[]{:S(2)}, u32[]{:S(2)}) %collective-permute-start.5) | collective-permute-done | bytes 160 | tf_op jit(solution)/shard_map/ppermute | solution.py:20
  80.4 1.9 %multiply_add_fusion.3 = f32[1,2,1,16]{3,2,1,0:T(1,128)S(1)} fusion(f32[1,2,1,16]{3,2,1,0:T(1,128)S(1)} %copy-done, f32[1,2,1,16]{3,2,1,0:T(1,128)S(1)} %get-tuple-element.154, f32[1,2,1,16]{3,2,1,0:T(1,128)S(1)} %collective-permute-done.5, f32[1,2,1,15]{3,2,1,0:T(1,128)S(1)} %copy-done.4, f32[1,2,1,15]{3,2,1,0:T(1,128)S(1)} %copy-done.3, ...), kind=kLoop, calls=%fused_computation.135 | loop fusion | flops 544 | bytes 1152 | tf_op jit(solution)/shard_map/add | solution.py:183
  84.2 3.4 %collective-permute-start.6 = (f32[1,2,1,16]{3,2,1,0:T(1,128)S(1)}, f32[1,2,1,16]{3,2,1,0:T(1,128)S(1)}, u32[]{:S(2)}, u32[]{:S(2)}) collective-permute-start(f32[1,2,1,16]{3,2,1,0:T(1,128)S(1)} %multiply_add_fusion.3), channel_id=1, source_target_pairs={{0,1},{1,2},{2,3},{3,4},{4,5},{5,6},{6,7},{7,8},{8,9},{9,10},{10,1... | collective-permute-start | bytes 392 | tf_op jit(solution)/shard_map/ppermute | solution.py:30
  87.7 3.3 %collective-permute-start.7 = (f32[1,2,1,16]{3,2,1,0:T(1,128)S(1)}, f32[1,2,1,16]{3,2,1,0:T(1,128)S(1)}, u32[]{:S(2)}, u32[]{:S(2)}) collective-permute-start(f32[1,2,1,16]{3,2,1,0:T(1,128)S(1)} %multiply_add_fusion.3), channel_id=1, source_target_pairs={{1,0},{2,1},{3,2},{4,3},{5,4},{6,5},{7,6},{8,7},{9,8},{10,9},{11,1... | collective-permute-start | bytes 392 | tf_op jit(solution)/shard_map/ppermute | solution.py:31
  93.0 6.5 %collective-permute-done.7 = f32[1,2,1,16]{3,2,1,0:T(1,128)S(1)} collective-permute-done((f32[1,2,1,16]{3,2,1,0:T(1,128)S(1)}, f32[1,2,1,16]{3,2,1,0:T(1,128)S(1)}, u32[]{:S(2)}, u32[]{:S(2)}) %collective-permute-start.7) | collective-permute-done | bytes 160 | tf_op jit(solution)/shard_map/ppermute | solution.py:31
  102.7 5.3 %collective-permute-start.10 = (f32[1,2,1,16]{3,2,1,0:T(1,128)S(1)}, f32[1,2,1,16]{3,2,1,0:T(1,128)S(1)}, u32[]{:S(2)}, u32[]{:S(2)}) collective-permute-start(f32[1,2,1,16]{3,2,1,0:T(1,128)S(1)} %multiply_add_fusion.2), channel_id=1, source_target_pairs={{0,1},{1,2},{2,3},{3,4},{4,5},{5,6},{6,7},{7,8},{8,9},{9,10},{10,1... | collective-permute-start | bytes 392 | tf_op jit(solution)/shard_map/ppermute | solution.py:30
  108.1 1.9 %collective-permute-start.11 = (f32[1,2,1,16]{3,2,1,0:T(1,128)S(1)}, f32[1,2,1,16]{3,2,1,0:T(1,128)S(1)}, u32[]{:S(2)}, u32[]{:S(2)}) collective-permute-start(f32[1,2,1,16]{3,2,1,0:T(1,128)S(1)} %multiply_add_fusion.2), channel_id=1, source_target_pairs={{1,0},{2,1},{3,2},{4,3},{5,4},{6,5},{7,6},{8,7},{9,8},{10,9},{11,1... | collective-permute-start | bytes 392 | tf_op jit(solution)/shard_map/ppermute | solution.py:31
  110.1 2.1 %collective-permute-start.13 = (f32[1,2,1,16]{3,2,1,0:T(1,128)S(1)}, f32[1,2,1,16]{3,2,1,0:T(1,128)S(1)}, u32[]{:S(2)}, u32[]{:S(2)}) collective-permute-start(f32[1,2,1,16]{3,2,1,0:T(1,128)S(1)} %subtract_multiply_fusion), channel_id=1, source_target_pairs={{0,128},{128,256},{256,384},{1,129},{129,257},{257,385},{2,130},{1... | collective-permute-start | bytes 392 | tf_op jit(solution)/shard_map/ppermute | solution.py:20
  112.2 7.6 %collective-permute-done.11 = f32[1,2,1,16]{3,2,1,0:T(1,128)S(1)} collective-permute-done((f32[1,2,1,16]{3,2,1,0:T(1,128)S(1)}, f32[1,2,1,16]{3,2,1,0:T(1,128)S(1)}, u32[]{:S(2)}, u32[]{:S(2)}) %collective-permute-start.11) | collective-permute-done | bytes 160 | tf_op jit(solution)/shard_map/ppermute | solution.py:31
  119.9 1.9 %multiply_add_fusion.1 = f32[1,2,1,16]{3,2,1,0:T(1,128)} fusion(f32[1,2,1,16]{3,2,1,0:T(1,128)S(1)} %multiply_add_fusion.2, f32[1,2,1,16]{3,2,1,0:T(1,128)S(1)} %subtract_multiply_fusion, f32[1,2,1,16]{3,2,1,0:T(1,128)S(1)} %collective-permute-done.13, f32[1,2,1,15]{3,2,1,0:T(1,128)S(1)} %get-tuple-element.177, f32[1,2,1,15]{3,2,1,0:T(1,128)S(1)} %get-tuple-element.176, ...), kind=kLoop, calls=%fused_computation.131 | loop fusion | flops 544 | bytes 1152 | tf_op jit(solution)/shard_map/add | solution.py:183
  (145 shorter events, 42.2 us)
Async XLA Ops:
  0.6 74.2 %collective-permute-start.4 = (f32[1,2,1,16]{3,2,1,0:T(1,128)}, f32[1,2,1,16]{3,2,1,0:T(1,128)}, u32[]{:S(2)}, u32[]{:S(2)}) collective-permute-start(f32[1,2,1,16]{3,2,1,0:T(1,128)} %param.8), channel_id=1, source_target_pairs={{128,0},{256,128},{384,256},{129,1},{257,129},{385,257},{130,2},{2... | collective-permute-start | bytes 392 | tf_op jit(solution)/shard_map/ppermute | solution.py:20
  3.3 74.6 %collective-permute-start.2 = (f32[1,2,1,16]{3,2,1,0:T(1,128)}, f32[1,2,1,16]{3,2,1,0:T(1,128)}, u32[]{:S(2)}, u32[]{:S(2)}) collective-permute-start(f32[1,2,1,16]{3,2,1,0:T(1,128)} %param.8), channel_id=1, source_target_pairs={{0,1},{1,2},{2,3},{3,4},{4,5},{5,6},{6,7},{7,8},{8,9},{9,10},{10,1... | collective-permute-start | bytes 392 | tf_op jit(solution)/shard_map/ppermute | solution.py:30
  8.2 69.7 %collective-permute-start.3 = (f32[1,2,1,16]{3,2,1,0:T(1,128)}, f32[1,2,1,16]{3,2,1,0:T(1,128)}, u32[]{:S(2)}, u32[]{:S(2)}) collective-permute-start(f32[1,2,1,16]{3,2,1,0:T(1,128)} %param.8), channel_id=1, source_target_pairs={{1,0},{2,1},{3,2},{4,3},{5,4},{6,5},{7,6},{8,7},{9,8},{10,9},{11,1... | collective-permute-start | bytes 392 | tf_op jit(solution)/shard_map/ppermute | solution.py:31
  10.1 18.1 %collective-permute-start = (bf16[1,64,1088]{2,1,0:T(8,128)(2,1)}, bf16[1,64,1088]{2,1,0:T(8,128)(2,1)S(1)}, u32[]{:S(2)}, u32[]{:S(2)}) collective-permute-start(bf16[1,64,1088]{2,1,0:T(8,128)(2,1)} %param.7), channel_id=1, source_target_pairs={{1,0},{2,1},{3,2},{4,3},{5,4},{6,5},{7,6},{8,7},{9,8},{10,9},{11,1... | collective-permute-start | bytes 417800 | tf_op jit(solution)/shard_map/ppermute | solution.py:20
  28.5 15.1 %collective-permute-start.1 = (bf16[128,1088]{1,0:T(8,128)(2,1)S(1)}, bf16[128,1088]{1,0:T(8,128)(2,1)S(1)}, u32[]{:S(2)}, u32[]{:S(2)}) collective-permute-start(bf16[128,1088]{1,0:T(8,128)(2,1)S(1)} %bitcast.157), channel_id=1, source_target_pairs={{128,0},{256,128},{384,256},{129,1},{257,129},{385,257},{130,2},{2... | collective-permute-start | bytes 835592 | tf_op jit(solution)/shard_map/ppermute | solution.py:20
  57.8 0.7 copy-start.5
  57.8 0.7 copy-start.6
  58.6 16.3 %copy-start = (f32[1,2,1,16]{3,2,1,0:T(1,128)S(1)}, f32[1,2,1,16]{3,2,1,0:T(1,128)}, u32[]{:S(2)}) copy-start(f32[1,2,1,16]{3,2,1,0:T(1,128)} %param.8) | copy-start | bytes 388
  58.6 21.8 %copy-start.2 = (f32[16]{0:T(128)S(1)}, f32[16]{0:T(128)}, u32[]{:S(2)}) copy-start(f32[16]{0:T(128)} %get-tuple-element.188) | copy-start | bytes 196
  58.6 21.8 %copy-start.3 = (f32[1,2,1,15]{3,2,1,0:T(1,128)S(1)}, f32[1,2,1,15]{3,2,1,0:T(1,128)}, u32[]{:S(2)}) copy-start(f32[1,2,1,15]{3,2,1,0:T(1,128)} %get-tuple-element.180) | copy-start | bytes 364
  58.6 21.8 %copy-start.4 = (f32[1,2,1,15]{3,2,1,0:T(1,128)S(1)}, f32[1,2,1,15]{3,2,1,0:T(1,128)}, u32[]{:S(2)}) copy-start(f32[1,2,1,15]{3,2,1,0:T(1,128)} %get-tuple-element.181) | copy-start | bytes 364
  75.5 46.3 %copy-start.1 = (f32[1,2,1,16]{3,2,1,0:T(1,128)}, f32[1,2,1,16]{3,2,1,0:T(1,128)S(1)}, u32[]{:S(2)}) copy-start(f32[1,2,1,16]{3,2,1,0:T(1,128)S(1)} %get-tuple-element.155) | copy-start | bytes 388
  75.5 4.9 %collective-permute-start.5 = (f32[1,2,1,16]{3,2,1,0:T(1,128)S(1)}, f32[1,2,1,16]{3,2,1,0:T(1,128)S(1)}, u32[]{:S(2)}, u32[]{:S(2)}) collective-permute-start(f32[1,2,1,16]{3,2,1,0:T(1,128)S(1)} %get-tuple-element.154), channel_id=1, source_target_pairs={{0,128},{128,256},{256,384},{1,129},{129,257},{257,385},{2,130},{1... | collective-permute-start | bytes 392 | tf_op jit(solution)/shard_map/ppermute | solution.py:20
  82.3 8.8 %collective-permute-start.8 = (f32[1,2,1,16]{3,2,1,0:T(1,128)S(1)}, f32[1,2,1,16]{3,2,1,0:T(1,128)S(1)}, u32[]{:S(2)}, u32[]{:S(2)}) collective-permute-start(f32[1,2,1,16]{3,2,1,0:T(1,128)S(1)} %multiply_add_fusion.3), channel_id=1, source_target_pairs={{128,0},{256,128},{384,256},{129,1},{257,129},{385,257},{130,2},{2... | collective-permute-start | bytes 392 | tf_op jit(solution)/shard_map/ppermute | solution.py:20
  84.2 8.8 %collective-permute-start.6 = (f32[1,2,1,16]{3,2,1,0:T(1,128)S(1)}, f32[1,2,1,16]{3,2,1,0:T(1,128)S(1)}, u32[]{:S(2)}, u32[]{:S(2)}) collective-permute-start(f32[1,2,1,16]{3,2,1,0:T(1,128)S(1)} %multiply_add_fusion.3), channel_id=1, source_target_pairs={{0,1},{1,2},{2,3},{3,4},{4,5},{5,6},{6,7},{7,8},{8,9},{9,10},{10,1... | collective-permute-start | bytes 392 | tf_op jit(solution)/shard_map/ppermute | solution.py:30
  87.7 11.8 %collective-permute-start.7 = (f32[1,2,1,16]{3,2,1,0:T(1,128)S(1)}, f32[1,2,1,16]{3,2,1,0:T(1,128)S(1)}, u32[]{:S(2)}, u32[]{:S(2)}) collective-permute-start(f32[1,2,1,16]{3,2,1,0:T(1,128)S(1)} %multiply_add_fusion.3), channel_id=1, source_target_pairs={{1,0},{2,1},{3,2},{4,3},{5,4},{6,5},{7,6},{8,7},{9,8},{10,9},{11,1... | collective-permute-start | bytes 392 | tf_op jit(solution)/shard_map/ppermute | solution.py:31
  91.1 8.4 %collective-permute-start.9 = (f32[1,2,1,16]{3,2,1,0:T(1,128)S(1)}, f32[1,2,1,16]{3,2,1,0:T(1,128)S(1)}, u32[]{:S(2)}, u32[]{:S(2)}) collective-permute-start(f32[1,2,1,16]{3,2,1,0:T(1,128)S(1)} %subtract_multiply_fusion.1), channel_id=1, source_target_pairs={{0,128},{128,256},{256,384},{1,129},{129,257},{257,385},{2,130},{1... | collective-permute-start | bytes 392 | tf_op jit(solution)/shard_map/ppermute | solution.py:20
  100.8 9.3 %collective-permute-start.12 = (f32[1,2,1,16]{3,2,1,0:T(1,128)S(1)}, f32[1,2,1,16]{3,2,1,0:T(1,128)S(1)}, u32[]{:S(2)}, u32[]{:S(2)}) collective-permute-start(f32[1,2,1,16]{3,2,1,0:T(1,128)S(1)} %multiply_add_fusion.2), channel_id=1, source_target_pairs={{128,0},{256,128},{384,256},{129,1},{257,129},{385,257},{130,2},{2... | collective-permute-start | bytes 392 | tf_op jit(solution)/shard_map/ppermute | solution.py:20
  102.7 9.5 %collective-permute-start.10 = (f32[1,2,1,16]{3,2,1,0:T(1,128)S(1)}, f32[1,2,1,16]{3,2,1,0:T(1,128)S(1)}, u32[]{:S(2)}, u32[]{:S(2)}) collective-permute-start(f32[1,2,1,16]{3,2,1,0:T(1,128)S(1)} %multiply_add_fusion.2), channel_id=1, source_target_pairs={{0,1},{1,2},{2,3},{3,4},{4,5},{5,6},{6,7},{7,8},{8,9},{9,10},{10,1... | collective-permute-start | bytes 392 | tf_op jit(solution)/shard_map/ppermute | solution.py:30
  108.1 11.8 %collective-permute-start.11 = (f32[1,2,1,16]{3,2,1,0:T(1,128)S(1)}, f32[1,2,1,16]{3,2,1,0:T(1,128)S(1)}, u32[]{:S(2)}, u32[]{:S(2)}) collective-permute-start(f32[1,2,1,16]{3,2,1,0:T(1,128)S(1)} %multiply_add_fusion.2), channel_id=1, source_target_pairs={{1,0},{2,1},{3,2},{4,3},{5,4},{6,5},{7,6},{8,7},{9,8},{10,9},{11,1... | collective-permute-start | bytes 392 | tf_op jit(solution)/shard_map/ppermute | solution.py:31
  110.1 9.8 %collective-permute-start.13 = (f32[1,2,1,16]{3,2,1,0:T(1,128)S(1)}, f32[1,2,1,16]{3,2,1,0:T(1,128)S(1)}, u32[]{:S(2)}, u32[]{:S(2)}) collective-permute-start(f32[1,2,1,16]{3,2,1,0:T(1,128)S(1)} %subtract_multiply_fusion), channel_id=1, source_target_pairs={{0,128},{128,256},{256,384},{1,129},{129,257},{257,385},{2,130},{1... | collective-permute-start | bytes 392 | tf_op jit(solution)/shard_map/ppermute | solution.py:20
where the time goes:
time: 122 us
  starting transfers between devices  40.9 us (34%)
  waiting for transfers between devices  20.7 us (17%)
  local copies, waits for them, and re-layouts  20.3 us (17%)
  other arithmetic  19.5 us (16%)
  matrix products  18.9 us (15%)
    ppermute x8, starting transfers between devices, shifted(): return lax.ppermute(block, axis, route)  20.1 us
    ppermute x3, waiting for transfers between devices, extended_2(): after = lax.ppermute(initial, axis, down)  14.1 us
    ppermute x3, starting transfers between devices, extended_2(): before = lax.ppermute(last, axis, up)  13.6 us
    slice x10, local copies, waits for them, and re-layouts, cut_patches(): tiling[i:i + height, :, j:j + across, :]  9.68 us
    ppermute x3, starting transfers between devices, extended_2(): after = lax.ppermute(initial, axis, down)  7.14 us
    ppermute x8, waiting for transfers between devices, shifted(): return lax.ppermute(block, axis, route)  6.54 us
    dot_general x2, matrix products, spectra(): jnp.einsum('ky,nyl->nkl', tables, segmented, preferred_element_type=jnp.f...  6.46 us
    another operation x5, other arithmetic  5.47 us
  transfers between devices with their start and end apart: 14, of which 4 were waited for; matrix products, arithmetic and copies ran while one was open for 44% of the time, Pallas kernels for 0%

commit v1 on v0

v1 whole, which is shorter than its diff:
```python
import math

import numpy as np
import jax
import jax.numpy as jnp
from jax import lax
from jax.experimental import pallas as pl
from jax.experimental.pallas import tpu as pltpu
from jax.sharding import PartitionSpec as P
import ml_dtypes

PATCH = 128
STRIDE = 64
HALF = 64
SWEEPS = 3
COLS = 16
PAIRS = 8
SECS = 4
RING = 4
SHIFTS = 16
REACH = 5
WIDTH = 1088
PADDED = 1152

step_size = 0.2
floor_ratio = 0.2

f32 = jnp.float32
bf16 = jnp.bfloat16


def dft_halves():
    freq = np.arange(PATCH)
    phase = freq[:, None] * freq[None, :] % PATCH
    folded = np.minimum(phase, PATCH - phase)
    angle = folded * (2.0 * math.pi / PATCH)
    sine = np.sin(angle) * np.where(2 * phase > PATCH, -1.0, 1.0)
    sine = np.where(2 * folded == PATCH, 0.0, sine)
    cosine = np.cos(angle)
    cosine = np.where(4 * folded == PATCH, np.cos(np.float32(math.pi / 2)), cosine)
    return cosine.astype(ml_dtypes.bfloat16), (-sine).astype(ml_dtypes.bfloat16)


def two_parts(table):
    high = table.astype(ml_dtypes.bfloat16)
    low = (table - high.astype(np.float64)).astype(ml_dtypes.bfloat16)
    return high, low


def constant_tables():
    cos_t, sin_t = dft_halves()
    cos_f = cos_t.astype(np.float32)
    sin_f = sin_t.astype(np.float32)
    rows = np.zeros((2 * PATCH, 2 * PATCH), np.float32)
    rows[0:PATCH, 0:HALF] = cos_f[:HALF].T
    rows[0:PATCH, PATCH : PATCH + HALF] = sin_f[:HALF].T
    rows[HALF : HALF + PATCH, HALF:PATCH] = cos_f[:HALF].T
    rows[HALF : HALF + PATCH, PATCH + HALF :] = sin_f[:HALF].T
    nyquist = np.zeros((PADDED, PATCH), np.float32)
    for c in range(COLS):
        nyquist[c * STRIDE : c * STRIDE + PATCH, c] = cos_f[HALF]
    columns = np.block([[cos_f, -sin_f], [sin_f, cos_f]])
    lags = np.arange(SHIFTS) - REACH
    used = (np.arange(SHIFTS) <= 2 * REACH).astype(np.float64)
    freq = np.arange(PATCH)
    turn = (freq[None, :] * lags[:, None] % PATCH) * (2.0 * math.pi / PATCH)
    cos_y = np.cos(turn) * used[:, None]
    sin_y = np.sin(turn) * used[:, None]
    high, low = two_parts(np.block([[cos_y, -sin_y], [sin_y, cos_y]]))
    lag_y = np.concatenate([high, low], axis=0)
    weight = np.where(freq[:HALF] == 0, 1.0, 2.0)
    across = np.zeros((3 * PATCH, PATCH))
    for p in range(2):
        cols = slice(p * HALF, p * HALF + SHIFTS)
        block = slice(p * HALF, (p + 1) * HALF)
        across[:PATCH][block, cols] = (cos_y[:, :HALF] * weight).T
        across[PATCH : 2 * PATCH][block, cols] = (-sin_y[:, :HALF] * weight).T
        for c in range(p, COLS, 2):
            across[2 * PATCH + c, cols] = np.where(lags % 2 == 0, 1.0, -1.0) * used
    high, low = two_parts(across)
    lag_x = np.concatenate([high, low], axis=1)
    lane = np.arange(PATCH)
    patch = (lane % COLS % 2)[None, :] == (lane // HALF)[:, None]
    gather = (patch & (lane < 2 * COLS)[None, :]).astype(np.float32)
    single = (patch & (lane < COLS)[None, :]).astype(np.float32)
    same = ((lane // HALF)[:, None] == (lane // HALF)[None, :]).astype(np.float32)
    blank = np.zeros((PATCH, PATCH), np.float32)
    spread = np.block([[same, gather], [single.T, blank]])
    as_bf16 = lambda t: np.asarray(t).astype(ml_dtypes.bfloat16)
    return [as_bf16(t) for t in (rows, nyquist, columns, lag_y, lag_x, spread)]


def three_parts(x):
    high = x.astype(bf16)
    rest = x - high.astype(f32)
    mid = rest.astype(bf16)
    low = (rest - mid.astype(f32)).astype(bf16)
    return jnp.concatenate([high, mid, low], axis=0)


def dot(a, b):
    return jnp.dot(a, b, preferred_element_type=f32)


def flow_kernel(
    own, below, near, near_below, record, rows_t, nyq_t, cols_t, lag_y, lag_x, spread_t, out, image, spec, lagged
):
    for i, ref in enumerate((own, below, near, near_below)):
        image[pl.ds(i * HALF, HALF), pl.ds(0, WIDTH)] = ref[0]
    image[:, pl.ds(WIDTH, PADDED - WIDTH)] = jnp.zeros((4 * HALF, PADDED - WIDTH), bf16)

    def finish_spectrum(m, stacked, table):
        product = dot(table, stacked).astype(bf16)
        spec[m] = product
        wide = product.astype(f32)
        return jnp.sum(wide * wide, axis=0, keepdims=True)

    energies = []
    for m in range(PAIRS):
        seg = dot(image[:, pl.ds(m * PATCH, 2 * PATCH)], rows_t[...]).astype(bf16)
        stacked = jnp.concatenate(
            [
                jnp.concatenate([seg[:PATCH, :PATCH], seg[PATCH:, :PATCH]], axis=1),
                jnp.concatenate([seg[:PATCH, PATCH:], seg[PATCH:, PATCH:]], axis=1),
            ],
            axis=0,
        )
        energies.append(finish_spectrum(m, stacked, cols_t[...]))
    seg = dot(image[...], nyq_t[...]).astype(bf16)
    stacked = jnp.concatenate([seg[:PATCH], seg[PATCH:]], axis=1)
    energy_64 = finish_spectrum(PAIRS, stacked, cols_t[:, pl.ds(0, PATCH)])

    lane = lax.broadcasted_iota(jnp.int32, (PAIRS, PATCH), 1)
    pair = lax.broadcasted_iota(jnp.int32, (PAIRS, PATCH), 0)
    own_pair = (lane % COLS) // 2 == pair
    first_16 = own_pair & (lane < COLS)
    weight = jnp.where(lane % HALF == 0, 1.0, 2.0)
    energy = jnp.concatenate(energies, axis=0)

    def halves(x):
        return x[:, :PATCH], x[:, PATCH:]

    def totals(main, extra):
        left = jnp.concatenate([main * weight, jnp.where(first_16, extra, 0.0)], axis=1)
        found = dot(three_parts(left), spread_t[...])
        found = found[:PAIRS] + found[PAIRS : 2 * PAIRS] + found[2 * PAIRS :]
        by_pair, by_patch = halves(found)
        by_patch = jnp.sum(jnp.where(first_16, by_patch, 0.0), axis=0, keepdims=True) + extra
        scale = 1.0 / (PATCH * PATCH)
        return jnp.sqrt(by_pair * scale + 1e-06), jnp.sqrt(by_patch * scale + 1e-06)

    low_e, up_e = halves(energy)
    low_x, up_x = halves(energy_64)
    low_pair, low_patch = totals(low_e, low_x)
    up_pair, up_patch = totals(up_e, up_x)
    floor_pair = floor_ratio * low_pair * up_pair
    floor_patch = floor_ratio * low_patch * up_patch

    for m in range(PAIRS + 1):
        floor = floor_pair[m : m + 1] if m < PAIRS else floor_patch
        low_re = spec[m, pl.ds(0, PATCH), pl.ds(0, PATCH)].astype(f32)
        low_im = spec[m, pl.ds(PATCH, PATCH), pl.ds(0, PATCH)].astype(f32)
        up_re = spec[m, pl.ds(0, PATCH), pl.ds(PATCH, PATCH)].astype(f32)
        up_im = spec[m, pl.ds(PATCH, PATCH), pl.ds(PATCH, PATCH)].astype(f32)
        cross_re = low_re * up_re + low_im * up_im
        cross_im = low_re * up_im - low_im * up_re
        square = cross_re * cross_re + cross_im * cross_im
        modulus = square * lax.rsqrt(jnp.maximum(square, 1e-36))
        inverse = 1.0 / (modulus + floor)
        white = jnp.concatenate([cross_re * inverse, cross_im * inverse], axis=0)
        high = white.astype(bf16)
        low = (white - high.astype(f32)).astype(bf16)
        found = dot(lag_y[...], jnp.concatenate([high, low], axis=1))
        part = found[: 2 * SHIFTS, :PATCH] + found[: 2 * SHIFTS, PATCH:] + found[2 * SHIFTS :, :PATCH]
        lagged[pl.ds(m * SHIFTS, SHIFTS), pl.ds(0, PATCH)] = part[:SHIFTS]
        lagged[pl.ds(m * SHIFTS, SHIFTS), pl.ds(PATCH, PATCH)] = part[SHIFTS:]

    extra = lagged[pl.ds(PAIRS * SHIFTS, SHIFTS), pl.ds(0, PATCH)]
    extra = jnp.where(first_16[:, None, :], extra[None], 0.0).reshape(PAIRS * SHIFTS, PATCH)
    left = jnp.concatenate([lagged[pl.ds(0, PAIRS * SHIFTS), :], extra], axis=1)
    high = left.astype(bf16)
    low = (left - high.astype(f32)).astype(bf16)
    rows_all = PAIRS * SHIFTS
    found = dot(jnp.concatenate([high, low], axis=0), lag_x[...])
    surface = found[:rows_all, :PATCH] + found[:rows_all, PATCH:] + found[rows_all:, :PATCH]
    surface = surface.reshape(PAIRS, SHIFTS, PATCH)

    rec = record[...]
    at_y = jnp.where(first_16, rec, 0.0)
    at_x = jnp.where(own_pair & (lane >= COLS) & (lane < 2 * COLS), rec, 0.0)
    gather = spread_t[pl.ds(0, PATCH), pl.ds(PATCH, PATCH)]
    shifts = lax.dot_general(
        jnp.concatenate([at_y, at_x], axis=0).astype(bf16),
        gather,
        (((1,), (1,)), ((), ())),
        preferred_element_type=f32,
    )
    lag_row = lax.broadcasted_iota(jnp.int32, (PAIRS, SHIFTS, PATCH), 1).astype(f32) - REACH
    lag_col = (lax.broadcasted_iota(jnp.int32, (PAIRS, SHIFTS, PATCH), 2) % HALF).astype(f32) - REACH
    dy = lag_row - shifts[:PAIRS][:, None, :]
    dx = lag_col - shifts[PAIRS:][:, None, :]
    mid_y, up_y, down_y = ((dy == k).astype(f32) for k in (0.0, 1.0, -1.0))
    mid_x, up_x, down_x = ((dx == k).astype(f32) for k in (0.0, 1.0, -1.0))
    at_mid_x = surface * mid_x
    at_mid_y = surface * mid_y
    picks = [
        jnp.sum(at_mid_x * (up_y - down_y), axis=1),
        jnp.sum(at_mid_x * (2.0 * mid_y - up_y - down_y), axis=1),
        jnp.sum(at_mid_y * (up_x - down_x), axis=1),
        jnp.sum(at_mid_y * (2.0 * mid_x - up_x - down_x), axis=1),
    ]
    found = dot(three_parts(jnp.concatenate(picks, axis=0)), gather)
    found = found[: 4 * PAIRS] + found[4 * PAIRS : 8 * PAIRS] + found[8 * PAIRS :]
    found = found.reshape(4, PAIRS, PATCH)
    found = jnp.sum(jnp.where(own_pair[None], found, 0.0), axis=1) * (1.0 / (PATCH * PATCH))
    lane_1 = lax.broadcasted_iota(jnp.int32, (1, PATCH), 1)
    slope = jnp.where(lane_1 < COLS, found[0:1], found[2:3])
    bend = jnp.where(lane_1 < COLS, found[1:2], found[3:4])
    flow = rec + 0.5 * slope / (1.0 + jnp.abs(bend))
    result = jnp.where(lane_1 < 2 * COLS, flow, rec)
    out[...] = jnp.broadcast_to(result[None], out.shape)


def vmem_spec():
    return pl.BlockSpec(memory_space=pltpu.VMEM)


def pair_flow(own, below, near, near_below, record, copies):
    tables = [jnp.asarray(t) for t in constant_tables()]
    return pl.pallas_call(
        flow_kernel,
        out_shape=jax.ShapeDtypeStruct((copies, 1, PATCH), f32),
        in_specs=[vmem_spec()] * (5 + len(tables)),
        out_specs=vmem_spec(),
        scratch_shapes=[
            pltpu.VMEM((4 * HALF, PADDED), bf16),
            pltpu.VMEM((PAIRS + 1, 2 * PATCH, 2 * PATCH), bf16),
            pltpu.VMEM(((PAIRS + 1) * SHIFTS, 2 * PATCH), f32),
        ],
        compiler_params=pltpu.CompilerParams(vmem_limit_bytes=32 * 1024 * 1024),
    )(own, below, near, near_below, record, *tables)


def relax_kernel(place, stiffness, plan, mid, before, after, flow_out, moving_out):
    sec = place[0]
    row = place[1]
    base = row - lax.rem(row, RING)
    count = SECS * RING
    node = lax.broadcasted_iota(jnp.int32, (count, PATCH), 0)
    lane = lax.broadcasted_iota(jnp.int32, (count, PATCH), 1)
    in_ring = node % RING
    section = node // RING
    blocks = [ref[...].reshape(count, PATCH) for ref in (before, mid, after)]
    valid = (section < SECS - 1) & (lane < 2 * COLS)
    flows = [jnp.where(valid, b, 0.0) for b in blocks]
    moving = [pltpu.roll(b, PATCH - 2 * COLS, 1) for b in blocks]
    valid_up = valid.astype(f32)
    has_left = (lane % COLS > 0).astype(f32)
    has_right = (lane % COLS < COLS - 1).astype(f32)
    rows = [base + in_ring + RING * (k - 1) for k in range(3)]
    has_up = [(r > 0).astype(f32) for r in rows]
    has_down = [(r < 127).astype(f32) for r in rows]

    def moved(x, by):
        by = by % count
        return jnp.concatenate([x[by:], x[:by]], axis=0) if by else x

    for sweep in range(SWEEPS):
        level = plan[sweep]
        spring = stiffness[level, 0]
        tether = stiffness[level, 1]
        fresh = []
        for k in range(3):
            x = moving[k]
            above = moving[k - 1] if k > 0 else x
            below = moving[k + 1] if k < 2 else x
            row_above = jnp.where(in_ring == 0, moved(above, RING - 1), moved(x, -1))
            row_below = jnp.where(in_ring == RING - 1, moved(below, 1 - RING), moved(x, 1))
            col_left = pltpu.roll(x, 1, 1)
            col_right = pltpu.roll(x, PATCH - 1, 1)
            laplace = (
                (row_above - x) * has_up[k]
                + (row_below - x) * has_down[k]
                + (col_left - x) * has_left
                + (col_right - x) * has_right
            )
            residual = (moved(x, RING) - x - flows[k]) * valid_up
            below_res = jnp.where(section == 0, 0.0, moved(residual, -RING))
            fresh.append(x + step_size * (spring * laplace + tether * (residual - below_res)))
        moving = fresh

    mine = (section == sec) & (in_ring == lax.rem(row, RING))
    for x, ref in ((flows[1], flow_out), (moving[1], moving_out)):
        line = jnp.sum(jnp.where(mine, x, 0.0), axis=0, keepdims=True)
        ref[0, 0] = line[:, :COLS]
        ref[0, 1] = line[:, COLS : 2 * COLS]


def relax(place, stiffness, plan, mid, before, after, shape):
    smem = pl.BlockSpec(memory_space=pltpu.SMEM)
    return pl.pallas_call(
        relax_kernel,
        out_shape=[jax.ShapeDtypeStruct(shape, f32)] * 2,
        in_specs=[smem] * 3 + [vmem_spec()] * 3,
        out_specs=[vmem_spec()] * 2,
    )(place, stiffness, plan, mid, before, after)


def shifted(block, axis, distance):
    devices = range(lax.axis_size(axis))
    route = [(i - distance, i) for i in devices if i - distance in devices]
    return lax.ppermute(block, axis, route)


def per_device(images, initial, offsets, stiffness, plan):
    rows = lax.axis_size("row")
    near = shifted(images, "sec", -1)
    below = shifted(images, "row", -1)
    near_below = shifted(below, "sec", -1)
    record = jnp.concatenate(
        [offsets.astype(f32).reshape(1, 2 * COLS), initial.reshape(1, 2 * COLS), jnp.zeros((1, 64), f32)], axis=1
    )
    mine = pair_flow(images, below, near, near_below, record, SECS * RING)
    groups = [
        [s * rows + RING * g + j for s in range(SECS) for j in range(RING)] for g in range(rows // RING)
    ]
    ring = lax.all_to_all(mine, ("sec", "row"), 0, 0, axis_index_groups=groups)
    before = shifted(ring, "row", RING)
    after = shifted(ring, "row", -RING)
    place = jnp.stack([lax.axis_index("sec"), lax.axis_index("row")]).astype(jnp.int32)
    return tuple(relax(place, stiffness, plan, ring, before, after, initial.shape))


def solution(mesh):
    return jax.shard_map(
        per_device,
        mesh=mesh,
        in_specs=(
            P("sec", "row", None),
            P("sec", None, "row", None),
            P("sec", None, "row", None),
            P(),
            P(),
        ),
        out_specs=(P("sec", None, "row", None), P("sec", None, "row", None)),
        check_vma=False,
    )
```

time: 122 us -> 60.1 us (0.49)
  the two profiles are of different devices: /device:TPU:254 before, /device:TPU:198 now
where the time goes in v1:
time: 60.1 us; the launch traced here: 59.5 us
  starting transfers between devices  26.3 us (44%)
  waiting for transfers between devices  17.4 us (29%)
  local copies, waits for them, and re-layouts  8.5 us (14%)
  Pallas kernels  4.71 us (8%)
  other arithmetic  1.99 us (3%)
  between operations  0.72 us (1%)
    ppermute x5, starting transfers between devices, shifted(): return lax.ppermute(block, axis, route)  14.8 us
    all_to_all x1, starting transfers between devices, per_device(): ring = lax.all_to_all(mine, ('sec', 'row'), 0, 0, axis_index_groups=groups)  11.4 us
    ppermute x5, waiting for transfers between devices, shifted(): return lax.ppermute(block, axis, route)  9.78 us
    unnamed x26, local copies, waits for them, and re-layouts  8.33 us
    all_to_all x1, waiting for transfers between devices, per_device(): ring = lax.all_to_all(mine, ('sec', 'row'), 0, 0, axis_index_groups=groups)  7.6 us
    pallas_call x1, Pallas kernels, pair_flow(): pl.pallas_call(flow_kernel, out_shape=jax.ShapeDtypeStruct((copies, 1, PA...  2.88 us
    pallas_call x1, Pallas kernels, relax(): pl.pallas_call(relax_kernel, out_shape=[jax.ShapeDtypeStruct(shape, f32)]...  1.83 us
  transfers between devices with their start and end apart: 6, of which 3 were waited for; matrix products, arithmetic and copies ran while one was open for 6% of the time, Pallas kernels for 0%

profile of v1, /device:TPU:198, one launch (start us, length us, event | category | flops | bytes accessed | tf_op | source)
XLA Modules:
  0.0 59.5 jit_solution(5891263359668761733)
XLA Ops:
  0.6 6.4 %collective-permute-start = (bf16[1,64,1088]{2,1,0:T(8,128)(2,1)}, bf16[1,64,1088]{2,1,0:T(8,128)(2,1)S(1)}, u32[]{:S(2)}, u32[]{:S(2)}) collective-permute-start(bf16[1,64,1088]{2,1,0:T(8,128)(2,1)} %own.1), channel_id=1, source_target_pairs={{1,0},{2,1},{3,2},{4,3},{5,4},{6,5},{7,6},{8,7},{9,8},{10,9},{11,1... | collective-permute-start | bytes 417800 | tf_op jit(solution)/shard_map/ppermute | solution.py:312
  7.1 1.3 %collective-permute-start.1 = (bf16[1,64,1088]{2,1,0:T(8,128)(2,1)}, bf16[1,64,1088]{2,1,0:T(8,128)(2,1)S(1)}, u32[]{:S(2)}, u32[]{:S(2)}) collective-permute-start(bf16[1,64,1088]{2,1,0:T(8,128)(2,1)} %own.1), channel_id=1, source_target_pairs={{128,0},{256,128},{384,256},{129,1},{257,129},{385,257},{130,2},{2... | collective-permute-start | bytes 417800 | tf_op jit(solution)/shard_map/ppermute | solution.py:312
  8.4 5.3 %collective-permute-done.below = bf16[1,64,1088]{2,1,0:T(8,128)(2,1)S(1)} collective-permute-done((bf16[1,64,1088]{2,1,0:T(8,128)(2,1)}, bf16[1,64,1088]{2,1,0:T(8,128)(2,1)S(1)}, u32[]{:S(2)}, u32[]{:S(2)}) %collective-permute-start) | collective-permute-done | bytes 139296 | tf_op jit(solution)/shard_map/ppermute | solution.py:312
  13.7 1.3 %collective-permute-start.2 = (bf16[1,64,1088]{2,1,0:T(8,128)(2,1)S(1)}, bf16[1,64,1088]{2,1,0:T(8,128)(2,1)S(1)}, u32[]{:S(2)}, u32[]{:S(2)}) collective-permute-start(bf16[1,64,1088]{2,1,0:T(8,128)(2,1)S(1)} %collective-permute-done.below), channel_id=1, source_target_pairs={{128,0},{256,128},{384,256},{129,1},{257,129},{385,257},{130,2},{2... | collective-permute-start | bytes 417800 | tf_op jit(solution)/shard_map/ppermute | solution.py:312
  14.9 0.7 %convert_reduce_fusion = f32[2,16]{1,0:T(2,128)S(1)} fusion(s32[1,2,1,16]{3,2,1,0:T(1,128)} %param.13), kind=kLoop, calls=%fused_computation | loop fusion | flops 32 | bytes 256 | tf_op jit(solution)/shard_map/convert_element_type | solution.py:321
  15.6 0.5 broadcast.7
  16.3 0.7 %reduce.7 = f32[2,16]{1,0:T(2,128)S(1)} reduce(f32[1,2,1,16]{3,2,1,0:T(1,128)S(1)} %copy-done.11, f32[]{:T(128)} %broadcast.7), dimensions={0,2}, to_apply=%param.12.reduce_sub_computation.3 | reduce | bytes 260 | tf_op args[1]
  17.3 1.0 %copy-done = bf16[1152,128]{1,0:T(8,128)(2,1)S(1)} copy-done((bf16[1152,128]{1,0:T(8,128)(2,1)S(1)}, bf16[1152,128]{1,0:T(8,128)(2,1)}, u32[]{:S(2)}) %copy-start) | copy-done | bytes 294936
  18.2 0.9 %copy-done.1 = bf16[384,256]{1,0:T(8,128)(2,1)S(1)} copy-done((bf16[384,256]{1,0:T(8,128)(2,1)S(1)}, bf16[384,256]{1,0:T(8,128)(2,1)}, u32[]{:S(2)}) %copy-start.1) | copy-done | bytes 196632
  19.1 0.9 %copy-done.2 = bf16[1,64,1088]{2,1,0:T(8,128)(2,1)S(1)} copy-done((bf16[1,64,1088]{2,1,0:T(8,128)(2,1)S(1)}, bf16[1,64,1088]{2,1,0:T(8,128)(2,1)}, u32[]{:S(2)}) %copy-start.2) | copy-done | bytes 139288
  20.1 0.9 %copy-done.3 = bf16[256,256]{1,0:T(8,128)(2,1)S(1)} copy-done((bf16[256,256]{1,0:T(8,128)(2,1)S(1)}, bf16[256,256]{1,0:T(8,128)(2,1)}, u32[]{:S(2)}) %copy-start.3) | copy-done | bytes 131096
  21.0 0.9 %copy-done.4 = bf16[256,256]{1,0:T(8,128)(2,1)S(1)} copy-done((bf16[256,256]{1,0:T(8,128)(2,1)S(1)}, bf16[256,256]{1,0:T(8,128)(2,1)}, u32[]{:S(2)}) %copy-start.4) | copy-done | bytes 131096
  21.9 0.9 %copy-done.5 = bf16[256,256]{1,0:T(8,128)(2,1)S(1)} copy-done((bf16[256,256]{1,0:T(8,128)(2,1)S(1)}, bf16[256,256]{1,0:T(8,128)(2,1)}, u32[]{:S(2)}) %copy-start.5) | copy-done | bytes 131096
  22.8 0.8 %copy-done.6 = bf16[64,256]{1,0:T(8,128)(2,1)S(1)} copy-done((bf16[64,256]{1,0:T(8,128)(2,1)S(1)}, bf16[64,256]{1,0:T(8,128)(2,1)}, u32[]{:S(2)}) %copy-start.6) | copy-done | bytes 32792
  23.5 2.9 %shard_map.122 = f32[16,1,128]{2,1,0:T(1,128)} custom-call(bf16[1,64,1088]{2,1,0:T(8,128)(2,1)S(1)} %copy-done.2, bf16[1,64,1088]{2,1,0:T(8,128)(2,1)S(1)} %collective-permute-done.below, bf16[1,64,1088]{2,1,0:T(8,128)(2,1)S(1)} %collective-permute-done.1.near, bf16[1,64,1088]{2,1,0:T(8,128)(2,1)S(1)} %collective-permute-done.2.near_below, ...), custom_call_target="tpu_custom_call" | custom-call | tf_op jit(solution)/shard_map/pallas_call | solution.py:230
  26.4 11.4 %all-to-all-start = ((f32[16,1,128]{2,1,0:T(1,128)}), f32[16,1,128]{2,1,0:T(1,128)S(1)}, u32[]{:S(2)}, u32[]{:S(2)}) async-start(f32[16,1,128]{2,1,0:T(1,128)} %shard_map.122), calls=%async_computation | async-start | bytes 16384 | tf_op jit(solution)/shard_map/all_to_all | solution.py:327
  37.8 7.6 %all-to-all-done.mid = f32[16,1,128]{2,1,0:T(1,128)S(1)} async-done(((f32[16,1,128]{2,1,0:T(1,128)}), f32[16,1,128]{2,1,0:T(1,128)S(1)}, u32[]{:S(2)}, u32[]{:S(2)}) %all-to-all-start) | async-done | bytes 8224 | tf_op jit(solution)/shard_map/all_to_all | solution.py:327
  45.4 2.8 %collective-permute-start.3 = (f32[16,1,128]{2,1,0:T(1,128)S(1)}, f32[16,1,128]{2,1,0:T(1,128)S(1)}, u32[]{:S(2)}, u32[]{:S(2)}) collective-permute-start(f32[16,1,128]{2,1,0:T(1,128)S(1)} %all-to-all-done.mid), channel_id=1, source_target_pairs={{0,4},{1,5},{2,6},{3,7},{4,8},{5,9},{6,10},{7,11},{8,12},{9,13},{1... | collective-permute-start | bytes 24584 | tf_op jit(solution)/shard_map/ppermute | solution.py:312
  48.3 3.0 %collective-permute-start.4 = (f32[16,1,128]{2,1,0:T(1,128)S(1)}, f32[16,1,128]{2,1,0:T(1,128)S(1)}, u32[]{:S(2)}, u32[]{:S(2)}) collective-permute-start(f32[16,1,128]{2,1,0:T(1,128)S(1)} %all-to-all-done.mid), channel_id=1, source_target_pairs={{4,0},{5,1},{6,2},{7,3},{8,4},{9,5},{10,6},{11,7},{12,8},{13,9},{1... | collective-permute-start | bytes 24584 | tf_op jit(solution)/shard_map/ppermute | solution.py:312
  51.3 0.6 pad_add_fusion.place
  52.0 0.7 %copy.13.stiffness = f32[8,2]{1,0:T(8,128)} copy(f32[8,2]{0,1:T(2,128)S(1)} %copy-done.10) | data formatting | bytes 128 | tf_op args[3]
  52.6 4.5 %collective-permute-done.4.after = f32[16,1,128]{2,1,0:T(1,128)S(1)} collective-permute-done((f32[16,1,128]{2,1,0:T(1,128)S(1)}, f32[16,1,128]{2,1,0:T(1,128)S(1)}, u32[]{:S(2)}, u32[]{:S(2)}) %collective-permute-start.4) | collective-permute-done | bytes 8224 | tf_op jit(solution)/shard_map/ppermute | solution.py:312
  57.1 0.6 copy-done.9
  57.7 1.8 %shard_map.123 = (f32[1,2,1,16]{3,2,1,0:T(1,128)}, f32[1,2,1,16]{3,2,1,0:T(1,128)}) custom-call(s32[2]{0:T(128)} %pad_add_fusion.place, f32[8,2]{1,0:T(8,128)} %copy.13.stiffness, s32[3]{0:T(128)} %plan.1, f32[16,1,128]{2,1,0:T(1,128)} %copy-done.7, f32[16,1,128]{2,1,0:T(1,128)} %copy-done.8, f32[16,1,128]{2,1,0:T(1,128)} %copy-done.9), custom_call_target="tpu_custom_call" | custom-call | tf_op jit(solution)/shard_map/pallas_call | solution.py:301
  (23 shorter events, 0.6 us)
Async XLA Ops:
  0.6 13.0 %collective-permute-start = (bf16[1,64,1088]{2,1,0:T(8,128)(2,1)}, bf16[1,64,1088]{2,1,0:T(8,128)(2,1)S(1)}, u32[]{:S(2)}, u32[]{:S(2)}) collective-permute-start(bf16[1,64,1088]{2,1,0:T(8,128)(2,1)} %own.1), channel_id=1, source_target_pairs={{1,0},{2,1},{3,2},{4,3},{5,4},{6,5},{7,6},{8,7},{9,8},{10,9},{11,1... | collective-permute-start | bytes 417800 | tf_op jit(solution)/shard_map/ppermute | solution.py:312
  7.1 10.2 %collective-permute-start.1 = (bf16[1,64,1088]{2,1,0:T(8,128)(2,1)}, bf16[1,64,1088]{2,1,0:T(8,128)(2,1)S(1)}, u32[]{:S(2)}, u32[]{:S(2)}) collective-permute-start(bf16[1,64,1088]{2,1,0:T(8,128)(2,1)} %own.1), channel_id=1, source_target_pairs={{128,0},{256,128},{384,256},{129,1},{257,129},{385,257},{130,2},{2... | collective-permute-start | bytes 417800 | tf_op jit(solution)/shard_map/ppermute | solution.py:312
  13.7 3.6 %collective-permute-start.2 = (bf16[1,64,1088]{2,1,0:T(8,128)(2,1)S(1)}, bf16[1,64,1088]{2,1,0:T(8,128)(2,1)S(1)}, u32[]{:S(2)}, u32[]{:S(2)}) collective-permute-start(bf16[1,64,1088]{2,1,0:T(8,128)(2,1)S(1)} %collective-permute-done.below), channel_id=1, source_target_pairs={{128,0},{256,128},{384,256},{129,1},{257,129},{385,257},{130,2},{2... | collective-permute-start | bytes 417800 | tf_op jit(solution)/shard_map/ppermute | solution.py:312
  15.6 0.7 %copy-start.11 = (f32[1,2,1,16]{3,2,1,0:T(1,128)S(1)}, f32[1,2,1,16]{3,2,1,0:T(1,128)}, u32[]{:S(2)}) copy-start(f32[1,2,1,16]{3,2,1,0:T(1,128)} %param.12) | copy-start | bytes 388
  17.2 1.0 %copy-start = (bf16[1152,128]{1,0:T(8,128)(2,1)S(1)}, bf16[1152,128]{1,0:T(8,128)(2,1)}, u32[]{:S(2)}) copy-start(bf16[1152,128]{1,0:T(8,128)(2,1)} %constant.24.clone.nyq_t) | copy-start | bytes 884740
  18.2 0.9 %copy-start.1 = (bf16[384,256]{1,0:T(8,128)(2,1)S(1)}, bf16[384,256]{1,0:T(8,128)(2,1)}, u32[]{:S(2)}) copy-start(bf16[384,256]{1,0:T(8,128)(2,1)} %constant.27.clone.lag_x) | copy-start | bytes 589828
  19.1 0.9 %copy-start.2 = (bf16[1,64,1088]{2,1,0:T(8,128)(2,1)S(1)}, bf16[1,64,1088]{2,1,0:T(8,128)(2,1)}, u32[]{:S(2)}) copy-start(bf16[1,64,1088]{2,1,0:T(8,128)(2,1)} %own.1) | copy-start | bytes 417796
  20.0 0.9 %copy-start.3 = (bf16[256,256]{1,0:T(8,128)(2,1)S(1)}, bf16[256,256]{1,0:T(8,128)(2,1)}, u32[]{:S(2)}) copy-start(bf16[256,256]{1,0:T(8,128)(2,1)} %constant.23.clone.rows_t) | copy-start | bytes 393220
  21.0 0.9 %copy-start.4 = (bf16[256,256]{1,0:T(8,128)(2,1)S(1)}, bf16[256,256]{1,0:T(8,128)(2,1)}, u32[]{:S(2)}) copy-start(bf16[256,256]{1,0:T(8,128)(2,1)} %constant.25.clone.cols_t) | copy-start | bytes 393220
  21.9 0.9 %copy-start.5 = (bf16[256,256]{1,0:T(8,128)(2,1)S(1)}, bf16[256,256]{1,0:T(8,128)(2,1)}, u32[]{:S(2)}) copy-start(bf16[256,256]{1,0:T(8,128)(2,1)} %constant.28.clone.spread_t) | copy-start | bytes 393220
  22.8 0.8 %copy-start.6 = (bf16[64,256]{1,0:T(8,128)(2,1)S(1)}, bf16[64,256]{1,0:T(8,128)(2,1)}, u32[]{:S(2)}) copy-start(bf16[64,256]{1,0:T(8,128)(2,1)} %constant.26.clone.lag_y) | copy-start | bytes 98308
  26.4 19.0 %all-to-all-start = ((f32[16,1,128]{2,1,0:T(1,128)}), f32[16,1,128]{2,1,0:T(1,128)S(1)}, u32[]{:S(2)}, u32[]{:S(2)}) async-start(f32[16,1,128]{2,1,0:T(1,128)} %shard_map.122), calls=%async_computation | async-start | bytes 16384 | tf_op jit(solution)/shard_map/all_to_all | solution.py:327
  45.4 11.7 %copy-start.7 = (f32[16,1,128]{2,1,0:T(1,128)}, f32[16,1,128]{2,1,0:T(1,128)S(1)}, u32[]{:S(2)}) copy-start(f32[16,1,128]{2,1,0:T(1,128)S(1)} %all-to-all-done.mid) | copy-start | bytes 24580
  45.4 7.2 %collective-permute-start.3 = (f32[16,1,128]{2,1,0:T(1,128)S(1)}, f32[16,1,128]{2,1,0:T(1,128)S(1)}, u32[]{:S(2)}, u32[]{:S(2)}) collective-permute-start(f32[16,1,128]{2,1,0:T(1,128)S(1)} %all-to-all-done.mid), channel_id=1, source_target_pairs={{0,4},{1,5},{2,6},{3,7},{4,8},{5,9},{6,10},{7,11},{8,12},{9,13},{1... | collective-permute-start | bytes 24584 | tf_op jit(solution)/shard_map/ppermute | solution.py:312
  48.3 8.9 %collective-permute-start.4 = (f32[16,1,128]{2,1,0:T(1,128)S(1)}, f32[16,1,128]{2,1,0:T(1,128)S(1)}, u32[]{:S(2)}, u32[]{:S(2)}) collective-permute-start(f32[16,1,128]{2,1,0:T(1,128)S(1)} %all-to-all-done.mid), channel_id=1, source_target_pairs={{4,0},{5,1},{6,2},{7,3},{8,4},{9,5},{10,6},{11,7},{12,8},{13,9},{1... | collective-permute-start | bytes 24584 | tf_op jit(solution)/shard_map/ppermute | solution.py:312
  51.3 0.7 %copy-start.10 = (f32[8,2]{0,1:T(2,128)S(1)}, f32[8,2]{0,1:T(2,128)}, u32[]{:S(2)}) copy-start(f32[8,2]{0,1:T(2,128)} %param.14) | copy-start | bytes 196
  52.6 4.5 %copy-start.8 = (f32[16,1,128]{2,1,0:T(1,128)}, f32[16,1,128]{2,1,0:T(1,128)S(1)}, u32[]{:S(2)}) copy-start(f32[16,1,128]{2,1,0:T(1,128)S(1)} %collective-permute-done.3.before) | copy-start | bytes 24580
  57.1 0.6 copy-start.9

commit v2 on v1

--- a/solution.py
+++ b/solution.py
@@ -20,7 +20,7 @@
 SHIFTS = 16
 REACH = 5
 WIDTH = 1088
-PADDED = 1152
+VMEM_LIMIT = 48 * 1024 * 1024
 
 step_size = 0.2
 floor_ratio = 0.2
@@ -56,9 +56,10 @@
     rows[0:PATCH, PATCH : PATCH + HALF] = sin_f[:HALF].T
     rows[HALF : HALF + PATCH, HALF:PATCH] = cos_f[:HALF].T
     rows[HALF : HALF + PATCH, PATCH + HALF :] = sin_f[:HALF].T
-    nyquist = np.zeros((PADDED, PATCH), np.float32)
-    for c in range(COLS):
-        nyquist[c * STRIDE : c * STRIDE + PATCH, c] = cos_f[HALF]
+    nyquist = np.zeros((2 * PATCH, PATCH), np.float32)
+    nyquist[0:PATCH, 0::2] = cos_f[HALF][:, None]
+    nyquist[HALF : HALF + PATCH, 1::2] = cos_f[HALF][:, None]
+    rows = np.concatenate([rows, nyquist], axis=1)
     columns = np.block([[cos_f, -sin_f], [sin_f, cos_f]])
     lags = np.arange(SHIFTS) - REACH
     used = (np.arange(SHIFTS) <= 2 * REACH).astype(np.float64)
@@ -87,7 +88,7 @@
     blank = np.zeros((PATCH, PATCH), np.float32)
     spread = np.block([[same, gather], [single.T, blank]])
     as_bf16 = lambda t: np.asarray(t).astype(ml_dtypes.bfloat16)
-    return [as_bf16(t) for t in (rows, nyquist, columns, lag_y, lag_x, spread)]
+    return [as_bf16(t) for t in (rows, columns, lag_y, lag_x, spread)]
 
 
 def three_parts(x):
@@ -103,11 +104,41 @@
 
 
 def flow_kernel(
-    own, below, near, near_below, record, rows_t, nyq_t, cols_t, lag_y, lag_x, spread_t, out, image, spec, lagged
+    own,
+    below,
+    near,
+    near_below,
+    offsets,
+    initial,
+    remote_initial,
+    rows_h,
+    cols_h,
+    lag_y_h,
+    lag_x_h,
+    spread_h,
+    out,
+    image,
+    rows_t,
+    cols_t,
+    lag_y,
+    lag_x,
+    spread_t,
+    shift_in,
+    node_in,
+    record,
+    spec,
+    lagged,
+    sems,
 ):
-    for i, ref in enumerate((own, below, near, near_below)):
-        image[pl.ds(i * HALF, HALF), pl.ds(0, WIDTH)] = ref[0]
-    image[:, pl.ds(WIDTH, PADDED - WIDTH)] = jnp.zeros((4 * HALF, PADDED - WIDTH), bf16)
+    moves = [(ref.at[0], image.at[pl.ds(i * HALF, HALF)]) for i, ref in enumerate((own, below, near, near_below))]
+    moves += [(rows_h, rows_t), (cols_h, cols_t)]
+    moves += [(offsets.at[0], shift_in), (initial.at[0], node_in.at[0]), (remote_initial.at[0], node_in.at[1])]
+    moves += [(spread_h, spread_t), (lag_y_h, lag_y), (lag_x_h, lag_x)]
+    copies = [pltpu.make_async_copy(src, dst, sems.at[i]) for i, (src, dst) in enumerate(moves)]
+    for copy in copies:
+        copy.start()
+    for copy in copies[:6]:
+        copy.wait()
 
     def finish_spectrum(m, stacked, table):
         product = dot(table, stacked).astype(bf16)
@@ -116,8 +147,13 @@
         return jnp.sum(wide * wide, axis=0, keepdims=True)
 
     energies = []
+    lane_4 = lax.broadcasted_iota(jnp.int32, (4 * HALF, PATCH), 1)
+    nyquist = jnp.zeros((4 * HALF, PATCH), f32)
     for m in range(PAIRS):
-        seg = dot(image[:, pl.ds(m * PATCH, 2 * PATCH)], rows_t[...]).astype(bf16)
+        span = 2 * PATCH if m < PAIRS - 1 else WIDTH - m * PATCH
+        seg = dot(image[:, pl.ds(m * PATCH, span)], rows_t[pl.ds(0, span), :])
+        nyquist = jnp.where(lane_4 // 2 == m, seg[:, 2 * PATCH :], nyquist)
+        seg = seg[:, : 2 * PATCH].astype(bf16)
         stacked = jnp.concatenate(
             [
                 jnp.concatenate([seg[:PATCH, :PATCH], seg[PATCH:, :PATCH]], axis=1),
@@ -126,9 +162,11 @@
             axis=0,
         )
         energies.append(finish_spectrum(m, stacked, cols_t[...]))
-    seg = dot(image[...], nyq_t[...]).astype(bf16)
+    seg = nyquist.astype(bf16)
     stacked = jnp.concatenate([seg[:PATCH], seg[PATCH:]], axis=1)
     energy_64 = finish_spectrum(PAIRS, stacked, cols_t[:, pl.ds(0, PATCH)])
+    for copy in copies[6:]:
+        copy.wait()
 
     lane = lax.broadcasted_iota(jnp.int32, (PAIRS, PATCH), 1)
     pair = lax.broadcasted_iota(jnp.int32, (PAIRS, PATCH), 0)
@@ -185,6 +223,11 @@
     surface = found[:rows_all, :PATCH] + found[:rows_all, PATCH:] + found[rows_all:, :PATCH]
     surface = surface.reshape(PAIRS, SHIFTS, PATCH)
 
+    record[...] = jnp.zeros((1, PATCH), f32)
+    for i in range(2):
+        record[:, pl.ds(i * COLS, COLS)] = shift_in[i].astype(f32)
+        record[:, pl.ds((2 + i) * COLS, COLS)] = node_in[0, i]
+        record[:, pl.ds((4 + i) * COLS, COLS)] = node_in[1, i]
     rec = record[...]
     at_y = jnp.where(first_16, rec, 0.0)
     at_x = jnp.where(own_pair & (lane >= COLS) & (lane < 2 * COLS), rec, 0.0)
@@ -218,69 +261,87 @@
     bend = jnp.where(lane_1 < COLS, found[1:2], found[3:4])
     flow = rec + 0.5 * slope / (1.0 + jnp.abs(bend))
     result = jnp.where(lane_1 < 2 * COLS, flow, rec)
-    out[...] = jnp.broadcast_to(result[None], out.shape)
-
-
-def vmem_spec():
-    return pl.BlockSpec(memory_space=pltpu.VMEM)
-
-
-def pair_flow(own, below, near, near_below, record, copies):
+    out[...] = jnp.broadcast_to(result, out.shape)
+
+
+def pair_flow(own, below, near, near_below, offsets, initial, remote_initial, copies):
     tables = [jnp.asarray(t) for t in constant_tables()]
+    operands = (own, below, near, near_below, offsets, initial, remote_initial, *tables)
     return pl.pallas_call(
         flow_kernel,
-        out_shape=jax.ShapeDtypeStruct((copies, 1, PATCH), f32),
-        in_specs=[vmem_spec()] * (5 + len(tables)),
-        out_specs=vmem_spec(),
+        out_shape=jax.ShapeDtypeStruct((copies, PATCH), f32),
+        in_specs=[pl.BlockSpec(memory_space=pl.ANY)] * len(operands),
+        out_specs=pl.BlockSpec(memory_space=pltpu.VMEM),
         scratch_shapes=[
-            pltpu.VMEM((4 * HALF, PADDED), bf16),
+            pltpu.VMEM((4 * HALF, WIDTH), bf16),
+            *[pltpu.VMEM(t.shape, bf16) for t in tables],
+            pltpu.VMEM(offsets.shape[1:], jnp.int32),
+            pltpu.VMEM((2,) + initial.shape[1:], f32),
+            pltpu.VMEM((1, PATCH), f32),
             pltpu.VMEM((PAIRS + 1, 2 * PATCH, 2 * PATCH), bf16),
             pltpu.VMEM(((PAIRS + 1) * SHIFTS, 2 * PATCH), f32),
+            pltpu.SemaphoreType.DMA((len(operands),)),
         ],
-        compiler_params=pltpu.CompilerParams(vmem_limit_bytes=32 * 1024 * 1024),
-    )(own, below, near, near_below, record, *tables)
-
-
-def relax_kernel(place, stiffness, plan, mid, before, after, flow_out, moving_out):
-    sec = place[0]
-    row = place[1]
-    base = row - lax.rem(row, RING)
+        compiler_params=pltpu.CompilerParams(vmem_limit_bytes=VMEM_LIMIT),
+    )(*operands)
+
+
+def relax_kernel(plan, stiffness_h, ring_h, other_h, flow_out, moving_out, stiffness, ring, other, sems):
+    moves = ((stiffness_h, stiffness), (ring_h, ring), (other_h, other))
+    copies = [pltpu.make_async_copy(src, dst, sems.at[i]) for i, (src, dst) in enumerate(moves)]
+    for copy in copies:
+        copy.start()
+    sec = lax.axis_index("sec")
+    row = lax.axis_index("row")
+    last_row = lax.axis_size("row") - 1
+    place = lax.rem(row, RING)
+    base = row - place
     count = SECS * RING
     node = lax.broadcasted_iota(jnp.int32, (count, PATCH), 0)
     lane = lax.broadcasted_iota(jnp.int32, (count, PATCH), 1)
     in_ring = node % RING
     section = node // RING
-    blocks = [ref[...].reshape(count, PATCH) for ref in (before, mid, after)]
+    other_first = jnp.broadcast_to(place, (count, PATCH)) < RING // 2
     valid = (section < SECS - 1) & (lane < 2 * COLS)
-    flows = [jnp.where(valid, b, 0.0) for b in blocks]
-    moving = [pltpu.roll(b, PATCH - 2 * COLS, 1) for b in blocks]
     valid_up = valid.astype(f32)
     has_left = (lane % COLS > 0).astype(f32)
     has_right = (lane % COLS < COLS - 1).astype(f32)
-    rows = [base + in_ring + RING * (k - 1) for k in range(3)]
-    has_up = [(r > 0).astype(f32) for r in rows]
-    has_down = [(r < 127).astype(f32) for r in rows]
+    row_here = base + in_ring
+    row_other = row_here + jnp.where(other_first, -RING, RING)
+    at_rows = (row_here, row_other)
+    has_up = [(r > 0).astype(f32) for r in at_rows]
+    has_down = [(r < last_row).astype(f32) for r in at_rows]
+    first = in_ring == 0
+    final = in_ring == RING - 1
+    for copy in copies:
+        copy.wait()
+    level_id = lax.broadcasted_iota(jnp.int32, stiffness.shape, 0)
+    here = ring[...]
+    beyond = other[...]
+    flows = [jnp.where(valid, b, 0.0) for b in (here, beyond)]
+    moving = [pltpu.roll(b, PATCH - 2 * COLS, 1) for b in (here, beyond)]
+    third = pltpu.roll(here, PATCH - 4 * COLS, 1)
 
     def moved(x, by):
         by = by % count
-        return jnp.concatenate([x[by:], x[:by]], axis=0) if by else x
+        return jnp.concatenate([x[by:], x[:by]], axis=0)
 
     for sweep in range(SWEEPS):
-        level = plan[sweep]
-        spring = stiffness[level, 0]
-        tether = stiffness[level, 1]
+        picked = jnp.sum(jnp.where(level_id == plan[sweep], stiffness[...], 0.0), axis=0, keepdims=True)
+        spring = picked[:, 0:1]
+        tether = picked[:, 1:2]
+        near_x, far_x = moving
+        edge_above = jnp.where(other_first, moved(far_x, RING - 1), moved(third, RING - 1))
+        edge_below = jnp.where(other_first, moved(third, 1 - RING), moved(far_x, 1 - RING))
+        above = (jnp.where(first, edge_above, moved(near_x, -1)), jnp.where(first, moved(near_x, RING - 1), moved(far_x, -1)))
+        below = (jnp.where(final, edge_below, moved(near_x, 1)), jnp.where(final, moved(near_x, 1 - RING), moved(far_x, 1)))
         fresh = []
-        for k in range(3):
-            x = moving[k]
-            above = moving[k - 1] if k > 0 else x
-            below = moving[k + 1] if k < 2 else x
-            row_above = jnp.where(in_ring == 0, moved(above, RING - 1), moved(x, -1))
-            row_below = jnp.where(in_ring == RING - 1, moved(below, 1 - RING), moved(x, 1))
+        for k, x in enumerate(moving):
             col_left = pltpu.roll(x, 1, 1)
             col_right = pltpu.roll(x, PATCH - 1, 1)
             laplace = (
-                (row_above - x) * has_up[k]
-                + (row_below - x) * has_down[k]
+                (above[k] - x) * has_up[k]
+                + (below[k] - x) * has_down[k]
                 + (col_left - x) * has_left
                 + (col_right - x) * has_right
             )
@@ -289,21 +350,28 @@
             fresh.append(x + step_size * (spring * laplace + tether * (residual - below_res)))
         moving = fresh
 
-    mine = (section == sec) & (in_ring == lax.rem(row, RING))
-    for x, ref in ((flows[1], flow_out), (moving[1], moving_out)):
+    mine = (section == sec) & (in_ring == place)
+    for x, ref in ((flows[0], flow_out), (moving[0], moving_out)):
         line = jnp.sum(jnp.where(mine, x, 0.0), axis=0, keepdims=True)
         ref[0, 0] = line[:, :COLS]
         ref[0, 1] = line[:, COLS : 2 * COLS]
 
 
-def relax(place, stiffness, plan, mid, before, after, shape):
-    smem = pl.BlockSpec(memory_space=pltpu.SMEM)
+def relax(plan, stiffness, ring, other, shape):
+    anywhere = pl.BlockSpec(memory_space=pl.ANY)
     return pl.pallas_call(
         relax_kernel,
         out_shape=[jax.ShapeDtypeStruct(shape, f32)] * 2,
-        in_specs=[smem] * 3 + [vmem_spec()] * 3,
-        out_specs=[vmem_spec()] * 2,
-    )(place, stiffness, plan, mid, before, after)
+        in_specs=[pl.BlockSpec(memory_space=pltpu.SMEM)] + [anywhere] * 3,
+        out_specs=[pl.BlockSpec(memory_space=pltpu.VMEM)] * 2,
+        scratch_shapes=[
+            pltpu.VMEM(stiffness.shape, f32),
+            pltpu.VMEM(ring.shape, f32),
+            pltpu.VMEM(ring.shape, f32),
+            pltpu.SemaphoreType.DMA((3,)),
+        ],
+        compiler_params=pltpu.CompilerParams(vmem_limit_bytes=VMEM_LIMIT),
+    )(plan, stiffness, ring, other)
 
 
 def shifted(block, axis, distance):
@@ -312,23 +380,31 @@
     return lax.ppermute(block, axis, route)
 
 
+def ring_route(rows, outward):
+    route = []
+    for r in range(rows):
+        step = RING if (r % RING < RING // 2) == outward else -RING
+        if 0 <= r - step < rows:
+            route.append((r - step, r))
+    return route
+
+
 def per_device(images, initial, offsets, stiffness, plan):
     rows = lax.axis_size("row")
     near = shifted(images, "sec", -1)
     below = shifted(images, "row", -1)
+    remote_initial = lax.ppermute(initial, "row", ring_route(rows, False))
     near_below = shifted(below, "sec", -1)
-    record = jnp.concatenate(
-        [offsets.astype(f32).reshape(1, 2 * COLS), initial.reshape(1, 2 * COLS), jnp.zeros((1, 64), f32)], axis=1
-    )
-    mine = pair_flow(images, below, near, near_below, record, SECS * RING)
+    count = SECS * RING
+    mine = pair_flow(images, below, near, near_below, offsets, initial, remote_initial, count)
     groups = [
         [s * rows + RING * g + j for s in range(SECS) for j in range(RING)] for g in range(rows // RING)
     ]
-    ring = lax.all_to_all(mine, ("sec", "row"), 0, 0, axis_index_groups=groups)
-    before = shifted(ring, "row", RING)
-    after = shifted(ring, "row", -RING)
-    place = jnp.stack([lax.axis_index("sec"), lax.axis_index("row")]).astype(jnp.int32)
-    return tuple(relax(place, stiffness, plan, ring, before, after, initial.shape))
+    ring = lax.all_to_all(mine.reshape(count, 1, PATCH), ("sec", "row"), 0, 0, axis_index_groups=groups)
+    other = lax.ppermute(ring, "row", ring_route(rows, True))
+    return tuple(
+        relax(plan, stiffness, ring.reshape(count, PATCH), other.reshape(count, PATCH), initial.shape)
+    )
 
 
 def solution(mesh):

time: 60.1 us -> 61.5 us (1.023)
  the two profiles are of different devices: /device:TPU:198 before, /device:TPU:256 now
where the time goes in v2:
time: 61.5 us; the launch traced here: 61.1 us
  blocking collectives  16.8 us (27%)
  waiting for transfers between devices  15.1 us (25%)
  starting transfers between devices  14.8 us (24%)
  local copies, waits for them, and re-layouts  7.42 us (12%)
  Pallas kernels  6.24 us (10%)
  between operations  0.7 us (1%)
    all_to_all x1, blocking collectives, per_device(): lax.all_to_all(mine.reshape(count, 1, PATCH), ('sec', 'row'), 0, 0, axis_...  16.8 us
    ppermute x3, starting transfers between devices, shifted(): return lax.ppermute(block, axis, route)  10 us
    unnamed x21, local copies, waits for them, and re-layouts  7.42 us
    ppermute x1, waiting for transfers between devices, per_device(): other = lax.ppermute(ring, 'row', ring_route(rows, True))  6.84 us
    ppermute x3, waiting for transfers between devices, shifted(): return lax.ppermute(block, axis, route)  5.3 us
    pallas_call x1, Pallas kernels, pair_flow(): pl.pallas_call(flow_kernel, out_shape=jax.ShapeDtypeStruct((copies, PATCH...  4.69 us
    ppermute x1, waiting for transfers between devices, per_device(): remote_initial = lax.ppermute(initial, 'row', ring_route(rows, False))  2.93 us
    ppermute x1, starting transfers between devices, per_device(): remote_initial = lax.ppermute(initial, 'row', ring_route(rows, False))  2.74 us
  transfers between devices with their start and end apart: 5, of which 3 were waited for; matrix products, arithmetic and copies ran while one was open for 0% of the time, Pallas kernels for 0%

profile of v2, /device:TPU:256, one launch (start us, length us, event | category | flops | bytes accessed | tf_op | source)
XLA Modules:
  0.0 61.1 jit_solution(2316062631244272796)
XLA Ops:
  0.6 7.4 %collective-permute-start = (bf16[1,64,1088]{2,1,0:T(8,128)(2,1)}, bf16[1,64,1088]{2,1,0:T(8,128)(2,1)S(1)}, u32[]{:S(2)}, u32[]{:S(2)}) collective-permute-start(bf16[1,64,1088]{2,1,0:T(8,128)(2,1)} %own.1), channel_id=1, source_target_pairs={{1,0},{2,1},{3,2},{4,3},{5,4},{6,5},{7,6},{8,7},{9,8},{10,9},{11,1... | collective-permute-start | bytes 417800 | tf_op jit(solution)/shard_map/ppermute | solution.py:380
  8.1 1.3 %collective-permute-start.1 = (bf16[1,64,1088]{2,1,0:T(8,128)(2,1)}, bf16[1,64,1088]{2,1,0:T(8,128)(2,1)S(1)}, u32[]{:S(2)}, u32[]{:S(2)}) collective-permute-start(bf16[1,64,1088]{2,1,0:T(8,128)(2,1)} %own.1), channel_id=1, source_target_pairs={{128,0},{256,128},{384,256},{129,1},{257,129},{385,257},{130,2},{2... | collective-permute-start | bytes 417800 | tf_op jit(solution)/shard_map/ppermute | solution.py:380
  9.4 5.3 %collective-permute-done.below = bf16[1,64,1088]{2,1,0:T(8,128)(2,1)S(1)} collective-permute-done((bf16[1,64,1088]{2,1,0:T(8,128)(2,1)}, bf16[1,64,1088]{2,1,0:T(8,128)(2,1)S(1)}, u32[]{:S(2)}, u32[]{:S(2)}) %collective-permute-start) | collective-permute-done | bytes 139296 | tf_op jit(solution)/shard_map/ppermute | solution.py:380
  14.7 1.3 %collective-permute-start.2 = (bf16[1,64,1088]{2,1,0:T(8,128)(2,1)S(1)}, bf16[1,64,1088]{2,1,0:T(8,128)(2,1)S(1)}, u32[]{:S(2)}, u32[]{:S(2)}) collective-permute-start(bf16[1,64,1088]{2,1,0:T(8,128)(2,1)S(1)} %collective-permute-done.below), channel_id=1, source_target_pairs={{128,0},{256,128},{384,256},{129,1},{257,129},{385,257},{130,2},{2... | collective-permute-start | bytes 417800 | tf_op jit(solution)/shard_map/ppermute | solution.py:380
  16.0 2.7 %collective-permute-start.3 = (f32[1,2,1,16]{3,2,1,0:T(1,128)}, f32[1,2,1,16]{3,2,1,0:T(1,128)S(1)}, u32[]{:S(2)}, u32[]{:S(2)}) collective-permute-start(f32[1,2,1,16]{3,2,1,0:T(1,128)} %initial.1), channel_id=1, source_target_pairs={{4,0},{5,1},{8,4},{9,5},{2,6},{3,7},{12,8},{13,9},{6,10},{7,11},{1... | collective-permute-start | bytes 392 | tf_op jit(solution)/shard_map/ppermute | solution.py:396
  18.7 2.9 %collective-permute-done.3.remote_initial = f32[1,2,1,16]{3,2,1,0:T(1,128)S(1)} collective-permute-done((f32[1,2,1,16]{3,2,1,0:T(1,128)}, f32[1,2,1,16]{3,2,1,0:T(1,128)S(1)}, u32[]{:S(2)}, u32[]{:S(2)}) %collective-permute-start.3) | collective-permute-done | bytes 160 | tf_op jit(solution)/shard_map/ppermute | solution.py:396
  21.6 0.0 collective-permute-done.1.near
  21.6 0.0 collective-permute-done.2.near_below
  21.6 0.9 %copy-done = bf16[256,384]{1,0:T(8,128)(2,1)S(1)} copy-done((bf16[256,384]{1,0:T(8,128)(2,1)S(1)}, bf16[256,384]{1,0:T(8,128)(2,1)}, u32[]{:S(2)}) %copy-start) | copy-done | bytes 196632
  22.6 0.9 %copy-done.1 = bf16[384,256]{1,0:T(8,128)(2,1)S(1)} copy-done((bf16[384,256]{1,0:T(8,128)(2,1)S(1)}, bf16[384,256]{1,0:T(8,128)(2,1)}, u32[]{:S(2)}) %copy-start.1) | copy-done | bytes 196632
  23.5 0.9 %copy-done.2 = bf16[1,64,1088]{2,1,0:T(8,128)(2,1)S(1)} copy-done((bf16[1,64,1088]{2,1,0:T(8,128)(2,1)S(1)}, bf16[1,64,1088]{2,1,0:T(8,128)(2,1)}, u32[]{:S(2)}) %copy-start.2) | copy-done | bytes 139288
  24.4 0.9 %copy-done.3 = bf16[256,256]{1,0:T(8,128)(2,1)S(1)} copy-done((bf16[256,256]{1,0:T(8,128)(2,1)S(1)}, bf16[256,256]{1,0:T(8,128)(2,1)}, u32[]{:S(2)}) %copy-start.3) | copy-done | bytes 131096
  25.3 0.9 %copy-done.4 = bf16[256,256]{1,0:T(8,128)(2,1)S(1)} copy-done((bf16[256,256]{1,0:T(8,128)(2,1)S(1)}, bf16[256,256]{1,0:T(8,128)(2,1)}, u32[]{:S(2)}) %copy-start.4) | copy-done | bytes 131096
  26.2 0.8 %copy-done.5 = bf16[64,256]{1,0:T(8,128)(2,1)S(1)} copy-done((bf16[64,256]{1,0:T(8,128)(2,1)S(1)}, bf16[64,256]{1,0:T(8,128)(2,1)}, u32[]{:S(2)}) %copy-start.5) | copy-done | bytes 32792
  27.0 0.7 %copy-done.6 = s32[1,2,1,16]{3,2,1,0:T(1,128)S(1)} copy-done((s32[1,2,1,16]{3,2,1,0:T(1,128)S(1)}, s32[1,2,1,16]{3,2,1,0:T(1,128)}, u32[]{:S(2)}) %copy-start.6) | copy-done | bytes 152
  27.7 0.7 %copy-done.7 = f32[1,2,1,16]{3,2,1,0:T(1,128)S(1)} copy-done((f32[1,2,1,16]{3,2,1,0:T(1,128)S(1)}, f32[1,2,1,16]{3,2,1,0:T(1,128)}, u32[]{:S(2)}) %copy-start.7) | copy-done | bytes 152
  28.3 4.7 %shard_map.113 = f32[16,128]{1,0:T(8,128)S(1)} custom-call(bf16[1,64,1088]{2,1,0:T(8,128)(2,1)S(1)} %copy-done.2, bf16[1,64,1088]{2,1,0:T(8,128)(2,1)S(1)} %collective-permute-done.below, bf16[1,64,1088]{2,1,0:T(8,128)(2,1)S(1)} %collective-permute-done.1.near, bf16[1,64,1088]{2,1,0:T(8,128)(2,1)S(1)} %collective-permute-done.2.near_below, ...), custom_call_target="tpu_custom_call" | custom-call | tf_op jit(solution)/shard_map/pallas_call | solution.py:270
  33.0 16.8 %all_to_all.5 = f32[16,1,128]{2,1,0:T(1,128)S(1)} all-to-all(f32[16,1,128]{2,1,0:T(1,128)S(1)} %bitcast.6), channel_id=1, replica_groups={{0,1,2,3,128,129,130,131,256,257,258,259,384,385,386,387},{4,5,6,7,132,..., dimensions={0} | all-to-all | bytes 16384 | tf_op jit(solution)/shard_map/all_to_all | solution.py:403
  49.9 2.0 %collective-permute-start.4 = (f32[16,1,128]{2,0,1:T(8,128)S(1)}, f32[16,1,128]{2,0,1:T(8,128)S(1)}, u32[]{:S(2)}, u32[]{:S(2)}) collective-permute-start(f32[16,1,128]{2,0,1:T(8,128)S(1)} %bitcast.7), channel_id=1, source_target_pairs={{6,2},{7,3},{0,4},{1,5},{10,6},{11,7},{4,8},{5,9},{14,10},{15,11},... | collective-permute-start | bytes 24584 | tf_op jit(solution)/shard_map/ppermute | solution.py:404
  51.9 0.0 copy-done.9
  51.9 0.1 copy.15.stiffness_h
  52.0 6.8 %collective-permute-done.4 = f32[16,1,128]{2,0,1:T(8,128)S(1)} collective-permute-done((f32[16,1,128]{2,0,1:T(8,128)S(1)}, f32[16,1,128]{2,0,1:T(8,128)S(1)}, u32[]{:S(2)}, u32[]{:S(2)}) %collective-permute-start.4) | collective-permute-done | bytes 8224 | tf_op jit(solution)/shard_map/ppermute | solution.py:404
  58.9 0.7 %copy-done.8 = s32[3]{0:T(128)S(1)} copy-done((s32[3]{0:T(128)S(1)}, s32[3]{0:T(128)}, u32[]{:S(2)}) %copy-start.8) | copy-done | bytes 36
  59.5 1.6 %shard_map.114 = (f32[1,2,1,16]{3,2,1,0:T(1,128)}, f32[1,2,1,16]{3,2,1,0:T(1,128)}) custom-call(s32[3]{0:T(128)S(1)} %copy-done.8, f32[8,2]{1,0:T(8,128)S(1)} %copy.15.stiffness_h, f32[16,128]{1,0:T(8,128)S(1)} %bitcast.8, f32[16,128]{1,0:T(8,128)S(1)} %bitcast.9), custom_call_target="tpu_custom_call" | custom-call | tf_op jit(solution)/shard_map/pallas_call | solution.py:362
  (10 shorter events, 0.0 us)
Async XLA Ops:
  0.6 14.0 %collective-permute-start = (bf16[1,64,1088]{2,1,0:T(8,128)(2,1)}, bf16[1,64,1088]{2,1,0:T(8,128)(2,1)S(1)}, u32[]{:S(2)}, u32[]{:S(2)}) collective-permute-start(bf16[1,64,1088]{2,1,0:T(8,128)(2,1)} %own.1), channel_id=1, source_target_pairs={{1,0},{2,1},{3,2},{4,3},{5,4},{6,5},{7,6},{8,7},{9,8},{10,9},{11,1... | collective-permute-start | bytes 417800 | tf_op jit(solution)/shard_map/ppermute | solution.py:380
  8.1 13.6 %collective-permute-start.1 = (bf16[1,64,1088]{2,1,0:T(8,128)(2,1)}, bf16[1,64,1088]{2,1,0:T(8,128)(2,1)S(1)}, u32[]{:S(2)}, u32[]{:S(2)}) collective-permute-start(bf16[1,64,1088]{2,1,0:T(8,128)(2,1)} %own.1), channel_id=1, source_target_pairs={{128,0},{256,128},{384,256},{129,1},{257,129},{385,257},{130,2},{2... | collective-permute-start | bytes 417800 | tf_op jit(solution)/shard_map/ppermute | solution.py:380
  14.7 7.0 %collective-permute-start.2 = (bf16[1,64,1088]{2,1,0:T(8,128)(2,1)S(1)}, bf16[1,64,1088]{2,1,0:T(8,128)(2,1)S(1)}, u32[]{:S(2)}, u32[]{:S(2)}) collective-permute-start(bf16[1,64,1088]{2,1,0:T(8,128)(2,1)S(1)} %collective-permute-done.below), channel_id=1, source_target_pairs={{128,0},{256,128},{384,256},{129,1},{257,129},{385,257},{130,2},{2... | collective-permute-start | bytes 417800 | tf_op jit(solution)/shard_map/ppermute | solution.py:380
  16.0 5.7 %collective-permute-start.3 = (f32[1,2,1,16]{3,2,1,0:T(1,128)}, f32[1,2,1,16]{3,2,1,0:T(1,128)S(1)}, u32[]{:S(2)}, u32[]{:S(2)}) collective-permute-start(f32[1,2,1,16]{3,2,1,0:T(1,128)} %initial.1), channel_id=1, source_target_pairs={{4,0},{5,1},{8,4},{9,5},{2,6},{3,7},{12,8},{13,9},{6,10},{7,11},{1... | collective-permute-start | bytes 392 | tf_op jit(solution)/shard_map/ppermute | solution.py:396
  21.6 0.9 %copy-start = (bf16[256,384]{1,0:T(8,128)(2,1)S(1)}, bf16[256,384]{1,0:T(8,128)(2,1)}, u32[]{:S(2)}) copy-start(bf16[256,384]{1,0:T(8,128)(2,1)} %constant.10.clone.rows_h) | copy-start | bytes 589828
  22.6 0.9 %copy-start.1 = (bf16[384,256]{1,0:T(8,128)(2,1)S(1)}, bf16[384,256]{1,0:T(8,128)(2,1)}, u32[]{:S(2)}) copy-start(bf16[384,256]{1,0:T(8,128)(2,1)} %constant.13.clone.lag_x_h) | copy-start | bytes 589828
  23.5 0.9 %copy-start.2 = (bf16[1,64,1088]{2,1,0:T(8,128)(2,1)S(1)}, bf16[1,64,1088]{2,1,0:T(8,128)(2,1)}, u32[]{:S(2)}) copy-start(bf16[1,64,1088]{2,1,0:T(8,128)(2,1)} %own.1) | copy-start | bytes 417796
  24.4 0.9 %copy-start.3 = (bf16[256,256]{1,0:T(8,128)(2,1)S(1)}, bf16[256,256]{1,0:T(8,128)(2,1)}, u32[]{:S(2)}) copy-start(bf16[256,256]{1,0:T(8,128)(2,1)} %constant.11.clone.cols_h) | copy-start | bytes 393220
  25.3 0.9 %copy-start.4 = (bf16[256,256]{1,0:T(8,128)(2,1)S(1)}, bf16[256,256]{1,0:T(8,128)(2,1)}, u32[]{:S(2)}) copy-start(bf16[256,256]{1,0:T(8,128)(2,1)} %constant.14.clone.spread_h) | copy-start | bytes 393220
  26.2 0.8 %copy-start.5 = (bf16[64,256]{1,0:T(8,128)(2,1)S(1)}, bf16[64,256]{1,0:T(8,128)(2,1)}, u32[]{:S(2)}) copy-start(bf16[64,256]{1,0:T(8,128)(2,1)} %constant.12.clone.lag_y_h) | copy-start | bytes 98308
  27.0 0.7 %copy-start.6 = (s32[1,2,1,16]{3,2,1,0:T(1,128)S(1)}, s32[1,2,1,16]{3,2,1,0:T(1,128)}, u32[]{:S(2)}) copy-start(s32[1,2,1,16]{3,2,1,0:T(1,128)} %offsets.1) | copy-start | bytes 388
  27.7 0.7 %copy-start.7 = (f32[1,2,1,16]{3,2,1,0:T(1,128)S(1)}, f32[1,2,1,16]{3,2,1,0:T(1,128)}, u32[]{:S(2)}) copy-start(f32[1,2,1,16]{3,2,1,0:T(1,128)} %initial.1) | copy-start | bytes 388
  49.9 2.1 %copy-start.9 = (f32[8,2]{0,1:T(2,128)S(1)}, f32[8,2]{0,1:T(2,128)}, u32[]{:S(2)}) copy-start(f32[8,2]{0,1:T(2,128)} %param.13) | copy-start | bytes 196
  49.9 9.0 %collective-permute-start.4 = (f32[16,1,128]{2,0,1:T(8,128)S(1)}, f32[16,1,128]{2,0,1:T(8,128)S(1)}, u32[]{:S(2)}, u32[]{:S(2)}) collective-permute-start(f32[16,1,128]{2,0,1:T(8,128)S(1)} %bitcast.7), channel_id=1, source_target_pairs={{6,2},{7,3},{0,4},{1,5},{10,6},{11,7},{4,8},{5,9},{14,10},{15,11},... | collective-permute-start | bytes 24584 | tf_op jit(solution)/shard_map/ppermute | solution.py:404
  58.9 0.7 %copy-start.8 = (s32[3]{0:T(128)S(1)}, s32[3]{0:T(128)}, u32[]{:S(2)}) copy-start(s32[3]{0:T(128)} %plan.1) | copy-start | bytes 40

commit v3 on v2

--- a/solution.py
+++ b/solution.py
@@ -20,10 +20,11 @@
 SHIFTS = 16
 REACH = 5
 WIDTH = 1088
-VMEM_LIMIT = 48 * 1024 * 1024
 
 step_size = 0.2
 floor_ratio = 0.2
+
+VMEM_LIMIT = 24 * 1024 * 1024
 
 f32 = jnp.float32
 bf16 = jnp.bfloat16
@@ -59,7 +60,6 @@
     nyquist = np.zeros((2 * PATCH, PATCH), np.float32)
     nyquist[0:PATCH, 0::2] = cos_f[HALF][:, None]
     nyquist[HALF : HALF + PATCH, 1::2] = cos_f[HALF][:, None]
-    rows = np.concatenate([rows, nyquist], axis=1)
     columns = np.block([[cos_f, -sin_f], [sin_f, cos_f]])
     lags = np.arange(SHIFTS) - REACH
     used = (np.arange(SHIFTS) <= 2 * REACH).astype(np.float64)
@@ -87,8 +87,17 @@
     same = ((lane // HALF)[:, None] == (lane // HALF)[None, :]).astype(np.float32)
     blank = np.zeros((PATCH, PATCH), np.float32)
     spread = np.block([[same, gather], [single.T, blank]])
-    as_bf16 = lambda t: np.asarray(t).astype(ml_dtypes.bfloat16)
-    return [as_bf16(t) for t in (rows, columns, lag_y, lag_x, spread)]
+    packed = [rows, np.concatenate([nyquist[:PATCH], nyquist[PATCH:]], axis=1), columns, spread, lag_y, lag_x]
+    return np.concatenate([np.asarray(t).astype(ml_dtypes.bfloat16) for t in packed], axis=0)
+
+
+TABLE_ROWS = {"rows": (0, 256), "nyquist": (256, 128), "columns": (384, 256), "spread": (640, 256)}
+TABLE_ROWS |= {"lag_y": (896, 64), "lag_x": (960, 384)}
+
+
+def table(ref, name):
+    start, length = TABLE_ROWS[name]
+    return ref[pl.ds(start, length), :]
 
 
 def three_parts(x):
@@ -103,42 +112,48 @@
     return jnp.dot(a, b, preferred_element_type=f32)
 
 
-def flow_kernel(
-    own,
-    below,
-    near,
-    near_below,
-    offsets,
-    initial,
-    remote_initial,
-    rows_h,
-    cols_h,
-    lag_y_h,
-    lag_x_h,
-    spread_h,
-    out,
-    image,
-    rows_t,
-    cols_t,
-    lag_y,
-    lag_x,
-    spread_t,
-    shift_in,
-    node_in,
-    record,
-    spec,
-    lagged,
-    sems,
-):
-    moves = [(ref.at[0], image.at[pl.ds(i * HALF, HALF)]) for i, ref in enumerate((own, below, near, near_below))]
-    moves += [(rows_h, rows_t), (cols_h, cols_t)]
-    moves += [(offsets.at[0], shift_in), (initial.at[0], node_in.at[0]), (remote_initial.at[0], node_in.at[1])]
-    moves += [(spread_h, spread_t), (lag_y_h, lag_y), (lag_x_h, lag_x)]
+def prepare_kernel(plan, images, tables, offsets, initial, stiffness, own_out, tables_out, record, springs, sems):
+    moves = ((images.at[0], own_out), (tables, tables_out))
     copies = [pltpu.make_async_copy(src, dst, sems.at[i]) for i, (src, dst) in enumerate(moves)]
     for copy in copies:
         copy.start()
-    for copy in copies[:6]:
+    record[...] = jnp.zeros((1, PATCH), f32)
+    for i in range(2):
+        record[:, pl.ds(i * COLS, COLS)] = offsets[0, i].astype(f32)
+        record[:, pl.ds((2 + i) * COLS, COLS)] = initial[0, i]
+    level_id = lax.broadcasted_iota(jnp.int32, stiffness.shape, 0)
+    for sweep in range(SWEEPS):
+        picked = jnp.sum(jnp.where(level_id == plan[sweep], stiffness[...], 0.0), axis=0, keepdims=True)
+        for i in range(2):
+            springs[pl.ds(2 * sweep + i, 1), :] = jnp.broadcast_to(picked[:, i : i + 1], (1, PATCH))
+    for copy in copies:
         copy.wait()
+
+
+def prepare(plan, images, offsets, initial, stiffness):
+    tables = jnp.asarray(constant_tables())
+    in_vmem = pl.BlockSpec(memory_space=pltpu.VMEM)
+    anywhere = pl.BlockSpec(memory_space=pl.ANY)
+    return pl.pallas_call(
+        prepare_kernel,
+        out_shape=[
+            jax.ShapeDtypeStruct(images.shape[1:], bf16),
+            jax.ShapeDtypeStruct(tables.shape, bf16),
+            jax.ShapeDtypeStruct((1, PATCH), f32),
+            jax.ShapeDtypeStruct((8, PATCH), f32),
+        ],
+        in_specs=[pl.BlockSpec(memory_space=pltpu.SMEM), anywhere, anywhere, in_vmem, in_vmem, in_vmem],
+        out_specs=[in_vmem] * 4,
+        scratch_shapes=[pltpu.SemaphoreType.DMA((2,))],
+        compiler_params=pltpu.CompilerParams(vmem_limit_bytes=VMEM_LIMIT),
+    )(plan, images, tables, offsets, initial, stiffness)
+
+
+def flow_kernel(own, below, near, near_below, record, remote, tables, out, spec, lagged):
+    columns = table(tables, "columns")
+    spread = table(tables, "spread")
+    nyq_t = table(tables, "nyquist")
+    rows_t = jnp.concatenate([table(tables, "rows"), jnp.concatenate([nyq_t[:, :PATCH], nyq_t[:, PATCH:]], axis=0)], axis=1)
 
     def finish_spectrum(m, stacked, table):
         product = dot(table, stacked).astype(bf16)
@@ -151,7 +166,9 @@
     nyquist = jnp.zeros((4 * HALF, PATCH), f32)
     for m in range(PAIRS):
         span = 2 * PATCH if m < PAIRS - 1 else WIDTH - m * PATCH
-        seg = dot(image[:, pl.ds(m * PATCH, span)], rows_t[pl.ds(0, span), :])
+        tiles = [ref[0, :, pl.ds(m * PATCH, span)] for ref in (below, near, near_below)]
+        tiles.insert(0, own[:, pl.ds(m * PATCH, span)])
+        seg = dot(jnp.concatenate(tiles, axis=0), rows_t[:span])
         nyquist = jnp.where(lane_4 // 2 == m, seg[:, 2 * PATCH :], nyquist)
         seg = seg[:, : 2 * PATCH].astype(bf16)
         stacked = jnp.concatenate(
@@ -161,12 +178,10 @@
             ],
             axis=0,
         )
-        energies.append(finish_spectrum(m, stacked, cols_t[...]))
+        energies.append(finish_spectrum(m, stacked, columns))
     seg = nyquist.astype(bf16)
     stacked = jnp.concatenate([seg[:PATCH], seg[PATCH:]], axis=1)
-    energy_64 = finish_spectrum(PAIRS, stacked, cols_t[:, pl.ds(0, PATCH)])
-    for copy in copies[6:]:
-        copy.wait()
+    energy_64 = finish_spectrum(PAIRS, stacked, columns[:, :PATCH])
 
     lane = lax.broadcasted_iota(jnp.int32, (PAIRS, PATCH), 1)
     pair = lax.broadcasted_iota(jnp.int32, (PAIRS, PATCH), 0)
@@ -180,7 +195,7 @@
 
     def totals(main, extra):
         left = jnp.concatenate([main * weight, jnp.where(first_16, extra, 0.0)], axis=1)
-        found = dot(three_parts(left), spread_t[...])
+        found = dot(three_parts(left), spread)
         found = found[:PAIRS] + found[PAIRS : 2 * PAIRS] + found[2 * PAIRS :]
         by_pair, by_patch = halves(found)
         by_patch = jnp.sum(jnp.where(first_16, by_patch, 0.0), axis=0, keepdims=True) + extra
@@ -208,7 +223,7 @@
         white = jnp.concatenate([cross_re * inverse, cross_im * inverse], axis=0)
         high = white.astype(bf16)
         low = (white - high.astype(f32)).astype(bf16)
-        found = dot(lag_y[...], jnp.concatenate([high, low], axis=1))
+        found = dot(table(tables, "lag_y"), jnp.concatenate([high, low], axis=1))
         part = found[: 2 * SHIFTS, :PATCH] + found[: 2 * SHIFTS, PATCH:] + found[2 * SHIFTS :, :PATCH]
         lagged[pl.ds(m * SHIFTS, SHIFTS), pl.ds(0, PATCH)] = part[:SHIFTS]
         lagged[pl.ds(m * SHIFTS, SHIFTS), pl.ds(PATCH, PATCH)] = part[SHIFTS:]
@@ -219,19 +234,14 @@
     high = left.astype(bf16)
     low = (left - high.astype(f32)).astype(bf16)
     rows_all = PAIRS * SHIFTS
-    found = dot(jnp.concatenate([high, low], axis=0), lag_x[...])
+    found = dot(jnp.concatenate([high, low], axis=0), table(tables, "lag_x"))
     surface = found[:rows_all, :PATCH] + found[:rows_all, PATCH:] + found[rows_all:, :PATCH]
     surface = surface.reshape(PAIRS, SHIFTS, PATCH)
 
-    record[...] = jnp.zeros((1, PATCH), f32)
-    for i in range(2):
-        record[:, pl.ds(i * COLS, COLS)] = shift_in[i].astype(f32)
-        record[:, pl.ds((2 + i) * COLS, COLS)] = node_in[0, i]
-        record[:, pl.ds((4 + i) * COLS, COLS)] = node_in[1, i]
     rec = record[...]
     at_y = jnp.where(first_16, rec, 0.0)
     at_x = jnp.where(own_pair & (lane >= COLS) & (lane < 2 * COLS), rec, 0.0)
-    gather = spread_t[pl.ds(0, PATCH), pl.ds(PATCH, PATCH)]
+    gather = spread[:PATCH, PATCH:]
     shifts = lax.dot_general(
         jnp.concatenate([at_y, at_x], axis=0).astype(bf16),
         gather,
@@ -262,35 +272,26 @@
     flow = rec + 0.5 * slope / (1.0 + jnp.abs(bend))
     result = jnp.where(lane_1 < 2 * COLS, flow, rec)
     out[...] = jnp.broadcast_to(result, out.shape)
-
-
-def pair_flow(own, below, near, near_below, offsets, initial, remote_initial, copies):
-    tables = [jnp.asarray(t) for t in constant_tables()]
-    operands = (own, below, near, near_below, offsets, initial, remote_initial, *tables)
+    for i in range(2):
+        out[:, pl.ds((4 + i) * COLS, COLS)] = jnp.broadcast_to(remote[0, i], (out.shape[0], COLS))
+
+
+def pair_flow(own, below, near, near_below, record, remote_initial, tables, copies):
+    operands = (own, below, near, near_below, record, remote_initial, tables)
     return pl.pallas_call(
         flow_kernel,
         out_shape=jax.ShapeDtypeStruct((copies, PATCH), f32),
-        in_specs=[pl.BlockSpec(memory_space=pl.ANY)] * len(operands),
+        in_specs=[pl.BlockSpec(memory_space=pltpu.VMEM)] * len(operands),
         out_specs=pl.BlockSpec(memory_space=pltpu.VMEM),
         scratch_shapes=[
-            pltpu.VMEM((4 * HALF, WIDTH), bf16),
-            *[pltpu.VMEM(t.shape, bf16) for t in tables],
-            pltpu.VMEM(offsets.shape[1:], jnp.int32),
-            pltpu.VMEM((2,) + initial.shape[1:], f32),
-            pltpu.VMEM((1, PATCH), f32),
             pltpu.VMEM((PAIRS + 1, 2 * PATCH, 2 * PATCH), bf16),
             pltpu.VMEM(((PAIRS + 1) * SHIFTS, 2 * PATCH), f32),
-            pltpu.SemaphoreType.DMA((len(operands),)),
         ],
         compiler_params=pltpu.CompilerParams(vmem_limit_bytes=VMEM_LIMIT),
     )(*operands)
 
 
-def relax_kernel(plan, stiffness_h, ring_h, other_h, flow_out, moving_out, stiffness, ring, other, sems):
-    moves = ((stiffness_h, stiffness), (ring_h, ring), (other_h, other))
-    copies = [pltpu.make_async_copy(src, dst, sems.at[i]) for i, (src, dst) in enumerate(moves)]
-    for copy in copies:
-        copy.start()
+def relax_kernel(springs, ring, other, flow_out, moving_out):
     sec = lax.axis_index("sec")
     row = lax.axis_index("row")
     last_row = lax.axis_size("row") - 1
@@ -313,9 +314,6 @@
     has_down = [(r < last_row).astype(f32) for r in at_rows]
     first = in_ring == 0
     final = in_ring == RING - 1
-    for copy in copies:
-        copy.wait()
-    level_id = lax.broadcasted_iota(jnp.int32, stiffness.shape, 0)
     here = ring[...]
     beyond = other[...]
     flows = [jnp.where(valid, b, 0.0) for b in (here, beyond)]
@@ -327,9 +325,8 @@
         return jnp.concatenate([x[by:], x[:by]], axis=0)
 
     for sweep in range(SWEEPS):
-        picked = jnp.sum(jnp.where(level_id == plan[sweep], stiffness[...], 0.0), axis=0, keepdims=True)
-        spring = picked[:, 0:1]
-        tether = picked[:, 1:2]
+        spring = springs[pl.ds(2 * sweep, 1), :]
+        tether = springs[pl.ds(2 * sweep + 1, 1), :]
         near_x, far_x = moving
         edge_above = jnp.where(other_first, moved(far_x, RING - 1), moved(third, RING - 1))
         edge_below = jnp.where(other_first, moved(third, 1 - RING), moved(far_x, 1 - RING))
@@ -357,21 +354,15 @@
         ref[0, 1] = line[:, COLS : 2 * COLS]
 
 
-def relax(plan, stiffness, ring, other, shape):
-    anywhere = pl.BlockSpec(memory_space=pl.ANY)
+def relax(springs, ring, other, shape):
+    in_vmem = pl.BlockSpec(memory_space=pltpu.VMEM)
     return pl.pallas_call(
         relax_kernel,
         out_shape=[jax.ShapeDtypeStruct(shape, f32)] * 2,
-        in_specs=[pl.BlockSpec(memory_space=pltpu.SMEM)] + [anywhere] * 3,
-        out_specs=[pl.BlockSpec(memory_space=pltpu.VMEM)] * 2,
-        scratch_shapes=[
-            pltpu.VMEM(stiffness.shape, f32),
-            pltpu.VMEM(ring.shape, f32),
-            pltpu.VMEM(ring.shape, f32),
-            pltpu.SemaphoreType.DMA((3,)),
-        ],
+        in_specs=[in_vmem] * 3,
+        out_specs=[in_vmem] * 2,
         compiler_params=pltpu.CompilerParams(vmem_limit_bytes=VMEM_LIMIT),
-    )(plan, stiffness, ring, other)
+    )(springs, ring, other)
 
 
 def shifted(block, axis, distance):
@@ -391,19 +382,23 @@
 
 def per_device(images, initial, offsets, stiffness, plan):
     rows = lax.axis_size("row")
-    near = shifted(images, "sec", -1)
     below = shifted(images, "row", -1)
     remote_initial = lax.ppermute(initial, "row", ring_route(rows, False))
+    near = shifted(images, "sec", -1)
+    own, tables, record, springs = prepare(plan, images, offsets, initial, stiffness)
+    below, remote_initial, own, tables, record, springs = lax.optimization_barrier(
+        (below, remote_initial, own, tables, record, springs)
+    )
     near_below = shifted(below, "sec", -1)
     count = SECS * RING
-    mine = pair_flow(images, below, near, near_below, offsets, initial, remote_initial, count)
+    mine = pair_flow(own, below, near, near_below, record, remote_initial, tables, count)
     groups = [
         [s * rows + RING * g + j for s in range(SECS) for j in range(RING)] for g in range(rows // RING)
     ]
     ring = lax.all_to_all(mine.reshape(count, 1, PATCH), ("sec", "row"), 0, 0, axis_index_groups=groups)
     other = lax.ppermute(ring, "row", ring_route(rows, True))
     return tuple(
-        relax(plan, stiffness, ring.reshape(count, PATCH), other.reshape(count, PATCH), initial.shape)
+        relax(springs, ring.reshape(count, PATCH), other.reshape(count, PATCH), initial.shape)
     )
 
 

time: 61.5 us -> 47.4 us (0.77)
  waiting for transfers between devices: 15.1 us -> 8.72 us
  local copies, waits for them, and re-layouts: 7.42 us -> 2.77 us
  blocking collectives: 16.8 us -> 14.8 us
  Pallas kernels: 6.24 us -> 4.75 us
    unnamed x21 -> x11, local copies, waits for them, and re-layouts: 7.42 us -> 2.77 us
    ppermute x3, waiting for transfers between devices: 5.3 us -> 2.31 us  [shifted(): return lax.ppermute(block, axis, route)]
    ppermute x1, waiting for transfers between devices: 2.93 us -> 0.01 us  [per_device(): remote_initial = lax.ppermute(initial, 'row', ring_route(rows, False))]
    all_to_all x1, blocking collectives: 16.8 us -> 14.8 us  [per_device(): lax.all_to_all(mine.reshape(count, 1, PATCH), ('sec', 'row'), 0, 0, axis_...]
    pallas_call x1, Pallas kernels: 4.69 us -> 2.71 us  [pair_flow(): pl.pallas_call(flow_kernel, out_shape=jax.ShapeDtypeStruct((copies, PATCH...]
    pallas_call x0 -> x1, Pallas kernels: none -> 1.1 us  [prepare(): pl.pallas_call(prepare_kernel, out_shape=[jax.ShapeDtypeStruct(images.sha...]
    pallas_call x1, Pallas kernels: 1.55 us -> 0.94 us  [relax(): pl.pallas_call(relax_kernel, out_shape=[jax.ShapeDtypeStruct(shape, f32)]...]
  transfers between devices with their start and end apart: 5 -> 5, of which waited for: 3 -> 2; matrix products, arithmetic and copies ran while one was open for 0% -> 2% of each run, Pallas kernels for 0% -> 2%
where the time goes in v3:
time: 47.4 us; the launch traced here: 47.1 us
  starting transfers between devices  15.3 us (32%)
  blocking collectives  14.8 us (31%)
  waiting for transfers between devices  8.72 us (18%)
  Pallas kernels  4.75 us (10%)
  local copies, waits for them, and re-layouts  2.77 us (6%)
  between operations  0.74 us (2%)
    all_to_all x1, blocking collectives, per_device(): lax.all_to_all(mine.reshape(count, 1, PATCH), ('sec', 'row'), 0, 0, axis_...  14.8 us
    ppermute x3, starting transfers between devices, shifted(): return lax.ppermute(block, axis, route)  10.2 us
    ppermute x1, waiting for transfers between devices, per_device(): other = lax.ppermute(ring, 'row', ring_route(rows, True))  6.41 us
    unnamed x11, local copies, waits for them, and re-layouts  2.77 us
    ppermute x1, starting transfers between devices, per_device(): remote_initial = lax.ppermute(initial, 'row', ring_route(rows, False))  2.74 us
    pallas_call x1, Pallas kernels, pair_flow(): pl.pallas_call(flow_kernel, out_shape=jax.ShapeDtypeStruct((copies, PATCH...  2.71 us
    ppermute x1, starting transfers between devices, per_device(): other = lax.ppermute(ring, 'row', ring_route(rows, True))  2.44 us
    ppermute x3, waiting for transfers between devices, shifted(): return lax.ppermute(block, axis, route)  2.31 us
  transfers between devices with their start and end apart: 5, of which 2 were waited for; matrix products, arithmetic and copies ran while one was open for 2% of the time, Pallas kernels for 2%

profile of v3, /device:TPU:256, one launch (start us, length us, event | category | flops | bytes accessed | tf_op | source)
XLA Modules:
  0.0 47.1 jit_solution(1966871076878560688)
XLA Ops:
  0.6 0.0 copy-start.3
  0.6 0.0 copy-start.4
  0.7 0.0 copy-start.2
  0.7 7.6 %collective-permute-start = (bf16[1,64,1088]{2,1,0:T(8,128)(2,1)}, bf16[1,64,1088]{2,1,0:T(8,128)(2,1)S(1)}, u32[]{:S(2)}, u32[]{:S(2)}) collective-permute-start(bf16[1,64,1088]{2,1,0:T(8,128)(2,1)} %images.1), channel_id=1, source_target_pairs={{1,0},{2,1},{3,2},{4,3},{5,4},{6,5},{7,6},{8,7},{9,8},{10,9},{11,1... | collective-permute-start | bytes 417800 | tf_op jit(solution)/shard_map/ppermute | solution.py:371
  8.2 1.3 %collective-permute-start.2 = (bf16[1,64,1088]{2,1,0:T(8,128)(2,1)}, bf16[1,64,1088]{2,1,0:T(8,128)(2,1)S(1)}, u32[]{:S(2)}, u32[]{:S(2)}) collective-permute-start(bf16[1,64,1088]{2,1,0:T(8,128)(2,1)} %images.1), channel_id=1, source_target_pairs={{128,0},{256,128},{384,256},{129,1},{257,129},{385,257},{130,2},{2... | collective-permute-start | bytes 417800 | tf_op jit(solution)/shard_map/ppermute | solution.py:371
  9.5 2.7 %collective-permute-start.1 = (f32[1,2,1,16]{3,2,1,0:T(1,128)}, f32[1,2,1,16]{3,2,1,0:T(1,128)S(1)}, u32[]{:S(2)}, u32[]{:S(2)}) collective-permute-start(f32[1,2,1,16]{3,2,1,0:T(1,128)} %initial.1), channel_id=1, source_target_pairs={{4,0},{5,1},{8,4},{9,5},{2,6},{3,7},{12,8},{13,9},{6,10},{7,11},{1... | collective-permute-start | bytes 392 | tf_op jit(solution)/shard_map/ppermute | solution.py:386
  12.3 0.8 %copy.9.stiffness = f32[8,2]{1,0:T(8,128)S(1)} copy(f32[8,2]{0,1:T(2,128)} %param.9) | data formatting | bytes 128 | tf_op args[3]
  13.0 0.0 copy-done.3
  13.1 0.0 copy-done.4
  13.1 0.0 copy-done.2
  13.1 0.0 copy-start
  13.1 1.1 %copy-done = bf16[1344,256]{1,0:T(8,128)(2,1)S(1)} copy-done((bf16[1344,256]{1,0:T(8,128)(2,1)S(1)}, bf16[1344,256]{1,0:T(8,128)(2,1)}, u32[]{:S(2)}) %copy-start) | copy-done | bytes 688152
  14.2 0.9 %copy-done.1 = bf16[1,64,1088]{2,1,0:T(8,128)(2,1)S(1)} copy-done((bf16[1,64,1088]{2,1,0:T(8,128)(2,1)S(1)}, bf16[1,64,1088]{2,1,0:T(8,128)(2,1)}, u32[]{:S(2)}) %copy-start.1) | copy-done | bytes 139288
  15.1 1.1 %shard_map.77 = (bf16[64,1088]{1,0:T(8,128)(2,1)S(1)}, bf16[1344,256]{1,0:T(8,128)(2,1)S(1)}, f32[1,128]{1,0:T(1,128)S(1)}, f32[8,128]{1,0:T(8,128)S(1)}) custom-call(s32[3]{0:T(128)S(1)} %copy-done.4, bf16[1,64,1088]{2,1,0:T(8,128)(2,1)S(1)} %copy-done.1, bf16[1344,256]{1,0:T(8,128)(2,1)S(1)} %copy-done, s32[1,2,1,16]{3,2,1,0:T(1,128)S(1)} %copy-done.2, ...), custom_call_target="tpu_custom_call" | custom-call | tf_op jit(solution)/shard_map/pallas_call | solution.py:137
  16.2 0.0 collective-permute-done.1.remote
  16.2 0.0 collective-permute-done.below
  16.2 1.3 %collective-permute-start.3 = (bf16[1,64,1088]{2,1,0:T(8,128)(2,1)S(1)}, bf16[1,64,1088]{2,1,0:T(8,128)(2,1)S(1)}, u32[]{:S(2)}, u32[]{:S(2)}) collective-permute-start(bf16[1,64,1088]{2,1,0:T(8,128)(2,1)S(1)} %collective-permute-done.below), channel_id=1, source_target_pairs={{128,0},{256,128},{384,256},{129,1},{257,129},{385,257},{130,2},{2... | collective-permute-start | bytes 417800 | tf_op jit(solution)/shard_map/ppermute | solution.py:371
  17.5 0.0 collective-permute-done.2.near
  17.5 2.3 %collective-permute-done.3.near_below = bf16[1,64,1088]{2,1,0:T(8,128)(2,1)S(1)} collective-permute-done((bf16[1,64,1088]{2,1,0:T(8,128)(2,1)S(1)}, bf16[1,64,1088]{2,1,0:T(8,128)(2,1)S(1)}, u32[]{:S(2)}, u32[]{:S(2)}) %collective-permute-start.3) | collective-permute-done | bytes 139296 | tf_op jit(solution)/shard_map/ppermute | solution.py:371
  19.8 2.7 %shard_map.78 = f32[16,128]{1,0:T(8,128)S(1)} custom-call(bf16[64,1088]{1,0:T(8,128)(2,1)S(1)} %get-tuple-element.17.own, bf16[1,64,1088]{2,1,0:T(8,128)(2,1)S(1)} %collective-permute-done.below, bf16[1,64,1088]{2,1,0:T(8,128)(2,1)S(1)} %collective-permute-done.2.near, bf16[1,64,1088]{2,1,0:T(8,128)(2,1)S(1)} %collective-permute-done.3.near_below, ...), custom_call_target="tpu_custom_call" | custom-call | tf_op jit(solution)/shard_map/pallas_call | solution.py:281
  22.5 14.8 %all_to_all.5 = f32[16,1,128]{2,1,0:T(1,128)S(1)} all-to-all(f32[16,1,128]{2,1,0:T(1,128)S(1)} %bitcast.6), channel_id=1, replica_groups={{0,1,2,3,128,129,130,131,256,257,258,259,384,385,386,387},{4,5,6,7,132,..., dimensions={0} | all-to-all | bytes 16384 | tf_op jit(solution)/shard_map/all_to_all | solution.py:398
  37.3 2.4 %collective-permute-start.4 = (f32[16,1,128]{2,0,1:T(8,128)S(1)}, f32[16,1,128]{2,0,1:T(8,128)S(1)}, u32[]{:S(2)}, u32[]{:S(2)}) collective-permute-start(f32[16,1,128]{2,0,1:T(8,128)S(1)} %bitcast.7), channel_id=1, source_target_pairs={{6,2},{7,3},{0,4},{1,5},{10,6},{11,7},{4,8},{5,9},{14,10},{15,11},... | collective-permute-start | bytes 24584 | tf_op jit(solution)/shard_map/ppermute | solution.py:399
  39.7 6.4 %collective-permute-done.4 = f32[16,1,128]{2,0,1:T(8,128)S(1)} collective-permute-done((f32[16,1,128]{2,0,1:T(8,128)S(1)}, f32[16,1,128]{2,0,1:T(8,128)S(1)}, u32[]{:S(2)}, u32[]{:S(2)}) %collective-permute-start.4) | collective-permute-done | bytes 8224 | tf_op jit(solution)/shard_map/ppermute | solution.py:399
  46.1 0.9 %shard_map.79 = (f32[1,2,1,16]{3,2,1,0:T(1,128)}, f32[1,2,1,16]{3,2,1,0:T(1,128)}) custom-call(f32[8,128]{1,0:T(8,128)S(1)} %get-tuple-element.16.springs, f32[16,128]{1,0:T(8,128)S(1)} %bitcast.8, f32[16,128]{1,0:T(8,128)S(1)} %bitcast.9), custom_call_target="tpu_custom_call" | custom-call | tf_op jit(solution)/shard_map/pallas_call | solution.py:359
  (1 shorter events, 0.0 us)
Async XLA Ops:
  0.6 12.4 %copy-start.3 = (f32[1,2,1,16]{3,2,1,0:T(1,128)S(1)}, f32[1,2,1,16]{3,2,1,0:T(1,128)}, u32[]{:S(2)}) copy-start(f32[1,2,1,16]{3,2,1,0:T(1,128)} %initial.1) | copy-start | bytes 388
  0.6 12.4 %copy-start.4 = (s32[3]{0:T(128)S(1)}, s32[3]{0:T(128)}, u32[]{:S(2)}) copy-start(s32[3]{0:T(128)} %plan.1) | copy-start | bytes 40
  0.7 12.4 %copy-start.2 = (s32[1,2,1,16]{3,2,1,0:T(1,128)S(1)}, s32[1,2,1,16]{3,2,1,0:T(1,128)}, u32[]{:S(2)}) copy-start(s32[1,2,1,16]{3,2,1,0:T(1,128)} %offsets.1) | copy-start | bytes 388
  0.7 15.5 %collective-permute-start = (bf16[1,64,1088]{2,1,0:T(8,128)(2,1)}, bf16[1,64,1088]{2,1,0:T(8,128)(2,1)S(1)}, u32[]{:S(2)}, u32[]{:S(2)}) collective-permute-start(bf16[1,64,1088]{2,1,0:T(8,128)(2,1)} %images.1), channel_id=1, source_target_pairs={{1,0},{2,1},{3,2},{4,3},{5,4},{6,5},{7,6},{8,7},{9,8},{10,9},{11,1... | collective-permute-start | bytes 417800 | tf_op jit(solution)/shard_map/ppermute | solution.py:371
  8.2 9.3 %collective-permute-start.2 = (bf16[1,64,1088]{2,1,0:T(8,128)(2,1)}, bf16[1,64,1088]{2,1,0:T(8,128)(2,1)S(1)}, u32[]{:S(2)}, u32[]{:S(2)}) collective-permute-start(bf16[1,64,1088]{2,1,0:T(8,128)(2,1)} %images.1), channel_id=1, source_target_pairs={{128,0},{256,128},{384,256},{129,1},{257,129},{385,257},{130,2},{2... | collective-permute-start | bytes 417800 | tf_op jit(solution)/shard_map/ppermute | solution.py:371
  9.5 6.6 %collective-permute-start.1 = (f32[1,2,1,16]{3,2,1,0:T(1,128)}, f32[1,2,1,16]{3,2,1,0:T(1,128)S(1)}, u32[]{:S(2)}, u32[]{:S(2)}) collective-permute-start(f32[1,2,1,16]{3,2,1,0:T(1,128)} %initial.1), channel_id=1, source_target_pairs={{4,0},{5,1},{8,4},{9,5},{2,6},{3,7},{12,8},{13,9},{6,10},{7,11},{1... | collective-permute-start | bytes 392 | tf_op jit(solution)/shard_map/ppermute | solution.py:386
  13.1 1.1 %copy-start = (bf16[1344,256]{1,0:T(8,128)(2,1)S(1)}, bf16[1344,256]{1,0:T(8,128)(2,1)}, u32[]{:S(2)}) copy-start(bf16[1344,256]{1,0:T(8,128)(2,1)} %constant.2.clone.tables) | copy-start | bytes 2064388
  14.2 0.9 %copy-start.1 = (bf16[1,64,1088]{2,1,0:T(8,128)(2,1)S(1)}, bf16[1,64,1088]{2,1,0:T(8,128)(2,1)}, u32[]{:S(2)}) copy-start(bf16[1,64,1088]{2,1,0:T(8,128)(2,1)} %images.1) | copy-start | bytes 417796
  16.2 3.6 %collective-permute-start.3 = (bf16[1,64,1088]{2,1,0:T(8,128)(2,1)S(1)}, bf16[1,64,1088]{2,1,0:T(8,128)(2,1)S(1)}, u32[]{:S(2)}, u32[]{:S(2)}) collective-permute-start(bf16[1,64,1088]{2,1,0:T(8,128)(2,1)S(1)} %collective-permute-done.below), channel_id=1, source_target_pairs={{128,0},{256,128},{384,256},{129,1},{257,129},{385,257},{130,2},{2... | collective-permute-start | bytes 417800 | tf_op jit(solution)/shard_map/ppermute | solution.py:371
  37.3 8.9 %collective-permute-start.4 = (f32[16,1,128]{2,0,1:T(8,128)S(1)}, f32[16,1,128]{2,0,1:T(8,128)S(1)}, u32[]{:S(2)}, u32[]{:S(2)}) collective-permute-start(f32[16,1,128]{2,0,1:T(8,128)S(1)} %bitcast.7), channel_id=1, source_target_pairs={{6,2},{7,3},{0,4},{1,5},{10,6},{11,7},{4,8},{5,9},{14,10},{15,11},... | collective-permute-start | bytes 24584 | tf_op jit(solution)/shard_map/ppermute | solution.py:399

commit v4 on v3

--- a/solution.py
+++ b/solution.py
@@ -19,6 +19,8 @@
 RING = 4
 SHIFTS = 16
 REACH = 5
+WINDOW = 8
+REACH_ROWS = 3
 WIDTH = 1088
 
 step_size = 0.2
@@ -87,12 +89,14 @@
     same = ((lane // HALF)[:, None] == (lane // HALF)[None, :]).astype(np.float32)
     blank = np.zeros((PATCH, PATCH), np.float32)
     spread = np.block([[same, gather], [single.T, blank]])
-    packed = [rows, np.concatenate([nyquist[:PATCH], nyquist[PATCH:]], axis=1), columns, spread, lag_y, lag_x]
+    turned = np.roll(columns.reshape(2 * PATCH, 2, PATCH), HALF, axis=2).reshape(2 * PATCH, 2 * PATCH)
+    packed = [rows, np.concatenate([nyquist[:PATCH], nyquist[PATCH:]], axis=1), spread, lag_y, lag_x, columns, turned]
     return np.concatenate([np.asarray(t).astype(ml_dtypes.bfloat16) for t in packed], axis=0)
 
 
-TABLE_ROWS = {"rows": (0, 256), "nyquist": (256, 128), "columns": (384, 256), "spread": (640, 256)}
-TABLE_ROWS |= {"lag_y": (896, 64), "lag_x": (960, 384)}
+TABLE_ROWS = {"rows": (0, 256), "nyquist": (256, 128), "spread": (384, 256)}
+TABLE_ROWS |= {"lag_y": (640, 64), "lag_x": (704, 384), "columns": (1088, 256)}
+FIXED_ROWS = 1088
 
 
 def table(ref, name):
@@ -112,11 +116,24 @@
     return jnp.dot(a, b, preferred_element_type=f32)
 
 
+def takes_row_above(sec):
+    return sec < 2
+
+
 def prepare_kernel(plan, images, tables, offsets, initial, stiffness, own_out, tables_out, record, springs, sems):
-    moves = ((images.at[0], own_out), (tables, tables_out))
+    downward = takes_row_above(lax.axis_index("sec"))
+    columns, length = TABLE_ROWS["columns"]
+    chosen = pl.multiple_of(columns + length * downward.astype(jnp.int32), length // 2)
+    moves = (
+        (tables.at[pl.ds(0, FIXED_ROWS)], tables_out.at[pl.ds(0, FIXED_ROWS)]),
+        (tables.at[pl.ds(chosen, length)], tables_out.at[pl.ds(columns, length)]),
+    )
     copies = [pltpu.make_async_copy(src, dst, sems.at[i]) for i, (src, dst) in enumerate(moves)]
     for copy in copies:
         copy.start()
+    past = downward & (lax.axis_index("row") == 0)
+    own = images[0]
+    own_out[...] = jnp.where(jnp.broadcast_to(past, own.shape), jnp.zeros_like(own), own)
     record[...] = jnp.zeros((1, PATCH), f32)
     for i in range(2):
         record[:, pl.ds(i * COLS, COLS)] = offsets[0, i].astype(f32)
@@ -132,24 +149,25 @@
 
 def prepare(plan, images, offsets, initial, stiffness):
     tables = jnp.asarray(constant_tables())
+    columns, length = TABLE_ROWS["columns"]
     in_vmem = pl.BlockSpec(memory_space=pltpu.VMEM)
     anywhere = pl.BlockSpec(memory_space=pl.ANY)
     return pl.pallas_call(
         prepare_kernel,
         out_shape=[
             jax.ShapeDtypeStruct(images.shape[1:], bf16),
-            jax.ShapeDtypeStruct(tables.shape, bf16),
+            jax.ShapeDtypeStruct((columns + length, 2 * PATCH), bf16),
             jax.ShapeDtypeStruct((1, PATCH), f32),
             jax.ShapeDtypeStruct((8, PATCH), f32),
         ],
-        in_specs=[pl.BlockSpec(memory_space=pltpu.SMEM), anywhere, anywhere, in_vmem, in_vmem, in_vmem],
+        in_specs=[pl.BlockSpec(memory_space=pltpu.SMEM), in_vmem, anywhere, in_vmem, in_vmem, in_vmem],
         out_specs=[in_vmem] * 4,
         scratch_shapes=[pltpu.SemaphoreType.DMA((2,))],
         compiler_params=pltpu.CompilerParams(vmem_limit_bytes=VMEM_LIMIT),
     )(plan, images, tables, offsets, initial, stiffness)
 
 
-def flow_kernel(own, below, near, near_below, record, remote, tables, out, spec, lagged):
+def flow_kernel(own, across, near, near_across, record, far_offsets, tables, out, spec, lagged, shift_row):
     columns = table(tables, "columns")
     spread = table(tables, "spread")
     nyq_t = table(tables, "nyquist")
@@ -166,7 +184,7 @@
     nyquist = jnp.zeros((4 * HALF, PATCH), f32)
     for m in range(PAIRS):
         span = 2 * PATCH if m < PAIRS - 1 else WIDTH - m * PATCH
-        tiles = [ref[0, :, pl.ds(m * PATCH, span)] for ref in (below, near, near_below)]
+        tiles = [ref[0, :, pl.ds(m * PATCH, span)] for ref in (across, near, near_across)]
         tiles.insert(0, own[:, pl.ds(m * PATCH, span)])
         seg = dot(jnp.concatenate(tiles, axis=0), rows_t[:span])
         nyquist = jnp.where(lane_4 // 2 == m, seg[:, 2 * PATCH :], nyquist)
@@ -238,7 +256,12 @@
     surface = found[:rows_all, :PATCH] + found[:rows_all, PATCH:] + found[rows_all:, :PATCH]
     surface = surface.reshape(PAIRS, SHIFTS, PATCH)
 
+    for i in range(2):
+        shift_row[:, pl.ds(i * COLS, COLS)] = far_offsets[0, i].astype(f32)
     rec = record[...]
+    lane_1 = lax.broadcasted_iota(jnp.int32, (1, PATCH), 1)
+    downward = jnp.broadcast_to(takes_row_above(lax.axis_index("sec")), (1, PATCH))
+    rec = jnp.where(downward & (lane_1 < 2 * COLS), shift_row[...], rec)
     at_y = jnp.where(first_16, rec, 0.0)
     at_x = jnp.where(own_pair & (lane >= COLS) & (lane < 2 * COLS), rec, 0.0)
     gather = spread[:PATCH, PATCH:]
@@ -266,18 +289,15 @@
     found = found[: 4 * PAIRS] + found[4 * PAIRS : 8 * PAIRS] + found[8 * PAIRS :]
     found = found.reshape(4, PAIRS, PATCH)
     found = jnp.sum(jnp.where(own_pair[None], found, 0.0), axis=1) * (1.0 / (PATCH * PATCH))
-    lane_1 = lax.broadcasted_iota(jnp.int32, (1, PATCH), 1)
     slope = jnp.where(lane_1 < COLS, found[0:1], found[2:3])
     bend = jnp.where(lane_1 < COLS, found[1:2], found[3:4])
     flow = rec + 0.5 * slope / (1.0 + jnp.abs(bend))
     result = jnp.where(lane_1 < 2 * COLS, flow, rec)
     out[...] = jnp.broadcast_to(result, out.shape)
-    for i in range(2):
-        out[:, pl.ds((4 + i) * COLS, COLS)] = jnp.broadcast_to(remote[0, i], (out.shape[0], COLS))
-
-
-def pair_flow(own, below, near, near_below, record, remote_initial, tables, copies):
-    operands = (own, below, near, near_below, record, remote_initial, tables)
+
+
+def pair_flow(own, across, near, near_across, record, far_offsets, tables, copies):
+    operands = (own, across, near, near_across, record, far_offsets, tables)
     return pl.pallas_call(
         flow_kernel,
         out_shape=jax.ShapeDtypeStruct((copies, PATCH), f32),
@@ -286,120 +306,119 @@
         scratch_shapes=[
             pltpu.VMEM((PAIRS + 1, 2 * PATCH, 2 * PATCH), bf16),
             pltpu.VMEM(((PAIRS + 1) * SHIFTS, 2 * PATCH), f32),
+            pltpu.VMEM((1, PATCH), f32),
         ],
         compiler_params=pltpu.CompilerParams(vmem_limit_bytes=VMEM_LIMIT),
     )(*operands)
 
 
-def relax_kernel(springs, ring, other, flow_out, moving_out):
+def relax_kernel(springs, before, mid, after, flow_out, moving_out, nodes):
     sec = lax.axis_index("sec")
     row = lax.axis_index("row")
     last_row = lax.axis_size("row") - 1
     place = lax.rem(row, RING)
-    base = row - place
-    count = SECS * RING
-    node = lax.broadcasted_iota(jnp.int32, (count, PATCH), 0)
-    lane = lax.broadcasted_iota(jnp.int32, (count, PATCH), 1)
-    in_ring = node % RING
-    section = node // RING
-    other_first = jnp.broadcast_to(place, (count, PATCH)) < RING // 2
-    valid = (section < SECS - 1) & (lane < 2 * COLS)
-    valid_up = valid.astype(f32)
-    has_left = (lane % COLS > 0).astype(f32)
-    has_right = (lane % COLS < COLS - 1).astype(f32)
-    row_here = base + in_ring
-    row_other = row_here + jnp.where(other_first, -RING, RING)
-    at_rows = (row_here, row_other)
-    has_up = [(r > 0).astype(f32) for r in at_rows]
-    has_down = [(r < last_row).astype(f32) for r in at_rows]
-    first = in_ring == 0
-    final = in_ring == RING - 1
-    here = ring[...]
-    beyond = other[...]
-    flows = [jnp.where(valid, b, 0.0) for b in (here, beyond)]
-    moving = [pltpu.roll(b, PATCH - 2 * COLS, 1) for b in (here, beyond)]
-    third = pltpu.roll(here, PATCH - 4 * COLS, 1)
-
-    def moved(x, by):
-        by = by % count
-        return jnp.concatenate([x[by:], x[:by]], axis=0)
+    for s in range(SECS):
+        for k, ref in enumerate((before, mid, after)):
+            nodes[s, pl.ds(k * RING, RING), :] = ref[pl.ds(s * RING, RING), :]
+        nodes[s, pl.ds(3 * RING, RING), :] = jnp.zeros((RING, PATCH), f32)
+    window = (WINDOW, PATCH)
+    lane = lax.broadcasted_iota(jnp.int32, window, 1)
+    here = lax.broadcasted_iota(jnp.int32, window, 0) + (row - REACH_ROWS)
+    used = lane < 2 * COLS
+    has_up = here > 0
+    has_down = here < last_row
+    has_left = lane % COLS > 0
+    has_right = lane % COLS < COLS - 1
+    start = place + RING - REACH_ROWS
+    moving = []
+    flows = []
+    for s in range(SECS):
+        records = nodes[s, pl.ds(start, WINDOW), :]
+        moving.append(pltpu.roll(records, PATCH - 2 * COLS, 1))
+        if s < SECS - 1:
+            found = nodes[s, pl.ds(start + 1, WINDOW), :] if takes_row_above(s) else records
+            flows.append(jnp.where(used, found, 0.0))
 
     for sweep in range(SWEEPS):
         spring = springs[pl.ds(2 * sweep, 1), :]
         tether = springs[pl.ds(2 * sweep + 1, 1), :]
-        near_x, far_x = moving
-        edge_above = jnp.where(other_first, moved(far_x, RING - 1), moved(third, RING - 1))
-        edge_below = jnp.where(other_first, moved(third, 1 - RING), moved(far_x, 1 - RING))
-        above = (jnp.where(first, edge_above, moved(near_x, -1)), jnp.where(first, moved(near_x, RING - 1), moved(far_x, -1)))
-        below = (jnp.where(final, edge_below, moved(near_x, 1)), jnp.where(final, moved(near_x, 1 - RING), moved(far_x, 1)))
+        residuals = [moving[s + 1] - moving[s] - flows[s] for s in range(SECS - 1)]
         fresh = []
-        for k, x in enumerate(moving):
-            col_left = pltpu.roll(x, 1, 1)
-            col_right = pltpu.roll(x, PATCH - 1, 1)
+        for s, x in enumerate(moving):
             laplace = (
-                (above[k] - x) * has_up[k]
-                + (below[k] - x) * has_down[k]
-                + (col_left - x) * has_left
-                + (col_right - x) * has_right
+                jnp.where(has_up, pltpu.roll(x, 1, 0) - x, 0.0)
+                + jnp.where(has_down, pltpu.roll(x, WINDOW - 1, 0) - x, 0.0)
+                + jnp.where(has_left, pltpu.roll(x, 1, 1) - x, 0.0)
+                + jnp.where(has_right, pltpu.roll(x, PATCH - 1, 1) - x, 0.0)
             )
-            residual = (moved(x, RING) - x - flows[k]) * valid_up
-            below_res = jnp.where(section == 0, 0.0, moved(residual, -RING))
-            fresh.append(x + step_size * (spring * laplace + tether * (residual - below_res)))
+            if s == 0:
+                pull = residuals[0]
+            elif s == SECS - 1:
+                pull = -residuals[s - 1]
+            else:
+                pull = residuals[s] - residuals[s - 1]
+            fresh.append(x + step_size * (spring * laplace + tether * pull))
         moving = fresh
 
-    mine = (section == sec) & (in_ring == place)
-    for x, ref in ((flows[0], flow_out), (moving[0], moving_out)):
-        line = jnp.sum(jnp.where(mine, x, 0.0), axis=0, keepdims=True)
+    flows.append(jnp.zeros(window, f32))
+    for parts, ref in ((flows, flow_out), (moving, moving_out)):
+        line = parts[0][REACH_ROWS : REACH_ROWS + 1]
+        for s in range(1, SECS):
+            line = jnp.where(jnp.broadcast_to(sec == s, line.shape), parts[s][REACH_ROWS : REACH_ROWS + 1], line)
         ref[0, 0] = line[:, :COLS]
         ref[0, 1] = line[:, COLS : 2 * COLS]
 
 
-def relax(springs, ring, other, shape):
+def relax(springs, before, mid, after, shape):
     in_vmem = pl.BlockSpec(memory_space=pltpu.VMEM)
     return pl.pallas_call(
         relax_kernel,
         out_shape=[jax.ShapeDtypeStruct(shape, f32)] * 2,
-        in_specs=[in_vmem] * 3,
+        in_specs=[in_vmem] * 4,
         out_specs=[in_vmem] * 2,
+        scratch_shapes=[pltpu.VMEM((SECS, 4 * RING, PATCH), f32)],
         compiler_params=pltpu.CompilerParams(vmem_limit_bytes=VMEM_LIMIT),
-    )(springs, ring, other)
-
-
-def shifted(block, axis, distance):
-    devices = range(lax.axis_size(axis))
-    route = [(i - distance, i) for i in devices if i - distance in devices]
-    return lax.ppermute(block, axis, route)
-
-
-def ring_route(rows, outward):
-    route = []
+    )(springs, before, mid, after)
+
+
+def image_routes(rows):
+    at = lambda s, r: s * rows + r % rows
+    across, near, near_across, shifts = [], [], [], []
     for r in range(rows):
-        step = RING if (r % RING < RING // 2) == outward else -RING
-        if 0 <= r - step < rows:
-            route.append((r - step, r))
-    return route
+        for s in range(SECS - 1):
+            if takes_row_above(s):
+                across.append((at(s, r - 1), at(s, r)))
+                shifts.append((at(s, r - 1), at(s, r)))
+                near_across.append((at(s + 1, r - 1), at(s, r)))
+                if r > 0:
+                    near.append((at(s + 1, r), at(s, r)))
+            else:
+                near.append((at(s + 1, r), at(s, r)))
+                if r < rows - 1:
+                    across.append((at(s, r + 1), at(s, r)))
+                    near_across.append((at(s + 1, r + 1), at(s, r)))
+    return across, near, near_across, shifts
 
 
 def per_device(images, initial, offsets, stiffness, plan):
     rows = lax.axis_size("row")
-    below = shifted(images, "row", -1)
-    remote_initial = lax.ppermute(initial, "row", ring_route(rows, False))
-    near = shifted(images, "sec", -1)
+    both = ("sec", "row")
+    across_route, near_route, near_across_route, shift_route = image_routes(rows)
+    across = lax.ppermute(images, both, across_route)
+    near_across = lax.ppermute(images, both, near_across_route)
+    near = lax.ppermute(images, both, near_route)
+    far_offsets = lax.ppermute(offsets, both, shift_route)
     own, tables, record, springs = prepare(plan, images, offsets, initial, stiffness)
-    below, remote_initial, own, tables, record, springs = lax.optimization_barrier(
-        (below, remote_initial, own, tables, record, springs)
-    )
-    near_below = shifted(below, "sec", -1)
     count = SECS * RING
-    mine = pair_flow(own, below, near, near_below, record, remote_initial, tables, count)
+    mine = pair_flow(own, across, near, near_across, record, far_offsets, tables, count)
     groups = [
         [s * rows + RING * g + j for s in range(SECS) for j in range(RING)] for g in range(rows // RING)
     ]
-    ring = lax.all_to_all(mine.reshape(count, 1, PATCH), ("sec", "row"), 0, 0, axis_index_groups=groups)
-    other = lax.ppermute(ring, "row", ring_route(rows, True))
-    return tuple(
-        relax(springs, ring.reshape(count, PATCH), other.reshape(count, PATCH), initial.shape)
-    )
+    ring = lax.all_to_all(mine.reshape(count, 1, PATCH), both, 0, 0, axis_index_groups=groups)
+    before = lax.ppermute(ring, "row", [(r, (r + RING) % rows) for r in range(rows)])
+    after = lax.ppermute(ring, "row", [((r + RING) % rows, r) for r in range(rows)])
+    blocks = [block.reshape(count, PATCH) for block in (before, ring, after)]
+    return tuple(relax(springs, *blocks, initial.shape))
 
 
 def solution(mesh):

time: 47.4 us -> 54.8 us (1.16)
  the two profiles are of different devices: /device:TPU:256 before, /device:TPU:1 now
where the time goes in v4:
time: 54.8 us; the launch traced here: 54.4 us
  starting transfers between devices  25.9 us (47%)
  waiting for transfers between devices  11.2 us (20%)
  blocking collectives  9.19 us (17%)
  Pallas kernels  4.57 us (8%)
  local copies, waits for them, and re-layouts  2.82 us (5%)
  between operations  0.74 us (1%)
    all_to_all x1, blocking collectives, per_device(): lax.all_to_all(mine.reshape(count, 1, PATCH), both, 0, 0, axis_index_grou...  9.19 us
    ppermute x1, starting transfers between devices, per_device(): lax.ppermute(ring, 'row', [((r + RING) % rows, r) for r in range(rows)])  8.19 us
    ppermute x1, starting transfers between devices, per_device(): near_across = lax.ppermute(images, both, near_across_route)  6.27 us
    ppermute x1, waiting for transfers between devices, per_device(): lax.ppermute(ring, 'row', [(r, (r + RING) % rows) for r in range(rows)])  5.78 us
    ppermute x1, starting transfers between devices, per_device(): across = lax.ppermute(images, both, across_route)  5.18 us
    ppermute x1, waiting for transfers between devices, per_device(): far_offsets = lax.ppermute(offsets, both, shift_route)  4.93 us
    ppermute x1, starting transfers between devices, per_device(): far_offsets = lax.ppermute(offsets, both, shift_route)  3.67 us
    unnamed x11, local copies, waits for them, and re-layouts  2.82 us
  transfers between devices with their start and end apart: 6, of which 3 were waited for; matrix products, arithmetic and copies ran while one was open for 1% of the time, Pallas kernels for 2%

profile of v4, /device:TPU:1, one launch (start us, length us, event | category | flops | bytes accessed | tf_op | source)
XLA Modules:
  0.0 54.4 jit_solution(151459063776253347)
XLA Ops:
  0.6 0.0 copy-start.3
  0.6 0.0 copy-start.4
  0.7 0.0 copy-start.2
  0.7 5.2 %collective-permute-start = (bf16[1,64,1088]{2,1,0:T(8,128)(2,1)}, bf16[1,64,1088]{2,1,0:T(8,128)(2,1)S(1)}, u32[]{:S(2)}, u32[]{:S(2)}) collective-permute-start(bf16[1,64,1088]{2,1,0:T(8,128)(2,1)} %images.1), channel_id=1, source_target_pairs={{127,0},{255,128},{257,256},{0,1},{128,129},{258,257},{1,2},{129,1... | collective-permute-start | bytes 417800 | tf_op jit(solution)/shard_map/ppermute | solution.py:407
  5.8 6.3 %collective-permute-start.2 = (bf16[1,64,1088]{2,1,0:T(8,128)(2,1)}, bf16[1,64,1088]{2,1,0:T(8,128)(2,1)S(1)}, u32[]{:S(2)}, u32[]{:S(2)}) collective-permute-start(bf16[1,64,1088]{2,1,0:T(8,128)(2,1)} %images.1), channel_id=1, source_target_pairs={{255,0},{383,128},{385,256},{128,1},{256,129},{386,257},{129,2},{2... | collective-permute-start | bytes 417800 | tf_op jit(solution)/shard_map/ppermute | solution.py:408
  12.1 0.7 %collective-permute-start.1 = (bf16[1,64,1088]{2,1,0:T(8,128)(2,1)}, bf16[1,64,1088]{2,1,0:T(8,128)(2,1)S(1)}, u32[]{:S(2)}, u32[]{:S(2)}) collective-permute-start(bf16[1,64,1088]{2,1,0:T(8,128)(2,1)} %images.1), channel_id=1, source_target_pairs={{384,256},{129,1},{257,129},{385,257},{130,2},{258,130},{386,258},... | collective-permute-start | bytes 417800 | tf_op jit(solution)/shard_map/ppermute | solution.py:409
  12.8 3.7 %collective-permute-start.3 = (s32[1,2,1,16]{3,2,1,0:T(1,128)}, s32[1,2,1,16]{3,2,1,0:T(1,128)S(1)}, u32[]{:S(2)}, u32[]{:S(2)}) collective-permute-start(s32[1,2,1,16]{3,2,1,0:T(1,128)} %offsets.1), channel_id=1, source_target_pairs={{127,0},{255,128},{0,1},{128,129},{1,2},{129,130},{2,3},{130,131},... | collective-permute-start | bytes 392 | tf_op jit(solution)/shard_map/ppermute | solution.py:410
  16.5 0.8 %copy.9.stiffness = f32[8,2]{1,0:T(8,128)S(1)} copy(f32[8,2]{0,1:T(2,128)} %param.9) | data formatting | bytes 128 | tf_op args[3]
  17.2 0.0 copy-done.3
  17.2 0.0 copy-done.4
  17.3 1.1 %copy-done = bf16[1600,256]{1,0:T(8,128)(2,1)S(1)} copy-done((bf16[1600,256]{1,0:T(8,128)(2,1)S(1)}, bf16[1600,256]{1,0:T(8,128)(2,1)}, u32[]{:S(2)}) %copy-start) | copy-done | bytes 819224
  18.4 0.9 %copy-done.1 = bf16[1,64,1088]{2,1,0:T(8,128)(2,1)S(1)} copy-done((bf16[1,64,1088]{2,1,0:T(8,128)(2,1)S(1)}, bf16[1,64,1088]{2,1,0:T(8,128)(2,1)}, u32[]{:S(2)}) %copy-start.1) | copy-done | bytes 139288
  19.3 0.9 %shard_map.77 = (bf16[64,1088]{1,0:T(8,128)(2,1)S(1)}, bf16[1344,256]{1,0:T(8,128)(2,1)S(1)}, f32[1,128]{1,0:T(1,128)S(1)}, f32[8,128]{1,0:T(8,128)S(1)}) custom-call(s32[3]{0:T(128)S(1)} %copy-done.4, bf16[1,64,1088]{2,1,0:T(8,128)(2,1)S(1)} %copy-done.1, bf16[1600,256]{1,0:T(8,128)(2,1)S(1)} %copy-done, s32[1,2,1,16]{3,2,1,0:T(1,128)S(1)} %copy-done.3, ...), custom_call_target="tpu_custom_call" | custom-call | tf_op jit(solution)/shard_map/pallas_call | solution.py:155
  20.2 4.9 %collective-permute-done.3.far_offsets = s32[1,2,1,16]{3,2,1,0:T(1,128)S(1)} collective-permute-done((s32[1,2,1,16]{3,2,1,0:T(1,128)}, s32[1,2,1,16]{3,2,1,0:T(1,128)S(1)}, u32[]{:S(2)}, u32[]{:S(2)}) %collective-permute-start.3) | collective-permute-done | bytes 160 | tf_op jit(solution)/shard_map/ppermute | solution.py:410
  25.2 0.0 collective-permute-done.across
  25.2 0.5 collective-permute-done.2.near_across
  25.7 0.0 collective-permute-done.1.near
  25.7 2.7 %shard_map.78 = f32[16,128]{1,0:T(8,128)S(1)} custom-call(bf16[64,1088]{1,0:T(8,128)(2,1)S(1)} %get-tuple-element.7.own, bf16[1,64,1088]{2,1,0:T(8,128)(2,1)S(1)} %collective-permute-done.across, bf16[1,64,1088]{2,1,0:T(8,128)(2,1)S(1)} %collective-permute-done.1.near, bf16[1,64,1088]{2,1,0:T(8,128)(2,1)S(1)} %collective-permute-done.2.near_across, ...), custom_call_target="tpu_custom_call" | custom-call | tf_op jit(solution)/shard_map/pallas_call | solution.py:301
  28.4 9.2 %all_to_all.5 = f32[16,1,128]{2,1,0:T(1,128)S(1)} all-to-all(f32[16,1,128]{2,1,0:T(1,128)S(1)} %bitcast.7), channel_id=1, replica_groups={{0,1,2,3,128,129,130,131,256,257,258,259,384,385,386,387},{4,5,6,7,132,..., dimensions={0} | all-to-all | bytes 16384 | tf_op jit(solution)/shard_map/all_to_all | solution.py:417
  37.6 8.2 %collective-permute-start.5 = (f32[16,1,128]{2,0,1:T(8,128)S(1)}, f32[16,1,128]{2,0,1:T(8,128)S(1)}, u32[]{:S(2)}, u32[]{:S(2)}) collective-permute-start(f32[16,1,128]{2,0,1:T(8,128)S(1)} %bitcast.8), channel_id=1, source_target_pairs={{4,0},{5,1},{6,2},{7,3},{8,4},{9,5},{10,6},{11,7},{12,8},{13,9},{1... | collective-permute-start | bytes 24584 | tf_op jit(solution)/shard_map/ppermute | solution.py:419
  45.8 1.9 %collective-permute-start.4 = (f32[16,1,128]{2,0,1:T(8,128)S(1)}, f32[16,1,128]{2,0,1:T(8,128)S(1)}, u32[]{:S(2)}, u32[]{:S(2)}) collective-permute-start(f32[16,1,128]{2,0,1:T(8,128)S(1)} %bitcast.9), channel_id=1, source_target_pairs={{0,4},{1,5},{2,6},{3,7},{4,8},{5,9},{6,10},{7,11},{8,12},{9,13},{1... | collective-permute-start | bytes 24584 | tf_op jit(solution)/shard_map/ppermute | solution.py:418
  47.7 0.0 collective-permute-done.5
  47.7 5.8 %collective-permute-done.4 = f32[16,1,128]{2,0,1:T(8,128)S(1)} collective-permute-done((f32[16,1,128]{2,0,1:T(8,128)S(1)}, f32[16,1,128]{2,0,1:T(8,128)S(1)}, u32[]{:S(2)}, u32[]{:S(2)}) %collective-permute-start.4) | collective-permute-done | bytes 8224 | tf_op jit(solution)/shard_map/ppermute | solution.py:418
  53.5 0.9 %shard_map.79 = (f32[1,2,1,16]{3,2,1,0:T(1,128)}, f32[1,2,1,16]{3,2,1,0:T(1,128)}) custom-call(f32[8,128]{1,0:T(8,128)S(1)} %get-tuple-element.6.springs, f32[16,128]{1,0:T(8,128)S(1)} %bitcast.12, f32[16,128]{1,0:T(8,128)S(1)} %bitcast.10, f32[16,128]{1,0:T(8,128)S(1)} %bitcast.11), custom_call_target="tpu_custom_call" | custom-call | tf_op jit(solution)/shard_map/pallas_call | solution.py:374
  (3 shorter events, 0.0 us)
Async XLA Ops:
  0.6 16.6 %copy-start.3 = (s32[1,2,1,16]{3,2,1,0:T(1,128)S(1)}, s32[1,2,1,16]{3,2,1,0:T(1,128)}, u32[]{:S(2)}) copy-start(s32[1,2,1,16]{3,2,1,0:T(1,128)} %offsets.1) | copy-start | bytes 388
  0.6 16.6 %copy-start.4 = (s32[3]{0:T(128)S(1)}, s32[3]{0:T(128)}, u32[]{:S(2)}) copy-start(s32[3]{0:T(128)} %plan.1) | copy-start | bytes 40
  0.7 16.6 %copy-start.2 = (f32[1,2,1,16]{3,2,1,0:T(1,128)S(1)}, f32[1,2,1,16]{3,2,1,0:T(1,128)}, u32[]{:S(2)}) copy-start(f32[1,2,1,16]{3,2,1,0:T(1,128)} %initial.1) | copy-start | bytes 388
  0.7 24.5 %collective-permute-start = (bf16[1,64,1088]{2,1,0:T(8,128)(2,1)}, bf16[1,64,1088]{2,1,0:T(8,128)(2,1)S(1)}, u32[]{:S(2)}, u32[]{:S(2)}) collective-permute-start(bf16[1,64,1088]{2,1,0:T(8,128)(2,1)} %images.1), channel_id=1, source_target_pairs={{127,0},{255,128},{257,256},{0,1},{128,129},{258,257},{1,2},{129,1... | collective-permute-start | bytes 417800 | tf_op jit(solution)/shard_map/ppermute | solution.py:407
  5.8 19.8 %collective-permute-start.2 = (bf16[1,64,1088]{2,1,0:T(8,128)(2,1)}, bf16[1,64,1088]{2,1,0:T(8,128)(2,1)S(1)}, u32[]{:S(2)}, u32[]{:S(2)}) collective-permute-start(bf16[1,64,1088]{2,1,0:T(8,128)(2,1)} %images.1), channel_id=1, source_target_pairs={{255,0},{383,128},{385,256},{128,1},{256,129},{386,257},{129,2},{2... | collective-permute-start | bytes 417800 | tf_op jit(solution)/shard_map/ppermute | solution.py:408
  12.1 13.6 %collective-permute-start.1 = (bf16[1,64,1088]{2,1,0:T(8,128)(2,1)}, bf16[1,64,1088]{2,1,0:T(8,128)(2,1)S(1)}, u32[]{:S(2)}, u32[]{:S(2)}) collective-permute-start(bf16[1,64,1088]{2,1,0:T(8,128)(2,1)} %images.1), channel_id=1, source_target_pairs={{384,256},{129,1},{257,129},{385,257},{130,2},{258,130},{386,258},... | collective-permute-start | bytes 417800 | tf_op jit(solution)/shard_map/ppermute | solution.py:409
  12.8 12.4 %collective-permute-start.3 = (s32[1,2,1,16]{3,2,1,0:T(1,128)}, s32[1,2,1,16]{3,2,1,0:T(1,128)S(1)}, u32[]{:S(2)}, u32[]{:S(2)}) collective-permute-start(s32[1,2,1,16]{3,2,1,0:T(1,128)} %offsets.1), channel_id=1, source_target_pairs={{127,0},{255,128},{0,1},{128,129},{1,2},{129,130},{2,3},{130,131},... | collective-permute-start | bytes 392 | tf_op jit(solution)/shard_map/ppermute | solution.py:410
  17.2 1.1 %copy-start = (bf16[1600,256]{1,0:T(8,128)(2,1)S(1)}, bf16[1600,256]{1,0:T(8,128)(2,1)}, u32[]{:S(2)}) copy-start(bf16[1600,256]{1,0:T(8,128)(2,1)} %constant.2.clone.tables) | copy-start | bytes 2457604
  18.4 0.9 %copy-start.1 = (bf16[1,64,1088]{2,1,0:T(8,128)(2,1)S(1)}, bf16[1,64,1088]{2,1,0:T(8,128)(2,1)}, u32[]{:S(2)}) copy-start(bf16[1,64,1088]{2,1,0:T(8,128)(2,1)} %images.1) | copy-start | bytes 417796
  37.6 10.1 %collective-permute-start.5 = (f32[16,1,128]{2,0,1:T(8,128)S(1)}, f32[16,1,128]{2,0,1:T(8,128)S(1)}, u32[]{:S(2)}, u32[]{:S(2)}) collective-permute-start(f32[16,1,128]{2,0,1:T(8,128)S(1)} %bitcast.8), channel_id=1, source_target_pairs={{4,0},{5,1},{6,2},{7,3},{8,4},{9,5},{10,6},{11,7},{12,8},{13,9},{1... | collective-permute-start | bytes 24584 | tf_op jit(solution)/shard_map/ppermute | solution.py:419
  45.8 7.7 %collective-permute-start.4 = (f32[16,1,128]{2,0,1:T(8,128)S(1)}, f32[16,1,128]{2,0,1:T(8,128)S(1)}, u32[]{:S(2)}, u32[]{:S(2)}) collective-permute-start(f32[16,1,128]{2,0,1:T(8,128)S(1)} %bitcast.9), channel_id=1, source_target_pairs={{0,4},{1,5},{2,6},{3,7},{4,8},{5,9},{6,10},{7,11},{8,12},{9,13},{1... | collective-permute-start | bytes 24584 | tf_op jit(solution)/shard_map/ppermute | solution.py:418

commit v5 on v3

--- a/solution.py
+++ b/solution.py
@@ -112,83 +112,103 @@
     return jnp.dot(a, b, preferred_element_type=f32)
 
 
-def prepare_kernel(plan, images, tables, offsets, initial, stiffness, own_out, tables_out, record, springs, sems):
-    moves = ((images.at[0], own_out), (tables, tables_out))
-    copies = [pltpu.make_async_copy(src, dst, sems.at[i]) for i, (src, dst) in enumerate(moves)]
-    for copy in copies:
-        copy.start()
+def prepare_kernel(plan, tables, offsets, initial, stiffness, tables_out, record, springs, sem):
+    copy = pltpu.make_async_copy(tables, tables_out, sem)
+    copy.start()
     record[...] = jnp.zeros((1, PATCH), f32)
     for i in range(2):
         record[:, pl.ds(i * COLS, COLS)] = offsets[0, i].astype(f32)
         record[:, pl.ds((2 + i) * COLS, COLS)] = initial[0, i]
-    level_id = lax.broadcasted_iota(jnp.int32, stiffness.shape, 0)
+    level_id = lax.broadcasted_iota(jnp.int32, stiffness.shape, 1)
     for sweep in range(SWEEPS):
-        picked = jnp.sum(jnp.where(level_id == plan[sweep], stiffness[...], 0.0), axis=0, keepdims=True)
-        for i in range(2):
-            springs[pl.ds(2 * sweep + i, 1), :] = jnp.broadcast_to(picked[:, i : i + 1], (1, PATCH))
-    for copy in copies:
-        copy.wait()
-
-
-def prepare(plan, images, offsets, initial, stiffness):
+        picked = jnp.sum(jnp.where(level_id == plan[sweep], stiffness[...], 0.0), axis=1, keepdims=True)
+        springs[pl.ds(2 * sweep, 2), :] = jnp.broadcast_to(picked, (2, PATCH))
+    copy.wait()
+
+
+def prepare(plan, offsets, initial, stiffness):
     tables = jnp.asarray(constant_tables())
     in_vmem = pl.BlockSpec(memory_space=pltpu.VMEM)
     anywhere = pl.BlockSpec(memory_space=pl.ANY)
     return pl.pallas_call(
         prepare_kernel,
         out_shape=[
-            jax.ShapeDtypeStruct(images.shape[1:], bf16),
             jax.ShapeDtypeStruct(tables.shape, bf16),
             jax.ShapeDtypeStruct((1, PATCH), f32),
             jax.ShapeDtypeStruct((8, PATCH), f32),
         ],
-        in_specs=[pl.BlockSpec(memory_space=pltpu.SMEM), anywhere, anywhere, in_vmem, in_vmem, in_vmem],
-        out_specs=[in_vmem] * 4,
-        scratch_shapes=[pltpu.SemaphoreType.DMA((2,))],
+        in_specs=[pl.BlockSpec(memory_space=pltpu.SMEM), anywhere, in_vmem, in_vmem, in_vmem],
+        out_specs=[in_vmem] * 3,
+        scratch_shapes=[pltpu.SemaphoreType.DMA],
         compiler_params=pltpu.CompilerParams(vmem_limit_bytes=VMEM_LIMIT),
-    )(plan, images, tables, offsets, initial, stiffness)
-
-
-def flow_kernel(own, below, near, near_below, record, remote, tables, out, spec, lagged):
+    )(plan, tables, offsets, initial, stiffness.T)
+
+
+def section_spectra(upper, lower, tables):
+    nyq_t = table(tables, "nyquist")
+    nyq_t = jnp.concatenate([nyq_t[:, :PATCH], nyq_t[:, PATCH:]], axis=0)
+    rows_t = jnp.concatenate([table(tables, "rows"), nyq_t], axis=1)
     columns = table(tables, "columns")
-    spread = table(tables, "spread")
-    nyq_t = table(tables, "nyquist")
-    rows_t = jnp.concatenate([table(tables, "rows"), jnp.concatenate([nyq_t[:, :PATCH], nyq_t[:, PATCH:]], axis=0)], axis=1)
-
-    def finish_spectrum(m, stacked, table):
-        product = dot(table, stacked).astype(bf16)
-        spec[m] = product
-        wide = product.astype(f32)
-        return jnp.sum(wide * wide, axis=0, keepdims=True)
-
-    energies = []
-    lane_4 = lax.broadcasted_iota(jnp.int32, (4 * HALF, PATCH), 1)
-    nyquist = jnp.zeros((4 * HALF, PATCH), f32)
+    lane = lax.broadcasted_iota(jnp.int32, (PATCH, PATCH), 1)
+    nyquist = jnp.zeros((PATCH, PATCH), f32)
+    stacked = []
     for m in range(PAIRS):
         span = 2 * PATCH if m < PAIRS - 1 else WIDTH - m * PATCH
-        tiles = [ref[0, :, pl.ds(m * PATCH, span)] for ref in (below, near, near_below)]
-        tiles.insert(0, own[:, pl.ds(m * PATCH, span)])
-        seg = dot(jnp.concatenate(tiles, axis=0), rows_t[:span])
-        nyquist = jnp.where(lane_4 // 2 == m, seg[:, 2 * PATCH :], nyquist)
+        tile = jnp.concatenate([upper(m * PATCH, span), lower(m * PATCH, span)], axis=0)
+        seg = dot(tile, rows_t[:span])
+        nyquist = jnp.where(lane // 2 == m, seg[:, 2 * PATCH :], nyquist)
         seg = seg[:, : 2 * PATCH].astype(bf16)
-        stacked = jnp.concatenate(
-            [
-                jnp.concatenate([seg[:PATCH, :PATCH], seg[PATCH:, :PATCH]], axis=1),
-                jnp.concatenate([seg[:PATCH, PATCH:], seg[PATCH:, PATCH:]], axis=1),
-            ],
-            axis=0,
-        )
-        energies.append(finish_spectrum(m, stacked, columns))
-    seg = nyquist.astype(bf16)
-    stacked = jnp.concatenate([seg[:PATCH], seg[PATCH:]], axis=1)
-    energy_64 = finish_spectrum(PAIRS, stacked, columns[:, :PATCH])
+        stacked.append(jnp.concatenate([seg[:, :PATCH], seg[:, PATCH:]], axis=0))
+    spectra = []
+    for m in range(0, PAIRS, 2):
+        product = dot(columns, jnp.concatenate(stacked[m : m + 2], axis=1)).astype(bf16)
+        spectra += [product[:, :PATCH], product[:, PATCH:]]
+    spectra.append(dot(columns[:, :PATCH], nyquist.astype(bf16)).astype(bf16))
+    return spectra
+
+
+def energy(spectrum):
+    wide = spectrum.astype(f32)
+    return jnp.sum(wide * wide, axis=0, keepdims=True)
+
+
+def block_tile(ref):
+    return lambda start, span: ref[0, :, pl.ds(start, span)]
+
+
+def own_kernel(own, below, tables, spec, energies):
+    for m, spectrum in enumerate(section_spectra(block_tile(own), block_tile(below), tables)):
+        spec[m] = spectrum
+        energies[pl.ds(m, 1), :] = energy(spectrum)
+
+
+def own_spectra(own, below, tables):
+    in_vmem = pl.BlockSpec(memory_space=pltpu.VMEM)
+    return pl.pallas_call(
+        own_kernel,
+        out_shape=[
+            jax.ShapeDtypeStruct((PAIRS + 1, 2 * PATCH, PATCH), bf16),
+            jax.ShapeDtypeStruct((2 * PAIRS, PATCH), f32),
+        ],
+        in_specs=[in_vmem] * 3,
+        out_specs=[in_vmem] * 2,
+        compiler_params=pltpu.CompilerParams(vmem_limit_bytes=VMEM_LIMIT),
+        cost_estimate=pl.CostEstimate(flops=600_000_000, bytes_accessed=2_000_000, transcendentals=0),
+    )(own, below, tables)
+
+
+def flow_kernel(own_spec, own_energies, near, near_below, record, remote, tables, out, spec, lagged):
+    spread = table(tables, "spread")
+    energies = []
+    for m, spectrum in enumerate(section_spectra(block_tile(near), block_tile(near_below), tables)):
+        spec[m] = spectrum
+        energies.append(energy(spectrum))
 
     lane = lax.broadcasted_iota(jnp.int32, (PAIRS, PATCH), 1)
     pair = lax.broadcasted_iota(jnp.int32, (PAIRS, PATCH), 0)
     own_pair = (lane % COLS) // 2 == pair
     first_16 = own_pair & (lane < COLS)
     weight = jnp.where(lane % HALF == 0, 1.0, 2.0)
-    energy = jnp.concatenate(energies, axis=0)
 
     def halves(x):
         return x[:, :PATCH], x[:, PATCH:]
@@ -202,19 +222,17 @@
         scale = 1.0 / (PATCH * PATCH)
         return jnp.sqrt(by_pair * scale + 1e-06), jnp.sqrt(by_patch * scale + 1e-06)
 
-    low_e, up_e = halves(energy)
-    low_x, up_x = halves(energy_64)
-    low_pair, low_patch = totals(low_e, low_x)
-    up_pair, up_patch = totals(up_e, up_x)
+    low_pair, low_patch = totals(own_energies[pl.ds(0, PAIRS), :], own_energies[pl.ds(PAIRS, 1), :])
+    up_pair, up_patch = totals(jnp.concatenate(energies[:PAIRS], axis=0), energies[PAIRS])
     floor_pair = floor_ratio * low_pair * up_pair
     floor_patch = floor_ratio * low_patch * up_patch
 
     for m in range(PAIRS + 1):
         floor = floor_pair[m : m + 1] if m < PAIRS else floor_patch
-        low_re = spec[m, pl.ds(0, PATCH), pl.ds(0, PATCH)].astype(f32)
-        low_im = spec[m, pl.ds(PATCH, PATCH), pl.ds(0, PATCH)].astype(f32)
-        up_re = spec[m, pl.ds(0, PATCH), pl.ds(PATCH, PATCH)].astype(f32)
-        up_im = spec[m, pl.ds(PATCH, PATCH), pl.ds(PATCH, PATCH)].astype(f32)
+        low_re = own_spec[m, pl.ds(0, PATCH)].astype(f32)
+        low_im = own_spec[m, pl.ds(PATCH, PATCH)].astype(f32)
+        up_re = spec[m, pl.ds(0, PATCH)].astype(f32)
+        up_im = spec[m, pl.ds(PATCH, PATCH)].astype(f32)
         cross_re = low_re * up_re + low_im * up_im
         cross_im = low_re * up_im - low_im * up_re
         square = cross_re * cross_re + cross_im * cross_im
@@ -276,15 +294,15 @@
         out[:, pl.ds((4 + i) * COLS, COLS)] = jnp.broadcast_to(remote[0, i], (out.shape[0], COLS))
 
 
-def pair_flow(own, below, near, near_below, record, remote_initial, tables, copies):
-    operands = (own, below, near, near_below, record, remote_initial, tables)
+def pair_flow(own_parts, near, near_below, record, remote_initial, tables, copies):
+    operands = (*own_parts, near, near_below, record, remote_initial, tables)
     return pl.pallas_call(
         flow_kernel,
         out_shape=jax.ShapeDtypeStruct((copies, PATCH), f32),
         in_specs=[pl.BlockSpec(memory_space=pltpu.VMEM)] * len(operands),
         out_specs=pl.BlockSpec(memory_space=pltpu.VMEM),
         scratch_shapes=[
-            pltpu.VMEM((PAIRS + 1, 2 * PATCH, 2 * PATCH), bf16),
+            pltpu.VMEM((PAIRS + 1, 2 * PATCH, PATCH), bf16),
             pltpu.VMEM(((PAIRS + 1) * SHIFTS, 2 * PATCH), f32),
         ],
         compiler_params=pltpu.CompilerParams(vmem_limit_bytes=VMEM_LIMIT),
@@ -385,13 +403,14 @@
     below = shifted(images, "row", -1)
     remote_initial = lax.ppermute(initial, "row", ring_route(rows, False))
     near = shifted(images, "sec", -1)
-    own, tables, record, springs = prepare(plan, images, offsets, initial, stiffness)
-    below, remote_initial, own, tables, record, springs = lax.optimization_barrier(
-        (below, remote_initial, own, tables, record, springs)
+    tables, record, springs = prepare(plan, offsets, initial, stiffness)
+    below, remote_initial, tables, record, springs = lax.optimization_barrier(
+        (below, remote_initial, tables, record, springs)
     )
     near_below = shifted(below, "sec", -1)
     count = SECS * RING
-    mine = pair_flow(own, below, near, near_below, record, remote_initial, tables, count)
+    own_parts = own_spectra(images, below, tables)
+    mine = pair_flow(own_parts, near, near_below, record, remote_initial, tables, count)
     groups = [
         [s * rows + RING * g + j for s in range(SECS) for j in range(RING)] for g in range(rows // RING)
     ]

time: 47.4 us -> 46.4 us (0.979)
  waiting for transfers between devices: 8.72 us -> 8.03 us
  Pallas kernels: 4.75 us -> 4.22 us
    pallas_call x1, Pallas kernels: 2.71 us -> 1.71 us  [pair_flow(): pl.pallas_call(flow_kernel, out_shape=jax.ShapeDtypeStruct((copies, PATCH...]
    ppermute x3, waiting for transfers between devices: 2.31 us -> 1.63 us  [shifted(): return lax.ppermute(block, axis, route)]
    all_to_all x1, blocking collectives: 14.8 us -> 15.2 us  [per_device(): lax.all_to_all(mine.reshape(count, 1, PATCH), ('sec', 'row'), 0, 0, axis_...]
    pallas_call x1 -> x2, Pallas kernels: 1.1 us -> 1.57 us  [the longest x1 0.9 us: prepare(): pl.pallas_call(prepare_kernel, out_shape=[jax.ShapeDtypeStruct(tables.sha...]
    unnamed x11 -> x12, local copies, waits for them, and re-layouts: 2.77 us -> 2.46 us
  transfers between devices with their start and end apart: 5 -> 5, of which waited for: 2 -> 2; matrix products, arithmetic and copies ran while one was open for 2% -> 0% of each run, Pallas kernels for 2% -> 3%
where the time goes in v5:
time: 46.4 us; the launch traced here: 46.1 us
  starting transfers between devices  15.3 us (33%)
  blocking collectives  15.2 us (33%)
  waiting for transfers between devices  8.03 us (17%)
  Pallas kernels  4.22 us (9%)
  local copies, waits for them, and re-layouts  2.46 us (5%)
  between operations  0.76 us (2%)
    all_to_all x1, blocking collectives, per_device(): lax.all_to_all(mine.reshape(count, 1, PATCH), ('sec', 'row'), 0, 0, axis_...  15.2 us
    ppermute x3, starting transfers between devices, shifted(): return lax.ppermute(block, axis, route)  10.2 us
    ppermute x1, waiting for transfers between devices, per_device(): other = lax.ppermute(ring, 'row', ring_route(rows, True))  6.4 us
    ppermute x1, starting transfers between devices, per_device(): remote_initial = lax.ppermute(initial, 'row', ring_route(rows, False))  2.74 us
    unnamed x12, local copies, waits for them, and re-layouts  2.46 us
    ppermute x1, starting transfers between devices, per_device(): other = lax.ppermute(ring, 'row', ring_route(rows, True))  2.44 us
    pallas_call x1, Pallas kernels, pair_flow(): pl.pallas_call(flow_kernel, out_shape=jax.ShapeDtypeStruct((copies, PATCH...  1.71 us
    ppermute x3, waiting for transfers between devices, shifted(): return lax.ppermute(block, axis, route)  1.63 us
  transfers between devices with their start and end apart: 5, of which 2 were waited for; matrix products, arithmetic and copies ran while one was open for 0% of the time, Pallas kernels for 3%

profile of v5, /device:TPU:256, one launch (start us, length us, event | category | flops | bytes accessed | tf_op | source)
XLA Modules:
  0.0 46.1 jit_solution(10484600682805879437)
XLA Ops:
  0.6 0.0 copy-start.4
  0.6 0.0 copy-start.1
  0.7 7.6 %collective-permute-start = (bf16[1,64,1088]{2,1,0:T(8,128)(2,1)}, bf16[1,64,1088]{2,1,0:T(8,128)(2,1)S(1)}, u32[]{:S(2)}, u32[]{:S(2)}) collective-permute-start(bf16[1,64,1088]{2,1,0:T(8,128)(2,1)} %own.1), channel_id=1, source_target_pairs={{1,0},{2,1},{3,2},{4,3},{5,4},{6,5},{7,6},{8,7},{9,8},{10,9},{11,1... | collective-permute-start | bytes 417800 | tf_op jit(solution)/shard_map/ppermute | solution.py:389
  8.2 1.3 %collective-permute-start.2 = (bf16[1,64,1088]{2,1,0:T(8,128)(2,1)}, bf16[1,64,1088]{2,1,0:T(8,128)(2,1)S(1)}, u32[]{:S(2)}, u32[]{:S(2)}) collective-permute-start(bf16[1,64,1088]{2,1,0:T(8,128)(2,1)} %own.1), channel_id=1, source_target_pairs={{128,0},{256,128},{384,256},{129,1},{257,129},{385,257},{130,2},{2... | collective-permute-start | bytes 417800 | tf_op jit(solution)/shard_map/ppermute | solution.py:389
  9.5 2.7 %collective-permute-start.1 = (f32[1,2,1,16]{3,2,1,0:T(1,128)}, f32[1,2,1,16]{3,2,1,0:T(1,128)S(1)}, u32[]{:S(2)}, u32[]{:S(2)}) collective-permute-start(f32[1,2,1,16]{3,2,1,0:T(1,128)} %initial.1), channel_id=1, source_target_pairs={{4,0},{5,1},{8,4},{9,5},{2,6},{3,7},{12,8},{13,9},{6,10},{7,11},{1... | collective-permute-start | bytes 392 | tf_op jit(solution)/shard_map/ppermute | solution.py:404
  12.3 0.0 copy-done.4
  12.3 0.0 copy-done.1
  12.3 0.0 copy-start
  12.3 1.1 %copy-done = bf16[1344,256]{1,0:T(8,128)(2,1)S(1)} copy-done((bf16[1344,256]{1,0:T(8,128)(2,1)S(1)}, bf16[1344,256]{1,0:T(8,128)(2,1)}, u32[]{:S(2)}) %copy-start) | copy-done | bytes 688152
  13.4 0.7 %copy-done.2 = f32[8,2]{0,1:T(2,128)S(1)} copy-done((f32[8,2]{0,1:T(2,128)S(1)}, f32[8,2]{0,1:T(2,128)}, u32[]{:S(2)}) %copy-start.2) | copy-done | bytes 88
  14.1 0.7 %copy-done.3 = f32[1,2,1,16]{3,2,1,0:T(1,128)S(1)} copy-done((f32[1,2,1,16]{3,2,1,0:T(1,128)S(1)}, f32[1,2,1,16]{3,2,1,0:T(1,128)}, u32[]{:S(2)}) %copy-start.3) | copy-done | bytes 152
  14.8 0.9 %shard_map.77 = (bf16[1344,256]{1,0:T(8,128)(2,1)S(1)}, f32[1,128]{1,0:T(1,128)S(1)}, f32[8,128]{1,0:T(8,128)S(1)}) custom-call(s32[3]{0:T(128)S(1)} %copy-done.4, bf16[1344,256]{1,0:T(8,128)(2,1)S(1)} %copy-done, s32[1,2,1,16]{3,2,1,0:T(1,128)S(1)} %copy-done.1, f32[1,2,1,16]{3,2,1,0:T(1,128)S(1)} %copy-done.3, f32[2,8]{1,0:T(2,128)S(1)} %bitcast.11), custom_call_target="tpu_custom_call" | custom-call | tf_op jit(solution)/shard_map/pallas_call | solution.py:133
  15.7 0.0 collective-permute-done.1.remote
  15.7 0.0 collective-permute-done.below
  15.7 1.3 %collective-permute-start.3 = (bf16[1,64,1088]{2,1,0:T(8,128)(2,1)S(1)}, bf16[1,64,1088]{2,1,0:T(8,128)(2,1)S(1)}, u32[]{:S(2)}, u32[]{:S(2)}) collective-permute-start(bf16[1,64,1088]{2,1,0:T(8,128)(2,1)S(1)} %collective-permute-done.below), channel_id=1, source_target_pairs={{128,0},{256,128},{384,256},{129,1},{257,129},{385,257},{130,2},{2... | collective-permute-start | bytes 417800 | tf_op jit(solution)/shard_map/ppermute | solution.py:389
  17.0 0.0 copy-done.5
  17.0 0.7 %shard_map.78 = (bf16[9,256,128]{2,1,0:T(8,128)(2,1)S(1)}, f32[16,128]{1,0:T(8,128)S(1)}) custom-call(bf16[1,64,1088]{2,1,0:T(8,128)(2,1)S(1)} %copy-done.5, bf16[1,64,1088]{2,1,0:T(8,128)(2,1)S(1)} %collective-permute-done.below, bf16[1344,256]{1,0:T(8,128)(2,1)S(1)} %get-tuple-element.17.tables), custom_call_target="tpu_custom_call" | custom-call | flops 600000000 | bytes 2000000 | tf_op jit(solution)/shard_map/pallas_call | solution.py:187
  17.7 0.0 collective-permute-done.2.near
  17.7 1.6 %collective-permute-done.3.near_below = bf16[1,64,1088]{2,1,0:T(8,128)(2,1)S(1)} collective-permute-done((bf16[1,64,1088]{2,1,0:T(8,128)(2,1)S(1)}, bf16[1,64,1088]{2,1,0:T(8,128)(2,1)S(1)}, u32[]{:S(2)}, u32[]{:S(2)}) %collective-permute-start.3) | collective-permute-done | bytes 139296 | tf_op jit(solution)/shard_map/ppermute | solution.py:389
  19.3 1.7 %shard_map.79 = f32[16,128]{1,0:T(8,128)S(1)} custom-call(bf16[9,256,128]{2,1,0:T(8,128)(2,1)S(1)} %get-tuple-element.18.own_spec, f32[16,128]{1,0:T(8,128)S(1)} %get-tuple-element.19.own_energies, bf16[1,64,1088]{2,1,0:T(8,128)(2,1)S(1)} %collective-permute-done.2.near, bf16[1,64,1088]{2,1,0:T(8,128)(2,1)S(1)} %collective-permute-done.3.near_below, ...), custom_call_target="tpu_custom_call" | custom-call | tf_op jit(solution)/shard_map/pallas_call | solution.py:299
  21.0 15.2 %all_to_all.5 = f32[16,1,128]{2,1,0:T(1,128)S(1)} all-to-all(f32[16,1,128]{2,1,0:T(1,128)S(1)} %bitcast.7), channel_id=1, replica_groups={{0,1,2,3,128,129,130,131,256,257,258,259,384,385,386,387},{4,5,6,7,132,..., dimensions={0} | all-to-all | bytes 16384 | tf_op jit(solution)/shard_map/all_to_all | solution.py:417
  36.3 2.4 %collective-permute-start.4 = (f32[16,1,128]{2,0,1:T(8,128)S(1)}, f32[16,1,128]{2,0,1:T(8,128)S(1)}, u32[]{:S(2)}, u32[]{:S(2)}) collective-permute-start(f32[16,1,128]{2,0,1:T(8,128)S(1)} %bitcast.8), channel_id=1, source_target_pairs={{6,2},{7,3},{0,4},{1,5},{10,6},{11,7},{4,8},{5,9},{14,10},{15,11},... | collective-permute-start | bytes 24584 | tf_op jit(solution)/shard_map/ppermute | solution.py:418
  38.7 6.4 %collective-permute-done.4 = f32[16,1,128]{2,0,1:T(8,128)S(1)} collective-permute-done((f32[16,1,128]{2,0,1:T(8,128)S(1)}, f32[16,1,128]{2,0,1:T(8,128)S(1)}, u32[]{:S(2)}, u32[]{:S(2)}) %collective-permute-start.4) | collective-permute-done | bytes 8224 | tf_op jit(solution)/shard_map/ppermute | solution.py:418
  45.1 0.9 %shard_map.80 = (f32[1,2,1,16]{3,2,1,0:T(1,128)}, f32[1,2,1,16]{3,2,1,0:T(1,128)}) custom-call(f32[8,128]{1,0:T(8,128)S(1)} %get-tuple-element.15.springs, f32[16,128]{1,0:T(8,128)S(1)} %bitcast.9, f32[16,128]{1,0:T(8,128)S(1)} %bitcast.10), custom_call_target="tpu_custom_call" | custom-call | tf_op jit(solution)/shard_map/pallas_call | solution.py:377
  (3 shorter events, 0.0 us)
Async XLA Ops:
  0.6 11.7 %copy-start.4 = (s32[3]{0:T(128)S(1)}, s32[3]{0:T(128)}, u32[]{:S(2)}) copy-start(s32[3]{0:T(128)} %plan.1) | copy-start | bytes 40
  0.6 11.7 %copy-start.1 = (s32[1,2,1,16]{3,2,1,0:T(1,128)S(1)}, s32[1,2,1,16]{3,2,1,0:T(1,128)}, u32[]{:S(2)}) copy-start(s32[1,2,1,16]{3,2,1,0:T(1,128)} %offsets.1) | copy-start | bytes 388
  0.7 15.0 %collective-permute-start = (bf16[1,64,1088]{2,1,0:T(8,128)(2,1)}, bf16[1,64,1088]{2,1,0:T(8,128)(2,1)S(1)}, u32[]{:S(2)}, u32[]{:S(2)}) collective-permute-start(bf16[1,64,1088]{2,1,0:T(8,128)(2,1)} %own.1), channel_id=1, source_target_pairs={{1,0},{2,1},{3,2},{4,3},{5,4},{6,5},{7,6},{8,7},{9,8},{10,9},{11,1... | collective-permute-start | bytes 417800 | tf_op jit(solution)/shard_map/ppermute | solution.py:389
  8.2 9.4 %collective-permute-start.2 = (bf16[1,64,1088]{2,1,0:T(8,128)(2,1)}, bf16[1,64,1088]{2,1,0:T(8,128)(2,1)S(1)}, u32[]{:S(2)}, u32[]{:S(2)}) collective-permute-start(bf16[1,64,1088]{2,1,0:T(8,128)(2,1)} %own.1), channel_id=1, source_target_pairs={{128,0},{256,128},{384,256},{129,1},{257,129},{385,257},{130,2},{2... | collective-permute-start | bytes 417800 | tf_op jit(solution)/shard_map/ppermute | solution.py:389
  9.5 6.1 %collective-permute-start.1 = (f32[1,2,1,16]{3,2,1,0:T(1,128)}, f32[1,2,1,16]{3,2,1,0:T(1,128)S(1)}, u32[]{:S(2)}, u32[]{:S(2)}) collective-permute-start(f32[1,2,1,16]{3,2,1,0:T(1,128)} %initial.1), channel_id=1, source_target_pairs={{4,0},{5,1},{8,4},{9,5},{2,6},{3,7},{12,8},{13,9},{6,10},{7,11},{1... | collective-permute-start | bytes 392 | tf_op jit(solution)/shard_map/ppermute | solution.py:404
  12.3 1.1 %copy-start = (bf16[1344,256]{1,0:T(8,128)(2,1)S(1)}, bf16[1344,256]{1,0:T(8,128)(2,1)}, u32[]{:S(2)}) copy-start(bf16[1344,256]{1,0:T(8,128)(2,1)} %constant.2.clone.tables) | copy-start | bytes 2064388
  13.4 0.7 %copy-start.2 = (f32[8,2]{0,1:T(2,128)S(1)}, f32[8,2]{0,1:T(2,128)}, u32[]{:S(2)}) copy-start(f32[8,2]{0,1:T(2,128)} %param.9) | copy-start | bytes 196
  14.1 0.7 %copy-start.3 = (f32[1,2,1,16]{3,2,1,0:T(1,128)S(1)}, f32[1,2,1,16]{3,2,1,0:T(1,128)}, u32[]{:S(2)}) copy-start(f32[1,2,1,16]{3,2,1,0:T(1,128)} %initial.1) | copy-start | bytes 388
  14.8 2.2 %copy-start.5 = (bf16[1,64,1088]{2,1,0:T(8,128)(2,1)S(1)}, bf16[1,64,1088]{2,1,0:T(8,128)(2,1)}, u32[]{:S(2)}) copy-start(bf16[1,64,1088]{2,1,0:T(8,128)(2,1)} %own.1) | copy-start | bytes 417796
  15.7 3.6 %collective-permute-start.3 = (bf16[1,64,1088]{2,1,0:T(8,128)(2,1)S(1)}, bf16[1,64,1088]{2,1,0:T(8,128)(2,1)S(1)}, u32[]{:S(2)}, u32[]{:S(2)}) collective-permute-start(bf16[1,64,1088]{2,1,0:T(8,128)(2,1)S(1)} %collective-permute-done.below), channel_id=1, source_target_pairs={{128,0},{256,128},{384,256},{129,1},{257,129},{385,257},{130,2},{2... | collective-permute-start | bytes 417800 | tf_op jit(solution)/shard_map/ppermute | solution.py:389
  36.3 8.9 %collective-permute-start.4 = (f32[16,1,128]{2,0,1:T(8,128)S(1)}, f32[16,1,128]{2,0,1:T(8,128)S(1)}, u32[]{:S(2)}, u32[]{:S(2)}) collective-permute-start(f32[16,1,128]{2,0,1:T(8,128)S(1)} %bitcast.8), channel_id=1, source_target_pairs={{6,2},{7,3},{0,4},{1,5},{10,6},{11,7},{4,8},{5,9},{14,10},{15,11},... | collective-permute-start | bytes 24584 | tf_op jit(solution)/shard_map/ppermute | solution.py:418

commit v6 on v5

--- a/solution.py
+++ b/solution.py
@@ -25,6 +25,7 @@
 floor_ratio = 0.2
 
 VMEM_LIMIT = 24 * 1024 * 1024
+PREPARE_FLOPS = 1_000_000_000
 
 f32 = jnp.float32
 bf16 = jnp.bfloat16
@@ -87,12 +88,13 @@
     same = ((lane // HALF)[:, None] == (lane // HALF)[None, :]).astype(np.float32)
     blank = np.zeros((PATCH, PATCH), np.float32)
     spread = np.block([[same, gather], [single.T, blank]])
-    packed = [rows, np.concatenate([nyquist[:PATCH], nyquist[PATCH:]], axis=1), columns, spread, lag_y, lag_x]
+    turned = np.roll(columns.reshape(2 * PATCH, 2, PATCH), HALF, axis=2).reshape(2 * PATCH, 2 * PATCH)
+    packed = [rows, np.concatenate([nyquist[:PATCH], nyquist[PATCH:]], axis=1), spread, lag_y, lag_x, columns, turned]
     return np.concatenate([np.asarray(t).astype(ml_dtypes.bfloat16) for t in packed], axis=0)
 
 
-TABLE_ROWS = {"rows": (0, 256), "nyquist": (256, 128), "columns": (384, 256), "spread": (640, 256)}
-TABLE_ROWS |= {"lag_y": (896, 64), "lag_x": (960, 384)}
+TABLE_ROWS = {"rows": (0, 256), "nyquist": (256, 128), "spread": (384, 256)}
+TABLE_ROWS |= {"lag_y": (640, 64), "lag_x": (704, 384), "columns": (1088, 256), "turned": (1344, 256)}
 
 
 def table(ref, name):
@@ -112,9 +114,15 @@
     return jnp.dot(a, b, preferred_element_type=f32)
 
 
-def prepare_kernel(plan, tables, offsets, initial, stiffness, tables_out, record, springs, sem):
-    copy = pltpu.make_async_copy(tables, tables_out, sem)
-    copy.start()
+def takes_row_above(sec):
+    return sec < 2
+
+
+def is_ring_head(sec, row):
+    return takes_row_above(sec) & (lax.rem(row, RING) == 0)
+
+
+def prepare_kernel(plan, offsets, initial, stiffness, record, springs):
     record[...] = jnp.zeros((1, PATCH), f32)
     for i in range(2):
         record[:, pl.ds(i * COLS, COLS)] = offsets[0, i].astype(f32)
@@ -123,38 +131,34 @@
     for sweep in range(SWEEPS):
         picked = jnp.sum(jnp.where(level_id == plan[sweep], stiffness[...], 0.0), axis=1, keepdims=True)
         springs[pl.ds(2 * sweep, 2), :] = jnp.broadcast_to(picked, (2, PATCH))
-    copy.wait()
 
 
 def prepare(plan, offsets, initial, stiffness):
-    tables = jnp.asarray(constant_tables())
     in_vmem = pl.BlockSpec(memory_space=pltpu.VMEM)
-    anywhere = pl.BlockSpec(memory_space=pl.ANY)
     return pl.pallas_call(
         prepare_kernel,
-        out_shape=[
-            jax.ShapeDtypeStruct(tables.shape, bf16),
-            jax.ShapeDtypeStruct((1, PATCH), f32),
-            jax.ShapeDtypeStruct((8, PATCH), f32),
-        ],
-        in_specs=[pl.BlockSpec(memory_space=pltpu.SMEM), anywhere, in_vmem, in_vmem, in_vmem],
-        out_specs=[in_vmem] * 3,
-        scratch_shapes=[pltpu.SemaphoreType.DMA],
+        out_shape=[jax.ShapeDtypeStruct((1, PATCH), f32), jax.ShapeDtypeStruct((8, PATCH), f32)],
+        in_specs=[pl.BlockSpec(memory_space=pltpu.SMEM), in_vmem, in_vmem, in_vmem],
+        out_specs=[in_vmem] * 2,
         compiler_params=pltpu.CompilerParams(vmem_limit_bytes=VMEM_LIMIT),
-    )(plan, tables, offsets, initial, stiffness.T)
-
-
-def section_spectra(upper, lower, tables):
+        cost_estimate=pl.CostEstimate(flops=PREPARE_FLOPS, bytes_accessed=10_000, transcendentals=0),
+    )(plan, offsets, initial, stiffness.T)
+
+
+def section_spectra(first, second, tables):
     nyq_t = table(tables, "nyquist")
     nyq_t = jnp.concatenate([nyq_t[:, :PATCH], nyq_t[:, PATCH:]], axis=0)
     rows_t = jnp.concatenate([table(tables, "rows"), nyq_t], axis=1)
-    columns = table(tables, "columns")
+    downward = takes_row_above(lax.axis_index("sec"))
+    columns = jnp.where(
+        jnp.broadcast_to(downward, (2 * PATCH, 2 * PATCH)), table(tables, "turned"), table(tables, "columns")
+    )
     lane = lax.broadcasted_iota(jnp.int32, (PATCH, PATCH), 1)
     nyquist = jnp.zeros((PATCH, PATCH), f32)
     stacked = []
     for m in range(PAIRS):
         span = 2 * PATCH if m < PAIRS - 1 else WIDTH - m * PATCH
-        tile = jnp.concatenate([upper(m * PATCH, span), lower(m * PATCH, span)], axis=0)
+        tile = jnp.concatenate([first(m * PATCH, span), second(m * PATCH, span)], axis=0)
         seg = dot(tile, rows_t[:span])
         nyquist = jnp.where(lane // 2 == m, seg[:, 2 * PATCH :], nyquist)
         seg = seg[:, : 2 * PATCH].astype(bf16)
@@ -176,13 +180,19 @@
     return lambda start, span: ref[0, :, pl.ds(start, span)]
 
 
-def own_kernel(own, below, tables, spec, energies):
-    for m, spectrum in enumerate(section_spectra(block_tile(own), block_tile(below), tables)):
+def own_kernel(images, head, across, tables, spec, energies):
+    at_head = is_ring_head(lax.axis_index("sec"), lax.axis_index("row"))
+
+    def own(start, span):
+        here = images[0, :, pl.ds(start, span)]
+        return jnp.where(jnp.broadcast_to(at_head, here.shape), head[0, :, pl.ds(start, span)], here)
+
+    for m, spectrum in enumerate(section_spectra(own, block_tile(across), tables)):
         spec[m] = spectrum
         energies[pl.ds(m, 1), :] = energy(spectrum)
 
 
-def own_spectra(own, below, tables):
+def own_spectra(images, head, across, tables):
     in_vmem = pl.BlockSpec(memory_space=pltpu.VMEM)
     return pl.pallas_call(
         own_kernel,
@@ -190,17 +200,23 @@
             jax.ShapeDtypeStruct((PAIRS + 1, 2 * PATCH, PATCH), bf16),
             jax.ShapeDtypeStruct((2 * PAIRS, PATCH), f32),
         ],
-        in_specs=[in_vmem] * 3,
+        in_specs=[in_vmem] * 4,
         out_specs=[in_vmem] * 2,
         compiler_params=pltpu.CompilerParams(vmem_limit_bytes=VMEM_LIMIT),
         cost_estimate=pl.CostEstimate(flops=600_000_000, bytes_accessed=2_000_000, transcendentals=0),
-    )(own, below, tables)
-
-
-def flow_kernel(own_spec, own_energies, near, near_below, record, remote, tables, out, spec, lagged):
+    )(images, head, across, tables)
+
+
+def flow_kernel(
+    own_spec, own_energies, near, near_far, near_across, record, remote, far_offsets, tables, out, spec, lagged, shift_row
+):
     spread = table(tables, "spread")
     energies = []
-    for m, spectrum in enumerate(section_spectra(block_tile(near), block_tile(near_below), tables)):
+
+    def second(start, span):
+        return near_far[0, :, pl.ds(start, span)] + near_across[0, :, pl.ds(start, span)]
+
+    for m, spectrum in enumerate(section_spectra(block_tile(near), second, tables)):
         spec[m] = spectrum
         energies.append(energy(spectrum))
 
@@ -256,7 +272,12 @@
     surface = found[:rows_all, :PATCH] + found[:rows_all, PATCH:] + found[rows_all:, :PATCH]
     surface = surface.reshape(PAIRS, SHIFTS, PATCH)
 
+    for i in range(2):
+        shift_row[:, pl.ds(i * COLS, COLS)] = far_offsets[0, i].astype(f32)
     rec = record[...]
+    lane_1 = lax.broadcasted_iota(jnp.int32, (1, PATCH), 1)
+    downward = jnp.broadcast_to(takes_row_above(lax.axis_index("sec")), (1, PATCH))
+    rec = jnp.where(downward & (lane_1 < 2 * COLS), shift_row[...], rec)
     at_y = jnp.where(first_16, rec, 0.0)
     at_x = jnp.where(own_pair & (lane >= COLS) & (lane < 2 * COLS), rec, 0.0)
     gather = spread[:PATCH, PATCH:]
@@ -284,7 +305,6 @@
     found = found[: 4 * PAIRS] + found[4 * PAIRS : 8 * PAIRS] + found[8 * PAIRS :]
     found = found.reshape(4, PAIRS, PATCH)
     found = jnp.sum(jnp.where(own_pair[None], found, 0.0), axis=1) * (1.0 / (PATCH * PATCH))
-    lane_1 = lax.broadcasted_iota(jnp.int32, (1, PATCH), 1)
     slope = jnp.where(lane_1 < COLS, found[0:1], found[2:3])
     bend = jnp.where(lane_1 < COLS, found[1:2], found[3:4])
     flow = rec + 0.5 * slope / (1.0 + jnp.abs(bend))
@@ -294,8 +314,8 @@
         out[:, pl.ds((4 + i) * COLS, COLS)] = jnp.broadcast_to(remote[0, i], (out.shape[0], COLS))
 
 
-def pair_flow(own_parts, near, near_below, record, remote_initial, tables, copies):
-    operands = (*own_parts, near, near_below, record, remote_initial, tables)
+def pair_flow(own_parts, blocks, record, remote_initial, far_offsets, tables, copies):
+    operands = (*own_parts, *blocks, record, remote_initial, far_offsets, tables)
     return pl.pallas_call(
         flow_kernel,
         out_shape=jax.ShapeDtypeStruct((copies, PATCH), f32),
@@ -304,6 +324,7 @@
         scratch_shapes=[
             pltpu.VMEM((PAIRS + 1, 2 * PATCH, PATCH), bf16),
             pltpu.VMEM(((PAIRS + 1) * SHIFTS, 2 * PATCH), f32),
+            pltpu.VMEM((1, PATCH), f32),
         ],
         compiler_params=pltpu.CompilerParams(vmem_limit_bytes=VMEM_LIMIT),
     )(*operands)
@@ -334,13 +355,17 @@
     final = in_ring == RING - 1
     here = ring[...]
     beyond = other[...]
-    flows = [jnp.where(valid, b, 0.0) for b in (here, beyond)]
     moving = [pltpu.roll(b, PATCH - 2 * COLS, 1) for b in (here, beyond)]
     third = pltpu.roll(here, PATCH - 4 * COLS, 1)
 
     def moved(x, by):
         by = by % count
         return jnp.concatenate([x[by:], x[:by]], axis=0)
+
+    flows = []
+    for b in (here, beyond):
+        found = jnp.where(takes_row_above(section), jnp.where(final, moved(b, 1 - RING), moved(b, 1)), b)
+        flows.append(jnp.where(valid, found, 0.0))
 
     for sweep in range(SWEEPS):
         spring = springs[pl.ds(2 * sweep, 1), :]
@@ -398,27 +423,58 @@
     return route
 
 
+def image_routes(rows):
+    at = lambda s, r: s * rows + r
+    across, near, far, head, shifts = [], [], [], [], []
+    for r in range(rows):
+        ring_head = r % RING == 0
+        above = r + RING - 1 if ring_head else r - 1
+        for s in range(SECS):
+            if takes_row_above(s):
+                across.append((at(s, above), at(s, r)))
+                shifts.append((at(s, above), at(s, r)))
+                beside = r + RING if ring_head else r
+                if beside < rows:
+                    near.append((at(s + 1, beside), at(s, r)))
+                    if ring_head:
+                        head.append((at(s, beside), at(s, r)))
+                if s == 1:
+                    far.append((at(2, above), at(1, r)))
+            else:
+                if r < rows - 1:
+                    across.append((at(s, r + 1), at(s, r)))
+                if s == 2:
+                    near.append((at(3, r), at(2, r)))
+    return across, near, far, head, shifts
+
+
 def per_device(images, initial, offsets, stiffness, plan):
     rows = lax.axis_size("row")
-    below = shifted(images, "row", -1)
+    both = ("sec", "row")
+    across_route, near_route, far_route, head_route, shift_route = image_routes(rows)
+    across = lax.ppermute(images, both, across_route)
+    near = lax.ppermute(images, both, near_route)
+    near_far = lax.ppermute(images, both, far_route)
+    head = lax.ppermute(images, both, head_route)
+    far_offsets = lax.ppermute(offsets, both, shift_route)
     remote_initial = lax.ppermute(initial, "row", ring_route(rows, False))
-    near = shifted(images, "sec", -1)
-    tables, record, springs = prepare(plan, offsets, initial, stiffness)
-    below, remote_initial, tables, record, springs = lax.optimization_barrier(
-        (below, remote_initial, tables, record, springs)
+    record, springs = prepare(plan, offsets, initial, stiffness)
+    across, near_far, head, far_offsets, remote_initial, record, springs = lax.optimization_barrier(
+        (across, near_far, head, far_offsets, remote_initial, record, springs)
     )
-    near_below = shifted(below, "sec", -1)
+    near_across = lax.ppermute(across, "sec", [(1, 0), (3, 2)])
     count = SECS * RING
-    own_parts = own_spectra(images, below, tables)
-    mine = pair_flow(own_parts, near, near_below, record, remote_initial, tables, count)
+    tables = jnp.asarray(constant_tables())
+    own_parts = own_spectra(images, head, across, tables)
+    mine = pair_flow(
+        own_parts, (near, near_far, near_across), record, remote_initial, far_offsets, tables, count
+    )
     groups = [
         [s * rows + RING * g + j for s in range(SECS) for j in range(RING)] for g in range(rows // RING)
     ]
-    ring = lax.all_to_all(mine.reshape(count, 1, PATCH), ("sec", "row"), 0, 0, axis_index_groups=groups)
+    ring = lax.all_to_all(mine.reshape(count, 1, PATCH), both, 0, 0, axis_index_groups=groups)
     other = lax.ppermute(ring, "row", ring_route(rows, True))
-    return tuple(
-        relax(springs, ring.reshape(count, PATCH), other.reshape(count, PATCH), initial.shape)
-    )
+    return tuple(relax(springs, ring.reshape(count, PATCH), other.reshape(count, PATCH), initial.shape))
 
 
 def solution(mesh):

time: 46.4 us -> 48.7 us (1.050)
  blocking collectives: 15.2 us -> 10.4 us
  starting transfers between devices: 15.3 us -> 19.9 us
  waiting for transfers between devices: 8.03 us -> 11.7 us
  local copies, waits for them, and re-layouts: 2.46 us -> 1.65 us
    all_to_all x1, blocking collectives: 15.2 us -> 10.4 us  [per_device(): lax.all_to_all(mine.reshape(count, 1, PATCH), both, 0, 0, axis_index_grou...]
    ppermute x3 -> x6, starting transfers between devices: 10.2 us -> 14.2 us  [the longest x1 4.63 us: per_device(): across = lax.ppermute(images, both, across_route)]
    ppermute x3 -> x6, waiting for transfers between devices: 1.63 us -> 4.73 us  [the longest x1 4.72 us: per_device(): near = lax.ppermute(images, both, near_route)]
    ppermute x1, starting transfers between devices: 2.74 us -> 3.76 us  [per_device(): remote_initial = lax.ppermute(initial, 'row', ring_route(rows, False))]
    unnamed x12, local copies, waits for them, and re-layouts: 2.46 us -> 1.65 us
    ppermute x1, starting transfers between devices: 2.44 us -> 1.91 us  [per_device(): other = lax.ppermute(ring, 'row', ring_route(rows, True))]
    ppermute x1, waiting for transfers between devices: 6.4 us -> 6.94 us  [per_device(): other = lax.ppermute(ring, 'row', ring_route(rows, True))]
  transfers between devices with their start and end apart: 5 -> 8, of which waited for: 2 -> 2; matrix products, arithmetic and copies ran while one was open for 0% -> 0% of each run, Pallas kernels for 3% -> 3%
where the time goes in v6:
time: 48.7 us; the launch traced here: 48.3 us
  starting transfers between devices  19.9 us (41%)
  waiting for transfers between devices  11.7 us (24%)
  blocking collectives  10.4 us (21%)
  Pallas kernels  3.94 us (8%)
  local copies, waits for them, and re-layouts  1.65 us (3%)
  between operations  0.79 us (2%)
    all_to_all x1, blocking collectives, per_device(): lax.all_to_all(mine.reshape(count, 1, PATCH), both, 0, 0, axis_index_grou...  10.4 us
    ppermute x1, waiting for transfers between devices, per_device(): other = lax.ppermute(ring, 'row', ring_route(rows, True))  6.94 us
    ppermute x1, waiting for transfers between devices, per_device(): near = lax.ppermute(images, both, near_route)  4.72 us
    ppermute x1, starting transfers between devices, per_device(): across = lax.ppermute(images, both, across_route)  4.63 us
    ppermute x1, starting transfers between devices, per_device(): head = lax.ppermute(images, both, head_route)  3.76 us
    ppermute x1, starting transfers between devices, per_device(): remote_initial = lax.ppermute(initial, 'row', ring_route(rows, False))  3.76 us
    ppermute x1, starting transfers between devices, per_device(): far_offsets = lax.ppermute(offsets, both, shift_route)  2.62 us
    ppermute x1, starting transfers between devices, per_device(): other = lax.ppermute(ring, 'row', ring_route(rows, True))  1.91 us
  transfers between devices with their start and end apart: 8, of which 2 were waited for; matrix products, arithmetic and copies ran while one was open for 0% of the time, Pallas kernels for 3%

profile of v6, /device:TPU:256, one launch (start us, length us, event | category | flops | bytes accessed | tf_op | source)
XLA Modules:
  0.0 48.3 jit_solution(62597601184861281)
XLA Ops:
  0.7 4.6 %collective-permute-start = (bf16[1,64,1088]{2,1,0:T(8,128)(2,1)}, bf16[1,64,1088]{2,1,0:T(8,128)(2,1)S(1)}, u32[]{:S(2)}, u32[]{:S(2)}) collective-permute-start(bf16[1,64,1088]{2,1,0:T(8,128)(2,1)} %images.1), channel_id=1, source_target_pairs={{3,0},{131,128},{257,256},{385,384},{0,1},{128,129},{258,257},{386... | collective-permute-start | bytes 417800 | tf_op jit(solution)/shard_map/ppermute | solution.py:455
  5.3 0.7 %collective-permute-start.1 = (bf16[1,64,1088]{2,1,0:T(8,128)(2,1)}, bf16[1,64,1088]{2,1,0:T(8,128)(2,1)S(1)}, u32[]{:S(2)}, u32[]{:S(2)}) collective-permute-start(bf16[1,64,1088]{2,1,0:T(8,128)(2,1)} %images.1), channel_id=1, source_target_pairs={{259,128},{256,129},{257,130},{258,131},{263,132},{260,133},{261,1... | collective-permute-start | bytes 417800 | tf_op jit(solution)/shard_map/ppermute | solution.py:457
  6.0 3.8 %collective-permute-start.2 = (bf16[1,64,1088]{2,1,0:T(8,128)(2,1)}, bf16[1,64,1088]{2,1,0:T(8,128)(2,1)S(1)}, u32[]{:S(2)}, u32[]{:S(2)}) collective-permute-start(bf16[1,64,1088]{2,1,0:T(8,128)(2,1)} %images.1), channel_id=1, source_target_pairs={{4,0},{132,128},{8,4},{136,132},{12,8},{140,136},{16,12},{144,140}... | collective-permute-start | bytes 417800 | tf_op jit(solution)/shard_map/ppermute | solution.py:458
  9.7 2.6 %collective-permute-start.3 = (s32[1,2,1,16]{3,2,1,0:T(1,128)}, s32[1,2,1,16]{3,2,1,0:T(1,128)S(1)}, u32[]{:S(2)}, u32[]{:S(2)}) collective-permute-start(s32[1,2,1,16]{3,2,1,0:T(1,128)} %offsets.1), channel_id=1, source_target_pairs={{3,0},{131,128},{0,1},{128,129},{1,2},{129,130},{2,3},{130,131},{7... | collective-permute-start | bytes 392 | tf_op jit(solution)/shard_map/ppermute | solution.py:459
  12.4 3.8 %collective-permute-start.4 = (f32[1,2,1,16]{3,2,1,0:T(1,128)}, f32[1,2,1,16]{3,2,1,0:T(1,128)S(1)}, u32[]{:S(2)}, u32[]{:S(2)}) collective-permute-start(f32[1,2,1,16]{3,2,1,0:T(1,128)} %initial.1), channel_id=1, source_target_pairs={{4,0},{5,1},{8,4},{9,5},{2,6},{3,7},{12,8},{13,9},{6,10},{7,11},{1... | collective-permute-start | bytes 392 | tf_op jit(solution)/shard_map/ppermute | solution.py:460
  16.2 0.7 %copy-done.3 = s32[1,2,1,16]{3,2,1,0:T(1,128)S(1)} copy-done((s32[1,2,1,16]{3,2,1,0:T(1,128)S(1)}, s32[1,2,1,16]{3,2,1,0:T(1,128)}, u32[]{:S(2)}) %copy-start.3) | copy-done | bytes 152
  16.8 0.7 %copy-done.4 = f32[1,2,1,16]{3,2,1,0:T(1,128)S(1)} copy-done((f32[1,2,1,16]{3,2,1,0:T(1,128)S(1)}, f32[1,2,1,16]{3,2,1,0:T(1,128)}, u32[]{:S(2)}) %copy-start.4) | copy-done | bytes 152
  17.5 0.6 %shard_map.77 = (f32[1,128]{1,0:T(1,128)S(1)}, f32[8,128]{1,0:T(8,128)S(1)}) custom-call(s32[3]{0:T(128)S(1)} %copy-done.5, s32[1,2,1,16]{3,2,1,0:T(1,128)S(1)} %copy-done.3, f32[1,2,1,16]{3,2,1,0:T(1,128)S(1)} %copy-done.4, f32[2,8]{1,0:T(2,128)S(1)} %bitcast.11), custom_call_target="tpu_custom_call" | custom-call | flops 1000000000 | bytes 10000 | tf_op jit(solution)/shard_map/pallas_call | solution.py:138
  18.1 0.0 collective-permute-done.3.far_offsets
  18.1 0.3 copy-done.1
  18.4 1.3 %collective-permute-start.5 = (bf16[1,64,1088]{2,1,0:T(8,128)(2,1)S(1)}, bf16[1,64,1088]{2,1,0:T(8,128)(2,1)S(1)}, u32[]{:S(2)}, u32[]{:S(2)}) collective-permute-start(bf16[1,64,1088]{2,1,0:T(8,128)(2,1)S(1)} %copy-done.1), channel_id=1, source_target_pairs={{132,0},{260,128},{384,256},{129,1},{257,129},{385,257},{130,2},{2... | collective-permute-start | bytes 417800 | tf_op jit(solution)/shard_map/ppermute | solution.py:456
  19.7 0.0 collective-permute-done.4.remote
  19.7 0.0 collective-permute-done.across
  19.7 0.0 collective-permute-done.1.near_far
  19.7 0.0 collective-permute-done.2.head
  19.7 1.3 %collective-permute-start.6 = (bf16[1,64,1088]{2,1,0:T(8,128)(2,1)S(1)}, bf16[1,64,1088]{2,1,0:T(8,128)(2,1)S(1)}, u32[]{:S(2)}, u32[]{:S(2)}) collective-permute-start(bf16[1,64,1088]{2,1,0:T(8,128)(2,1)S(1)} %collective-permute-done.across), channel_id=1, source_target_pairs={{128,0},{384,256},{129,1},{385,257},{130,2},{386,258},{131,3},{387... | collective-permute-start | bytes 417800 | tf_op jit(solution)/shard_map/ppermute | solution.py:465
  21.1 0.7 %shard_map.78 = (bf16[9,256,128]{2,1,0:T(8,128)(2,1)S(1)}, f32[16,128]{1,0:T(8,128)S(1)}) custom-call(bf16[1,64,1088]{2,1,0:T(8,128)(2,1)S(1)} %copy-done.1, bf16[1,64,1088]{2,1,0:T(8,128)(2,1)S(1)} %collective-permute-done.2.head, bf16[1,64,1088]{2,1,0:T(8,128)(2,1)S(1)} %collective-permute-done.across, bf16[1600,256]{1,0:T(8,128)(2,1)S(1)} %copy-done), custom_call_target="tpu_custom_call" | custom-call | flops 600000000 | bytes 2000000 | tf_op jit(solution)/shard_map/pallas_call | solution.py:197
  21.7 4.7 %collective-permute-done.5.near = bf16[1,64,1088]{2,1,0:T(8,128)(2,1)S(1)} collective-permute-done((bf16[1,64,1088]{2,1,0:T(8,128)(2,1)S(1)}, bf16[1,64,1088]{2,1,0:T(8,128)(2,1)S(1)}, u32[]{:S(2)}, u32[]{:S(2)}) %collective-permute-start.5) | collective-permute-done | bytes 139296 | tf_op jit(solution)/shard_map/ppermute | solution.py:456
  26.4 0.0 collective-permute-done.6.near_across
  26.4 1.7 %shard_map.79 = f32[16,128]{1,0:T(8,128)S(1)} custom-call(bf16[9,256,128]{2,1,0:T(8,128)(2,1)S(1)} %get-tuple-element.18.own_spec, f32[16,128]{1,0:T(8,128)S(1)} %get-tuple-element.19.own_energies, bf16[1,64,1088]{2,1,0:T(8,128)(2,1)S(1)} %collective-permute-done.5.near, bf16[1,64,1088]{2,1,0:T(8,128)(2,1)S(1)} %collective-permute-done.1.near_far, ...), custom_call_target="tpu_custom_call" | custom-call | tf_op jit(solution)/shard_map/pallas_call | solution.py:319
  28.2 10.4 %all_to_all.5 = f32[16,1,128]{2,1,0:T(1,128)S(1)} all-to-all(f32[16,1,128]{2,1,0:T(1,128)S(1)} %bitcast.7), channel_id=1, replica_groups={{0,1,2,3,128,129,130,131,256,257,258,259,384,385,386,387},{4,5,6,7,132,..., dimensions={0} | all-to-all | bytes 16384 | tf_op jit(solution)/shard_map/all_to_all | solution.py:475
  38.5 1.9 %collective-permute-start.7 = (f32[16,1,128]{2,0,1:T(8,128)S(1)}, f32[16,1,128]{2,0,1:T(8,128)S(1)}, u32[]{:S(2)}, u32[]{:S(2)}) collective-permute-start(f32[16,1,128]{2,0,1:T(8,128)S(1)} %bitcast.8), channel_id=1, source_target_pairs={{6,2},{7,3},{0,4},{1,5},{10,6},{11,7},{4,8},{5,9},{14,10},{15,11},... | collective-permute-start | bytes 24584 | tf_op jit(solution)/shard_map/ppermute | solution.py:476
  40.5 6.9 %collective-permute-done.7 = f32[16,1,128]{2,0,1:T(8,128)S(1)} collective-permute-done((f32[16,1,128]{2,0,1:T(8,128)S(1)}, f32[16,1,128]{2,0,1:T(8,128)S(1)}, u32[]{:S(2)}, u32[]{:S(2)}) %collective-permute-start.7) | collective-permute-done | bytes 8224 | tf_op jit(solution)/shard_map/ppermute | solution.py:476
  47.4 0.9 %shard_map.80 = (f32[1,2,1,16]{3,2,1,0:T(1,128)}, f32[1,2,1,16]{3,2,1,0:T(1,128)}) custom-call(f32[8,128]{1,0:T(8,128)S(1)} %get-tuple-element.15.springs, f32[16,128]{1,0:T(8,128)S(1)} %bitcast.9, f32[16,128]{1,0:T(8,128)S(1)} %bitcast.10), custom_call_target="tpu_custom_call" | custom-call | tf_op jit(solution)/shard_map/pallas_call | solution.py:402
  (9 shorter events, 0.0 us)
Async XLA Ops:
  0.6 15.5 %copy-start.2 = (f32[8,2]{0,1:T(2,128)S(1)}, f32[8,2]{0,1:T(2,128)}, u32[]{:S(2)}) copy-start(f32[8,2]{0,1:T(2,128)} %param.9) | copy-start | bytes 196
  0.6 15.5 %copy-start.5 = (s32[3]{0:T(128)S(1)}, s32[3]{0:T(128)}, u32[]{:S(2)}) copy-start(s32[3]{0:T(128)} %plan.1) | copy-start | bytes 40
  0.7 19.1 %collective-permute-start = (bf16[1,64,1088]{2,1,0:T(8,128)(2,1)}, bf16[1,64,1088]{2,1,0:T(8,128)(2,1)S(1)}, u32[]{:S(2)}, u32[]{:S(2)}) collective-permute-start(bf16[1,64,1088]{2,1,0:T(8,128)(2,1)} %images.1), channel_id=1, source_target_pairs={{3,0},{131,128},{257,256},{385,384},{0,1},{128,129},{258,257},{386... | collective-permute-start | bytes 417800 | tf_op jit(solution)/shard_map/ppermute | solution.py:455
  5.3 14.4 %collective-permute-start.1 = (bf16[1,64,1088]{2,1,0:T(8,128)(2,1)}, bf16[1,64,1088]{2,1,0:T(8,128)(2,1)S(1)}, u32[]{:S(2)}, u32[]{:S(2)}) collective-permute-start(bf16[1,64,1088]{2,1,0:T(8,128)(2,1)} %images.1), channel_id=1, source_target_pairs={{259,128},{256,129},{257,130},{258,131},{263,132},{260,133},{261,1... | collective-permute-start | bytes 417800 | tf_op jit(solution)/shard_map/ppermute | solution.py:457
  6.0 13.8 %collective-permute-start.2 = (bf16[1,64,1088]{2,1,0:T(8,128)(2,1)}, bf16[1,64,1088]{2,1,0:T(8,128)(2,1)S(1)}, u32[]{:S(2)}, u32[]{:S(2)}) collective-permute-start(bf16[1,64,1088]{2,1,0:T(8,128)(2,1)} %images.1), channel_id=1, source_target_pairs={{4,0},{132,128},{8,4},{136,132},{12,8},{140,136},{16,12},{144,140}... | collective-permute-start | bytes 417800 | tf_op jit(solution)/shard_map/ppermute | solution.py:458
  9.7 8.4 %collective-permute-start.3 = (s32[1,2,1,16]{3,2,1,0:T(1,128)}, s32[1,2,1,16]{3,2,1,0:T(1,128)S(1)}, u32[]{:S(2)}, u32[]{:S(2)}) collective-permute-start(s32[1,2,1,16]{3,2,1,0:T(1,128)} %offsets.1), channel_id=1, source_target_pairs={{3,0},{131,128},{0,1},{128,129},{1,2},{129,130},{2,3},{130,131},{7... | collective-permute-start | bytes 392 | tf_op jit(solution)/shard_map/ppermute | solution.py:459
  12.4 7.3 %collective-permute-start.4 = (f32[1,2,1,16]{3,2,1,0:T(1,128)}, f32[1,2,1,16]{3,2,1,0:T(1,128)S(1)}, u32[]{:S(2)}, u32[]{:S(2)}) collective-permute-start(f32[1,2,1,16]{3,2,1,0:T(1,128)} %initial.1), channel_id=1, source_target_pairs={{4,0},{5,1},{8,4},{9,5},{2,6},{3,7},{12,8},{13,9},{6,10},{7,11},{1... | collective-permute-start | bytes 392 | tf_op jit(solution)/shard_map/ppermute | solution.py:460
  16.1 0.7 %copy-start.3 = (s32[1,2,1,16]{3,2,1,0:T(1,128)S(1)}, s32[1,2,1,16]{3,2,1,0:T(1,128)}, u32[]{:S(2)}) copy-start(s32[1,2,1,16]{3,2,1,0:T(1,128)} %offsets.1) | copy-start | bytes 388
  16.8 0.7 %copy-start.4 = (f32[1,2,1,16]{3,2,1,0:T(1,128)S(1)}, f32[1,2,1,16]{3,2,1,0:T(1,128)}, u32[]{:S(2)}) copy-start(f32[1,2,1,16]{3,2,1,0:T(1,128)} %initial.1) | copy-start | bytes 388
  17.5 0.9 %copy-start.1 = (bf16[1,64,1088]{2,1,0:T(8,128)(2,1)S(1)}, bf16[1,64,1088]{2,1,0:T(8,128)(2,1)}, u32[]{:S(2)}) copy-start(bf16[1,64,1088]{2,1,0:T(8,128)(2,1)} %images.1) | copy-start | bytes 417796
  17.5 3.5 %copy-start = (bf16[1600,256]{1,0:T(8,128)(2,1)S(1)}, bf16[1600,256]{1,0:T(8,128)(2,1)}, u32[]{:S(2)}) copy-start(bf16[1600,256]{1,0:T(8,128)(2,1)} %constant.2.clone.tables) | copy-start | bytes 2457604
  18.4 8.0 %collective-permute-start.5 = (bf16[1,64,1088]{2,1,0:T(8,128)(2,1)S(1)}, bf16[1,64,1088]{2,1,0:T(8,128)(2,1)S(1)}, u32[]{:S(2)}, u32[]{:S(2)}) collective-permute-start(bf16[1,64,1088]{2,1,0:T(8,128)(2,1)S(1)} %copy-done.1), channel_id=1, source_target_pairs={{132,0},{260,128},{384,256},{129,1},{257,129},{385,257},{130,2},{2... | collective-permute-start | bytes 417800 | tf_op jit(solution)/shard_map/ppermute | solution.py:456
  19.7 6.7 %collective-permute-start.6 = (bf16[1,64,1088]{2,1,0:T(8,128)(2,1)S(1)}, bf16[1,64,1088]{2,1,0:T(8,128)(2,1)S(1)}, u32[]{:S(2)}, u32[]{:S(2)}) collective-permute-start(bf16[1,64,1088]{2,1,0:T(8,128)(2,1)S(1)} %collective-permute-done.across), channel_id=1, source_target_pairs={{128,0},{384,256},{129,1},{385,257},{130,2},{386,258},{131,3},{387... | collective-permute-start | bytes 417800 | tf_op jit(solution)/shard_map/ppermute | solution.py:465
  38.5 8.9 %collective-permute-start.7 = (f32[16,1,128]{2,0,1:T(8,128)S(1)}, f32[16,1,128]{2,0,1:T(8,128)S(1)}, u32[]{:S(2)}, u32[]{:S(2)}) collective-permute-start(f32[16,1,128]{2,0,1:T(8,128)S(1)} %bitcast.8), channel_id=1, source_target_pairs={{6,2},{7,3},{0,4},{1,5},{10,6},{11,7},{4,8},{5,9},{14,10},{15,11},... | collective-permute-start | bytes 24584 | tf_op jit(solution)/shard_map/ppermute | solution.py:476

commit v7 on v5

--- a/solution.py
+++ b/solution.py
@@ -25,6 +25,7 @@
 floor_ratio = 0.2
 
 VMEM_LIMIT = 24 * 1024 * 1024
+PREPARE_FLOPS = 1_000_000_000
 
 f32 = jnp.float32
 bf16 = jnp.bfloat16
@@ -112,36 +113,26 @@
     return jnp.dot(a, b, preferred_element_type=f32)
 
 
-def prepare_kernel(plan, tables, offsets, initial, stiffness, tables_out, record, springs, sem):
-    copy = pltpu.make_async_copy(tables, tables_out, sem)
-    copy.start()
+def prepare_kernel(plan, initial, stiffness, record, springs):
     record[...] = jnp.zeros((1, PATCH), f32)
     for i in range(2):
-        record[:, pl.ds(i * COLS, COLS)] = offsets[0, i].astype(f32)
         record[:, pl.ds((2 + i) * COLS, COLS)] = initial[0, i]
     level_id = lax.broadcasted_iota(jnp.int32, stiffness.shape, 1)
     for sweep in range(SWEEPS):
         picked = jnp.sum(jnp.where(level_id == plan[sweep], stiffness[...], 0.0), axis=1, keepdims=True)
         springs[pl.ds(2 * sweep, 2), :] = jnp.broadcast_to(picked, (2, PATCH))
-    copy.wait()
-
-
-def prepare(plan, offsets, initial, stiffness):
-    tables = jnp.asarray(constant_tables())
+
+
+def prepare(plan, initial, stiffness):
     in_vmem = pl.BlockSpec(memory_space=pltpu.VMEM)
-    anywhere = pl.BlockSpec(memory_space=pl.ANY)
     return pl.pallas_call(
         prepare_kernel,
-        out_shape=[
-            jax.ShapeDtypeStruct(tables.shape, bf16),
-            jax.ShapeDtypeStruct((1, PATCH), f32),
-            jax.ShapeDtypeStruct((8, PATCH), f32),
-        ],
-        in_specs=[pl.BlockSpec(memory_space=pltpu.SMEM), anywhere, in_vmem, in_vmem, in_vmem],
-        out_specs=[in_vmem] * 3,
-        scratch_shapes=[pltpu.SemaphoreType.DMA],
+        out_shape=[jax.ShapeDtypeStruct((1, PATCH), f32), jax.ShapeDtypeStruct((8, PATCH), f32)],
+        in_specs=[pl.BlockSpec(memory_space=pltpu.SMEM), in_vmem, in_vmem],
+        out_specs=[in_vmem] * 2,
         compiler_params=pltpu.CompilerParams(vmem_limit_bytes=VMEM_LIMIT),
-    )(plan, tables, offsets, initial, stiffness.T)
+        cost_estimate=pl.CostEstimate(flops=PREPARE_FLOPS, bytes_accessed=10_000, transcendentals=0),
+    )(plan, initial, stiffness.T)
 
 
 def section_spectra(upper, lower, tables):
@@ -197,7 +188,7 @@
     )(own, below, tables)
 
 
-def flow_kernel(own_spec, own_energies, near, near_below, record, remote, tables, out, spec, lagged):
+def flow_kernel(own_spec, own_energies, near, near_below, record, remote, shifts_in, tables, out, spec, lagged, shift_row):
     spread = table(tables, "spread")
     energies = []
     for m, spectrum in enumerate(section_spectra(block_tile(near), block_tile(near_below), tables)):
@@ -222,17 +213,17 @@
         scale = 1.0 / (PATCH * PATCH)
         return jnp.sqrt(by_pair * scale + 1e-06), jnp.sqrt(by_patch * scale + 1e-06)
 
-    low_pair, low_patch = totals(own_energies[pl.ds(0, PAIRS), :], own_energies[pl.ds(PAIRS, 1), :])
-    up_pair, up_patch = totals(jnp.concatenate(energies[:PAIRS], axis=0), energies[PAIRS])
+    low_pair, low_patch = totals(jnp.concatenate(energies[:PAIRS], axis=0), energies[PAIRS])
+    up_pair, up_patch = totals(own_energies[pl.ds(0, PAIRS), :], own_energies[pl.ds(PAIRS, 1), :])
     floor_pair = floor_ratio * low_pair * up_pair
     floor_patch = floor_ratio * low_patch * up_patch
 
     for m in range(PAIRS + 1):
         floor = floor_pair[m : m + 1] if m < PAIRS else floor_patch
-        low_re = own_spec[m, pl.ds(0, PATCH)].astype(f32)
-        low_im = own_spec[m, pl.ds(PATCH, PATCH)].astype(f32)
-        up_re = spec[m, pl.ds(0, PATCH)].astype(f32)
-        up_im = spec[m, pl.ds(PATCH, PATCH)].astype(f32)
+        low_re = spec[m, pl.ds(0, PATCH)].astype(f32)
+        low_im = spec[m, pl.ds(PATCH, PATCH)].astype(f32)
+        up_re = own_spec[m, pl.ds(0, PATCH)].astype(f32)
+        up_im = own_spec[m, pl.ds(PATCH, PATCH)].astype(f32)
         cross_re = low_re * up_re + low_im * up_im
         cross_im = low_re * up_im - low_im * up_re
         square = cross_re * cross_re + cross_im * cross_im
@@ -256,7 +247,10 @@
     surface = found[:rows_all, :PATCH] + found[:rows_all, PATCH:] + found[rows_all:, :PATCH]
     surface = surface.reshape(PAIRS, SHIFTS, PATCH)
 
-    rec = record[...]
+    shift_row[...] = record[...]
+    for i in range(2):
+        shift_row[:, pl.ds(i * COLS, COLS)] = shifts_in[0, i].astype(f32)
+    rec = shift_row[...]
     at_y = jnp.where(first_16, rec, 0.0)
     at_x = jnp.where(own_pair & (lane >= COLS) & (lane < 2 * COLS), rec, 0.0)
     gather = spread[:PATCH, PATCH:]
@@ -294,8 +288,8 @@
         out[:, pl.ds((4 + i) * COLS, COLS)] = jnp.broadcast_to(remote[0, i], (out.shape[0], COLS))
 
 
-def pair_flow(own_parts, near, near_below, record, remote_initial, tables, copies):
-    operands = (*own_parts, near, near_below, record, remote_initial, tables)
+def pair_flow(own_parts, near, near_below, record, remote_initial, offsets, tables, copies):
+    operands = (*own_parts, near, near_below, record, remote_initial, offsets, tables)
     return pl.pallas_call(
         flow_kernel,
         out_shape=jax.ShapeDtypeStruct((copies, PATCH), f32),
@@ -304,6 +298,7 @@
         scratch_shapes=[
             pltpu.VMEM((PAIRS + 1, 2 * PATCH, PATCH), bf16),
             pltpu.VMEM(((PAIRS + 1) * SHIFTS, 2 * PATCH), f32),
+            pltpu.VMEM((1, PATCH), f32),
         ],
         compiler_params=pltpu.CompilerParams(vmem_limit_bytes=VMEM_LIMIT),
     )(*operands)
@@ -334,13 +329,14 @@
     final = in_ring == RING - 1
     here = ring[...]
     beyond = other[...]
-    flows = [jnp.where(valid, b, 0.0) for b in (here, beyond)]
     moving = [pltpu.roll(b, PATCH - 2 * COLS, 1) for b in (here, beyond)]
     third = pltpu.roll(here, PATCH - 4 * COLS, 1)
 
     def moved(x, by):
         by = by % count
         return jnp.concatenate([x[by:], x[:by]], axis=0)
+
+    flows = [jnp.where(valid, moved(b, RING), 0.0) for b in (here, beyond)]
 
     for sweep in range(SWEEPS):
         spring = springs[pl.ds(2 * sweep, 1), :]
@@ -401,16 +397,18 @@
 def per_device(images, initial, offsets, stiffness, plan):
     rows = lax.axis_size("row")
     below = shifted(images, "row", -1)
+    near = shifted(images, "sec", 1)
+    near_offsets = shifted(offsets, "sec", 1)
     remote_initial = lax.ppermute(initial, "row", ring_route(rows, False))
-    near = shifted(images, "sec", -1)
-    tables, record, springs = prepare(plan, offsets, initial, stiffness)
-    below, remote_initial, tables, record, springs = lax.optimization_barrier(
-        (below, remote_initial, tables, record, springs)
+    record, springs = prepare(plan, initial, stiffness)
+    below, near_offsets, remote_initial, record, springs = lax.optimization_barrier(
+        (below, near_offsets, remote_initial, record, springs)
     )
-    near_below = shifted(below, "sec", -1)
+    near_below = shifted(below, "sec", 1)
     count = SECS * RING
+    tables = jnp.asarray(constant_tables())
     own_parts = own_spectra(images, below, tables)
-    mine = pair_flow(own_parts, near, near_below, record, remote_initial, tables, count)
+    mine = pair_flow(own_parts, near, near_below, record, remote_initial, near_offsets, tables, count)
     groups = [
         [s * rows + RING * g + j for s in range(SECS) for j in range(RING)] for g in range(rows // RING)
     ]

time: 46.4 us -> 48.9 us (1.054)
  starting transfers between devices: 15.3 us -> 18.1 us
  local copies, waits for them, and re-layouts: 2.46 us -> 0.72 us
  blocking collectives: 15.2 us -> 16.2 us
  waiting for transfers between devices: 8.03 us -> 8.8 us
    ppermute x3 -> x4, starting transfers between devices: 10.2 us -> 13.5 us  [shifted(): return lax.ppermute(block, axis, route)]
    unnamed x12 -> x10, local copies, waits for them, and re-layouts: 2.46 us -> 0.72 us
    ppermute x1, waiting for transfers between devices: 0.01 us -> 1.58 us  [per_device(): remote_initial = lax.ppermute(initial, 'row', ring_route(rows, False))]
    ppermute x3 -> x4, waiting for transfers between devices: 1.63 us -> 0.29 us  [shifted(): return lax.ppermute(block, axis, route)]
    all_to_all x1, blocking collectives: 15.2 us -> 16.2 us  [per_device(): lax.all_to_all(mine.reshape(count, 1, PATCH), ('sec', 'row'), 0, 0, axis_...]
    ppermute x1, starting transfers between devices: 2.44 us -> 1.91 us  [per_device(): other = lax.ppermute(ring, 'row', ring_route(rows, True))]
    ppermute x1, waiting for transfers between devices: 6.4 us -> 6.94 us  [per_device(): other = lax.ppermute(ring, 'row', ring_route(rows, True))]
  transfers between devices with their start and end apart: 5 -> 6, of which waited for: 2 -> 3; matrix products, arithmetic and copies ran while one was open for 0% -> 0% of each run, Pallas kernels for 3% -> 3%
where the time goes in v7:
time: 48.9 us; the launch traced here: 48.6 us
  starting transfers between devices  18.1 us (37%)
  blocking collectives  16.2 us (33%)
  waiting for transfers between devices  8.8 us (18%)
  Pallas kernels  3.95 us (8%)
  between operations  0.75 us (2%)
  local copies, waits for them, and re-layouts  0.72 us (1%)
    all_to_all x1, blocking collectives, per_device(): lax.all_to_all(mine.reshape(count, 1, PATCH), ('sec', 'row'), 0, 0, axis_...  16.2 us
    ppermute x4, starting transfers between devices, shifted(): return lax.ppermute(block, axis, route)  13.5 us
    ppermute x1, waiting for transfers between devices, per_device(): other = lax.ppermute(ring, 'row', ring_route(rows, True))  6.94 us
    ppermute x1, starting transfers between devices, per_device(): remote_initial = lax.ppermute(initial, 'row', ring_route(rows, False))  2.74 us
    ppermute x1, starting transfers between devices, per_device(): other = lax.ppermute(ring, 'row', ring_route(rows, True))  1.91 us
    pallas_call x1, Pallas kernels, pair_flow(): pl.pallas_call(flow_kernel, out_shape=jax.ShapeDtypeStruct((copies, PATCH...  1.72 us
    ppermute x1, waiting for transfers between devices, per_device(): remote_initial = lax.ppermute(initial, 'row', ring_route(rows, False))  1.58 us
  transfers between devices with their start and end apart: 6, of which 3 were waited for; matrix products, arithmetic and copies ran while one was open for 0% of the time, Pallas kernels for 3%

profile of v7, /device:TPU:256, one launch (start us, length us, event | category | flops | bytes accessed | tf_op | source)
XLA Modules:
  0.0 48.6 jit_solution(673634331436872382)
XLA Ops:
  0.6 0.0 copy-start.2
  0.6 0.0 copy-start.4
  0.7 7.6 %collective-permute-start = (bf16[1,64,1088]{2,1,0:T(8,128)(2,1)}, bf16[1,64,1088]{2,1,0:T(8,128)(2,1)S(1)}, u32[]{:S(2)}, u32[]{:S(2)}) collective-permute-start(bf16[1,64,1088]{2,1,0:T(8,128)(2,1)} %own.1), channel_id=1, source_target_pairs={{1,0},{2,1},{3,2},{4,3},{5,4},{6,5},{7,6},{8,7},{9,8},{10,9},{11,1... | collective-permute-start | bytes 417800 | tf_op jit(solution)/shard_map/ppermute | solution.py:385
  8.2 1.5 %collective-permute-start.3 = (bf16[1,64,1088]{2,1,0:T(8,128)(2,1)}, bf16[1,64,1088]{2,1,0:T(8,128)(2,1)S(1)}, u32[]{:S(2)}, u32[]{:S(2)}) collective-permute-start(bf16[1,64,1088]{2,1,0:T(8,128)(2,1)} %own.1), channel_id=1, source_target_pairs={{0,128},{128,256},{256,384},{1,129},{129,257},{257,385},{2,130},{1... | collective-permute-start | bytes 417800 | tf_op jit(solution)/shard_map/ppermute | solution.py:385
  9.7 3.1 %collective-permute-start.1 = (s32[1,2,1,16]{3,2,1,0:T(1,128)}, s32[1,2,1,16]{3,2,1,0:T(1,128)S(1)}, u32[]{:S(2)}, u32[]{:S(2)}) collective-permute-start(s32[1,2,1,16]{3,2,1,0:T(1,128)} %param.8), channel_id=1, source_target_pairs={{0,128},{128,256},{256,384},{1,129},{129,257},{257,385},{2,130},{1... | collective-permute-start | bytes 392 | tf_op jit(solution)/shard_map/ppermute | solution.py:385
  12.9 2.7 %collective-permute-start.2 = (f32[1,2,1,16]{3,2,1,0:T(1,128)}, f32[1,2,1,16]{3,2,1,0:T(1,128)S(1)}, u32[]{:S(2)}, u32[]{:S(2)}) collective-permute-start(f32[1,2,1,16]{3,2,1,0:T(1,128)} %initial.1), channel_id=1, source_target_pairs={{4,0},{5,1},{8,4},{9,5},{2,6},{3,7},{12,8},{13,9},{6,10},{7,11},{1... | collective-permute-start | bytes 392 | tf_op jit(solution)/shard_map/ppermute | solution.py:402
  15.6 0.0 copy-done.2
  15.6 0.0 copy-done.4
  15.6 0.0 copy-start.3
  15.6 0.7 %copy-done.3 = f32[1,2,1,16]{3,2,1,0:T(1,128)S(1)} copy-done((f32[1,2,1,16]{3,2,1,0:T(1,128)S(1)}, f32[1,2,1,16]{3,2,1,0:T(1,128)}, u32[]{:S(2)}) %copy-start.3) | copy-done | bytes 152
  16.3 0.6 %shard_map.77 = (f32[1,128]{1,0:T(1,128)S(1)}, f32[8,128]{1,0:T(8,128)S(1)}) custom-call(s32[3]{0:T(128)S(1)} %copy-done.4, f32[1,2,1,16]{3,2,1,0:T(1,128)S(1)} %copy-done.3, f32[2,8]{1,0:T(2,128)S(1)} %bitcast.11), custom_call_target="tpu_custom_call" | custom-call | flops 1000000000 | bytes 10000 | tf_op jit(solution)/shard_map/pallas_call | solution.py:128
  16.9 0.0 collective-permute-done.1.shifts_in
  17.0 1.6 %collective-permute-done.2.remote = f32[1,2,1,16]{3,2,1,0:T(1,128)S(1)} collective-permute-done((f32[1,2,1,16]{3,2,1,0:T(1,128)}, f32[1,2,1,16]{3,2,1,0:T(1,128)S(1)}, u32[]{:S(2)}, u32[]{:S(2)}) %collective-permute-start.2) | collective-permute-done | bytes 160 | tf_op jit(solution)/shard_map/ppermute | solution.py:402
  18.5 0.0 collective-permute-done.below
  18.5 1.3 %collective-permute-start.4 = (bf16[1,64,1088]{2,1,0:T(8,128)(2,1)S(1)}, bf16[1,64,1088]{2,1,0:T(8,128)(2,1)S(1)}, u32[]{:S(2)}, u32[]{:S(2)}) collective-permute-start(bf16[1,64,1088]{2,1,0:T(8,128)(2,1)S(1)} %collective-permute-done.below), channel_id=1, source_target_pairs={{0,128},{128,256},{256,384},{1,129},{129,257},{257,385},{2,130},{1... | collective-permute-start | bytes 417800 | tf_op jit(solution)/shard_map/ppermute | solution.py:385
  19.8 0.0 copy-done
  19.8 0.7 %shard_map.78 = (bf16[9,256,128]{2,1,0:T(8,128)(2,1)S(1)}, f32[16,128]{1,0:T(8,128)S(1)}) custom-call(bf16[1,64,1088]{2,1,0:T(8,128)(2,1)S(1)} %copy-done.1, bf16[1,64,1088]{2,1,0:T(8,128)(2,1)S(1)} %collective-permute-done.below, bf16[1344,256]{1,0:T(8,128)(2,1)S(1)} %copy-done), custom_call_target="tpu_custom_call" | custom-call | flops 600000000 | bytes 2000000 | tf_op jit(solution)/shard_map/pallas_call | solution.py:178
  20.5 0.0 collective-permute-done.3.near
  20.5 0.3 collective-permute-done.4.near_below
  20.8 1.7 %shard_map.79 = f32[16,128]{1,0:T(8,128)S(1)} custom-call(bf16[9,256,128]{2,1,0:T(8,128)(2,1)S(1)} %get-tuple-element.15.own_spec, f32[16,128]{1,0:T(8,128)S(1)} %get-tuple-element.16.own_energies, bf16[1,64,1088]{2,1,0:T(8,128)(2,1)S(1)} %collective-permute-done.3.near, bf16[1,64,1088]{2,1,0:T(8,128)(2,1)S(1)} %collective-permute-done.4.near_below, ...), custom_call_target="tpu_custom_call" | custom-call | tf_op jit(solution)/shard_map/pallas_call | solution.py:293
  22.5 16.2 %all_to_all.5 = f32[16,1,128]{2,1,0:T(1,128)S(1)} all-to-all(f32[16,1,128]{2,1,0:T(1,128)S(1)} %bitcast.7), channel_id=1, replica_groups={{0,1,2,3,128,129,130,131,256,257,258,259,384,385,386,387},{4,5,6,7,132,..., dimensions={0} | all-to-all | bytes 16384 | tf_op jit(solution)/shard_map/all_to_all | solution.py:415
  38.8 1.9 %collective-permute-start.5 = (f32[16,1,128]{2,0,1:T(8,128)S(1)}, f32[16,1,128]{2,0,1:T(8,128)S(1)}, u32[]{:S(2)}, u32[]{:S(2)}) collective-permute-start(f32[16,1,128]{2,0,1:T(8,128)S(1)} %bitcast.8), channel_id=1, source_target_pairs={{6,2},{7,3},{0,4},{1,5},{10,6},{11,7},{4,8},{5,9},{14,10},{15,11},... | collective-permute-start | bytes 24584 | tf_op jit(solution)/shard_map/ppermute | solution.py:416
  40.7 6.9 %collective-permute-done.5 = f32[16,1,128]{2,0,1:T(8,128)S(1)} collective-permute-done((f32[16,1,128]{2,0,1:T(8,128)S(1)}, f32[16,1,128]{2,0,1:T(8,128)S(1)}, u32[]{:S(2)}, u32[]{:S(2)}) %collective-permute-start.5) | collective-permute-done | bytes 8224 | tf_op jit(solution)/shard_map/ppermute | solution.py:416
  47.6 0.9 %shard_map.80 = (f32[1,2,1,16]{3,2,1,0:T(1,128)}, f32[1,2,1,16]{3,2,1,0:T(1,128)}) custom-call(f32[8,128]{1,0:T(8,128)S(1)} %get-tuple-element.13.springs, f32[16,128]{1,0:T(8,128)S(1)} %bitcast.9, f32[16,128]{1,0:T(8,128)S(1)} %bitcast.10), custom_call_target="tpu_custom_call" | custom-call | tf_op jit(solution)/shard_map/pallas_call | solution.py:373
  (3 shorter events, 0.0 us)
Async XLA Ops:
  0.6 15.0 %copy-start.2 = (f32[8,2]{0,1:T(2,128)S(1)}, f32[8,2]{0,1:T(2,128)}, u32[]{:S(2)}) copy-start(f32[8,2]{0,1:T(2,128)} %param.9) | copy-start | bytes 196
  0.6 15.0 %copy-start.4 = (s32[3]{0:T(128)S(1)}, s32[3]{0:T(128)}, u32[]{:S(2)}) copy-start(s32[3]{0:T(128)} %plan.1) | copy-start | bytes 40
  0.7 17.9 %collective-permute-start = (bf16[1,64,1088]{2,1,0:T(8,128)(2,1)}, bf16[1,64,1088]{2,1,0:T(8,128)(2,1)S(1)}, u32[]{:S(2)}, u32[]{:S(2)}) collective-permute-start(bf16[1,64,1088]{2,1,0:T(8,128)(2,1)} %own.1), channel_id=1, source_target_pairs={{1,0},{2,1},{3,2},{4,3},{5,4},{6,5},{7,6},{8,7},{9,8},{10,9},{11,1... | collective-permute-start | bytes 417800 | tf_op jit(solution)/shard_map/ppermute | solution.py:385
  8.2 12.3 %collective-permute-start.3 = (bf16[1,64,1088]{2,1,0:T(8,128)(2,1)}, bf16[1,64,1088]{2,1,0:T(8,128)(2,1)S(1)}, u32[]{:S(2)}, u32[]{:S(2)}) collective-permute-start(bf16[1,64,1088]{2,1,0:T(8,128)(2,1)} %own.1), channel_id=1, source_target_pairs={{0,128},{128,256},{256,384},{1,129},{129,257},{257,385},{2,130},{1... | collective-permute-start | bytes 417800 | tf_op jit(solution)/shard_map/ppermute | solution.py:385
  9.7 7.2 %collective-permute-start.1 = (s32[1,2,1,16]{3,2,1,0:T(1,128)}, s32[1,2,1,16]{3,2,1,0:T(1,128)S(1)}, u32[]{:S(2)}, u32[]{:S(2)}) collective-permute-start(s32[1,2,1,16]{3,2,1,0:T(1,128)} %param.8), channel_id=1, source_target_pairs={{0,128},{128,256},{256,384},{1,129},{129,257},{257,385},{2,130},{1... | collective-permute-start | bytes 392 | tf_op jit(solution)/shard_map/ppermute | solution.py:385
  12.9 5.7 %collective-permute-start.2 = (f32[1,2,1,16]{3,2,1,0:T(1,128)}, f32[1,2,1,16]{3,2,1,0:T(1,128)S(1)}, u32[]{:S(2)}, u32[]{:S(2)}) collective-permute-start(f32[1,2,1,16]{3,2,1,0:T(1,128)} %initial.1), channel_id=1, source_target_pairs={{4,0},{5,1},{8,4},{9,5},{2,6},{3,7},{12,8},{13,9},{6,10},{7,11},{1... | collective-permute-start | bytes 392 | tf_op jit(solution)/shard_map/ppermute | solution.py:402
  15.6 0.7 %copy-start.3 = (f32[1,2,1,16]{3,2,1,0:T(1,128)S(1)}, f32[1,2,1,16]{3,2,1,0:T(1,128)}, u32[]{:S(2)}) copy-start(f32[1,2,1,16]{3,2,1,0:T(1,128)} %initial.1) | copy-start | bytes 388
  16.3 3.5 %copy-start = (bf16[1344,256]{1,0:T(8,128)(2,1)S(1)}, bf16[1344,256]{1,0:T(8,128)(2,1)}, u32[]{:S(2)}) copy-start(bf16[1344,256]{1,0:T(8,128)(2,1)} %constant.2.clone.tables) | copy-start | bytes 2064388
  16.3 3.5 %copy-start.1 = (bf16[1,64,1088]{2,1,0:T(8,128)(2,1)S(1)}, bf16[1,64,1088]{2,1,0:T(8,128)(2,1)}, u32[]{:S(2)}) copy-start(bf16[1,64,1088]{2,1,0:T(8,128)(2,1)} %own.1) | copy-start | bytes 417796
  18.5 2.3 %collective-permute-start.4 = (bf16[1,64,1088]{2,1,0:T(8,128)(2,1)S(1)}, bf16[1,64,1088]{2,1,0:T(8,128)(2,1)S(1)}, u32[]{:S(2)}, u32[]{:S(2)}) collective-permute-start(bf16[1,64,1088]{2,1,0:T(8,128)(2,1)S(1)} %collective-permute-done.below), channel_id=1, source_target_pairs={{0,128},{128,256},{256,384},{1,129},{129,257},{257,385},{2,130},{1... | collective-permute-start | bytes 417800 | tf_op jit(solution)/shard_map/ppermute | solution.py:385
  38.8 8.9 %collective-permute-start.5 = (f32[16,1,128]{2,0,1:T(8,128)S(1)}, f32[16,1,128]{2,0,1:T(8,128)S(1)}, u32[]{:S(2)}, u32[]{:S(2)}) collective-permute-start(f32[16,1,128]{2,0,1:T(8,128)S(1)} %bitcast.8), channel_id=1, source_target_pairs={{6,2},{7,3},{0,4},{1,5},{10,6},{11,7},{4,8},{5,9},{14,10},{15,11},... | collective-permute-start | bytes 24584 | tf_op jit(solution)/shard_map/ppermute | solution.py:416

commit v8 on v7

--- a/solution.py
+++ b/solution.py
@@ -20,6 +20,7 @@
 SHIFTS = 16
 REACH = 5
 WIDTH = 1088
+EXTRA = 16
 
 step_size = 0.2
 floor_ratio = 0.2
@@ -113,26 +114,37 @@
     return jnp.dot(a, b, preferred_element_type=f32)
 
 
-def prepare_kernel(plan, initial, stiffness, record, springs):
+def prepare_kernel(plan, images, offsets, initial, stiffness, remote, sent, record, springs, shifts):
+    sent[0, pl.ds(0, HALF), :] = images[0]
+    sent[0, pl.ds(HALF, EXTRA), :] = jnp.zeros((EXTRA, WIDTH), bf16)
+    shifts[...] = jnp.zeros((EXTRA, PATCH), f32)
     record[...] = jnp.zeros((1, PATCH), f32)
     for i in range(2):
         record[:, pl.ds((2 + i) * COLS, COLS)] = initial[0, i]
+        record[:, pl.ds((4 + i) * COLS, COLS)] = remote[0, i]
+        shifts[pl.ds(0, 1), pl.ds(i * COLS, COLS)] = offsets[0, i].astype(f32)
+    sent[0, pl.ds(HALF, EXTRA), pl.ds(0, PATCH)] = shifts[...].astype(bf16)
     level_id = lax.broadcasted_iota(jnp.int32, stiffness.shape, 1)
     for sweep in range(SWEEPS):
         picked = jnp.sum(jnp.where(level_id == plan[sweep], stiffness[...], 0.0), axis=1, keepdims=True)
         springs[pl.ds(2 * sweep, 2), :] = jnp.broadcast_to(picked, (2, PATCH))
 
 
-def prepare(plan, initial, stiffness):
+def prepare(plan, images, offsets, initial, stiffness, remote_initial):
     in_vmem = pl.BlockSpec(memory_space=pltpu.VMEM)
     return pl.pallas_call(
         prepare_kernel,
-        out_shape=[jax.ShapeDtypeStruct((1, PATCH), f32), jax.ShapeDtypeStruct((8, PATCH), f32)],
-        in_specs=[pl.BlockSpec(memory_space=pltpu.SMEM), in_vmem, in_vmem],
-        out_specs=[in_vmem] * 2,
+        out_shape=[
+            jax.ShapeDtypeStruct((1, HALF + EXTRA, WIDTH), bf16),
+            jax.ShapeDtypeStruct((1, PATCH), f32),
+            jax.ShapeDtypeStruct((8, PATCH), f32),
+        ],
+        in_specs=[pl.BlockSpec(memory_space=pltpu.SMEM)] + [in_vmem] * 5,
+        out_specs=[in_vmem] * 3,
+        scratch_shapes=[pltpu.VMEM((EXTRA, PATCH), f32)],
         compiler_params=pltpu.CompilerParams(vmem_limit_bytes=VMEM_LIMIT),
         cost_estimate=pl.CostEstimate(flops=PREPARE_FLOPS, bytes_accessed=10_000, transcendentals=0),
-    )(plan, initial, stiffness.T)
+    )(plan, images, offsets, initial, stiffness.T, remote_initial)
 
 
 def section_spectra(upper, lower, tables):
@@ -164,7 +176,7 @@
 
 
 def block_tile(ref):
-    return lambda start, span: ref[0, :, pl.ds(start, span)]
+    return lambda start, span: ref[0, pl.ds(0, HALF), pl.ds(start, span)]
 
 
 def own_kernel(own, below, tables, spec, energies):
@@ -188,7 +200,7 @@
     )(own, below, tables)
 
 
-def flow_kernel(own_spec, own_energies, near, near_below, record, remote, shifts_in, tables, out, spec, lagged, shift_row):
+def flow_kernel(own_spec, own_energies, near, near_below, record, tables, out, spec, lagged):
     spread = table(tables, "spread")
     energies = []
     for m, spectrum in enumerate(section_spectra(block_tile(near), block_tile(near_below), tables)):
@@ -247,10 +259,7 @@
     surface = found[:rows_all, :PATCH] + found[:rows_all, PATCH:] + found[rows_all:, :PATCH]
     surface = surface.reshape(PAIRS, SHIFTS, PATCH)
 
-    shift_row[...] = record[...]
-    for i in range(2):
-        shift_row[:, pl.ds(i * COLS, COLS)] = shifts_in[0, i].astype(f32)
-    rec = shift_row[...]
+    rec = near[0, pl.ds(HALF, EXTRA), pl.ds(0, PATCH)].astype(f32)[0:1]
     at_y = jnp.where(first_16, rec, 0.0)
     at_x = jnp.where(own_pair & (lane >= COLS) & (lane < 2 * COLS), rec, 0.0)
     gather = spread[:PATCH, PATCH:]
@@ -282,14 +291,11 @@
     slope = jnp.where(lane_1 < COLS, found[0:1], found[2:3])
     bend = jnp.where(lane_1 < COLS, found[1:2], found[3:4])
     flow = rec + 0.5 * slope / (1.0 + jnp.abs(bend))
-    result = jnp.where(lane_1 < 2 * COLS, flow, rec)
-    out[...] = jnp.broadcast_to(result, out.shape)
-    for i in range(2):
-        out[:, pl.ds((4 + i) * COLS, COLS)] = jnp.broadcast_to(remote[0, i], (out.shape[0], COLS))
-
-
-def pair_flow(own_parts, near, near_below, record, remote_initial, offsets, tables, copies):
-    operands = (*own_parts, near, near_below, record, remote_initial, offsets, tables)
+    out[...] = jnp.broadcast_to(jnp.where(lane_1 < 2 * COLS, flow, record[...]), out.shape)
+
+
+def pair_flow(own_parts, near, near_below, record, tables, copies):
+    operands = (*own_parts, near, near_below, record, tables)
     return pl.pallas_call(
         flow_kernel,
         out_shape=jax.ShapeDtypeStruct((copies, PATCH), f32),
@@ -298,7 +304,6 @@
         scratch_shapes=[
             pltpu.VMEM((PAIRS + 1, 2 * PATCH, PATCH), bf16),
             pltpu.VMEM(((PAIRS + 1) * SHIFTS, 2 * PATCH), f32),
-            pltpu.VMEM((1, PATCH), f32),
         ],
         compiler_params=pltpu.CompilerParams(vmem_limit_bytes=VMEM_LIMIT),
     )(*operands)
@@ -397,18 +402,15 @@
 def per_device(images, initial, offsets, stiffness, plan):
     rows = lax.axis_size("row")
     below = shifted(images, "row", -1)
-    near = shifted(images, "sec", 1)
-    near_offsets = shifted(offsets, "sec", 1)
     remote_initial = lax.ppermute(initial, "row", ring_route(rows, False))
-    record, springs = prepare(plan, initial, stiffness)
-    below, near_offsets, remote_initial, record, springs = lax.optimization_barrier(
-        (below, near_offsets, remote_initial, record, springs)
-    )
+    sent, record, springs = prepare(plan, images, offsets, initial, stiffness, remote_initial)
+    near = shifted(sent, "sec", 1)
+    below, record, springs = lax.optimization_barrier((below, record, springs))
     near_below = shifted(below, "sec", 1)
     count = SECS * RING
     tables = jnp.asarray(constant_tables())
-    own_parts = own_spectra(images, below, tables)
-    mine = pair_flow(own_parts, near, near_below, record, remote_initial, near_offsets, tables, count)
+    own_parts = own_spectra(sent, below, tables)
+    mine = pair_flow(own_parts, near, near_below, record, tables, count)
     groups = [
         [s * rows + RING * g + j for s in range(SECS) for j in range(RING)] for g in range(rows // RING)
     ]

time: 48.9 us -> 49.9 us (1.020)
  local copies, waits for them, and re-layouts: 0.72 us -> 2.28 us
  waiting for transfers between devices: 8.8 us -> 10.2 us
  starting transfers between devices: 18.1 us -> 16.8 us
  blocking collectives: 16.2 us -> 15.6 us
    unnamed x10 -> x12, local copies, waits for them, and re-layouts: 0.72 us -> 2.28 us
    ppermute x1, waiting for transfers between devices: 1.58 us -> 2.93 us  [per_device(): remote_initial = lax.ppermute(initial, 'row', ring_route(rows, False))]
    ppermute x4 -> x3, starting transfers between devices: 13.5 us -> 12.2 us  [shifted(): return lax.ppermute(block, axis, route)]
    all_to_all x1, blocking collectives: 16.2 us -> 15.6 us  [per_device(): lax.all_to_all(mine.reshape(count, 1, PATCH), ('sec', 'row'), 0, 0, axis_...]
  transfers between devices with their start and end apart: 6 -> 5, of which waited for: 3 -> 3; matrix products, arithmetic and copies ran while one was open for 0% -> 0% of each run, Pallas kernels for 3% -> 3%
where the time goes in v8:
time: 49.9 us; the launch traced here: 49.6 us
  starting transfers between devices  16.8 us (34%)
  blocking collectives  15.6 us (31%)
  waiting for transfers between devices  10.2 us (20%)
  Pallas kernels  3.97 us (8%)
  local copies, waits for them, and re-layouts  2.28 us (5%)
  between operations  0.72 us (1%)
    all_to_all x1, blocking collectives, per_device(): lax.all_to_all(mine.reshape(count, 1, PATCH), ('sec', 'row'), 0, 0, axis_...  15.6 us
    ppermute x3, starting transfers between devices, shifted(): return lax.ppermute(block, axis, route)  12.2 us
    ppermute x1, waiting for transfers between devices, per_device(): other = lax.ppermute(ring, 'row', ring_route(rows, True))  6.94 us
    ppermute x1, waiting for transfers between devices, per_device(): remote_initial = lax.ppermute(initial, 'row', ring_route(rows, False))  2.93 us
    ppermute x1, starting transfers between devices, per_device(): remote_initial = lax.ppermute(initial, 'row', ring_route(rows, False))  2.74 us
    unnamed x12, local copies, waits for them, and re-layouts  2.28 us
    ppermute x1, starting transfers between devices, per_device(): other = lax.ppermute(ring, 'row', ring_route(rows, True))  1.91 us
    pallas_call x1, Pallas kernels, pair_flow(): pl.pallas_call(flow_kernel, out_shape=jax.ShapeDtypeStruct((copies, PATCH...  1.73 us
  transfers between devices with their start and end apart: 5, of which 3 were waited for; matrix products, arithmetic and copies ran while one was open for 0% of the time, Pallas kernels for 3%

profile of v8, /device:TPU:256, one launch (start us, length us, event | category | flops | bytes accessed | tf_op | source)
XLA Modules:
  0.0 49.6 jit_solution(7824239602816162782)
XLA Ops:
  0.6 0.0 copy-start.5
  0.6 0.0 copy-start.2
  0.7 7.6 %collective-permute-start = (bf16[1,64,1088]{2,1,0:T(8,128)(2,1)}, bf16[1,64,1088]{2,1,0:T(8,128)(2,1)S(1)}, u32[]{:S(2)}, u32[]{:S(2)}) collective-permute-start(bf16[1,64,1088]{2,1,0:T(8,128)(2,1)} %images.1), channel_id=1, source_target_pairs={{1,0},{2,1},{3,2},{4,3},{5,4},{6,5},{7,6},{8,7},{9,8},{10,9},{11,1... | collective-permute-start | bytes 417800 | tf_op jit(solution)/shard_map/ppermute | solution.py:390
  8.2 2.7 %collective-permute-start.1 = (f32[1,2,1,16]{3,2,1,0:T(1,128)}, f32[1,2,1,16]{3,2,1,0:T(1,128)S(1)}, u32[]{:S(2)}, u32[]{:S(2)}) collective-permute-start(f32[1,2,1,16]{3,2,1,0:T(1,128)} %initial.1), channel_id=1, source_target_pairs={{4,0},{5,1},{8,4},{9,5},{2,6},{3,7},{12,8},{13,9},{6,10},{7,11},{1... | collective-permute-start | bytes 392 | tf_op jit(solution)/shard_map/ppermute | solution.py:405
  11.0 2.9 %collective-permute-done.1.remote = f32[1,2,1,16]{3,2,1,0:T(1,128)S(1)} collective-permute-done((f32[1,2,1,16]{3,2,1,0:T(1,128)}, f32[1,2,1,16]{3,2,1,0:T(1,128)S(1)}, u32[]{:S(2)}, u32[]{:S(2)}) %collective-permute-start.1) | collective-permute-done | bytes 160 | tf_op jit(solution)/shard_map/ppermute | solution.py:405
  13.9 0.0 copy-done.5
  13.9 0.0 copy-done.2
  13.9 0.0 copy-start.1
  13.9 0.9 %copy-done.1 = bf16[1,64,1088]{2,1,0:T(8,128)(2,1)S(1)} copy-done((bf16[1,64,1088]{2,1,0:T(8,128)(2,1)S(1)}, bf16[1,64,1088]{2,1,0:T(8,128)(2,1)}, u32[]{:S(2)}) %copy-start.1) | copy-done | bytes 139288
  14.8 0.7 %copy-done.3 = f32[1,2,1,16]{3,2,1,0:T(1,128)S(1)} copy-done((f32[1,2,1,16]{3,2,1,0:T(1,128)S(1)}, f32[1,2,1,16]{3,2,1,0:T(1,128)}, u32[]{:S(2)}) %copy-start.3) | copy-done | bytes 152
  15.5 0.7 %copy-done.4 = f32[8,2]{0,1:T(2,128)S(1)} copy-done((f32[8,2]{0,1:T(2,128)S(1)}, f32[8,2]{0,1:T(2,128)}, u32[]{:S(2)}) %copy-start.4) | copy-done | bytes 88
  16.2 0.6 %shard_map.77 = (bf16[1,80,1088]{2,1,0:T(8,128)(2,1)S(1)}, f32[1,128]{1,0:T(1,128)S(1)}, f32[8,128]{1,0:T(8,128)S(1)}) custom-call(s32[3]{0:T(128)S(1)} %copy-done.5, bf16[1,64,1088]{2,1,0:T(8,128)(2,1)S(1)} %copy-done.1, s32[1,2,1,16]{3,2,1,0:T(1,128)S(1)} %copy-done.2, f32[1,2,1,16]{3,2,1,0:T(1,128)S(1)} %copy-done.3, f32[2,8]{1,0:T(2,128)S(1)} %bitcast.11, ...), custom_call_target="tpu_custom_call" | custom-call | flops 1000000000 | bytes 10000 | tf_op jit(solution)/shard_map/pallas_call | solution.py:135
  16.8 1.3 %collective-permute-start.2 = (bf16[1,80,1088]{2,1,0:T(8,128)(2,1)S(1)}, bf16[1,80,1088]{2,1,0:T(8,128)(2,1)S(1)}, u32[]{:S(2)}, u32[]{:S(2)}) collective-permute-start(bf16[1,80,1088]{2,1,0:T(8,128)(2,1)S(1)} %get-tuple-element.13.own), channel_id=1, source_target_pairs={{0,128},{128,256},{256,384},{1,129},{129,257},{257,385},{2,130},{1... | collective-permute-start | bytes 522248 | tf_op jit(solution)/shard_map/ppermute | solution.py:390
  18.1 0.0 collective-permute-done.below
  18.1 3.3 %collective-permute-start.3 = (bf16[1,64,1088]{2,1,0:T(8,128)(2,1)S(1)}, bf16[1,64,1088]{2,1,0:T(8,128)(2,1)S(1)}, u32[]{:S(2)}, u32[]{:S(2)}) collective-permute-start(bf16[1,64,1088]{2,1,0:T(8,128)(2,1)S(1)} %collective-permute-done.below), channel_id=1, source_target_pairs={{0,128},{128,256},{256,384},{1,129},{129,257},{257,385},{2,130},{1... | collective-permute-start | bytes 417800 | tf_op jit(solution)/shard_map/ppermute | solution.py:390
  21.5 0.0 copy-done
  21.5 0.7 %shard_map.78 = (bf16[9,256,128]{2,1,0:T(8,128)(2,1)S(1)}, f32[16,128]{1,0:T(8,128)S(1)}) custom-call(bf16[1,80,1088]{2,1,0:T(8,128)(2,1)S(1)} %get-tuple-element.13.own, bf16[1,64,1088]{2,1,0:T(8,128)(2,1)S(1)} %collective-permute-done.below, bf16[1344,256]{1,0:T(8,128)(2,1)S(1)} %copy-done), custom_call_target="tpu_custom_call" | custom-call | flops 600000000 | bytes 2000000 | tf_op jit(solution)/shard_map/pallas_call | solution.py:190
  22.1 0.0 collective-permute-done.2.near
  22.1 0.3 collective-permute-done.3.near_below
  22.4 1.7 %shard_map.79 = f32[16,128]{1,0:T(8,128)S(1)} custom-call(bf16[9,256,128]{2,1,0:T(8,128)(2,1)S(1)} %get-tuple-element.15.own_spec, f32[16,128]{1,0:T(8,128)S(1)} %get-tuple-element.16.own_energies, bf16[1,80,1088]{2,1,0:T(8,128)(2,1)S(1)} %collective-permute-done.2.near, bf16[1,64,1088]{2,1,0:T(8,128)(2,1)S(1)} %collective-permute-done.3.near_below, ...), custom_call_target="tpu_custom_call" | custom-call | tf_op jit(solution)/shard_map/pallas_call | solution.py:299
  24.2 15.6 %all_to_all.5 = f32[16,1,128]{2,1,0:T(1,128)S(1)} all-to-all(f32[16,1,128]{2,1,0:T(1,128)S(1)} %bitcast.7), channel_id=1, replica_groups={{0,1,2,3,128,129,130,131,256,257,258,259,384,385,386,387},{4,5,6,7,132,..., dimensions={0} | all-to-all | bytes 16384 | tf_op jit(solution)/shard_map/all_to_all | solution.py:417
  39.8 1.9 %collective-permute-start.4 = (f32[16,1,128]{2,0,1:T(8,128)S(1)}, f32[16,1,128]{2,0,1:T(8,128)S(1)}, u32[]{:S(2)}, u32[]{:S(2)}) collective-permute-start(f32[16,1,128]{2,0,1:T(8,128)S(1)} %bitcast.8), channel_id=1, source_target_pairs={{6,2},{7,3},{0,4},{1,5},{10,6},{11,7},{4,8},{5,9},{14,10},{15,11},... | collective-permute-start | bytes 24584 | tf_op jit(solution)/shard_map/ppermute | solution.py:418
  41.7 6.9 %collective-permute-done.4 = f32[16,1,128]{2,0,1:T(8,128)S(1)} collective-permute-done((f32[16,1,128]{2,0,1:T(8,128)S(1)}, f32[16,1,128]{2,0,1:T(8,128)S(1)}, u32[]{:S(2)}, u32[]{:S(2)}) %collective-permute-start.4) | collective-permute-done | bytes 8224 | tf_op jit(solution)/shard_map/ppermute | solution.py:418
  48.7 0.9 %shard_map.80 = (f32[1,2,1,16]{3,2,1,0:T(1,128)}, f32[1,2,1,16]{3,2,1,0:T(1,128)}) custom-call(f32[8,128]{1,0:T(8,128)S(1)} %get-tuple-element.12.springs, f32[16,128]{1,0:T(8,128)S(1)} %bitcast.9, f32[16,128]{1,0:T(8,128)S(1)} %bitcast.10), custom_call_target="tpu_custom_call" | custom-call | tf_op jit(solution)/shard_map/pallas_call | solution.py:378
  (3 shorter events, 0.0 us)
Async XLA Ops:
  0.6 13.3 %copy-start.5 = (s32[3]{0:T(128)S(1)}, s32[3]{0:T(128)}, u32[]{:S(2)}) copy-start(s32[3]{0:T(128)} %plan.1) | copy-start | bytes 40
  0.6 13.3 %copy-start.2 = (s32[1,2,1,16]{3,2,1,0:T(1,128)S(1)}, s32[1,2,1,16]{3,2,1,0:T(1,128)}, u32[]{:S(2)}) copy-start(s32[1,2,1,16]{3,2,1,0:T(1,128)} %offsets.1) | copy-start | bytes 388
  0.7 17.5 %collective-permute-start = (bf16[1,64,1088]{2,1,0:T(8,128)(2,1)}, bf16[1,64,1088]{2,1,0:T(8,128)(2,1)S(1)}, u32[]{:S(2)}, u32[]{:S(2)}) collective-permute-start(bf16[1,64,1088]{2,1,0:T(8,128)(2,1)} %images.1), channel_id=1, source_target_pairs={{1,0},{2,1},{3,2},{4,3},{5,4},{6,5},{7,6},{8,7},{9,8},{10,9},{11,1... | collective-permute-start | bytes 417800 | tf_op jit(solution)/shard_map/ppermute | solution.py:390
  8.2 5.7 %collective-permute-start.1 = (f32[1,2,1,16]{3,2,1,0:T(1,128)}, f32[1,2,1,16]{3,2,1,0:T(1,128)S(1)}, u32[]{:S(2)}, u32[]{:S(2)}) collective-permute-start(f32[1,2,1,16]{3,2,1,0:T(1,128)} %initial.1), channel_id=1, source_target_pairs={{4,0},{5,1},{8,4},{9,5},{2,6},{3,7},{12,8},{13,9},{6,10},{7,11},{1... | collective-permute-start | bytes 392 | tf_op jit(solution)/shard_map/ppermute | solution.py:405
  13.9 0.9 %copy-start.1 = (bf16[1,64,1088]{2,1,0:T(8,128)(2,1)S(1)}, bf16[1,64,1088]{2,1,0:T(8,128)(2,1)}, u32[]{:S(2)}) copy-start(bf16[1,64,1088]{2,1,0:T(8,128)(2,1)} %images.1) | copy-start | bytes 417796
  14.8 0.7 %copy-start.3 = (f32[1,2,1,16]{3,2,1,0:T(1,128)S(1)}, f32[1,2,1,16]{3,2,1,0:T(1,128)}, u32[]{:S(2)}) copy-start(f32[1,2,1,16]{3,2,1,0:T(1,128)} %initial.1) | copy-start | bytes 388
  15.5 0.7 %copy-start.4 = (f32[8,2]{0,1:T(2,128)S(1)}, f32[8,2]{0,1:T(2,128)}, u32[]{:S(2)}) copy-start(f32[8,2]{0,1:T(2,128)} %param.9) | copy-start | bytes 196
  16.2 5.3 %copy-start = (bf16[1344,256]{1,0:T(8,128)(2,1)S(1)}, bf16[1344,256]{1,0:T(8,128)(2,1)}, u32[]{:S(2)}) copy-start(bf16[1344,256]{1,0:T(8,128)(2,1)} %constant.2.clone.tables) | copy-start | bytes 2064388
  16.8 5.3 %collective-permute-start.2 = (bf16[1,80,1088]{2,1,0:T(8,128)(2,1)S(1)}, bf16[1,80,1088]{2,1,0:T(8,128)(2,1)S(1)}, u32[]{:S(2)}, u32[]{:S(2)}) collective-permute-start(bf16[1,80,1088]{2,1,0:T(8,128)(2,1)S(1)} %get-tuple-element.13.own), channel_id=1, source_target_pairs={{0,128},{128,256},{256,384},{1,129},{129,257},{257,385},{2,130},{1... | collective-permute-start | bytes 522248 | tf_op jit(solution)/shard_map/ppermute | solution.py:390
  18.1 4.3 %collective-permute-start.3 = (bf16[1,64,1088]{2,1,0:T(8,128)(2,1)S(1)}, bf16[1,64,1088]{2,1,0:T(8,128)(2,1)S(1)}, u32[]{:S(2)}, u32[]{:S(2)}) collective-permute-start(bf16[1,64,1088]{2,1,0:T(8,128)(2,1)S(1)} %collective-permute-done.below), channel_id=1, source_target_pairs={{0,128},{128,256},{256,384},{1,129},{129,257},{257,385},{2,130},{1... | collective-permute-start | bytes 417800 | tf_op jit(solution)/shard_map/ppermute | solution.py:390
  39.8 8.9 %collective-permute-start.4 = (f32[16,1,128]{2,0,1:T(8,128)S(1)}, f32[16,1,128]{2,0,1:T(8,128)S(1)}, u32[]{:S(2)}, u32[]{:S(2)}) collective-permute-start(f32[16,1,128]{2,0,1:T(8,128)S(1)} %bitcast.8), channel_id=1, source_target_pairs={{6,2},{7,3},{0,4},{1,5},{10,6},{11,7},{4,8},{5,9},{14,10},{15,11},... | collective-permute-start | bytes 24584 | tf_op jit(solution)/shard_map/ppermute | solution.py:418

commit v9 on v5

--- a/solution.py
+++ b/solution.py
@@ -25,6 +25,7 @@
 floor_ratio = 0.2
 
 VMEM_LIMIT = 24 * 1024 * 1024
+PREPARE_FLOPS = 1_000_000_000
 
 f32 = jnp.float32
 bf16 = jnp.bfloat16
@@ -112,36 +113,28 @@
     return jnp.dot(a, b, preferred_element_type=f32)
 
 
-def prepare_kernel(plan, tables, offsets, initial, stiffness, tables_out, record, springs, sem):
-    copy = pltpu.make_async_copy(tables, tables_out, sem)
-    copy.start()
+def prepare_kernel(plan, offsets, initial, stiffness, remote, record, springs):
     record[...] = jnp.zeros((1, PATCH), f32)
     for i in range(2):
         record[:, pl.ds(i * COLS, COLS)] = offsets[0, i].astype(f32)
         record[:, pl.ds((2 + i) * COLS, COLS)] = initial[0, i]
+        record[:, pl.ds((4 + i) * COLS, COLS)] = remote[0, i]
     level_id = lax.broadcasted_iota(jnp.int32, stiffness.shape, 1)
     for sweep in range(SWEEPS):
         picked = jnp.sum(jnp.where(level_id == plan[sweep], stiffness[...], 0.0), axis=1, keepdims=True)
         springs[pl.ds(2 * sweep, 2), :] = jnp.broadcast_to(picked, (2, PATCH))
-    copy.wait()
-
-
-def prepare(plan, offsets, initial, stiffness):
-    tables = jnp.asarray(constant_tables())
+
+
+def prepare(plan, offsets, initial, stiffness, remote_initial):
     in_vmem = pl.BlockSpec(memory_space=pltpu.VMEM)
-    anywhere = pl.BlockSpec(memory_space=pl.ANY)
     return pl.pallas_call(
         prepare_kernel,
-        out_shape=[
-            jax.ShapeDtypeStruct(tables.shape, bf16),
-            jax.ShapeDtypeStruct((1, PATCH), f32),
-            jax.ShapeDtypeStruct((8, PATCH), f32),
-        ],
-        in_specs=[pl.BlockSpec(memory_space=pltpu.SMEM), anywhere, in_vmem, in_vmem, in_vmem],
-        out_specs=[in_vmem] * 3,
-        scratch_shapes=[pltpu.SemaphoreType.DMA],
+        out_shape=[jax.ShapeDtypeStruct((1, PATCH), f32), jax.ShapeDtypeStruct((8, PATCH), f32)],
+        in_specs=[pl.BlockSpec(memory_space=pltpu.SMEM)] + [in_vmem] * 4,
+        out_specs=[in_vmem] * 2,
         compiler_params=pltpu.CompilerParams(vmem_limit_bytes=VMEM_LIMIT),
-    )(plan, tables, offsets, initial, stiffness.T)
+        cost_estimate=pl.CostEstimate(flops=PREPARE_FLOPS, bytes_accessed=10_000, transcendentals=0),
+    )(plan, offsets, initial, stiffness.T, remote_initial)
 
 
 def section_spectra(upper, lower, tables):
@@ -197,7 +190,7 @@
     )(own, below, tables)
 
 
-def flow_kernel(own_spec, own_energies, near, near_below, record, remote, tables, out, spec, lagged):
+def flow_kernel(own_spec, own_energies, near, near_below, record, tables, out, spec, lagged):
     spread = table(tables, "spread")
     energies = []
     for m, spectrum in enumerate(section_spectra(block_tile(near), block_tile(near_below), tables)):
@@ -290,12 +283,10 @@
     flow = rec + 0.5 * slope / (1.0 + jnp.abs(bend))
     result = jnp.where(lane_1 < 2 * COLS, flow, rec)
     out[...] = jnp.broadcast_to(result, out.shape)
-    for i in range(2):
-        out[:, pl.ds((4 + i) * COLS, COLS)] = jnp.broadcast_to(remote[0, i], (out.shape[0], COLS))
-
-
-def pair_flow(own_parts, near, near_below, record, remote_initial, tables, copies):
-    operands = (*own_parts, near, near_below, record, remote_initial, tables)
+
+
+def pair_flow(own_parts, near, near_below, record, tables, copies):
+    operands = (*own_parts, near, near_below, record, tables)
     return pl.pallas_call(
         flow_kernel,
         out_shape=jax.ShapeDtypeStruct((copies, PATCH), f32),
@@ -403,14 +394,13 @@
     below = shifted(images, "row", -1)
     remote_initial = lax.ppermute(initial, "row", ring_route(rows, False))
     near = shifted(images, "sec", -1)
-    tables, record, springs = prepare(plan, offsets, initial, stiffness)
-    below, remote_initial, tables, record, springs = lax.optimization_barrier(
-        (below, remote_initial, tables, record, springs)
-    )
+    below, remote_initial = lax.optimization_barrier((below, remote_initial))
     near_below = shifted(below, "sec", -1)
+    record, springs = prepare(plan, offsets, initial, stiffness, remote_initial)
     count = SECS * RING
+    tables = jnp.asarray(constant_tables())
     own_parts = own_spectra(images, below, tables)
-    mine = pair_flow(own_parts, near, near_below, record, remote_initial, tables, count)
+    mine = pair_flow(own_parts, near, near_below, record, tables, count)
     groups = [
         [s * rows + RING * g + j for s in range(SECS) for j in range(RING)] for g in range(rows // RING)
     ]

time: 46.4 us -> 46.4 us (level)
  the two profiles are of different devices: /device:TPU:256 before, /device:TPU:254 now
where the time goes in v9:
time: 46.4 us; the launch traced here: 46 us
  starting transfers between devices  16.6 us (36%)
  waiting for transfers between devices  11.4 us (25%)
  blocking collectives  10.2 us (22%)
  Pallas kernels  3.93 us (8%)
  local copies, waits for them, and re-layouts  3.12 us (7%)
  between operations  0.74 us (2%)
    all_to_all x1, blocking collectives, per_device(): lax.all_to_all(mine.reshape(count, 1, PATCH), ('sec', 'row'), 0, 0, axis_...  10.2 us
    ppermute x3, starting transfers between devices, shifted(): return lax.ppermute(block, axis, route)  9.31 us
    ppermute x1, waiting for transfers between devices, per_device(): other = lax.ppermute(ring, 'row', ring_route(rows, True))  6.94 us
    ppermute x1, starting transfers between devices, per_device(): remote_initial = lax.ppermute(initial, 'row', ring_route(rows, False))  5.41 us
    ppermute x3, waiting for transfers between devices, shifted(): return lax.ppermute(block, axis, route)  4.46 us
    unnamed x14, local copies, waits for them, and re-layouts  3.12 us
    ppermute x1, starting transfers between devices, per_device(): other = lax.ppermute(ring, 'row', ring_route(rows, True))  1.91 us
    pallas_call x1, Pallas kernels, pair_flow(): pl.pallas_call(flow_kernel, out_shape=jax.ShapeDtypeStruct((copies, PATCH...  1.71 us
  transfers between devices with their start and end apart: 5, of which 2 were waited for; matrix products, arithmetic and copies ran while one was open for 0% of the time, Pallas kernels for 3%

profile of v9, /device:TPU:254, one launch (start us, length us, event | category | flops | bytes accessed | tf_op | source)
XLA Modules:
  0.0 46.0 jit_solution(6488713383509284163)
XLA Ops:
  0.6 4.0 %collective-permute-start = (bf16[1,64,1088]{2,1,0:T(8,128)(2,1)}, bf16[1,64,1088]{2,1,0:T(8,128)(2,1)S(1)}, u32[]{:S(2)}, u32[]{:S(2)}) collective-permute-start(bf16[1,64,1088]{2,1,0:T(8,128)(2,1)} %own.1), channel_id=1, source_target_pairs={{1,0},{2,1},{3,2},{4,3},{5,4},{6,5},{7,6},{8,7},{9,8},{10,9},{11,1... | collective-permute-start | bytes 417800 | tf_op jit(solution)/shard_map/ppermute | solution.py:380
  4.7 5.4 %collective-permute-start.1 = (f32[1,2,1,16]{3,2,1,0:T(1,128)}, f32[1,2,1,16]{3,2,1,0:T(1,128)S(1)}, u32[]{:S(2)}, u32[]{:S(2)}) collective-permute-start(f32[1,2,1,16]{3,2,1,0:T(1,128)} %initial.1), channel_id=1, source_target_pairs={{4,0},{5,1},{8,4},{9,5},{2,6},{3,7},{12,8},{13,9},{6,10},{7,11},{1... | collective-permute-start | bytes 392 | tf_op jit(solution)/shard_map/ppermute | solution.py:395
  10.1 2.1 %collective-permute-start.2 = (bf16[1,64,1088]{2,1,0:T(8,128)(2,1)}, bf16[1,64,1088]{2,1,0:T(8,128)(2,1)S(1)}, u32[]{:S(2)}, u32[]{:S(2)}) collective-permute-start(bf16[1,64,1088]{2,1,0:T(8,128)(2,1)} %own.1), channel_id=1, source_target_pairs={{128,0},{256,128},{384,256},{129,1},{257,129},{385,257},{130,2},{2... | collective-permute-start | bytes 417800 | tf_op jit(solution)/shard_map/ppermute | solution.py:380
  12.2 0.0 collective-permute-done.1.remote
  12.2 4.5 %collective-permute-done.below = bf16[1,64,1088]{2,1,0:T(8,128)(2,1)S(1)} collective-permute-done((bf16[1,64,1088]{2,1,0:T(8,128)(2,1)}, bf16[1,64,1088]{2,1,0:T(8,128)(2,1)S(1)}, u32[]{:S(2)}, u32[]{:S(2)}) %collective-permute-start) | collective-permute-done | bytes 139296 | tf_op jit(solution)/shard_map/ppermute | solution.py:380
  16.7 3.1 %collective-permute-start.3 = (bf16[1,64,1088]{2,1,0:T(8,128)(2,1)S(1)}, bf16[1,64,1088]{2,1,0:T(8,128)(2,1)S(1)}, u32[]{:S(2)}, u32[]{:S(2)}) collective-permute-start(bf16[1,64,1088]{2,1,0:T(8,128)(2,1)S(1)} %collective-permute-done.below), channel_id=1, source_target_pairs={{128,0},{256,128},{384,256},{129,1},{257,129},{385,257},{130,2},{2... | collective-permute-start | bytes 417800 | tf_op jit(solution)/shard_map/ppermute | solution.py:380
  19.8 0.0 copy-start
  19.8 1.1 %copy-done = bf16[1344,256]{1,0:T(8,128)(2,1)S(1)} copy-done((bf16[1344,256]{1,0:T(8,128)(2,1)S(1)}, bf16[1344,256]{1,0:T(8,128)(2,1)}, u32[]{:S(2)}) %copy-start) | copy-done | bytes 688152
  20.9 0.9 %copy-done.2 = bf16[1,64,1088]{2,1,0:T(8,128)(2,1)S(1)} copy-done((bf16[1,64,1088]{2,1,0:T(8,128)(2,1)S(1)}, bf16[1,64,1088]{2,1,0:T(8,128)(2,1)}, u32[]{:S(2)}) %copy-start.2) | copy-done | bytes 139288
  21.9 0.7 %shard_map.78 = (bf16[9,256,128]{2,1,0:T(8,128)(2,1)S(1)}, f32[16,128]{1,0:T(8,128)S(1)}) custom-call(bf16[1,64,1088]{2,1,0:T(8,128)(2,1)S(1)} %copy-done.2, bf16[1,64,1088]{2,1,0:T(8,128)(2,1)S(1)} %collective-permute-done.below, bf16[1344,256]{1,0:T(8,128)(2,1)S(1)} %copy-done), custom_call_target="tpu_custom_call" | custom-call | flops 600000000 | bytes 2000000 | tf_op jit(solution)/shard_map/pallas_call | solution.py:180
  22.5 0.0 copy-start.3
  22.5 0.0 copy-start.6
  22.5 0.0 copy-done.4
  22.6 0.0 copy-done.5
  22.6 0.6 %copy-done.3 = s32[1,2,1,16]{3,2,1,0:T(1,128)S(1)} copy-done((s32[1,2,1,16]{3,2,1,0:T(1,128)S(1)}, s32[1,2,1,16]{3,2,1,0:T(1,128)}, u32[]{:S(2)}) %copy-start.3) | copy-done | bytes 152
  23.2 0.6 %shard_map.77 = (f32[1,128]{1,0:T(1,128)S(1)}, f32[8,128]{1,0:T(8,128)S(1)}) custom-call(s32[3]{0:T(128)S(1)} %copy-done.6, s32[1,2,1,16]{3,2,1,0:T(1,128)S(1)} %copy-done.3, f32[1,2,1,16]{3,2,1,0:T(1,128)S(1)} %copy-done.4, f32[2,8]{1,0:T(2,128)S(1)} %bitcast.11, f32[1,2,1,16]{3,2,1,0:T(1,128)S(1)} %collective-permute-done.1.remote), custom_call_target="tpu_custom_call" | custom-call | flops 1000000000 | bytes 10000 | tf_op jit(solution)/shard_map/pallas_call | solution.py:130
  23.8 0.0 collective-permute-done.2.near
  23.8 0.0 collective-permute-done.3.near_below
  23.8 0.5 copy-done.1
  24.3 1.7 %shard_map.79 = f32[16,128]{1,0:T(8,128)S(1)} custom-call(bf16[9,256,128]{2,1,0:T(8,128)(2,1)S(1)} %get-tuple-element.11.own_spec, f32[16,128]{1,0:T(8,128)S(1)} %get-tuple-element.12.own_energies, bf16[1,64,1088]{2,1,0:T(8,128)(2,1)S(1)} %collective-permute-done.2.near, bf16[1,64,1088]{2,1,0:T(8,128)(2,1)S(1)} %collective-permute-done.3.near_below, ...), custom_call_target="tpu_custom_call" | custom-call | tf_op jit(solution)/shard_map/pallas_call | solution.py:290
  26.0 10.2 %all_to_all.5 = f32[16,1,128]{2,1,0:T(1,128)S(1)} all-to-all(f32[16,1,128]{2,1,0:T(1,128)S(1)} %bitcast.7), channel_id=1, replica_groups={{0,1,2,3,128,129,130,131,256,257,258,259,384,385,386,387},{4,5,6,7,132,..., dimensions={0} | all-to-all | bytes 16384 | tf_op jit(solution)/shard_map/all_to_all | solution.py:407
  36.2 1.9 %collective-permute-start.4 = (f32[16,1,128]{2,0,1:T(8,128)S(1)}, f32[16,1,128]{2,0,1:T(8,128)S(1)}, u32[]{:S(2)}, u32[]{:S(2)}) collective-permute-start(f32[16,1,128]{2,0,1:T(8,128)S(1)} %bitcast.8), channel_id=1, source_target_pairs={{6,2},{7,3},{0,4},{1,5},{10,6},{11,7},{4,8},{5,9},{14,10},{15,11},... | collective-permute-start | bytes 24584 | tf_op jit(solution)/shard_map/ppermute | solution.py:408
  38.2 6.9 %collective-permute-done.4 = f32[16,1,128]{2,0,1:T(8,128)S(1)} collective-permute-done((f32[16,1,128]{2,0,1:T(8,128)S(1)}, f32[16,1,128]{2,0,1:T(8,128)S(1)}, u32[]{:S(2)}, u32[]{:S(2)}) %collective-permute-start.4) | collective-permute-done | bytes 8224 | tf_op jit(solution)/shard_map/ppermute | solution.py:408
  45.1 0.9 %shard_map.80 = (f32[1,2,1,16]{3,2,1,0:T(1,128)}, f32[1,2,1,16]{3,2,1,0:T(1,128)}) custom-call(f32[8,128]{1,0:T(8,128)S(1)} %get-tuple-element.9.springs, f32[16,128]{1,0:T(8,128)S(1)} %bitcast.9, f32[16,128]{1,0:T(8,128)S(1)} %bitcast.10), custom_call_target="tpu_custom_call" | custom-call | tf_op jit(solution)/shard_map/pallas_call | solution.py:368
  (5 shorter events, 0.0 us)
Async XLA Ops:
  0.6 16.1 %collective-permute-start = (bf16[1,64,1088]{2,1,0:T(8,128)(2,1)}, bf16[1,64,1088]{2,1,0:T(8,128)(2,1)S(1)}, u32[]{:S(2)}, u32[]{:S(2)}) collective-permute-start(bf16[1,64,1088]{2,1,0:T(8,128)(2,1)} %own.1), channel_id=1, source_target_pairs={{1,0},{2,1},{3,2},{4,3},{5,4},{6,5},{7,6},{8,7},{9,8},{10,9},{11,1... | collective-permute-start | bytes 417800 | tf_op jit(solution)/shard_map/ppermute | solution.py:380
  4.7 7.6 %collective-permute-start.1 = (f32[1,2,1,16]{3,2,1,0:T(1,128)}, f32[1,2,1,16]{3,2,1,0:T(1,128)S(1)}, u32[]{:S(2)}, u32[]{:S(2)}) collective-permute-start(f32[1,2,1,16]{3,2,1,0:T(1,128)} %initial.1), channel_id=1, source_target_pairs={{4,0},{5,1},{8,4},{9,5},{2,6},{3,7},{12,8},{13,9},{6,10},{7,11},{1... | collective-permute-start | bytes 392 | tf_op jit(solution)/shard_map/ppermute | solution.py:395
  10.1 13.7 %collective-permute-start.2 = (bf16[1,64,1088]{2,1,0:T(8,128)(2,1)}, bf16[1,64,1088]{2,1,0:T(8,128)(2,1)S(1)}, u32[]{:S(2)}, u32[]{:S(2)}) collective-permute-start(bf16[1,64,1088]{2,1,0:T(8,128)(2,1)} %own.1), channel_id=1, source_target_pairs={{128,0},{256,128},{384,256},{129,1},{257,129},{385,257},{130,2},{2... | collective-permute-start | bytes 417800 | tf_op jit(solution)/shard_map/ppermute | solution.py:380
  16.7 7.1 %collective-permute-start.3 = (bf16[1,64,1088]{2,1,0:T(8,128)(2,1)S(1)}, bf16[1,64,1088]{2,1,0:T(8,128)(2,1)S(1)}, u32[]{:S(2)}, u32[]{:S(2)}) collective-permute-start(bf16[1,64,1088]{2,1,0:T(8,128)(2,1)S(1)} %collective-permute-done.below), channel_id=1, source_target_pairs={{128,0},{256,128},{384,256},{129,1},{257,129},{385,257},{130,2},{2... | collective-permute-start | bytes 417800 | tf_op jit(solution)/shard_map/ppermute | solution.py:380
  19.8 1.1 %copy-start = (bf16[1344,256]{1,0:T(8,128)(2,1)S(1)}, bf16[1344,256]{1,0:T(8,128)(2,1)}, u32[]{:S(2)}) copy-start(bf16[1344,256]{1,0:T(8,128)(2,1)} %constant.2.clone.tables) | copy-start | bytes 2064388
  20.9 0.9 %copy-start.2 = (bf16[1,64,1088]{2,1,0:T(8,128)(2,1)S(1)}, bf16[1,64,1088]{2,1,0:T(8,128)(2,1)}, u32[]{:S(2)}) copy-start(bf16[1,64,1088]{2,1,0:T(8,128)(2,1)} %own.1) | copy-start | bytes 417796
  21.8 0.7 %copy-start.4 = (f32[1,2,1,16]{3,2,1,0:T(1,128)S(1)}, f32[1,2,1,16]{3,2,1,0:T(1,128)}, u32[]{:S(2)}) copy-start(f32[1,2,1,16]{3,2,1,0:T(1,128)} %initial.1) | copy-start | bytes 388
  21.9 0.7 %copy-start.5 = (f32[8,2]{0,1:T(2,128)S(1)}, f32[8,2]{0,1:T(2,128)}, u32[]{:S(2)}) copy-start(f32[8,2]{0,1:T(2,128)} %param.9) | copy-start | bytes 196
  22.5 0.7 %copy-start.3 = (s32[1,2,1,16]{3,2,1,0:T(1,128)S(1)}, s32[1,2,1,16]{3,2,1,0:T(1,128)}, u32[]{:S(2)}) copy-start(s32[1,2,1,16]{3,2,1,0:T(1,128)} %offsets.1) | copy-start | bytes 388
  22.5 0.7 %copy-start.6 = (s32[3]{0:T(128)S(1)}, s32[3]{0:T(128)}, u32[]{:S(2)}) copy-start(s32[3]{0:T(128)} %plan.1) | copy-start | bytes 40
  23.2 1.1 %copy-start.1 = (bf16[1344,256]{1,0:T(8,128)(2,1)S(1)}, bf16[1344,256]{1,0:T(8,128)(2,1)}, u32[]{:S(2)}) copy-start(bf16[1344,256]{1,0:T(8,128)(2,1)} %constant.2.clone.tables) | copy-start | bytes 2064388
  36.2 8.9 %collective-permute-start.4 = (f32[16,1,128]{2,0,1:T(8,128)S(1)}, f32[16,1,128]{2,0,1:T(8,128)S(1)}, u32[]{:S(2)}, u32[]{:S(2)}) collective-permute-start(f32[16,1,128]{2,0,1:T(8,128)S(1)} %bitcast.8), channel_id=1, source_target_pairs={{6,2},{7,3},{0,4},{1,5},{10,6},{11,7},{4,8},{5,9},{14,10},{15,11},... | collective-permute-start | bytes 24584 | tf_op jit(solution)/shard_map/ppermute | solution.py:408

commit v10 on v7

--- a/solution.py
+++ b/solution.py
@@ -397,10 +397,11 @@
 def per_device(images, initial, offsets, stiffness, plan):
     rows = lax.axis_size("row")
     below = shifted(images, "row", -1)
-    near = shifted(images, "sec", 1)
+    remote_initial = lax.ppermute(initial, "row", ring_route(rows, False))
     near_offsets = shifted(offsets, "sec", 1)
-    remote_initial = lax.ppermute(initial, "row", ring_route(rows, False))
     record, springs = prepare(plan, initial, stiffness)
+    later_images, record, springs = lax.optimization_barrier((images, record, springs))
+    near = shifted(later_images, "sec", 1)
     below, near_offsets, remote_initial, record, springs = lax.optimization_barrier(
         (below, near_offsets, remote_initial, record, springs)
     )

time: 48.9 us -> 47 us (0.961)
  waiting for transfers between devices: 8.8 us -> 7.24 us
  blocking collectives: 16.2 us -> 14.9 us
  starting transfers between devices: 18.1 us -> 18.7 us
    ppermute x1, waiting for transfers between devices: 1.58 us -> 0.01 us  [per_device(): remote_initial = lax.ppermute(initial, 'row', ring_route(rows, False))]
    all_to_all x1, blocking collectives: 16.2 us -> 14.9 us  [per_device(): lax.all_to_all(mine.reshape(count, 1, PATCH), ('sec', 'row'), 0, 0, axis_...]
    ppermute x4, starting transfers between devices: 13.5 us -> 14.1 us  [shifted(): return lax.ppermute(block, axis, route)]
  transfers between devices with their start and end apart: 6 -> 6, of which waited for: 3 -> 2; matrix products, arithmetic and copies ran while one was open for 0% -> 0% of each run, Pallas kernels for 3% -> 3%
where the time goes in v10:
time: 47 us; the launch traced here: 46.6 us
  starting transfers between devices  18.7 us (40%)
  blocking collectives  14.9 us (32%)
  waiting for transfers between devices  7.24 us (15%)
  Pallas kernels  3.95 us (8%)
  local copies, waits for them, and re-layouts  1.01 us (2%)
  between operations  0.77 us (2%)
    all_to_all x1, blocking collectives, per_device(): lax.all_to_all(mine.reshape(count, 1, PATCH), ('sec', 'row'), 0, 0, axis_...  14.9 us
    ppermute x4, starting transfers between devices, shifted(): return lax.ppermute(block, axis, route)  14.1 us
    ppermute x1, waiting for transfers between devices, per_device(): other = lax.ppermute(ring, 'row', ring_route(rows, True))  6.94 us
    ppermute x1, starting transfers between devices, per_device(): remote_initial = lax.ppermute(initial, 'row', ring_route(rows, False))  2.74 us
    ppermute x1, starting transfers between devices, per_device(): other = lax.ppermute(ring, 'row', ring_route(rows, True))  1.91 us
    pallas_call x1, Pallas kernels, pair_flow(): pl.pallas_call(flow_kernel, out_shape=jax.ShapeDtypeStruct((copies, PATCH...  1.72 us
    unnamed x10, local copies, waits for them, and re-layouts  1.01 us
  transfers between devices with their start and end apart: 6, of which 2 were waited for; matrix products, arithmetic and copies ran while one was open for 0% of the time, Pallas kernels for 3%

profile of v10, /device:TPU:256, one launch (start us, length us, event | category | flops | bytes accessed | tf_op | source)
XLA Modules:
  0.0 46.6 jit_solution(8537856478984826463)
XLA Ops:
  0.6 0.0 copy-start.2
  0.6 0.0 copy-start.4
  0.7 7.6 %collective-permute-start = (bf16[1,64,1088]{2,1,0:T(8,128)(2,1)}, bf16[1,64,1088]{2,1,0:T(8,128)(2,1)S(1)}, u32[]{:S(2)}, u32[]{:S(2)}) collective-permute-start(bf16[1,64,1088]{2,1,0:T(8,128)(2,1)} %own.1), channel_id=1, source_target_pairs={{1,0},{2,1},{3,2},{4,3},{5,4},{6,5},{7,6},{8,7},{9,8},{10,9},{11,1... | collective-permute-start | bytes 417800 | tf_op jit(solution)/shard_map/ppermute | solution.py:385
  8.2 1.5 %collective-permute-start.1 = (s32[1,2,1,16]{3,2,1,0:T(1,128)}, s32[1,2,1,16]{3,2,1,0:T(1,128)S(1)}, u32[]{:S(2)}, u32[]{:S(2)}) collective-permute-start(s32[1,2,1,16]{3,2,1,0:T(1,128)} %param.8), channel_id=1, source_target_pairs={{0,128},{128,256},{256,384},{1,129},{129,257},{257,385},{2,130},{1... | collective-permute-start | bytes 392 | tf_op jit(solution)/shard_map/ppermute | solution.py:385
  9.7 2.7 %collective-permute-start.2 = (f32[1,2,1,16]{3,2,1,0:T(1,128)}, f32[1,2,1,16]{3,2,1,0:T(1,128)S(1)}, u32[]{:S(2)}, u32[]{:S(2)}) collective-permute-start(f32[1,2,1,16]{3,2,1,0:T(1,128)} %initial.1), channel_id=1, source_target_pairs={{4,0},{5,1},{8,4},{9,5},{2,6},{3,7},{12,8},{13,9},{6,10},{7,11},{1... | collective-permute-start | bytes 392 | tf_op jit(solution)/shard_map/ppermute | solution.py:400
  12.4 0.0 copy-done.2
  12.5 0.0 copy-done.4
  12.5 0.0 copy-start.3
  12.5 0.7 %copy-done.3 = f32[1,2,1,16]{3,2,1,0:T(1,128)S(1)} copy-done((f32[1,2,1,16]{3,2,1,0:T(1,128)S(1)}, f32[1,2,1,16]{3,2,1,0:T(1,128)}, u32[]{:S(2)}) %copy-start.3) | copy-done | bytes 152
  13.2 0.6 %shard_map.77 = (f32[1,128]{1,0:T(1,128)S(1)}, f32[8,128]{1,0:T(8,128)S(1)}) custom-call(s32[3]{0:T(128)S(1)} %copy-done.4, f32[1,2,1,16]{3,2,1,0:T(1,128)S(1)} %copy-done.3, f32[2,8]{1,0:T(2,128)S(1)} %bitcast.11), custom_call_target="tpu_custom_call" | custom-call | flops 1000000000 | bytes 10000 | tf_op jit(solution)/shard_map/pallas_call | solution.py:128
  13.8 0.3 copy-done.1
  14.1 2.9 %collective-permute-start.3 = (bf16[1,64,1088]{2,1,0:T(8,128)(2,1)S(1)}, bf16[1,64,1088]{2,1,0:T(8,128)(2,1)S(1)}, u32[]{:S(2)}, u32[]{:S(2)}) collective-permute-start(bf16[1,64,1088]{2,1,0:T(8,128)(2,1)S(1)} %copy-done.1), channel_id=1, source_target_pairs={{0,128},{128,256},{256,384},{1,129},{129,257},{257,385},{2,130},{1... | collective-permute-start | bytes 417800 | tf_op jit(solution)/shard_map/ppermute | solution.py:385
  17.0 0.0 collective-permute-done.1.shifts_in
  17.0 0.0 collective-permute-done.2.remote
  17.0 0.0 collective-permute-done.below
  17.0 2.2 %collective-permute-start.4 = (bf16[1,64,1088]{2,1,0:T(8,128)(2,1)S(1)}, bf16[1,64,1088]{2,1,0:T(8,128)(2,1)S(1)}, u32[]{:S(2)}, u32[]{:S(2)}) collective-permute-start(bf16[1,64,1088]{2,1,0:T(8,128)(2,1)S(1)} %collective-permute-done.below), channel_id=1, source_target_pairs={{0,128},{128,256},{256,384},{1,129},{129,257},{257,385},{2,130},{1... | collective-permute-start | bytes 417800 | tf_op jit(solution)/shard_map/ppermute | solution.py:385
  19.2 0.7 %shard_map.78 = (bf16[9,256,128]{2,1,0:T(8,128)(2,1)S(1)}, f32[16,128]{1,0:T(8,128)S(1)}) custom-call(bf16[1,64,1088]{2,1,0:T(8,128)(2,1)S(1)} %copy-done.1, bf16[1,64,1088]{2,1,0:T(8,128)(2,1)S(1)} %collective-permute-done.below, bf16[1344,256]{1,0:T(8,128)(2,1)S(1)} %copy-done), custom_call_target="tpu_custom_call" | custom-call | flops 600000000 | bytes 2000000 | tf_op jit(solution)/shard_map/pallas_call | solution.py:178
  19.9 0.0 collective-permute-done.3.near
  19.9 0.3 collective-permute-done.4.near_below
  20.2 1.7 %shard_map.79 = f32[16,128]{1,0:T(8,128)S(1)} custom-call(bf16[9,256,128]{2,1,0:T(8,128)(2,1)S(1)} %get-tuple-element.20.own_spec, f32[16,128]{1,0:T(8,128)S(1)} %get-tuple-element.21.own_energies, bf16[1,64,1088]{2,1,0:T(8,128)(2,1)S(1)} %collective-permute-done.3.near, bf16[1,64,1088]{2,1,0:T(8,128)(2,1)S(1)} %collective-permute-done.4.near_below, ...), custom_call_target="tpu_custom_call" | custom-call | tf_op jit(solution)/shard_map/pallas_call | solution.py:293
  21.9 14.9 %all_to_all.5 = f32[16,1,128]{2,1,0:T(1,128)S(1)} all-to-all(f32[16,1,128]{2,1,0:T(1,128)S(1)} %bitcast.7), channel_id=1, replica_groups={{0,1,2,3,128,129,130,131,256,257,258,259,384,385,386,387},{4,5,6,7,132,..., dimensions={0} | all-to-all | bytes 16384 | tf_op jit(solution)/shard_map/all_to_all | solution.py:416
  36.8 1.9 %collective-permute-start.5 = (f32[16,1,128]{2,0,1:T(8,128)S(1)}, f32[16,1,128]{2,0,1:T(8,128)S(1)}, u32[]{:S(2)}, u32[]{:S(2)}) collective-permute-start(f32[16,1,128]{2,0,1:T(8,128)S(1)} %bitcast.8), channel_id=1, source_target_pairs={{6,2},{7,3},{0,4},{1,5},{10,6},{11,7},{4,8},{5,9},{14,10},{15,11},... | collective-permute-start | bytes 24584 | tf_op jit(solution)/shard_map/ppermute | solution.py:417
  38.8 6.9 %collective-permute-done.5 = f32[16,1,128]{2,0,1:T(8,128)S(1)} collective-permute-done((f32[16,1,128]{2,0,1:T(8,128)S(1)}, f32[16,1,128]{2,0,1:T(8,128)S(1)}, u32[]{:S(2)}, u32[]{:S(2)}) %collective-permute-start.5) | collective-permute-done | bytes 8224 | tf_op jit(solution)/shard_map/ppermute | solution.py:417
  45.7 0.9 %shard_map.80 = (f32[1,2,1,16]{3,2,1,0:T(1,128)}, f32[1,2,1,16]{3,2,1,0:T(1,128)}) custom-call(f32[8,128]{1,0:T(8,128)S(1)} %get-tuple-element.18.springs, f32[16,128]{1,0:T(8,128)S(1)} %bitcast.9, f32[16,128]{1,0:T(8,128)S(1)} %bitcast.10), custom_call_target="tpu_custom_call" | custom-call | tf_op jit(solution)/shard_map/pallas_call | solution.py:373
  (3 shorter events, 0.0 us)
Async XLA Ops:
  0.6 11.8 %copy-start.2 = (f32[8,2]{0,1:T(2,128)S(1)}, f32[8,2]{0,1:T(2,128)}, u32[]{:S(2)}) copy-start(f32[8,2]{0,1:T(2,128)} %param.9) | copy-start | bytes 196
  0.6 11.8 %copy-start.4 = (s32[3]{0:T(128)S(1)}, s32[3]{0:T(128)}, u32[]{:S(2)}) copy-start(s32[3]{0:T(128)} %plan.1) | copy-start | bytes 40
  0.7 16.3 %collective-permute-start = (bf16[1,64,1088]{2,1,0:T(8,128)(2,1)}, bf16[1,64,1088]{2,1,0:T(8,128)(2,1)S(1)}, u32[]{:S(2)}, u32[]{:S(2)}) collective-permute-start(bf16[1,64,1088]{2,1,0:T(8,128)(2,1)} %own.1), channel_id=1, source_target_pairs={{1,0},{2,1},{3,2},{4,3},{5,4},{6,5},{7,6},{8,7},{9,8},{10,9},{11,1... | collective-permute-start | bytes 417800 | tf_op jit(solution)/shard_map/ppermute | solution.py:385
  8.2 8.7 %collective-permute-start.1 = (s32[1,2,1,16]{3,2,1,0:T(1,128)}, s32[1,2,1,16]{3,2,1,0:T(1,128)S(1)}, u32[]{:S(2)}, u32[]{:S(2)}) collective-permute-start(s32[1,2,1,16]{3,2,1,0:T(1,128)} %param.8), channel_id=1, source_target_pairs={{0,128},{128,256},{256,384},{1,129},{129,257},{257,385},{2,130},{1... | collective-permute-start | bytes 392 | tf_op jit(solution)/shard_map/ppermute | solution.py:385
  9.7 7.3 %collective-permute-start.2 = (f32[1,2,1,16]{3,2,1,0:T(1,128)}, f32[1,2,1,16]{3,2,1,0:T(1,128)S(1)}, u32[]{:S(2)}, u32[]{:S(2)}) collective-permute-start(f32[1,2,1,16]{3,2,1,0:T(1,128)} %initial.1), channel_id=1, source_target_pairs={{4,0},{5,1},{8,4},{9,5},{2,6},{3,7},{12,8},{13,9},{6,10},{7,11},{1... | collective-permute-start | bytes 392 | tf_op jit(solution)/shard_map/ppermute | solution.py:400
  12.5 0.7 %copy-start.3 = (f32[1,2,1,16]{3,2,1,0:T(1,128)S(1)}, f32[1,2,1,16]{3,2,1,0:T(1,128)}, u32[]{:S(2)}) copy-start(f32[1,2,1,16]{3,2,1,0:T(1,128)} %initial.1) | copy-start | bytes 388
  13.2 0.9 %copy-start.1 = (bf16[1,64,1088]{2,1,0:T(8,128)(2,1)S(1)}, bf16[1,64,1088]{2,1,0:T(8,128)(2,1)}, u32[]{:S(2)}) copy-start(bf16[1,64,1088]{2,1,0:T(8,128)(2,1)} %own.1) | copy-start | bytes 417796
  13.2 6.0 %copy-start = (bf16[1344,256]{1,0:T(8,128)(2,1)S(1)}, bf16[1344,256]{1,0:T(8,128)(2,1)}, u32[]{:S(2)}) copy-start(bf16[1344,256]{1,0:T(8,128)(2,1)} %constant.2.clone.tables) | copy-start | bytes 2064388
  14.1 5.8 %collective-permute-start.3 = (bf16[1,64,1088]{2,1,0:T(8,128)(2,1)S(1)}, bf16[1,64,1088]{2,1,0:T(8,128)(2,1)S(1)}, u32[]{:S(2)}, u32[]{:S(2)}) collective-permute-start(bf16[1,64,1088]{2,1,0:T(8,128)(2,1)S(1)} %copy-done.1), channel_id=1, source_target_pairs={{0,128},{128,256},{256,384},{1,129},{129,257},{257,385},{2,130},{1... | collective-permute-start | bytes 417800 | tf_op jit(solution)/shard_map/ppermute | solution.py:385
  17.0 3.2 %collective-permute-start.4 = (bf16[1,64,1088]{2,1,0:T(8,128)(2,1)S(1)}, bf16[1,64,1088]{2,1,0:T(8,128)(2,1)S(1)}, u32[]{:S(2)}, u32[]{:S(2)}) collective-permute-start(bf16[1,64,1088]{2,1,0:T(8,128)(2,1)S(1)} %collective-permute-done.below), channel_id=1, source_target_pairs={{0,128},{128,256},{256,384},{1,129},{129,257},{257,385},{2,130},{1... | collective-permute-start | bytes 417800 | tf_op jit(solution)/shard_map/ppermute | solution.py:385
  36.8 8.9 %collective-permute-start.5 = (f32[16,1,128]{2,0,1:T(8,128)S(1)}, f32[16,1,128]{2,0,1:T(8,128)S(1)}, u32[]{:S(2)}, u32[]{:S(2)}) collective-permute-start(f32[16,1,128]{2,0,1:T(8,128)S(1)} %bitcast.8), channel_id=1, source_target_pairs={{6,2},{7,3},{0,4},{1,5},{10,6},{11,7},{4,8},{5,9},{14,10},{15,11},... | collective-permute-start | bytes 24584 | tf_op jit(solution)/shard_map/ppermute | solution.py:417

commit v11 on v10

--- a/solution.py
+++ b/solution.py
@@ -188,10 +188,16 @@
     )(own, below, tables)
 
 
-def flow_kernel(own_spec, own_energies, near, near_below, record, remote, shifts_in, tables, out, spec, lagged, shift_row):
+def flow_kernel(
+    own_spec, own_energies, near, near_below, lower, record, remote, shifts_in, tables, out, spec, lagged, shift_row
+):
     spread = table(tables, "spread")
     energies = []
-    for m, spectrum in enumerate(section_spectra(block_tile(near), block_tile(near_below), tables)):
+
+    def second(start, span):
+        return near_below[0, :, pl.ds(start, span)] + lower[0, :, pl.ds(start, span)]
+
+    for m, spectrum in enumerate(section_spectra(block_tile(near), second, tables)):
         spec[m] = spectrum
         energies.append(energy(spectrum))
 
@@ -288,8 +294,8 @@
         out[:, pl.ds((4 + i) * COLS, COLS)] = jnp.broadcast_to(remote[0, i], (out.shape[0], COLS))
 
 
-def pair_flow(own_parts, near, near_below, record, remote_initial, offsets, tables, copies):
-    operands = (*own_parts, near, near_below, record, remote_initial, offsets, tables)
+def pair_flow(own_parts, near, near_below, lower, record, remote_initial, offsets, tables, copies):
+    operands = (*own_parts, near, near_below, lower, record, remote_initial, offsets, tables)
     return pl.pallas_call(
         flow_kernel,
         out_shape=jax.ShapeDtypeStruct((copies, PATCH), f32),
@@ -394,10 +400,20 @@
     return route
 
 
+def edge_route(rows):
+    route = []
+    for r in range(rows):
+        target = {0: r - RING, RING - 1: r + RING}.get(r % RING, -1)
+        if 0 <= target < rows:
+            route.append((r, target))
+    return route
+
+
 def per_device(images, initial, offsets, stiffness, plan):
     rows = lax.axis_size("row")
     below = shifted(images, "row", -1)
-    remote_initial = lax.ppermute(initial, "row", ring_route(rows, False))
+    lower = lax.ppermute(images, ("sec", "row"), [(rows + r + 1, 2 * rows + r) for r in range(rows - 1)])
+    remote_initial = lax.ppermute(initial, "row", edge_route(rows))
     near_offsets = shifted(offsets, "sec", 1)
     record, springs = prepare(plan, initial, stiffness)
     later_images, record, springs = lax.optimization_barrier((images, record, springs))
@@ -405,11 +421,11 @@
     below, near_offsets, remote_initial, record, springs = lax.optimization_barrier(
         (below, near_offsets, remote_initial, record, springs)
     )
-    near_below = shifted(below, "sec", 1)
+    near_below = lax.ppermute(below, "sec", [(0, 1), (2, 3)])
     count = SECS * RING
     tables = jnp.asarray(constant_tables())
     own_parts = own_spectra(images, below, tables)
-    mine = pair_flow(own_parts, near, near_below, record, remote_initial, near_offsets, tables, count)
+    mine = pair_flow(own_parts, near, near_below, lower, record, remote_initial, near_offsets, tables, count)
     groups = [
         [s * rows + RING * g + j for s in range(SECS) for j in range(RING)] for g in range(rows // RING)
     ]

time: 47 us -> 45.4 us (0.966)
  blocking collectives: 14.9 us -> 11 us
  starting transfers between devices: 18.7 us -> 21.5 us
    all_to_all x1, blocking collectives: 14.9 us -> 11 us  [per_device(): lax.all_to_all(mine.reshape(count, 1, PATCH), ('sec', 'row'), 0, 0, axis_...]
    ppermute x1 -> x3, starting transfers between devices: 2.74 us -> 5.33 us  [the longest x1 2.74 us: per_device(): remote_initial = lax.ppermute(initial, 'row', edge_route(rows))]
    ppermute x4 -> x3, starting transfers between devices: 14.1 us -> 13.8 us  [shifted(): return lax.ppermute(block, axis, route)]
  transfers between devices with their start and end apart: 6 -> 7, of which waited for: 2 -> 2; matrix products, arithmetic and copies ran while one was open for 0% -> 0% of each run, Pallas kernels for 3% -> 3%
where the time goes in v11:
time: 45.4 us; the launch traced here: 45.1 us
  starting transfers between devices  21.5 us (47%)
  blocking collectives  11 us (24%)
  waiting for transfers between devices  6.8 us (15%)
  Pallas kernels  3.95 us (9%)
  local copies, waits for them, and re-layouts  1.01 us (2%)
  between operations  0.78 us (2%)
    ppermute x3, starting transfers between devices, shifted(): return lax.ppermute(block, axis, route)  13.8 us
    all_to_all x1, blocking collectives, per_device(): lax.all_to_all(mine.reshape(count, 1, PATCH), ('sec', 'row'), 0, 0, axis_...  11 us
    ppermute x1, waiting for transfers between devices, per_device(): other = lax.ppermute(ring, 'row', ring_route(rows, True))  6.51 us
    ppermute x1, starting transfers between devices, per_device(): remote_initial = lax.ppermute(initial, 'row', edge_route(rows))  2.74 us
    ppermute x1, starting transfers between devices, per_device(): other = lax.ppermute(ring, 'row', ring_route(rows, True))  2.33 us
    ppermute x1, starting transfers between devices, per_device(): near_below = lax.ppermute(below, 'sec', [(0, 1), (2, 3)])  1.92 us
    pallas_call x1, Pallas kernels, pair_flow(): pl.pallas_call(flow_kernel, out_shape=jax.ShapeDtypeStruct((copies, PATCH...  1.72 us
    unnamed x10, local copies, waits for them, and re-layouts  1.01 us
  transfers between devices with their start and end apart: 7, of which 2 were waited for; matrix products, arithmetic and copies ran while one was open for 0% of the time, Pallas kernels for 3%

profile of v11, /device:TPU:256, one launch (start us, length us, event | category | flops | bytes accessed | tf_op | source)
XLA Modules:
  0.0 45.1 jit_solution(13874820562407014307)
XLA Ops:
  0.6 0.0 copy-start.2
  0.6 0.0 copy-start.4
  0.7 7.6 %collective-permute-start = (bf16[1,64,1088]{2,1,0:T(8,128)(2,1)}, bf16[1,64,1088]{2,1,0:T(8,128)(2,1)S(1)}, u32[]{:S(2)}, u32[]{:S(2)}) collective-permute-start(bf16[1,64,1088]{2,1,0:T(8,128)(2,1)} %own.1), channel_id=1, source_target_pairs={{1,0},{2,1},{3,2},{4,3},{5,4},{6,5},{7,6},{8,7},{9,8},{10,9},{11,1... | collective-permute-start | bytes 417800 | tf_op jit(solution)/shard_map/ppermute | solution.py:391
  8.2 0.7 %collective-permute-start.5 = (bf16[1,64,1088]{2,1,0:T(8,128)(2,1)}, bf16[1,64,1088]{2,1,0:T(8,128)(2,1)S(1)}, u32[]{:S(2)}, u32[]{:S(2)}) collective-permute-start(bf16[1,64,1088]{2,1,0:T(8,128)(2,1)} %own.1), channel_id=1, source_target_pairs={{129,256},{130,257},{131,258},{132,259},{133,260},{134,261},{135,2... | collective-permute-start | bytes 417800 | tf_op jit(solution)/shard_map/ppermute | solution.py:415
  8.9 4.6 %collective-permute-start.1 = (s32[1,2,1,16]{3,2,1,0:T(1,128)}, s32[1,2,1,16]{3,2,1,0:T(1,128)S(1)}, u32[]{:S(2)}, u32[]{:S(2)}) collective-permute-start(s32[1,2,1,16]{3,2,1,0:T(1,128)} %param.8), channel_id=1, source_target_pairs={{0,128},{128,256},{256,384},{1,129},{129,257},{257,385},{2,130},{1... | collective-permute-start | bytes 392 | tf_op jit(solution)/shard_map/ppermute | solution.py:391
  13.5 2.7 %collective-permute-start.2 = (f32[1,2,1,16]{3,2,1,0:T(1,128)}, f32[1,2,1,16]{3,2,1,0:T(1,128)S(1)}, u32[]{:S(2)}, u32[]{:S(2)}) collective-permute-start(f32[1,2,1,16]{3,2,1,0:T(1,128)} %initial.1), channel_id=1, source_target_pairs={{3,7},{4,0},{7,11},{8,4},{11,15},{12,8},{15,19},{16,12},{19,23},{2... | collective-permute-start | bytes 392 | tf_op jit(solution)/shard_map/ppermute | solution.py:416
  16.3 0.0 copy-done.2
  16.3 0.7 %copy-done.3 = f32[1,2,1,16]{3,2,1,0:T(1,128)S(1)} copy-done((f32[1,2,1,16]{3,2,1,0:T(1,128)S(1)}, f32[1,2,1,16]{3,2,1,0:T(1,128)}, u32[]{:S(2)}) %copy-start.3) | copy-done | bytes 152
  17.0 0.6 %shard_map.77 = (f32[1,128]{1,0:T(1,128)S(1)}, f32[8,128]{1,0:T(8,128)S(1)}) custom-call(s32[3]{0:T(128)S(1)} %copy-done.4, f32[1,2,1,16]{3,2,1,0:T(1,128)S(1)} %copy-done.3, f32[2,8]{1,0:T(2,128)S(1)} %bitcast.11), custom_call_target="tpu_custom_call" | custom-call | flops 1000000000 | bytes 10000 | tf_op jit(solution)/shard_map/pallas_call | solution.py:128
  17.6 0.3 copy-done.1
  17.9 1.6 %collective-permute-start.3 = (bf16[1,64,1088]{2,1,0:T(8,128)(2,1)S(1)}, bf16[1,64,1088]{2,1,0:T(8,128)(2,1)S(1)}, u32[]{:S(2)}, u32[]{:S(2)}) collective-permute-start(bf16[1,64,1088]{2,1,0:T(8,128)(2,1)S(1)} %copy-done.1), channel_id=1, source_target_pairs={{0,128},{128,256},{256,384},{1,129},{129,257},{257,385},{2,130},{1... | collective-permute-start | bytes 417800 | tf_op jit(solution)/shard_map/ppermute | solution.py:391
  19.6 0.0 collective-permute-done.1.shifts_in
  19.6 0.0 collective-permute-done.2.remote
  19.6 0.0 collective-permute-done.below
  19.6 1.9 %collective-permute-start.4 = (bf16[1,64,1088]{2,1,0:T(8,128)(2,1)S(1)}, bf16[1,64,1088]{2,1,0:T(8,128)(2,1)S(1)}, u32[]{:S(2)}, u32[]{:S(2)}) collective-permute-start(bf16[1,64,1088]{2,1,0:T(8,128)(2,1)S(1)} %collective-permute-done.below), channel_id=1, source_target_pairs={{0,128},{256,384},{1,129},{257,385},{2,130},{258,386},{3,131},{259... | collective-permute-start | bytes 417800 | tf_op jit(solution)/shard_map/ppermute | solution.py:424
  21.5 0.7 %shard_map.78 = (bf16[9,256,128]{2,1,0:T(8,128)(2,1)S(1)}, f32[16,128]{1,0:T(8,128)S(1)}) custom-call(bf16[1,64,1088]{2,1,0:T(8,128)(2,1)S(1)} %copy-done.1, bf16[1,64,1088]{2,1,0:T(8,128)(2,1)S(1)} %collective-permute-done.below, bf16[1344,256]{1,0:T(8,128)(2,1)S(1)} %copy-done), custom_call_target="tpu_custom_call" | custom-call | flops 600000000 | bytes 2000000 | tf_op jit(solution)/shard_map/pallas_call | solution.py:178
  22.2 0.0 collective-permute-done.3.near
  22.2 0.0 collective-permute-done.5.lower
  22.2 0.3 collective-permute-done.4.near_below
  22.5 1.7 %shard_map.79 = f32[16,128]{1,0:T(8,128)S(1)} custom-call(bf16[9,256,128]{2,1,0:T(8,128)(2,1)S(1)} %get-tuple-element.20.own_spec, f32[16,128]{1,0:T(8,128)S(1)} %get-tuple-element.21.own_energies, bf16[1,64,1088]{2,1,0:T(8,128)(2,1)S(1)} %collective-permute-done.3.near, bf16[1,64,1088]{2,1,0:T(8,128)(2,1)S(1)} %collective-permute-done.4.near_below, ...), custom_call_target="tpu_custom_call" | custom-call | tf_op jit(solution)/shard_map/pallas_call | solution.py:299
  24.2 11.0 %all_to_all.5 = f32[16,1,128]{2,1,0:T(1,128)S(1)} all-to-all(f32[16,1,128]{2,1,0:T(1,128)S(1)} %bitcast.7), channel_id=1, replica_groups={{0,1,2,3,128,129,130,131,256,257,258,259,384,385,386,387},{4,5,6,7,132,..., dimensions={0} | all-to-all | bytes 16384 | tf_op jit(solution)/shard_map/all_to_all | solution.py:432
  35.3 2.3 %collective-permute-start.6 = (f32[16,1,128]{2,0,1:T(8,128)S(1)}, f32[16,1,128]{2,0,1:T(8,128)S(1)}, u32[]{:S(2)}, u32[]{:S(2)}) collective-permute-start(f32[16,1,128]{2,0,1:T(8,128)S(1)} %bitcast.8), channel_id=1, source_target_pairs={{6,2},{7,3},{0,4},{1,5},{10,6},{11,7},{4,8},{5,9},{14,10},{15,11},... | collective-permute-start | bytes 24584 | tf_op jit(solution)/shard_map/ppermute | solution.py:433
  37.6 6.5 %collective-permute-done.6 = f32[16,1,128]{2,0,1:T(8,128)S(1)} collective-permute-done((f32[16,1,128]{2,0,1:T(8,128)S(1)}, f32[16,1,128]{2,0,1:T(8,128)S(1)}, u32[]{:S(2)}, u32[]{:S(2)}) %collective-permute-start.6) | collective-permute-done | bytes 8224 | tf_op jit(solution)/shard_map/ppermute | solution.py:433
  44.1 0.9 %shard_map.80 = (f32[1,2,1,16]{3,2,1,0:T(1,128)}, f32[1,2,1,16]{3,2,1,0:T(1,128)}) custom-call(f32[8,128]{1,0:T(8,128)S(1)} %get-tuple-element.18.springs, f32[16,128]{1,0:T(8,128)S(1)} %bitcast.9, f32[16,128]{1,0:T(8,128)S(1)} %bitcast.10), custom_call_target="tpu_custom_call" | custom-call | tf_op jit(solution)/shard_map/pallas_call | solution.py:379
  (5 shorter events, 0.0 us)
Async XLA Ops:
  0.6 15.6 %copy-start.2 = (f32[8,2]{0,1:T(2,128)S(1)}, f32[8,2]{0,1:T(2,128)}, u32[]{:S(2)}) copy-start(f32[8,2]{0,1:T(2,128)} %param.9) | copy-start | bytes 196
  0.6 15.6 %copy-start.4 = (s32[3]{0:T(128)S(1)}, s32[3]{0:T(128)}, u32[]{:S(2)}) copy-start(s32[3]{0:T(128)} %plan.1) | copy-start | bytes 40
  0.7 18.9 %collective-permute-start = (bf16[1,64,1088]{2,1,0:T(8,128)(2,1)}, bf16[1,64,1088]{2,1,0:T(8,128)(2,1)S(1)}, u32[]{:S(2)}, u32[]{:S(2)}) collective-permute-start(bf16[1,64,1088]{2,1,0:T(8,128)(2,1)} %own.1), channel_id=1, source_target_pairs={{1,0},{2,1},{3,2},{4,3},{5,4},{6,5},{7,6},{8,7},{9,8},{10,9},{11,1... | collective-permute-start | bytes 417800 | tf_op jit(solution)/shard_map/ppermute | solution.py:391
  8.2 14.0 %collective-permute-start.5 = (bf16[1,64,1088]{2,1,0:T(8,128)(2,1)}, bf16[1,64,1088]{2,1,0:T(8,128)(2,1)S(1)}, u32[]{:S(2)}, u32[]{:S(2)}) collective-permute-start(bf16[1,64,1088]{2,1,0:T(8,128)(2,1)} %own.1), channel_id=1, source_target_pairs={{129,256},{130,257},{131,258},{132,259},{133,260},{134,261},{135,2... | collective-permute-start | bytes 417800 | tf_op jit(solution)/shard_map/ppermute | solution.py:415
  8.9 10.6 %collective-permute-start.1 = (s32[1,2,1,16]{3,2,1,0:T(1,128)}, s32[1,2,1,16]{3,2,1,0:T(1,128)S(1)}, u32[]{:S(2)}, u32[]{:S(2)}) collective-permute-start(s32[1,2,1,16]{3,2,1,0:T(1,128)} %param.8), channel_id=1, source_target_pairs={{0,128},{128,256},{256,384},{1,129},{129,257},{257,385},{2,130},{1... | collective-permute-start | bytes 392 | tf_op jit(solution)/shard_map/ppermute | solution.py:391
  13.5 6.0 %collective-permute-start.2 = (f32[1,2,1,16]{3,2,1,0:T(1,128)}, f32[1,2,1,16]{3,2,1,0:T(1,128)S(1)}, u32[]{:S(2)}, u32[]{:S(2)}) collective-permute-start(f32[1,2,1,16]{3,2,1,0:T(1,128)} %initial.1), channel_id=1, source_target_pairs={{3,7},{4,0},{7,11},{8,4},{11,15},{12,8},{15,19},{16,12},{19,23},{2... | collective-permute-start | bytes 392 | tf_op jit(solution)/shard_map/ppermute | solution.py:416
  16.3 0.7 %copy-start.3 = (f32[1,2,1,16]{3,2,1,0:T(1,128)S(1)}, f32[1,2,1,16]{3,2,1,0:T(1,128)}, u32[]{:S(2)}) copy-start(f32[1,2,1,16]{3,2,1,0:T(1,128)} %initial.1) | copy-start | bytes 388
  17.0 0.9 %copy-start.1 = (bf16[1,64,1088]{2,1,0:T(8,128)(2,1)S(1)}, bf16[1,64,1088]{2,1,0:T(8,128)(2,1)}, u32[]{:S(2)}) copy-start(bf16[1,64,1088]{2,1,0:T(8,128)(2,1)} %own.1) | copy-start | bytes 417796
  17.0 4.5 %copy-start = (bf16[1344,256]{1,0:T(8,128)(2,1)S(1)}, bf16[1344,256]{1,0:T(8,128)(2,1)}, u32[]{:S(2)}) copy-start(bf16[1344,256]{1,0:T(8,128)(2,1)} %constant.2.clone.tables) | copy-start | bytes 2064388
  17.9 4.3 %collective-permute-start.3 = (bf16[1,64,1088]{2,1,0:T(8,128)(2,1)S(1)}, bf16[1,64,1088]{2,1,0:T(8,128)(2,1)S(1)}, u32[]{:S(2)}, u32[]{:S(2)}) collective-permute-start(bf16[1,64,1088]{2,1,0:T(8,128)(2,1)S(1)} %copy-done.1), channel_id=1, source_target_pairs={{0,128},{128,256},{256,384},{1,129},{129,257},{257,385},{2,130},{1... | collective-permute-start | bytes 417800 | tf_op jit(solution)/shard_map/ppermute | solution.py:391
  19.6 2.9 %collective-permute-start.4 = (bf16[1,64,1088]{2,1,0:T(8,128)(2,1)S(1)}, bf16[1,64,1088]{2,1,0:T(8,128)(2,1)S(1)}, u32[]{:S(2)}, u32[]{:S(2)}) collective-permute-start(bf16[1,64,1088]{2,1,0:T(8,128)(2,1)S(1)} %collective-permute-done.below), channel_id=1, source_target_pairs={{0,128},{256,384},{1,129},{257,385},{2,130},{258,386},{3,131},{259... | collective-permute-start | bytes 417800 | tf_op jit(solution)/shard_map/ppermute | solution.py:424
  35.3 8.9 %collective-permute-start.6 = (f32[16,1,128]{2,0,1:T(8,128)S(1)}, f32[16,1,128]{2,0,1:T(8,128)S(1)}, u32[]{:S(2)}, u32[]{:S(2)}) collective-permute-start(f32[16,1,128]{2,0,1:T(8,128)S(1)} %bitcast.8), channel_id=1, source_target_pairs={{6,2},{7,3},{0,4},{1,5},{10,6},{11,7},{4,8},{5,9},{14,10},{15,11},... | collective-permute-start | bytes 24584 | tf_op jit(solution)/shard_map/ppermute | solution.py:433

commit v12 on v10

--- a/solution.py
+++ b/solution.py
@@ -188,10 +188,16 @@
     )(own, below, tables)
 
 
-def flow_kernel(own_spec, own_energies, near, near_below, record, remote, shifts_in, tables, out, spec, lagged, shift_row):
+def flow_kernel(
+    own_spec, own_energies, near, near_below, lower, record, shifts_in, tables, out, spec, lagged, shift_row
+):
     spread = table(tables, "spread")
     energies = []
-    for m, spectrum in enumerate(section_spectra(block_tile(near), block_tile(near_below), tables)):
+
+    def second(start, span):
+        return near_below[0, :, pl.ds(start, span)] + lower[0, :, pl.ds(start, span)]
+
+    for m, spectrum in enumerate(section_spectra(block_tile(near), second, tables)):
         spec[m] = spectrum
         energies.append(energy(spectrum))
 
@@ -284,12 +290,10 @@
     flow = rec + 0.5 * slope / (1.0 + jnp.abs(bend))
     result = jnp.where(lane_1 < 2 * COLS, flow, rec)
     out[...] = jnp.broadcast_to(result, out.shape)
-    for i in range(2):
-        out[:, pl.ds((4 + i) * COLS, COLS)] = jnp.broadcast_to(remote[0, i], (out.shape[0], COLS))
-
-
-def pair_flow(own_parts, near, near_below, record, remote_initial, offsets, tables, copies):
-    operands = (*own_parts, near, near_below, record, remote_initial, offsets, tables)
+
+
+def pair_flow(own_parts, near, near_below, lower, record, offsets, tables, copies):
+    operands = (*own_parts, near, near_below, lower, record, offsets, tables)
     return pl.pallas_call(
         flow_kernel,
         out_shape=jax.ShapeDtypeStruct((copies, PATCH), f32),
@@ -304,7 +308,7 @@
     )(*operands)
 
 
-def relax_kernel(springs, ring, other, flow_out, moving_out):
+def relax_kernel(springs, ring, first_ring, second_ring, flow_out, moving_out):
     sec = lax.axis_index("sec")
     row = lax.axis_index("row")
     last_row = lax.axis_size("row") - 1
@@ -328,9 +332,11 @@
     first = in_ring == 0
     final = in_ring == RING - 1
     here = ring[...]
-    beyond = other[...]
+    odd = jnp.broadcast_to(lax.rem(row // RING, 2), (count, PATCH)) == 1
+    beyond = jnp.where(other_first == odd, second_ring[...], first_ring[...])
+    far_side = jnp.where(other_first == odd, first_ring[...], second_ring[...])
     moving = [pltpu.roll(b, PATCH - 2 * COLS, 1) for b in (here, beyond)]
-    third = pltpu.roll(here, PATCH - 4 * COLS, 1)
+    third = pltpu.roll(far_side, PATCH - 2 * COLS, 1)
 
     def moved(x, by):
         by = by % count
@@ -368,15 +374,15 @@
         ref[0, 1] = line[:, COLS : 2 * COLS]
 
 
-def relax(springs, ring, other, shape):
+def relax(springs, ring, first_ring, second_ring, shape):
     in_vmem = pl.BlockSpec(memory_space=pltpu.VMEM)
     return pl.pallas_call(
         relax_kernel,
         out_shape=[jax.ShapeDtypeStruct(shape, f32)] * 2,
-        in_specs=[in_vmem] * 3,
+        in_specs=[in_vmem] * 4,
         out_specs=[in_vmem] * 2,
         compiler_params=pltpu.CompilerParams(vmem_limit_bytes=VMEM_LIMIT),
-    )(springs, ring, other)
+    )(springs, ring, first_ring, second_ring)
 
 
 def shifted(block, axis, distance):
@@ -385,39 +391,42 @@
     return lax.ppermute(block, axis, route)
 
 
-def ring_route(rows, outward):
-    route = []
+def ring_routes(rows):
+    routes = ([], [])
     for r in range(rows):
-        step = RING if (r % RING < RING // 2) == outward else -RING
-        if 0 <= r - step < rows:
-            route.append((r - step, r))
-    return route
+        ring = r // RING
+        if r % RING < RING - 1 and r >= RING:
+            routes[ring % 2].append((r - RING, r))
+        if r % RING > 0 and r + RING < rows:
+            routes[1 - ring % 2].append((r + RING, r))
+    return routes
 
 
 def per_device(images, initial, offsets, stiffness, plan):
     rows = lax.axis_size("row")
-    below = shifted(images, "row", -1)
-    remote_initial = lax.ppermute(initial, "row", ring_route(rows, False))
+    at = lambda s, r: s * rows + r
+    below = lax.ppermute(
+        images, ("sec", "row"), [(at(s, r + 1), at(s, r)) for s in range(1, SECS) for r in range(rows - 1)]
+    )
+    lower = lax.ppermute(
+        images, ("sec", "row"), [(at(s, r + 1), at(s + 1, r)) for s in range(2) for r in range(rows - 1)]
+    )
     near_offsets = shifted(offsets, "sec", 1)
     record, springs = prepare(plan, initial, stiffness)
     later_images, record, springs = lax.optimization_barrier((images, record, springs))
     near = shifted(later_images, "sec", 1)
-    below, near_offsets, remote_initial, record, springs = lax.optimization_barrier(
-        (below, near_offsets, remote_initial, record, springs)
-    )
-    near_below = shifted(below, "sec", 1)
+    below, near_offsets, record, springs = lax.optimization_barrier((below, near_offsets, record, springs))
+    near_below = lax.ppermute(below, "sec", [(2, 3)])
     count = SECS * RING
     tables = jnp.asarray(constant_tables())
     own_parts = own_spectra(images, below, tables)
-    mine = pair_flow(own_parts, near, near_below, record, remote_initial, near_offsets, tables, count)
+    mine = pair_flow(own_parts, near, near_below, lower, record, near_offsets, tables, count)
     groups = [
         [s * rows + RING * g + j for s in range(SECS) for j in range(RING)] for g in range(rows // RING)
     ]
     ring = lax.all_to_all(mine.reshape(count, 1, PATCH), ("sec", "row"), 0, 0, axis_index_groups=groups)
-    other = lax.ppermute(ring, "row", ring_route(rows, True))
-    return tuple(
-        relax(springs, ring.reshape(count, PATCH), other.reshape(count, PATCH), initial.shape)
-    )
+    blocks = [ring] + [lax.ppermute(ring, "row", route) for route in ring_routes(rows)]
+    return tuple(relax(springs, *(block.reshape(count, PATCH) for block in blocks), initial.shape))
 
 
 def solution(mesh):

time: 47 us -> 44.4 us (0.945)
  the two profiles are of different devices: /device:TPU:256 before, /device:TPU:198 now
where the time goes in v12:
time: 44.4 us; the launch traced here: 44.1 us
  starting transfers between devices  19.9 us (45%)
  blocking collectives  14.2 us (32%)
  waiting for transfers between devices  4.26 us (10%)
  Pallas kernels  3.96 us (9%)
  local copies, waits for them, and re-layouts  0.98 us (2%)
  between operations  0.78 us (2%)
    all_to_all x1, blocking collectives, per_device(): lax.all_to_all(mine.reshape(count, 1, PATCH), ('sec', 'row'), 0, 0, axis_...  14.2 us
    ppermute x1, starting transfers between devices, per_device(): lax.ppermute(images, ('sec', 'row'), [(at(s, r + 1), at(s + 1, r)) for s...  8.96 us
    ppermute x2, starting transfers between devices, per_device(): lax.ppermute(ring, 'row', route)  5.52 us
    ppermute x2, waiting for transfers between devices, per_device(): lax.ppermute(ring, 'row', route)  4.24 us
    ppermute x2, starting transfers between devices, shifted(): return lax.ppermute(block, axis, route)  3.99 us
    pallas_call x1, Pallas kernels, pair_flow(): pl.pallas_call(flow_kernel, out_shape=jax.ShapeDtypeStruct((copies, PATCH...  1.73 us
    unnamed x10, local copies, waits for them, and re-layouts  0.98 us
    pallas_call x1, Pallas kernels, relax(): pl.pallas_call(relax_kernel, out_shape=[jax.ShapeDtypeStruct(shape, f32)]...  0.94 us
  transfers between devices with their start and end apart: 7, of which 1 were waited for; matrix products, arithmetic and copies ran while one was open for 0% of the time, Pallas kernels for 3%

profile of v12, /device:TPU:198, one launch (start us, length us, event | category | flops | bytes accessed | tf_op | source)
XLA Modules:
  0.0 44.1 jit_solution(9880392501171736479)
XLA Ops:
  0.7 0.8 %collective-permute-start = (bf16[1,64,1088]{2,1,0:T(8,128)(2,1)}, bf16[1,64,1088]{2,1,0:T(8,128)(2,1)S(1)}, u32[]{:S(2)}, u32[]{:S(2)}) collective-permute-start(bf16[1,64,1088]{2,1,0:T(8,128)(2,1)} %own.1), channel_id=1, source_target_pairs={{129,128},{130,129},{131,130},{132,131},{133,132},{134,133},{135,1... | collective-permute-start | bytes 417800 | tf_op jit(solution)/shard_map/ppermute | solution.py:408
  1.5 9.0 %collective-permute-start.4 = (bf16[1,64,1088]{2,1,0:T(8,128)(2,1)}, bf16[1,64,1088]{2,1,0:T(8,128)(2,1)S(1)}, u32[]{:S(2)}, u32[]{:S(2)}) collective-permute-start(bf16[1,64,1088]{2,1,0:T(8,128)(2,1)} %own.1), channel_id=1, source_target_pairs={{1,128},{2,129},{3,130},{4,131},{5,132},{6,133},{7,134},{8,135},{9... | collective-permute-start | bytes 417800 | tf_op jit(solution)/shard_map/ppermute | solution.py:411
  10.4 2.1 %collective-permute-start.1 = (s32[1,2,1,16]{3,2,1,0:T(1,128)}, s32[1,2,1,16]{3,2,1,0:T(1,128)S(1)}, u32[]{:S(2)}, u32[]{:S(2)}) collective-permute-start(s32[1,2,1,16]{3,2,1,0:T(1,128)} %param.8), channel_id=1, source_target_pairs={{0,128},{128,256},{256,384},{1,129},{129,257},{257,385},{2,130},{1... | collective-permute-start | bytes 392 | tf_op jit(solution)/shard_map/ppermute | solution.py:391
  12.5 0.0 copy-done.4
  12.5 0.0 copy-done.2
  12.5 0.0 copy-start.3
  12.5 0.7 %copy-done.3 = f32[8,2]{0,1:T(2,128)S(1)} copy-done((f32[8,2]{0,1:T(2,128)S(1)}, f32[8,2]{0,1:T(2,128)}, u32[]{:S(2)}) %copy-start.3) | copy-done | bytes 88
  13.2 0.6 %shard_map.77 = (f32[1,128]{1,0:T(1,128)S(1)}, f32[8,128]{1,0:T(8,128)S(1)}) custom-call(s32[3]{0:T(128)S(1)} %copy-done.4, f32[1,2,1,16]{3,2,1,0:T(1,128)S(1)} %copy-done.2, f32[2,8]{1,0:T(2,128)S(1)} %bitcast.14), custom_call_target="tpu_custom_call" | custom-call | flops 1000000000 | bytes 10000 | tf_op jit(solution)/shard_map/pallas_call | solution.py:128
  13.8 0.3 copy-done.1
  14.1 1.9 %collective-permute-start.2 = (bf16[1,64,1088]{2,1,0:T(8,128)(2,1)S(1)}, bf16[1,64,1088]{2,1,0:T(8,128)(2,1)S(1)}, u32[]{:S(2)}, u32[]{:S(2)}) collective-permute-start(bf16[1,64,1088]{2,1,0:T(8,128)(2,1)S(1)} %copy-done.1), channel_id=1, source_target_pairs={{0,128},{128,256},{256,384},{1,129},{129,257},{257,385},{2,130},{1... | collective-permute-start | bytes 417800 | tf_op jit(solution)/shard_map/ppermute | solution.py:391
  16.0 0.0 collective-permute-done.1.shifts_in
  16.1 0.0 collective-permute-done.below
  16.1 0.7 %collective-permute-start.3 = (bf16[1,64,1088]{2,1,0:T(8,128)(2,1)S(1)}, bf16[1,64,1088]{2,1,0:T(8,128)(2,1)S(1)}, u32[]{:S(2)}, u32[]{:S(2)}) collective-permute-start(bf16[1,64,1088]{2,1,0:T(8,128)(2,1)S(1)} %collective-permute-done.below), channel_id=1, source_target_pairs={{256,384},{257,385},{258,386},{259,387},{260,388},{261,389},{262,3... | collective-permute-start | bytes 417800 | tf_op jit(solution)/shard_map/ppermute | solution.py:419
  16.8 0.7 %shard_map.78 = (bf16[9,256,128]{2,1,0:T(8,128)(2,1)S(1)}, f32[16,128]{1,0:T(8,128)S(1)}) custom-call(bf16[1,64,1088]{2,1,0:T(8,128)(2,1)S(1)} %copy-done.1, bf16[1,64,1088]{2,1,0:T(8,128)(2,1)S(1)} %collective-permute-done.below, bf16[1344,256]{1,0:T(8,128)(2,1)S(1)} %copy-done), custom_call_target="tpu_custom_call" | custom-call | flops 600000000 | bytes 2000000 | tf_op jit(solution)/shard_map/pallas_call | solution.py:178
  17.4 0.0 collective-permute-done.2.near
  17.4 0.0 collective-permute-done.4.lower
  17.4 0.0 collective-permute-done.3.near_below
  17.5 1.7 %shard_map.79 = f32[16,128]{1,0:T(8,128)S(1)} custom-call(bf16[9,256,128]{2,1,0:T(8,128)(2,1)S(1)} %get-tuple-element.19.own_spec, f32[16,128]{1,0:T(8,128)S(1)} %get-tuple-element.20.own_energies, bf16[1,64,1088]{2,1,0:T(8,128)(2,1)S(1)} %collective-permute-done.2.near, bf16[1,64,1088]{2,1,0:T(8,128)(2,1)S(1)} %collective-permute-done.3.near_below, ...), custom_call_target="tpu_custom_call" | custom-call | tf_op jit(solution)/shard_map/pallas_call | solution.py:297
  19.2 14.2 %all_to_all.5 = f32[16,1,128]{2,1,0:T(1,128)S(1)} all-to-all(f32[16,1,128]{2,1,0:T(1,128)S(1)} %bitcast.8), channel_id=1, replica_groups={{0,1,2,3,128,129,130,131,256,257,258,259,384,385,386,387},{4,5,6,7,132,..., dimensions={0} | all-to-all | bytes 16384 | tf_op jit(solution)/shard_map/all_to_all | solution.py:427
  33.4 4.2 %collective-permute-start.5 = (f32[16,1,128]{2,0,1:T(8,128)S(1)}, f32[16,1,128]{2,0,1:T(8,128)S(1)}, u32[]{:S(2)}, u32[]{:S(2)}) collective-permute-start(f32[16,1,128]{2,0,1:T(8,128)S(1)} %bitcast.9), channel_id=1, source_target_pairs={{9,5},{10,6},{11,7},{4,8},{5,9},{6,10},{17,13},{18,14},{19,15},{12... | collective-permute-start | bytes 24584 | tf_op jit(solution)/shard_map/ppermute | solution.py:428
  37.6 1.3 %collective-permute-start.6 = (f32[16,1,128]{2,0,1:T(8,128)S(1)}, f32[16,1,128]{2,0,1:T(8,128)S(1)}, u32[]{:S(2)}, u32[]{:S(2)}) collective-permute-start(f32[16,1,128]{2,0,1:T(8,128)S(1)} %bitcast.10), channel_id=1, source_target_pairs={{5,1},{6,2},{7,3},{0,4},{1,5},{2,6},{13,9},{14,10},{15,11},{8,12},... | collective-permute-start | bytes 24584 | tf_op jit(solution)/shard_map/ppermute | solution.py:428
  38.9 0.0 collective-permute-done.5
  39.0 4.2 %collective-permute-done.6 = f32[16,1,128]{2,0,1:T(8,128)S(1)} collective-permute-done((f32[16,1,128]{2,0,1:T(8,128)S(1)}, f32[16,1,128]{2,0,1:T(8,128)S(1)}, u32[]{:S(2)}, u32[]{:S(2)}) %collective-permute-start.6) | collective-permute-done | bytes 8224 | tf_op jit(solution)/shard_map/ppermute | solution.py:428
  43.2 0.9 %shard_map.80 = (f32[1,2,1,16]{3,2,1,0:T(1,128)}, f32[1,2,1,16]{3,2,1,0:T(1,128)}) custom-call(f32[8,128]{1,0:T(8,128)S(1)} %get-tuple-element.17.springs, f32[16,128]{1,0:T(8,128)S(1)} %bitcast.11, f32[16,128]{1,0:T(8,128)S(1)} %bitcast.12, f32[16,128]{1,0:T(8,128)S(1)} %bitcast.13), custom_call_target="tpu_custom_call" | custom-call | tf_op jit(solution)/shard_map/pallas_call | solution.py:379
  (5 shorter events, 0.0 us)
Async XLA Ops:
  0.6 11.9 %copy-start.4 = (s32[3]{0:T(128)S(1)}, s32[3]{0:T(128)}, u32[]{:S(2)}) copy-start(s32[3]{0:T(128)} %plan.1) | copy-start | bytes 40
  0.6 11.9 %copy-start.2 = (f32[1,2,1,16]{3,2,1,0:T(1,128)S(1)}, f32[1,2,1,16]{3,2,1,0:T(1,128)}, u32[]{:S(2)}) copy-start(f32[1,2,1,16]{3,2,1,0:T(1,128)} %initial.1) | copy-start | bytes 388
  0.7 15.4 %collective-permute-start = (bf16[1,64,1088]{2,1,0:T(8,128)(2,1)}, bf16[1,64,1088]{2,1,0:T(8,128)(2,1)S(1)}, u32[]{:S(2)}, u32[]{:S(2)}) collective-permute-start(bf16[1,64,1088]{2,1,0:T(8,128)(2,1)} %own.1), channel_id=1, source_target_pairs={{129,128},{130,129},{131,130},{132,131},{133,132},{134,133},{135,1... | collective-permute-start | bytes 417800 | tf_op jit(solution)/shard_map/ppermute | solution.py:408
  1.5 16.0 %collective-permute-start.4 = (bf16[1,64,1088]{2,1,0:T(8,128)(2,1)}, bf16[1,64,1088]{2,1,0:T(8,128)(2,1)S(1)}, u32[]{:S(2)}, u32[]{:S(2)}) collective-permute-start(bf16[1,64,1088]{2,1,0:T(8,128)(2,1)} %own.1), channel_id=1, source_target_pairs={{1,128},{2,129},{3,130},{4,131},{5,132},{6,133},{7,134},{8,135},{9... | collective-permute-start | bytes 417800 | tf_op jit(solution)/shard_map/ppermute | solution.py:411
  10.4 5.6 %collective-permute-start.1 = (s32[1,2,1,16]{3,2,1,0:T(1,128)}, s32[1,2,1,16]{3,2,1,0:T(1,128)S(1)}, u32[]{:S(2)}, u32[]{:S(2)}) collective-permute-start(s32[1,2,1,16]{3,2,1,0:T(1,128)} %param.8), channel_id=1, source_target_pairs={{0,128},{128,256},{256,384},{1,129},{129,257},{257,385},{2,130},{1... | collective-permute-start | bytes 392 | tf_op jit(solution)/shard_map/ppermute | solution.py:391
  12.5 0.7 %copy-start.3 = (f32[8,2]{0,1:T(2,128)S(1)}, f32[8,2]{0,1:T(2,128)}, u32[]{:S(2)}) copy-start(f32[8,2]{0,1:T(2,128)} %param.9) | copy-start | bytes 196
  13.2 0.9 %copy-start.1 = (bf16[1,64,1088]{2,1,0:T(8,128)(2,1)S(1)}, bf16[1,64,1088]{2,1,0:T(8,128)(2,1)}, u32[]{:S(2)}) copy-start(bf16[1,64,1088]{2,1,0:T(8,128)(2,1)} %own.1) | copy-start | bytes 417796
  13.2 3.5 %copy-start = (bf16[1344,256]{1,0:T(8,128)(2,1)S(1)}, bf16[1344,256]{1,0:T(8,128)(2,1)}, u32[]{:S(2)}) copy-start(bf16[1344,256]{1,0:T(8,128)(2,1)} %constant.2.clone.tables) | copy-start | bytes 2064388
  14.1 3.3 %collective-permute-start.2 = (bf16[1,64,1088]{2,1,0:T(8,128)(2,1)S(1)}, bf16[1,64,1088]{2,1,0:T(8,128)(2,1)S(1)}, u32[]{:S(2)}, u32[]{:S(2)}) collective-permute-start(bf16[1,64,1088]{2,1,0:T(8,128)(2,1)S(1)} %copy-done.1), channel_id=1, source_target_pairs={{0,128},{128,256},{256,384},{1,129},{129,257},{257,385},{2,130},{1... | collective-permute-start | bytes 417800 | tf_op jit(solution)/shard_map/ppermute | solution.py:391
  16.1 1.4 %collective-permute-start.3 = (bf16[1,64,1088]{2,1,0:T(8,128)(2,1)S(1)}, bf16[1,64,1088]{2,1,0:T(8,128)(2,1)S(1)}, u32[]{:S(2)}, u32[]{:S(2)}) collective-permute-start(bf16[1,64,1088]{2,1,0:T(8,128)(2,1)S(1)} %collective-permute-done.below), channel_id=1, source_target_pairs={{256,384},{257,385},{258,386},{259,387},{260,388},{261,389},{262,3... | collective-permute-start | bytes 417800 | tf_op jit(solution)/shard_map/ppermute | solution.py:419
  33.4 5.6 %collective-permute-start.5 = (f32[16,1,128]{2,0,1:T(8,128)S(1)}, f32[16,1,128]{2,0,1:T(8,128)S(1)}, u32[]{:S(2)}, u32[]{:S(2)}) collective-permute-start(f32[16,1,128]{2,0,1:T(8,128)S(1)} %bitcast.9), channel_id=1, source_target_pairs={{9,5},{10,6},{11,7},{4,8},{5,9},{6,10},{17,13},{18,14},{19,15},{12... | collective-permute-start | bytes 24584 | tf_op jit(solution)/shard_map/ppermute | solution.py:428
  37.6 5.5 %collective-permute-start.6 = (f32[16,1,128]{2,0,1:T(8,128)S(1)}, f32[16,1,128]{2,0,1:T(8,128)S(1)}, u32[]{:S(2)}, u32[]{:S(2)}) collective-permute-start(f32[16,1,128]{2,0,1:T(8,128)S(1)} %bitcast.10), channel_id=1, source_target_pairs={{5,1},{6,2},{7,3},{0,4},{1,5},{2,6},{13,9},{14,10},{15,11},{8,12},... | collective-permute-start | bytes 24584 | tf_op jit(solution)/shard_map/ppermute | solution.py:428

commit v13 on v12

--- a/solution.py
+++ b/solution.py
@@ -333,8 +333,10 @@
     final = in_ring == RING - 1
     here = ring[...]
     odd = jnp.broadcast_to(lax.rem(row // RING, 2), (count, PATCH)) == 1
-    beyond = jnp.where(other_first == odd, second_ring[...], first_ring[...])
-    far_side = jnp.where(other_first == odd, first_ring[...], second_ring[...])
+    inner = (jnp.broadcast_to(place, (count, PATCH)) > 0) & (jnp.broadcast_to(place, (count, PATCH)) < RING - 1)
+    in_second = inner & (other_first == odd)
+    beyond = jnp.where(in_second, second_ring[...], first_ring[...])
+    far_side = jnp.where(in_second, first_ring[...], second_ring[...])
     moving = [pltpu.roll(b, PATCH - 2 * COLS, 1) for b in (here, beyond)]
     third = pltpu.roll(far_side, PATCH - 2 * COLS, 1)
 
@@ -394,11 +396,12 @@
 def ring_routes(rows):
     routes = ([], [])
     for r in range(rows):
-        ring = r // RING
-        if r % RING < RING - 1 and r >= RING:
-            routes[ring % 2].append((r - RING, r))
-        if r % RING > 0 and r + RING < rows:
-            routes[1 - ring % 2].append((r + RING, r))
+        odd, place = r // RING % 2, r % RING
+        inner = 0 < place < RING - 1
+        if place < RING - 1 and r >= RING:
+            routes[odd if inner else 0].append((r - RING, r))
+        if place > 0 and r + RING < rows:
+            routes[1 - odd if inner else 0].append((r + RING, r))
     return routes
 
 

time: 44.4 us -> 42.5 us (0.957)
  the two profiles are of different devices: /device:TPU:198 before, /device:TPU:214 now
where the time goes in v13:
time: 42.5 us; the launch traced here: 42.1 us
  starting transfers between devices  18.8 us (44%)
  blocking collectives  14 us (33%)
  Pallas kernels  3.96 us (9%)
  waiting for transfers between devices  3.63 us (9%)
  local copies, waits for them, and re-layouts  0.98 us (2%)
  between operations  0.78 us (2%)
    all_to_all x1, blocking collectives, per_device(): lax.all_to_all(mine.reshape(count, 1, PATCH), ('sec', 'row'), 0, 0, axis_...  14 us
    ppermute x1, starting transfers between devices, per_device(): lax.ppermute(images, ('sec', 'row'), [(at(s, r + 1), at(s + 1, r)) for s...  7.16 us
    ppermute x2, starting transfers between devices, per_device(): lax.ppermute(ring, 'row', route)  6.15 us
    ppermute x2, starting transfers between devices, shifted(): return lax.ppermute(block, axis, route)  3.99 us
    ppermute x2, waiting for transfers between devices, per_device(): lax.ppermute(ring, 'row', route)  3.62 us
    pallas_call x1, Pallas kernels, pair_flow(): pl.pallas_call(flow_kernel, out_shape=jax.ShapeDtypeStruct((copies, PATCH...  1.73 us
    unnamed x10, local copies, waits for them, and re-layouts  0.98 us
    pallas_call x1, Pallas kernels, relax(): pl.pallas_call(relax_kernel, out_shape=[jax.ShapeDtypeStruct(shape, f32)]...  0.94 us
  transfers between devices with their start and end apart: 7, of which 2 were waited for; matrix products, arithmetic and copies ran while one was open for 0% of the time, Pallas kernels for 3%

profile of v13, /device:TPU:214, one launch (start us, length us, event | category | flops | bytes accessed | tf_op | source)
XLA Modules:
  0.0 42.1 jit_solution(8946540663551312431)
XLA Ops:
  0.6 0.0 copy-start.4
  0.6 0.0 copy-start.2
  0.7 0.8 %collective-permute-start = (bf16[1,64,1088]{2,1,0:T(8,128)(2,1)}, bf16[1,64,1088]{2,1,0:T(8,128)(2,1)S(1)}, u32[]{:S(2)}, u32[]{:S(2)}) collective-permute-start(bf16[1,64,1088]{2,1,0:T(8,128)(2,1)} %own.1), channel_id=1, source_target_pairs={{129,128},{130,129},{131,130},{132,131},{133,132},{134,133},{135,1... | collective-permute-start | bytes 417800 | tf_op jit(solution)/shard_map/ppermute | solution.py:411
  1.5 7.2 %collective-permute-start.4 = (bf16[1,64,1088]{2,1,0:T(8,128)(2,1)}, bf16[1,64,1088]{2,1,0:T(8,128)(2,1)S(1)}, u32[]{:S(2)}, u32[]{:S(2)}) collective-permute-start(bf16[1,64,1088]{2,1,0:T(8,128)(2,1)} %own.1), channel_id=1, source_target_pairs={{1,128},{2,129},{3,130},{4,131},{5,132},{6,133},{7,134},{8,135},{9... | collective-permute-start | bytes 417800 | tf_op jit(solution)/shard_map/ppermute | solution.py:414
  8.6 2.1 %collective-permute-start.1 = (s32[1,2,1,16]{3,2,1,0:T(1,128)}, s32[1,2,1,16]{3,2,1,0:T(1,128)S(1)}, u32[]{:S(2)}, u32[]{:S(2)}) collective-permute-start(s32[1,2,1,16]{3,2,1,0:T(1,128)} %param.8), channel_id=1, source_target_pairs={{0,128},{128,256},{256,384},{1,129},{129,257},{257,385},{2,130},{1... | collective-permute-start | bytes 392 | tf_op jit(solution)/shard_map/ppermute | solution.py:393
  10.7 0.0 copy-done.4
  10.7 0.7 %copy-done.3 = f32[8,2]{0,1:T(2,128)S(1)} copy-done((f32[8,2]{0,1:T(2,128)S(1)}, f32[8,2]{0,1:T(2,128)}, u32[]{:S(2)}) %copy-start.3) | copy-done | bytes 88
  11.4 0.6 %shard_map.77 = (f32[1,128]{1,0:T(1,128)S(1)}, f32[8,128]{1,0:T(8,128)S(1)}) custom-call(s32[3]{0:T(128)S(1)} %copy-done.4, f32[1,2,1,16]{3,2,1,0:T(1,128)S(1)} %copy-done.2, f32[2,8]{1,0:T(2,128)S(1)} %bitcast.14), custom_call_target="tpu_custom_call" | custom-call | flops 1000000000 | bytes 10000 | tf_op jit(solution)/shard_map/pallas_call | solution.py:128
  12.0 0.3 copy-done.1
  12.3 1.9 %collective-permute-start.2 = (bf16[1,64,1088]{2,1,0:T(8,128)(2,1)S(1)}, bf16[1,64,1088]{2,1,0:T(8,128)(2,1)S(1)}, u32[]{:S(2)}, u32[]{:S(2)}) collective-permute-start(bf16[1,64,1088]{2,1,0:T(8,128)(2,1)S(1)} %copy-done.1), channel_id=1, source_target_pairs={{0,128},{128,256},{256,384},{1,129},{129,257},{257,385},{2,130},{1... | collective-permute-start | bytes 417800 | tf_op jit(solution)/shard_map/ppermute | solution.py:393
  14.2 0.0 collective-permute-done.1.shifts_in
  14.3 0.0 collective-permute-done.below
  14.3 0.7 %collective-permute-start.3 = (bf16[1,64,1088]{2,1,0:T(8,128)(2,1)S(1)}, bf16[1,64,1088]{2,1,0:T(8,128)(2,1)S(1)}, u32[]{:S(2)}, u32[]{:S(2)}) collective-permute-start(bf16[1,64,1088]{2,1,0:T(8,128)(2,1)S(1)} %collective-permute-done.below), channel_id=1, source_target_pairs={{256,384},{257,385},{258,386},{259,387},{260,388},{261,389},{262,3... | collective-permute-start | bytes 417800 | tf_op jit(solution)/shard_map/ppermute | solution.py:422
  15.0 0.7 %shard_map.78 = (bf16[9,256,128]{2,1,0:T(8,128)(2,1)S(1)}, f32[16,128]{1,0:T(8,128)S(1)}) custom-call(bf16[1,64,1088]{2,1,0:T(8,128)(2,1)S(1)} %copy-done.1, bf16[1,64,1088]{2,1,0:T(8,128)(2,1)S(1)} %collective-permute-done.below, bf16[1344,256]{1,0:T(8,128)(2,1)S(1)} %copy-done), custom_call_target="tpu_custom_call" | custom-call | flops 600000000 | bytes 2000000 | tf_op jit(solution)/shard_map/pallas_call | solution.py:178
  15.6 0.0 collective-permute-done.2.near
  15.6 0.0 collective-permute-done.4.lower
  15.7 0.0 collective-permute-done.3.near_below
  15.7 1.7 %shard_map.79 = f32[16,128]{1,0:T(8,128)S(1)} custom-call(bf16[9,256,128]{2,1,0:T(8,128)(2,1)S(1)} %get-tuple-element.19.own_spec, f32[16,128]{1,0:T(8,128)S(1)} %get-tuple-element.20.own_energies, bf16[1,64,1088]{2,1,0:T(8,128)(2,1)S(1)} %collective-permute-done.2.near, bf16[1,64,1088]{2,1,0:T(8,128)(2,1)S(1)} %collective-permute-done.3.near_below, ...), custom_call_target="tpu_custom_call" | custom-call | tf_op jit(solution)/shard_map/pallas_call | solution.py:297
  17.4 14.0 %all_to_all.5 = f32[16,1,128]{2,1,0:T(1,128)S(1)} all-to-all(f32[16,1,128]{2,1,0:T(1,128)S(1)} %bitcast.8), channel_id=1, replica_groups={{0,1,2,3,128,129,130,131,256,257,258,259,384,385,386,387},{4,5,6,7,132,..., dimensions={0} | all-to-all | bytes 16384 | tf_op jit(solution)/shard_map/all_to_all | solution.py:430
  31.4 4.2 %collective-permute-start.5 = (f32[16,1,128]{2,0,1:T(8,128)S(1)}, f32[16,1,128]{2,0,1:T(8,128)S(1)}, u32[]{:S(2)}, u32[]{:S(2)}) collective-permute-start(f32[16,1,128]{2,0,1:T(8,128)S(1)} %bitcast.9), channel_id=1, source_target_pairs={{7,3},{0,4},{9,5},{10,6},{11,7},{4,8},{5,9},{6,10},{15,11},{8,12},... | collective-permute-start | bytes 24584 | tf_op jit(solution)/shard_map/ppermute | solution.py:431
  35.7 1.9 %collective-permute-start.6 = (f32[16,1,128]{2,0,1:T(8,128)S(1)}, f32[16,1,128]{2,0,1:T(8,128)S(1)}, u32[]{:S(2)}, u32[]{:S(2)}) collective-permute-start(f32[16,1,128]{2,0,1:T(8,128)S(1)} %bitcast.10), channel_id=1, source_target_pairs={{5,1},{6,2},{1,5},{2,6},{13,9},{14,10},{9,13},{10,14},{21,17},{22,... | collective-permute-start | bytes 24584 | tf_op jit(solution)/shard_map/ppermute | solution.py:431
  37.6 2.7 %collective-permute-done.5 = f32[16,1,128]{2,0,1:T(8,128)S(1)} collective-permute-done((f32[16,1,128]{2,0,1:T(8,128)S(1)}, f32[16,1,128]{2,0,1:T(8,128)S(1)}, u32[]{:S(2)}, u32[]{:S(2)}) %collective-permute-start.5) | collective-permute-done | bytes 8224 | tf_op jit(solution)/shard_map/ppermute | solution.py:431
  40.3 0.9 %collective-permute-done.6 = f32[16,1,128]{2,0,1:T(8,128)S(1)} collective-permute-done((f32[16,1,128]{2,0,1:T(8,128)S(1)}, f32[16,1,128]{2,0,1:T(8,128)S(1)}, u32[]{:S(2)}, u32[]{:S(2)}) %collective-permute-start.6) | collective-permute-done | bytes 8224 | tf_op jit(solution)/shard_map/ppermute | solution.py:431
  41.2 0.9 %shard_map.80 = (f32[1,2,1,16]{3,2,1,0:T(1,128)}, f32[1,2,1,16]{3,2,1,0:T(1,128)}) custom-call(f32[8,128]{1,0:T(8,128)S(1)} %get-tuple-element.17.springs, f32[16,128]{1,0:T(8,128)S(1)} %bitcast.11, f32[16,128]{1,0:T(8,128)S(1)} %bitcast.12, f32[16,128]{1,0:T(8,128)S(1)} %bitcast.13), custom_call_target="tpu_custom_call" | custom-call | tf_op jit(solution)/shard_map/pallas_call | solution.py:381
  (5 shorter events, 0.0 us)
Async XLA Ops:
  0.6 10.1 %copy-start.4 = (s32[3]{0:T(128)S(1)}, s32[3]{0:T(128)}, u32[]{:S(2)}) copy-start(s32[3]{0:T(128)} %plan.1) | copy-start | bytes 40
  0.6 10.1 %copy-start.2 = (f32[1,2,1,16]{3,2,1,0:T(1,128)S(1)}, f32[1,2,1,16]{3,2,1,0:T(1,128)}, u32[]{:S(2)}) copy-start(f32[1,2,1,16]{3,2,1,0:T(1,128)} %initial.1) | copy-start | bytes 388
  0.7 13.6 %collective-permute-start = (bf16[1,64,1088]{2,1,0:T(8,128)(2,1)}, bf16[1,64,1088]{2,1,0:T(8,128)(2,1)S(1)}, u32[]{:S(2)}, u32[]{:S(2)}) collective-permute-start(bf16[1,64,1088]{2,1,0:T(8,128)(2,1)} %own.1), channel_id=1, source_target_pairs={{129,128},{130,129},{131,130},{132,131},{133,132},{134,133},{135,1... | collective-permute-start | bytes 417800 | tf_op jit(solution)/shard_map/ppermute | solution.py:411
  1.5 14.2 %collective-permute-start.4 = (bf16[1,64,1088]{2,1,0:T(8,128)(2,1)}, bf16[1,64,1088]{2,1,0:T(8,128)(2,1)S(1)}, u32[]{:S(2)}, u32[]{:S(2)}) collective-permute-start(bf16[1,64,1088]{2,1,0:T(8,128)(2,1)} %own.1), channel_id=1, source_target_pairs={{1,128},{2,129},{3,130},{4,131},{5,132},{6,133},{7,134},{8,135},{9... | collective-permute-start | bytes 417800 | tf_op jit(solution)/shard_map/ppermute | solution.py:414
  8.6 5.6 %collective-permute-start.1 = (s32[1,2,1,16]{3,2,1,0:T(1,128)}, s32[1,2,1,16]{3,2,1,0:T(1,128)S(1)}, u32[]{:S(2)}, u32[]{:S(2)}) collective-permute-start(s32[1,2,1,16]{3,2,1,0:T(1,128)} %param.8), channel_id=1, source_target_pairs={{0,128},{128,256},{256,384},{1,129},{129,257},{257,385},{2,130},{1... | collective-permute-start | bytes 392 | tf_op jit(solution)/shard_map/ppermute | solution.py:393
  10.7 0.7 %copy-start.3 = (f32[8,2]{0,1:T(2,128)S(1)}, f32[8,2]{0,1:T(2,128)}, u32[]{:S(2)}) copy-start(f32[8,2]{0,1:T(2,128)} %param.9) | copy-start | bytes 196
  11.4 0.9 %copy-start.1 = (bf16[1,64,1088]{2,1,0:T(8,128)(2,1)S(1)}, bf16[1,64,1088]{2,1,0:T(8,128)(2,1)}, u32[]{:S(2)}) copy-start(bf16[1,64,1088]{2,1,0:T(8,128)(2,1)} %own.1) | copy-start | bytes 417796
  11.4 3.5 %copy-start = (bf16[1344,256]{1,0:T(8,128)(2,1)S(1)}, bf16[1344,256]{1,0:T(8,128)(2,1)}, u32[]{:S(2)}) copy-start(bf16[1344,256]{1,0:T(8,128)(2,1)} %constant.2.clone.tables) | copy-start | bytes 2064388
  12.3 3.3 %collective-permute-start.2 = (bf16[1,64,1088]{2,1,0:T(8,128)(2,1)S(1)}, bf16[1,64,1088]{2,1,0:T(8,128)(2,1)S(1)}, u32[]{:S(2)}, u32[]{:S(2)}) collective-permute-start(bf16[1,64,1088]{2,1,0:T(8,128)(2,1)S(1)} %copy-done.1), channel_id=1, source_target_pairs={{0,128},{128,256},{256,384},{1,129},{129,257},{257,385},{2,130},{1... | collective-permute-start | bytes 417800 | tf_op jit(solution)/shard_map/ppermute | solution.py:393
  14.3 1.4 %collective-permute-start.3 = (bf16[1,64,1088]{2,1,0:T(8,128)(2,1)S(1)}, bf16[1,64,1088]{2,1,0:T(8,128)(2,1)S(1)}, u32[]{:S(2)}, u32[]{:S(2)}) collective-permute-start(bf16[1,64,1088]{2,1,0:T(8,128)(2,1)S(1)} %collective-permute-done.below), channel_id=1, source_target_pairs={{256,384},{257,385},{258,386},{259,387},{260,388},{261,389},{262,3... | collective-permute-start | bytes 417800 | tf_op jit(solution)/shard_map/ppermute | solution.py:422
  31.4 8.9 %collective-permute-start.5 = (f32[16,1,128]{2,0,1:T(8,128)S(1)}, f32[16,1,128]{2,0,1:T(8,128)S(1)}, u32[]{:S(2)}, u32[]{:S(2)}) collective-permute-start(f32[16,1,128]{2,0,1:T(8,128)S(1)} %bitcast.9), channel_id=1, source_target_pairs={{7,3},{0,4},{9,5},{10,6},{11,7},{4,8},{5,9},{6,10},{15,11},{8,12},... | collective-permute-start | bytes 24584 | tf_op jit(solution)/shard_map/ppermute | solution.py:431
  35.7 5.5 %collective-permute-start.6 = (f32[16,1,128]{2,0,1:T(8,128)S(1)}, f32[16,1,128]{2,0,1:T(8,128)S(1)}, u32[]{:S(2)}, u32[]{:S(2)}) collective-permute-start(f32[16,1,128]{2,0,1:T(8,128)S(1)} %bitcast.10), channel_id=1, source_target_pairs={{5,1},{6,2},{1,5},{2,6},{13,9},{14,10},{9,13},{10,14},{21,17},{22,... | collective-permute-start | bytes 24584 | tf_op jit(solution)/shard_map/ppermute | solution.py:431

commit v14 on v13

--- a/solution.py
+++ b/solution.py
@@ -189,7 +189,7 @@
 
 
 def flow_kernel(
-    own_spec, own_energies, near, near_below, lower, record, shifts_in, tables, out, spec, lagged, shift_row
+    own_spec, own_energies, lower, near, near_below, record, shifts_in, tables, out, spec, lagged, shift_row
 ):
     spread = table(tables, "spread")
     energies = []
@@ -293,7 +293,7 @@
 
 
 def pair_flow(own_parts, near, near_below, lower, record, offsets, tables, copies):
-    operands = (*own_parts, near, near_below, lower, record, offsets, tables)
+    operands = (*own_parts, lower, near, near_below, record, offsets, tables)
     return pl.pallas_call(
         flow_kernel,
         out_shape=jax.ShapeDtypeStruct((copies, PATCH), f32),
@@ -407,6 +407,7 @@
 
 def per_device(images, initial, offsets, stiffness, plan):
     rows = lax.axis_size("row")
+    near = shifted(images, "sec", 1)
     at = lambda s, r: s * rows + r
     below = lax.ppermute(
         images, ("sec", "row"), [(at(s, r + 1), at(s, r)) for s in range(1, SECS) for r in range(rows - 1)]
@@ -416,8 +417,6 @@
     )
     near_offsets = shifted(offsets, "sec", 1)
     record, springs = prepare(plan, initial, stiffness)
-    later_images, record, springs = lax.optimization_barrier((images, record, springs))
-    near = shifted(later_images, "sec", 1)
     below, near_offsets, record, springs = lax.optimization_barrier((below, near_offsets, record, springs))
     near_below = lax.ppermute(below, "sec", [(2, 3)])
     count = SECS * RING

time: 42.5 us -> 42 us (0.988)
  the two profiles are of different devices: /device:TPU:214 before, /device:TPU:272 now
where the time goes in v14:
time: 42 us; the launch traced here: 41.7 us
  starting transfers between devices  21.2 us (50%)
  blocking collectives  11.4 us (27%)
  Pallas kernels  3.96 us (9%)
  waiting for transfers between devices  3.63 us (9%)
  between operations  0.78 us (2%)
  local copies, waits for them, and re-layouts  0.69 us (2%)
    all_to_all x1, blocking collectives, per_device(): lax.all_to_all(mine.reshape(count, 1, PATCH), ('sec', 'row'), 0, 0, axis_...  11.4 us
    ppermute x1, starting transfers between devices, per_device(): lax.ppermute(images, ('sec', 'row'), [(at(s, r + 1), at(s + 1, r)) for s...  8.18 us
    ppermute x2, starting transfers between devices, per_device(): lax.ppermute(ring, 'row', route)  7.51 us
    ppermute x2, starting transfers between devices, shifted(): return lax.ppermute(block, axis, route)  3.99 us
    ppermute x2, waiting for transfers between devices, per_device(): lax.ppermute(ring, 'row', route)  3.62 us
    pallas_call x1, Pallas kernels, pair_flow(): pl.pallas_call(flow_kernel, out_shape=jax.ShapeDtypeStruct((copies, PATCH...  1.73 us
    pallas_call x1, Pallas kernels, relax(): pl.pallas_call(relax_kernel, out_shape=[jax.ShapeDtypeStruct(shape, f32)]...  0.94 us
  transfers between devices with their start and end apart: 7, of which 2 were waited for; matrix products, arithmetic and copies ran while one was open for 0% of the time, Pallas kernels for 3%

profile of v14, /device:TPU:272, one launch (start us, length us, event | category | flops | bytes accessed | tf_op | source)
XLA Modules:
  0.0 41.7 jit_solution(12104315540769776599)
XLA Ops:
  0.6 0.0 copy-start.4
  0.7 0.8 %collective-permute-start = (bf16[1,64,1088]{2,1,0:T(8,128)(2,1)}, bf16[1,64,1088]{2,1,0:T(8,128)(2,1)S(1)}, u32[]{:S(2)}, u32[]{:S(2)}) collective-permute-start(bf16[1,64,1088]{2,1,0:T(8,128)(2,1)} %own.1), channel_id=1, source_target_pairs={{129,128},{130,129},{131,130},{132,131},{133,132},{134,133},{135,1... | collective-permute-start | bytes 417800 | tf_op jit(solution)/shard_map/ppermute | solution.py:412
  1.5 8.2 %collective-permute-start.2 = (bf16[1,64,1088]{2,1,0:T(8,128)(2,1)}, bf16[1,64,1088]{2,1,0:T(8,128)(2,1)S(1)}, u32[]{:S(2)}, u32[]{:S(2)}) collective-permute-start(bf16[1,64,1088]{2,1,0:T(8,128)(2,1)} %own.1), channel_id=1, source_target_pairs={{1,128},{2,129},{3,130},{4,131},{5,132},{6,133},{7,134},{8,135},{9... | collective-permute-start | bytes 417800 | tf_op jit(solution)/shard_map/ppermute | solution.py:415
  9.7 2.1 %collective-permute-start.3 = (bf16[1,64,1088]{2,1,0:T(8,128)(2,1)}, bf16[1,64,1088]{2,1,0:T(8,128)(2,1)S(1)}, u32[]{:S(2)}, u32[]{:S(2)}) collective-permute-start(bf16[1,64,1088]{2,1,0:T(8,128)(2,1)} %own.1), channel_id=1, source_target_pairs={{0,128},{128,256},{256,384},{1,129},{129,257},{257,385},{2,130},{1... | collective-permute-start | bytes 417800 | tf_op jit(solution)/shard_map/ppermute | solution.py:393
  11.7 1.9 %collective-permute-start.1 = (s32[1,2,1,16]{3,2,1,0:T(1,128)}, s32[1,2,1,16]{3,2,1,0:T(1,128)S(1)}, u32[]{:S(2)}, u32[]{:S(2)}) collective-permute-start(s32[1,2,1,16]{3,2,1,0:T(1,128)} %param.8), channel_id=1, source_target_pairs={{0,128},{128,256},{256,384},{1,129},{129,257},{257,385},{2,130},{1... | collective-permute-start | bytes 392 | tf_op jit(solution)/shard_map/ppermute | solution.py:393
  13.7 0.0 copy-done.4
  13.7 0.0 copy-done.2
  13.7 0.0 copy-start.3
  13.7 0.7 %copy-done.3 = f32[8,2]{0,1:T(2,128)S(1)} copy-done((f32[8,2]{0,1:T(2,128)S(1)}, f32[8,2]{0,1:T(2,128)}, u32[]{:S(2)}) %copy-start.3) | copy-done | bytes 88
  14.4 0.6 %shard_map.77 = (f32[1,128]{1,0:T(1,128)S(1)}, f32[8,128]{1,0:T(8,128)S(1)}) custom-call(s32[3]{0:T(128)S(1)} %copy-done.4, f32[1,2,1,16]{3,2,1,0:T(1,128)S(1)} %copy-done.2, f32[2,8]{1,0:T(2,128)S(1)} %bitcast.14), custom_call_target="tpu_custom_call" | custom-call | flops 1000000000 | bytes 10000 | tf_op jit(solution)/shard_map/pallas_call | solution.py:128
  15.0 0.0 collective-permute-done.1.shifts_in
  15.0 0.0 collective-permute-done.below
  15.0 0.7 %collective-permute-start.4 = (bf16[1,64,1088]{2,1,0:T(8,128)(2,1)S(1)}, bf16[1,64,1088]{2,1,0:T(8,128)(2,1)S(1)}, u32[]{:S(2)}, u32[]{:S(2)}) collective-permute-start(bf16[1,64,1088]{2,1,0:T(8,128)(2,1)S(1)} %collective-permute-done.below), channel_id=1, source_target_pairs={{256,384},{257,385},{258,386},{259,387},{260,388},{261,389},{262,3... | collective-permute-start | bytes 417800 | tf_op jit(solution)/shard_map/ppermute | solution.py:421
  15.7 0.7 %shard_map.78 = (bf16[9,256,128]{2,1,0:T(8,128)(2,1)S(1)}, f32[16,128]{1,0:T(8,128)S(1)}) custom-call(bf16[1,64,1088]{2,1,0:T(8,128)(2,1)S(1)} %copy-done.1, bf16[1,64,1088]{2,1,0:T(8,128)(2,1)S(1)} %collective-permute-done.below, bf16[1344,256]{1,0:T(8,128)(2,1)S(1)} %copy-done), custom_call_target="tpu_custom_call" | custom-call | flops 600000000 | bytes 2000000 | tf_op jit(solution)/shard_map/pallas_call | solution.py:178
  16.4 0.0 collective-permute-done.2.lower
  16.4 0.0 collective-permute-done.3.near
  16.4 0.0 collective-permute-done.4.near_below
  16.4 1.7 %shard_map.79 = f32[16,128]{1,0:T(8,128)S(1)} custom-call(bf16[9,256,128]{2,1,0:T(8,128)(2,1)S(1)} %get-tuple-element.14.own_spec, f32[16,128]{1,0:T(8,128)S(1)} %get-tuple-element.15.own_energies, bf16[1,64,1088]{2,1,0:T(8,128)(2,1)S(1)} %collective-permute-done.2.lower, bf16[1,64,1088]{2,1,0:T(8,128)(2,1)S(1)} %collective-permute-done.3.near, ...), custom_call_target="tpu_custom_call" | custom-call | tf_op jit(solution)/shard_map/pallas_call | solution.py:297
  18.1 11.4 %all_to_all.5 = f32[16,1,128]{2,1,0:T(1,128)S(1)} all-to-all(f32[16,1,128]{2,1,0:T(1,128)S(1)} %bitcast.8), channel_id=1, replica_groups={{0,1,2,3,128,129,130,131,256,257,258,259,384,385,386,387},{4,5,6,7,132,..., dimensions={0} | all-to-all | bytes 16384 | tf_op jit(solution)/shard_map/all_to_all | solution.py:429
  29.6 5.6 %collective-permute-start.5 = (f32[16,1,128]{2,0,1:T(8,128)S(1)}, f32[16,1,128]{2,0,1:T(8,128)S(1)}, u32[]{:S(2)}, u32[]{:S(2)}) collective-permute-start(f32[16,1,128]{2,0,1:T(8,128)S(1)} %bitcast.9), channel_id=1, source_target_pairs={{7,3},{0,4},{9,5},{10,6},{11,7},{4,8},{5,9},{6,10},{15,11},{8,12},... | collective-permute-start | bytes 24584 | tf_op jit(solution)/shard_map/ppermute | solution.py:430
  35.2 1.9 %collective-permute-start.6 = (f32[16,1,128]{2,0,1:T(8,128)S(1)}, f32[16,1,128]{2,0,1:T(8,128)S(1)}, u32[]{:S(2)}, u32[]{:S(2)}) collective-permute-start(f32[16,1,128]{2,0,1:T(8,128)S(1)} %bitcast.10), channel_id=1, source_target_pairs={{5,1},{6,2},{1,5},{2,6},{13,9},{14,10},{9,13},{10,14},{21,17},{22,... | collective-permute-start | bytes 24584 | tf_op jit(solution)/shard_map/ppermute | solution.py:430
  37.1 1.3 %collective-permute-done.5 = f32[16,1,128]{2,0,1:T(8,128)S(1)} collective-permute-done((f32[16,1,128]{2,0,1:T(8,128)S(1)}, f32[16,1,128]{2,0,1:T(8,128)S(1)}, u32[]{:S(2)}, u32[]{:S(2)}) %collective-permute-start.5) | collective-permute-done | bytes 8224 | tf_op jit(solution)/shard_map/ppermute | solution.py:430
  38.4 2.3 %collective-permute-done.6 = f32[16,1,128]{2,0,1:T(8,128)S(1)} collective-permute-done((f32[16,1,128]{2,0,1:T(8,128)S(1)}, f32[16,1,128]{2,0,1:T(8,128)S(1)}, u32[]{:S(2)}, u32[]{:S(2)}) %collective-permute-start.6) | collective-permute-done | bytes 8224 | tf_op jit(solution)/shard_map/ppermute | solution.py:430
  40.7 0.9 %shard_map.80 = (f32[1,2,1,16]{3,2,1,0:T(1,128)}, f32[1,2,1,16]{3,2,1,0:T(1,128)}) custom-call(f32[8,128]{1,0:T(8,128)S(1)} %get-tuple-element.12.springs, f32[16,128]{1,0:T(8,128)S(1)} %bitcast.11, f32[16,128]{1,0:T(8,128)S(1)} %bitcast.12, f32[16,128]{1,0:T(8,128)S(1)} %bitcast.13), custom_call_target="tpu_custom_call" | custom-call | tf_op jit(solution)/shard_map/pallas_call | solution.py:381
  (5 shorter events, 0.0 us)
Async XLA Ops:
  0.6 13.0 %copy-start.4 = (s32[3]{0:T(128)S(1)}, s32[3]{0:T(128)}, u32[]{:S(2)}) copy-start(s32[3]{0:T(128)} %plan.1) | copy-start | bytes 40
  0.6 13.0 %copy-start.2 = (f32[1,2,1,16]{3,2,1,0:T(1,128)S(1)}, f32[1,2,1,16]{3,2,1,0:T(1,128)}, u32[]{:S(2)}) copy-start(f32[1,2,1,16]{3,2,1,0:T(1,128)} %initial.1) | copy-start | bytes 388
  0.7 14.3 %collective-permute-start = (bf16[1,64,1088]{2,1,0:T(8,128)(2,1)}, bf16[1,64,1088]{2,1,0:T(8,128)(2,1)S(1)}, u32[]{:S(2)}, u32[]{:S(2)}) collective-permute-start(bf16[1,64,1088]{2,1,0:T(8,128)(2,1)} %own.1), channel_id=1, source_target_pairs={{129,128},{130,129},{131,130},{132,131},{133,132},{134,133},{135,1... | collective-permute-start | bytes 417800 | tf_op jit(solution)/shard_map/ppermute | solution.py:412
  1.5 14.9 %collective-permute-start.2 = (bf16[1,64,1088]{2,1,0:T(8,128)(2,1)}, bf16[1,64,1088]{2,1,0:T(8,128)(2,1)S(1)}, u32[]{:S(2)}, u32[]{:S(2)}) collective-permute-start(bf16[1,64,1088]{2,1,0:T(8,128)(2,1)} %own.1), channel_id=1, source_target_pairs={{1,128},{2,129},{3,130},{4,131},{5,132},{6,133},{7,134},{8,135},{9... | collective-permute-start | bytes 417800 | tf_op jit(solution)/shard_map/ppermute | solution.py:415
  9.7 6.7 %collective-permute-start.3 = (bf16[1,64,1088]{2,1,0:T(8,128)(2,1)}, bf16[1,64,1088]{2,1,0:T(8,128)(2,1)S(1)}, u32[]{:S(2)}, u32[]{:S(2)}) collective-permute-start(bf16[1,64,1088]{2,1,0:T(8,128)(2,1)} %own.1), channel_id=1, source_target_pairs={{0,128},{128,256},{256,384},{1,129},{129,257},{257,385},{2,130},{1... | collective-permute-start | bytes 417800 | tf_op jit(solution)/shard_map/ppermute | solution.py:393
  11.7 3.2 %collective-permute-start.1 = (s32[1,2,1,16]{3,2,1,0:T(1,128)}, s32[1,2,1,16]{3,2,1,0:T(1,128)S(1)}, u32[]{:S(2)}, u32[]{:S(2)}) collective-permute-start(s32[1,2,1,16]{3,2,1,0:T(1,128)} %param.8), channel_id=1, source_target_pairs={{0,128},{128,256},{256,384},{1,129},{129,257},{257,385},{2,130},{1... | collective-permute-start | bytes 392 | tf_op jit(solution)/shard_map/ppermute | solution.py:393
  13.7 0.7 %copy-start.3 = (f32[8,2]{0,1:T(2,128)S(1)}, f32[8,2]{0,1:T(2,128)}, u32[]{:S(2)}) copy-start(f32[8,2]{0,1:T(2,128)} %param.9) | copy-start | bytes 196
  14.4 1.3 %copy-start = (bf16[1344,256]{1,0:T(8,128)(2,1)S(1)}, bf16[1344,256]{1,0:T(8,128)(2,1)}, u32[]{:S(2)}) copy-start(bf16[1344,256]{1,0:T(8,128)(2,1)} %constant.2.clone.tables) | copy-start | bytes 2064388
  14.4 1.3 %copy-start.1 = (bf16[1,64,1088]{2,1,0:T(8,128)(2,1)S(1)}, bf16[1,64,1088]{2,1,0:T(8,128)(2,1)}, u32[]{:S(2)}) copy-start(bf16[1,64,1088]{2,1,0:T(8,128)(2,1)} %own.1) | copy-start | bytes 417796
  15.0 1.4 %collective-permute-start.4 = (bf16[1,64,1088]{2,1,0:T(8,128)(2,1)S(1)}, bf16[1,64,1088]{2,1,0:T(8,128)(2,1)S(1)}, u32[]{:S(2)}, u32[]{:S(2)}) collective-permute-start(bf16[1,64,1088]{2,1,0:T(8,128)(2,1)S(1)} %collective-permute-done.below), channel_id=1, source_target_pairs={{256,384},{257,385},{258,386},{259,387},{260,388},{261,389},{262,3... | collective-permute-start | bytes 417800 | tf_op jit(solution)/shard_map/ppermute | solution.py:421
  29.6 8.9 %collective-permute-start.5 = (f32[16,1,128]{2,0,1:T(8,128)S(1)}, f32[16,1,128]{2,0,1:T(8,128)S(1)}, u32[]{:S(2)}, u32[]{:S(2)}) collective-permute-start(f32[16,1,128]{2,0,1:T(8,128)S(1)} %bitcast.9), channel_id=1, source_target_pairs={{7,3},{0,4},{9,5},{10,6},{11,7},{4,8},{5,9},{6,10},{15,11},{8,12},... | collective-permute-start | bytes 24584 | tf_op jit(solution)/shard_map/ppermute | solution.py:430
  35.2 5.5 %collective-permute-start.6 = (f32[16,1,128]{2,0,1:T(8,128)S(1)}, f32[16,1,128]{2,0,1:T(8,128)S(1)}, u32[]{:S(2)}, u32[]{:S(2)}) collective-permute-start(f32[16,1,128]{2,0,1:T(8,128)S(1)} %bitcast.10), channel_id=1, source_target_pairs={{5,1},{6,2},{1,5},{2,6},{13,9},{14,10},{9,13},{10,14},{21,17},{22,... | collective-permute-start | bytes 24584 | tf_op jit(solution)/shard_map/ppermute | solution.py:430

commit v15 on v14

--- a/solution.py
+++ b/solution.py
@@ -113,26 +113,23 @@
     return jnp.dot(a, b, preferred_element_type=f32)
 
 
-def prepare_kernel(plan, initial, stiffness, record, springs):
-    record[...] = jnp.zeros((1, PATCH), f32)
-    for i in range(2):
-        record[:, pl.ds((2 + i) * COLS, COLS)] = initial[0, i]
+def spring_kernel(plan, stiffness, springs):
     level_id = lax.broadcasted_iota(jnp.int32, stiffness.shape, 1)
     for sweep in range(SWEEPS):
         picked = jnp.sum(jnp.where(level_id == plan[sweep], stiffness[...], 0.0), axis=1, keepdims=True)
         springs[pl.ds(2 * sweep, 2), :] = jnp.broadcast_to(picked, (2, PATCH))
 
 
-def prepare(plan, initial, stiffness):
+def spring_rows(plan, stiffness):
     in_vmem = pl.BlockSpec(memory_space=pltpu.VMEM)
     return pl.pallas_call(
-        prepare_kernel,
-        out_shape=[jax.ShapeDtypeStruct((1, PATCH), f32), jax.ShapeDtypeStruct((8, PATCH), f32)],
-        in_specs=[pl.BlockSpec(memory_space=pltpu.SMEM), in_vmem, in_vmem],
-        out_specs=[in_vmem] * 2,
+        spring_kernel,
+        out_shape=jax.ShapeDtypeStruct((8, PATCH), f32),
+        in_specs=[pl.BlockSpec(memory_space=pltpu.SMEM), in_vmem],
+        out_specs=in_vmem,
         compiler_params=pltpu.CompilerParams(vmem_limit_bytes=VMEM_LIMIT),
         cost_estimate=pl.CostEstimate(flops=PREPARE_FLOPS, bytes_accessed=10_000, transcendentals=0),
-    )(plan, initial, stiffness.T)
+    )(plan, stiffness.T)
 
 
 def section_spectra(upper, lower, tables):
@@ -167,29 +164,33 @@
     return lambda start, span: ref[0, :, pl.ds(start, span)]
 
 
-def own_kernel(own, below, tables, spec, energies):
+def own_kernel(own, below, initial, tables, spec, energies, record):
+    record[...] = jnp.zeros((1, PATCH), f32)
+    for i in range(2):
+        record[:, pl.ds((2 + i) * COLS, COLS)] = initial[0, i]
     for m, spectrum in enumerate(section_spectra(block_tile(own), block_tile(below), tables)):
         spec[m] = spectrum
         energies[pl.ds(m, 1), :] = energy(spectrum)
 
 
-def own_spectra(own, below, tables):
+def own_spectra(own, below, initial, tables):
     in_vmem = pl.BlockSpec(memory_space=pltpu.VMEM)
     return pl.pallas_call(
         own_kernel,
         out_shape=[
             jax.ShapeDtypeStruct((PAIRS + 1, 2 * PATCH, PATCH), bf16),
             jax.ShapeDtypeStruct((2 * PAIRS, PATCH), f32),
+            jax.ShapeDtypeStruct((1, PATCH), f32),
         ],
-        in_specs=[in_vmem] * 3,
-        out_specs=[in_vmem] * 2,
+        in_specs=[in_vmem] * 4,
+        out_specs=[in_vmem] * 3,
         compiler_params=pltpu.CompilerParams(vmem_limit_bytes=VMEM_LIMIT),
         cost_estimate=pl.CostEstimate(flops=600_000_000, bytes_accessed=2_000_000, transcendentals=0),
-    )(own, below, tables)
+    )(own, below, initial, tables)
 
 
 def flow_kernel(
-    own_spec, own_energies, lower, near, near_below, record, shifts_in, tables, out, spec, lagged, shift_row
+    own_spec, own_energies, record, lower, near, near_below, shifts_in, tables, out, spec, lagged, shift_row
 ):
     spread = table(tables, "spread")
     energies = []
@@ -236,10 +237,8 @@
         modulus = square * lax.rsqrt(jnp.maximum(square, 1e-36))
         inverse = 1.0 / (modulus + floor)
         white = jnp.concatenate([cross_re * inverse, cross_im * inverse], axis=0)
-        high = white.astype(bf16)
-        low = (white - high.astype(f32)).astype(bf16)
-        found = dot(table(tables, "lag_y"), jnp.concatenate([high, low], axis=1))
-        part = found[: 2 * SHIFTS, :PATCH] + found[: 2 * SHIFTS, PATCH:] + found[2 * SHIFTS :, :PATCH]
+        found = dot(table(tables, "lag_y"), white.astype(bf16))
+        part = found[: 2 * SHIFTS] + found[2 * SHIFTS :]
         lagged[pl.ds(m * SHIFTS, SHIFTS), pl.ds(0, PATCH)] = part[:SHIFTS]
         lagged[pl.ds(m * SHIFTS, SHIFTS), pl.ds(PATCH, PATCH)] = part[SHIFTS:]
 
@@ -292,8 +291,8 @@
     out[...] = jnp.broadcast_to(result, out.shape)
 
 
-def pair_flow(own_parts, near, near_below, lower, record, offsets, tables, copies):
-    operands = (*own_parts, lower, near, near_below, record, offsets, tables)
+def pair_flow(own_parts, near, near_below, lower, offsets, tables, copies):
+    operands = (*own_parts, lower, near, near_below, offsets, tables)
     return pl.pallas_call(
         flow_kernel,
         out_shape=jax.ShapeDtypeStruct((copies, PATCH), f32),
@@ -416,13 +415,13 @@
         images, ("sec", "row"), [(at(s, r + 1), at(s + 1, r)) for s in range(2) for r in range(rows - 1)]
     )
     near_offsets = shifted(offsets, "sec", 1)
-    record, springs = prepare(plan, initial, stiffness)
-    below, near_offsets, record, springs = lax.optimization_barrier((below, near_offsets, record, springs))
+    springs = spring_rows(plan, stiffness)
+    below, near_offsets, springs = lax.optimization_barrier((below, near_offsets, springs))
     near_below = lax.ppermute(below, "sec", [(2, 3)])
     count = SECS * RING
     tables = jnp.asarray(constant_tables())
-    own_parts = own_spectra(images, below, tables)
-    mine = pair_flow(own_parts, near, near_below, lower, record, near_offsets, tables, count)
+    own_parts = own_spectra(images, below, initial, tables)
+    mine = pair_flow(own_parts, near, near_below, lower, near_offsets, tables, count)
     groups = [
         [s * rows + RING * g + j for s in range(SECS) for j in range(RING)] for g in range(rows // RING)
     ]

time: 42 us -> 41.9 us (level)
  local copies, waits for them, and re-layouts: 0.69 us -> 0.02 us
    unnamed x10, local copies, waits for them, and re-layouts: 0.69 us -> 0.02 us
  transfers between devices with their start and end apart: 7 -> 7, of which waited for: 2 -> 3; matrix products, arithmetic and copies ran while one was open for 0% -> 0% of each run, Pallas kernels for 3% -> 3%
where the time goes in v15:
time: 41.9 us; the launch traced here: 41.6 us
  starting transfers between devices  21.1 us (50%)
  blocking collectives  11.8 us (28%)
  waiting for transfers between devices  3.96 us (9%)
  Pallas kernels  3.89 us (9%)
  between operations  0.8 us (2%)
    all_to_all x1, blocking collectives, per_device(): lax.all_to_all(mine.reshape(count, 1, PATCH), ('sec', 'row'), 0, 0, axis_...  11.8 us
    ppermute x1, starting transfers between devices, per_device(): lax.ppermute(images, ('sec', 'row'), [(at(s, r + 1), at(s + 1, r)) for s...  8.18 us
    ppermute x2, starting transfers between devices, per_device(): lax.ppermute(ring, 'row', route)  7.51 us
    ppermute x2, starting transfers between devices, shifted(): return lax.ppermute(block, axis, route)  3.99 us
    ppermute x2, waiting for transfers between devices, per_device(): lax.ppermute(ring, 'row', route)  3.62 us
    pallas_call x1, Pallas kernels, pair_flow(): pl.pallas_call(flow_kernel, out_shape=jax.ShapeDtypeStruct((copies, PATCH...  1.65 us
    pallas_call x1, Pallas kernels, relax(): pl.pallas_call(relax_kernel, out_shape=[jax.ShapeDtypeStruct(shape, f32)]...  0.94 us
  transfers between devices with their start and end apart: 7, of which 3 were waited for; matrix products, arithmetic and copies ran while one was open for 0% of the time, Pallas kernels for 3%

profile of v15, /device:TPU:272, one launch (start us, length us, event | category | flops | bytes accessed | tf_op | source)
XLA Modules:
  0.0 41.6 jit_solution(17954083675487987597)
XLA Ops:
  0.6 0.0 copy-start.2
  0.6 0.0 copy-start.4
  0.7 0.8 %collective-permute-start = (bf16[1,64,1088]{2,1,0:T(8,128)(2,1)}, bf16[1,64,1088]{2,1,0:T(8,128)(2,1)S(1)}, u32[]{:S(2)}, u32[]{:S(2)}) collective-permute-start(bf16[1,64,1088]{2,1,0:T(8,128)(2,1)} %own.1), channel_id=1, source_target_pairs={{129,128},{130,129},{131,130},{132,131},{133,132},{134,133},{135,1... | collective-permute-start | bytes 417800 | tf_op jit(solution)/shard_map/ppermute | solution.py:411
  1.5 8.2 %collective-permute-start.2 = (bf16[1,64,1088]{2,1,0:T(8,128)(2,1)}, bf16[1,64,1088]{2,1,0:T(8,128)(2,1)S(1)}, u32[]{:S(2)}, u32[]{:S(2)}) collective-permute-start(bf16[1,64,1088]{2,1,0:T(8,128)(2,1)} %own.1), channel_id=1, source_target_pairs={{1,128},{2,129},{3,130},{4,131},{5,132},{6,133},{7,134},{8,135},{9... | collective-permute-start | bytes 417800 | tf_op jit(solution)/shard_map/ppermute | solution.py:414
  9.7 2.1 %collective-permute-start.3 = (bf16[1,64,1088]{2,1,0:T(8,128)(2,1)}, bf16[1,64,1088]{2,1,0:T(8,128)(2,1)S(1)}, u32[]{:S(2)}, u32[]{:S(2)}) collective-permute-start(bf16[1,64,1088]{2,1,0:T(8,128)(2,1)} %own.1), channel_id=1, source_target_pairs={{0,128},{128,256},{256,384},{1,129},{129,257},{257,385},{2,130},{1... | collective-permute-start | bytes 417800 | tf_op jit(solution)/shard_map/ppermute | solution.py:392
  11.7 1.9 %collective-permute-start.1 = (s32[1,2,1,16]{3,2,1,0:T(1,128)}, s32[1,2,1,16]{3,2,1,0:T(1,128)S(1)}, u32[]{:S(2)}, u32[]{:S(2)}) collective-permute-start(s32[1,2,1,16]{3,2,1,0:T(1,128)} %param.8), channel_id=1, source_target_pairs={{0,128},{128,256},{256,384},{1,129},{129,257},{257,385},{2,130},{1... | collective-permute-start | bytes 392 | tf_op jit(solution)/shard_map/ppermute | solution.py:392
  13.7 0.0 copy-done.2
  13.7 0.0 copy-done.4
  13.7 0.0 copy-start
  13.7 0.6 %shard_map.77.springs = f32[8,128]{1,0:T(8,128)S(1)} custom-call(s32[3]{0:T(128)S(1)} %copy-done.4, f32[2,8]{1,0:T(2,128)S(1)} %bitcast.14), custom_call_target="tpu_custom_call" | custom-call | flops 1000000000 | bytes 10000 | tf_op jit(solution)/shard_map/pallas_call | solution.py:125
  14.3 0.3 collective-permute-done.1.shifts_in
  14.7 0.0 collective-permute-done.below
  14.7 0.7 %collective-permute-start.4 = (bf16[1,64,1088]{2,1,0:T(8,128)(2,1)S(1)}, bf16[1,64,1088]{2,1,0:T(8,128)(2,1)S(1)}, u32[]{:S(2)}, u32[]{:S(2)}) collective-permute-start(bf16[1,64,1088]{2,1,0:T(8,128)(2,1)S(1)} %collective-permute-done.below), channel_id=1, source_target_pairs={{256,384},{257,385},{258,386},{259,387},{260,388},{261,389},{262,3... | collective-permute-start | bytes 417800 | tf_op jit(solution)/shard_map/ppermute | solution.py:420
  15.4 0.7 %shard_map.78 = (bf16[9,256,128]{2,1,0:T(8,128)(2,1)S(1)}, f32[16,128]{1,0:T(8,128)S(1)}, f32[1,128]{1,0:T(1,128)S(1)}) custom-call(bf16[1,64,1088]{2,1,0:T(8,128)(2,1)S(1)} %copy-done.1, bf16[1,64,1088]{2,1,0:T(8,128)(2,1)S(1)} %collective-permute-done.below, f32[1,2,1,16]{3,2,1,0:T(1,128)S(1)} %copy-done.3, bf16[1344,256]{1,0:T(8,128)(2,1)S(1)} %copy-done), custom_call_target="tpu_custom_call" | custom-call | flops 600000000 | bytes 2000000 | tf_op jit(solution)/shard_map/pallas_call | solution.py:178
  16.0 0.0 collective-permute-done.2.lower
  16.1 0.0 collective-permute-done.3.near
  16.1 0.0 collective-permute-done.4.near_below
  16.1 1.7 %shard_map.79 = f32[16,128]{1,0:T(8,128)S(1)} custom-call(bf16[9,256,128]{2,1,0:T(8,128)(2,1)S(1)} %get-tuple-element.10.own_spec, f32[16,128]{1,0:T(8,128)S(1)} %get-tuple-element.11.own_energies, f32[1,128]{1,0:T(1,128)S(1)} %get-tuple-element.12.record, bf16[1,64,1088]{2,1,0:T(8,128)(2,1)S(1)} %collective-permute-done.2.lower, ...), custom_call_target="tpu_custom_call" | custom-call | tf_op jit(solution)/shard_map/pallas_call | solution.py:296
  17.7 11.8 %all_to_all.5 = f32[16,1,128]{2,1,0:T(1,128)S(1)} all-to-all(f32[16,1,128]{2,1,0:T(1,128)S(1)} %bitcast.8), channel_id=1, replica_groups={{0,1,2,3,128,129,130,131,256,257,258,259,384,385,386,387},{4,5,6,7,132,..., dimensions={0} | all-to-all | bytes 16384 | tf_op jit(solution)/shard_map/all_to_all | solution.py:428
  29.5 5.6 %collective-permute-start.5 = (f32[16,1,128]{2,0,1:T(8,128)S(1)}, f32[16,1,128]{2,0,1:T(8,128)S(1)}, u32[]{:S(2)}, u32[]{:S(2)}) collective-permute-start(f32[16,1,128]{2,0,1:T(8,128)S(1)} %bitcast.9), channel_id=1, source_target_pairs={{7,3},{0,4},{9,5},{10,6},{11,7},{4,8},{5,9},{6,10},{15,11},{8,12},... | collective-permute-start | bytes 24584 | tf_op jit(solution)/shard_map/ppermute | solution.py:429
  35.1 1.9 %collective-permute-start.6 = (f32[16,1,128]{2,0,1:T(8,128)S(1)}, f32[16,1,128]{2,0,1:T(8,128)S(1)}, u32[]{:S(2)}, u32[]{:S(2)}) collective-permute-start(f32[16,1,128]{2,0,1:T(8,128)S(1)} %bitcast.10), channel_id=1, source_target_pairs={{5,1},{6,2},{1,5},{2,6},{13,9},{14,10},{9,13},{10,14},{21,17},{22,... | collective-permute-start | bytes 24584 | tf_op jit(solution)/shard_map/ppermute | solution.py:429
  37.0 1.3 %collective-permute-done.5 = f32[16,1,128]{2,0,1:T(8,128)S(1)} collective-permute-done((f32[16,1,128]{2,0,1:T(8,128)S(1)}, f32[16,1,128]{2,0,1:T(8,128)S(1)}, u32[]{:S(2)}, u32[]{:S(2)}) %collective-permute-start.5) | collective-permute-done | bytes 8224 | tf_op jit(solution)/shard_map/ppermute | solution.py:429
  38.3 2.3 %collective-permute-done.6 = f32[16,1,128]{2,0,1:T(8,128)S(1)} collective-permute-done((f32[16,1,128]{2,0,1:T(8,128)S(1)}, f32[16,1,128]{2,0,1:T(8,128)S(1)}, u32[]{:S(2)}, u32[]{:S(2)}) %collective-permute-start.6) | collective-permute-done | bytes 8224 | tf_op jit(solution)/shard_map/ppermute | solution.py:429
  40.6 0.9 %shard_map.80 = (f32[1,2,1,16]{3,2,1,0:T(1,128)}, f32[1,2,1,16]{3,2,1,0:T(1,128)}) custom-call(f32[8,128]{1,0:T(8,128)S(1)} %shard_map.77.springs, f32[16,128]{1,0:T(8,128)S(1)} %bitcast.11, f32[16,128]{1,0:T(8,128)S(1)} %bitcast.12, f32[16,128]{1,0:T(8,128)S(1)} %bitcast.13), custom_call_target="tpu_custom_call" | custom-call | tf_op jit(solution)/shard_map/pallas_call | solution.py:380
  (5 shorter events, 0.0 us)
Async XLA Ops:
  0.6 13.0 %copy-start.2 = (f32[8,2]{0,1:T(2,128)S(1)}, f32[8,2]{0,1:T(2,128)}, u32[]{:S(2)}) copy-start(f32[8,2]{0,1:T(2,128)} %param.9) | copy-start | bytes 196
  0.6 13.0 %copy-start.4 = (s32[3]{0:T(128)S(1)}, s32[3]{0:T(128)}, u32[]{:S(2)}) copy-start(s32[3]{0:T(128)} %plan.1) | copy-start | bytes 40
  0.7 14.0 %collective-permute-start = (bf16[1,64,1088]{2,1,0:T(8,128)(2,1)}, bf16[1,64,1088]{2,1,0:T(8,128)(2,1)S(1)}, u32[]{:S(2)}, u32[]{:S(2)}) collective-permute-start(bf16[1,64,1088]{2,1,0:T(8,128)(2,1)} %own.1), channel_id=1, source_target_pairs={{129,128},{130,129},{131,130},{132,131},{133,132},{134,133},{135,1... | collective-permute-start | bytes 417800 | tf_op jit(solution)/shard_map/ppermute | solution.py:411
  1.5 14.6 %collective-permute-start.2 = (bf16[1,64,1088]{2,1,0:T(8,128)(2,1)}, bf16[1,64,1088]{2,1,0:T(8,128)(2,1)S(1)}, u32[]{:S(2)}, u32[]{:S(2)}) collective-permute-start(bf16[1,64,1088]{2,1,0:T(8,128)(2,1)} %own.1), channel_id=1, source_target_pairs={{1,128},{2,129},{3,130},{4,131},{5,132},{6,133},{7,134},{8,135},{9... | collective-permute-start | bytes 417800 | tf_op jit(solution)/shard_map/ppermute | solution.py:414
  9.7 6.4 %collective-permute-start.3 = (bf16[1,64,1088]{2,1,0:T(8,128)(2,1)}, bf16[1,64,1088]{2,1,0:T(8,128)(2,1)S(1)}, u32[]{:S(2)}, u32[]{:S(2)}) collective-permute-start(bf16[1,64,1088]{2,1,0:T(8,128)(2,1)} %own.1), channel_id=1, source_target_pairs={{0,128},{128,256},{256,384},{1,129},{129,257},{257,385},{2,130},{1... | collective-permute-start | bytes 417800 | tf_op jit(solution)/shard_map/ppermute | solution.py:392
  11.7 2.9 %collective-permute-start.1 = (s32[1,2,1,16]{3,2,1,0:T(1,128)}, s32[1,2,1,16]{3,2,1,0:T(1,128)S(1)}, u32[]{:S(2)}, u32[]{:S(2)}) collective-permute-start(s32[1,2,1,16]{3,2,1,0:T(1,128)} %param.8), channel_id=1, source_target_pairs={{0,128},{128,256},{256,384},{1,129},{129,257},{257,385},{2,130},{1... | collective-permute-start | bytes 392 | tf_op jit(solution)/shard_map/ppermute | solution.py:392
  13.7 1.7 %copy-start = (bf16[1344,256]{1,0:T(8,128)(2,1)S(1)}, bf16[1344,256]{1,0:T(8,128)(2,1)}, u32[]{:S(2)}) copy-start(bf16[1344,256]{1,0:T(8,128)(2,1)} %constant.2.clone.tables) | copy-start | bytes 2064388
  13.7 1.7 %copy-start.1 = (bf16[1,64,1088]{2,1,0:T(8,128)(2,1)S(1)}, bf16[1,64,1088]{2,1,0:T(8,128)(2,1)}, u32[]{:S(2)}) copy-start(bf16[1,64,1088]{2,1,0:T(8,128)(2,1)} %own.1) | copy-start | bytes 417796
  13.7 1.7 %copy-start.3 = (f32[1,2,1,16]{3,2,1,0:T(1,128)S(1)}, f32[1,2,1,16]{3,2,1,0:T(1,128)}, u32[]{:S(2)}) copy-start(f32[1,2,1,16]{3,2,1,0:T(1,128)} %initial.1) | copy-start | bytes 388
  14.7 1.4 %collective-permute-start.4 = (bf16[1,64,1088]{2,1,0:T(8,128)(2,1)S(1)}, bf16[1,64,1088]{2,1,0:T(8,128)(2,1)S(1)}, u32[]{:S(2)}, u32[]{:S(2)}) collective-permute-start(bf16[1,64,1088]{2,1,0:T(8,128)(2,1)S(1)} %collective-permute-done.below), channel_id=1, source_target_pairs={{256,384},{257,385},{258,386},{259,387},{260,388},{261,389},{262,3... | collective-permute-start | bytes 417800 | tf_op jit(solution)/shard_map/ppermute | solution.py:420
  29.5 8.9 %collective-permute-start.5 = (f32[16,1,128]{2,0,1:T(8,128)S(1)}, f32[16,1,128]{2,0,1:T(8,128)S(1)}, u32[]{:S(2)}, u32[]{:S(2)}) collective-permute-start(f32[16,1,128]{2,0,1:T(8,128)S(1)} %bitcast.9), channel_id=1, source_target_pairs={{7,3},{0,4},{9,5},{10,6},{11,7},{4,8},{5,9},{6,10},{15,11},{8,12},... | collective-permute-start | bytes 24584 | tf_op jit(solution)/shard_map/ppermute | solution.py:429
  35.1 5.5 %collective-permute-start.6 = (f32[16,1,128]{2,0,1:T(8,128)S(1)}, f32[16,1,128]{2,0,1:T(8,128)S(1)}, u32[]{:S(2)}, u32[]{:S(2)}) collective-permute-start(f32[16,1,128]{2,0,1:T(8,128)S(1)} %bitcast.10), channel_id=1, source_target_pairs={{5,1},{6,2},{1,5},{2,6},{13,9},{14,10},{9,13},{10,14},{21,17},{22,... | collective-permute-start | bytes 24584 | tf_op jit(solution)/shard_map/ppermute | solution.py:429

commit v16 on v15

--- a/solution.py
+++ b/solution.py
@@ -416,12 +416,12 @@
     )
     near_offsets = shifted(offsets, "sec", 1)
     springs = spring_rows(plan, stiffness)
-    below, near_offsets, springs = lax.optimization_barrier((below, near_offsets, springs))
-    near_below = lax.ppermute(below, "sec", [(2, 3)])
     count = SECS * RING
     tables = jnp.asarray(constant_tables())
-    own_parts = own_spectra(images, below, initial, tables)
-    mine = pair_flow(own_parts, near, near_below, lower, near_offsets, tables, count)
+    spec, energies, record = own_spectra(images, below, initial, tables)
+    sent_on, near_offsets, springs, record = lax.optimization_barrier((below, near_offsets, springs, record))
+    near_below = lax.ppermute(sent_on, "sec", [(2, 3)])
+    mine = pair_flow((spec, energies, record), near, near_below, lower, near_offsets, tables, count)
     groups = [
         [s * rows + RING * g + j for s in range(SECS) for j in range(RING)] for g in range(rows // RING)
     ]

time: 41.9 us -> 41.9 us (level)
  local copies, waits for them, and re-layouts: 0.02 us -> 0.48 us
    unnamed x10, local copies, waits for them, and re-layouts: 0.02 us -> 0.48 us
  transfers between devices with their start and end apart: 7 -> 7, of which waited for: 3 -> 2; matrix products, arithmetic and copies ran while one was open for 0% -> 0% of each run, Pallas kernels for 3% -> 3%
where the time goes in v16:
time: 41.9 us; the launch traced here: 41.6 us
  starting transfers between devices  21.2 us (51%)
  blocking collectives  11.6 us (28%)
  Pallas kernels  3.89 us (9%)
  waiting for transfers between devices  3.63 us (9%)
  between operations  0.78 us (2%)
  local copies, waits for them, and re-layouts  0.48 us (1%)
    all_to_all x1, blocking collectives, per_device(): lax.all_to_all(mine.reshape(count, 1, PATCH), ('sec', 'row'), 0, 0, axis_...  11.6 us
    ppermute x1, starting transfers between devices, per_device(): lax.ppermute(images, ('sec', 'row'), [(at(s, r + 1), at(s + 1, r)) for s...  8.18 us
    ppermute x2, starting transfers between devices, per_device(): lax.ppermute(ring, 'row', route)  7.51 us
    ppermute x2, starting transfers between devices, shifted(): return lax.ppermute(block, axis, route)  3.99 us
    ppermute x2, waiting for transfers between devices, per_device(): lax.ppermute(ring, 'row', route)  3.62 us
    pallas_call x1, Pallas kernels, pair_flow(): pl.pallas_call(flow_kernel, out_shape=jax.ShapeDtypeStruct((copies, PATCH...  1.65 us
    pallas_call x1, Pallas kernels, relax(): pl.pallas_call(relax_kernel, out_shape=[jax.ShapeDtypeStruct(shape, f32)]...  0.94 us
  transfers between devices with their start and end apart: 7, of which 2 were waited for; matrix products, arithmetic and copies ran while one was open for 0% of the time, Pallas kernels for 3%

profile of v16, /device:TPU:272, one launch (start us, length us, event | category | flops | bytes accessed | tf_op | source)
XLA Modules:
  0.0 41.6 jit_solution(4641635503271957302)
XLA Ops:
  0.6 0.0 copy-start.2
  0.6 0.0 copy-start.4
  0.7 0.8 %collective-permute-start = (bf16[1,64,1088]{2,1,0:T(8,128)(2,1)}, bf16[1,64,1088]{2,1,0:T(8,128)(2,1)S(1)}, u32[]{:S(2)}, u32[]{:S(2)}) collective-permute-start(bf16[1,64,1088]{2,1,0:T(8,128)(2,1)} %own.1), channel_id=1, source_target_pairs={{129,128},{130,129},{131,130},{132,131},{133,132},{134,133},{135,1... | collective-permute-start | bytes 417800 | tf_op jit(solution)/shard_map/ppermute | solution.py:411
  1.5 8.2 %collective-permute-start.2 = (bf16[1,64,1088]{2,1,0:T(8,128)(2,1)}, bf16[1,64,1088]{2,1,0:T(8,128)(2,1)S(1)}, u32[]{:S(2)}, u32[]{:S(2)}) collective-permute-start(bf16[1,64,1088]{2,1,0:T(8,128)(2,1)} %own.1), channel_id=1, source_target_pairs={{1,128},{2,129},{3,130},{4,131},{5,132},{6,133},{7,134},{8,135},{9... | collective-permute-start | bytes 417800 | tf_op jit(solution)/shard_map/ppermute | solution.py:414
  9.7 2.1 %collective-permute-start.3 = (bf16[1,64,1088]{2,1,0:T(8,128)(2,1)}, bf16[1,64,1088]{2,1,0:T(8,128)(2,1)S(1)}, u32[]{:S(2)}, u32[]{:S(2)}) collective-permute-start(bf16[1,64,1088]{2,1,0:T(8,128)(2,1)} %own.1), channel_id=1, source_target_pairs={{0,128},{128,256},{256,384},{1,129},{129,257},{257,385},{2,130},{1... | collective-permute-start | bytes 417800 | tf_op jit(solution)/shard_map/ppermute | solution.py:392
  11.7 1.9 %collective-permute-start.1 = (s32[1,2,1,16]{3,2,1,0:T(1,128)}, s32[1,2,1,16]{3,2,1,0:T(1,128)S(1)}, u32[]{:S(2)}, u32[]{:S(2)}) collective-permute-start(s32[1,2,1,16]{3,2,1,0:T(1,128)} %param.8), channel_id=1, source_target_pairs={{0,128},{128,256},{256,384},{1,129},{129,257},{257,385},{2,130},{1... | collective-permute-start | bytes 392 | tf_op jit(solution)/shard_map/ppermute | solution.py:392
  13.7 0.0 copy-start
  13.7 0.6 %shard_map.77.springs = f32[8,128]{1,0:T(8,128)S(1)} custom-call(s32[3]{0:T(128)S(1)} %copy-done.4, f32[2,8]{1,0:T(2,128)S(1)} %bitcast.14), custom_call_target="tpu_custom_call" | custom-call | flops 1000000000 | bytes 10000 | tf_op jit(solution)/shard_map/pallas_call | solution.py:125
  14.3 0.0 collective-permute-done.below
  14.3 0.4 %copy-done = bf16[1344,256]{1,0:T(8,128)(2,1)S(1)} copy-done((bf16[1344,256]{1,0:T(8,128)(2,1)S(1)}, bf16[1344,256]{1,0:T(8,128)(2,1)}, u32[]{:S(2)}) %copy-start) | copy-done | bytes 688152
  14.8 0.0 copy-done.1
  14.8 0.7 %shard_map.78 = (bf16[9,256,128]{2,1,0:T(8,128)(2,1)S(1)}, f32[16,128]{1,0:T(8,128)S(1)}, f32[1,128]{1,0:T(1,128)S(1)}) custom-call(bf16[1,64,1088]{2,1,0:T(8,128)(2,1)S(1)} %copy-done.1, bf16[1,64,1088]{2,1,0:T(8,128)(2,1)S(1)} %collective-permute-done.below, f32[1,2,1,16]{3,2,1,0:T(1,128)S(1)} %copy-done.3, bf16[1344,256]{1,0:T(8,128)(2,1)S(1)} %copy-done), custom_call_target="tpu_custom_call" | custom-call | flops 600000000 | bytes 2000000 | tf_op jit(solution)/shard_map/pallas_call | solution.py:178
  15.5 0.0 collective-permute-done.1.shifts_in
  15.5 0.7 %collective-permute-start.4 = (bf16[1,64,1088]{2,1,0:T(8,128)(2,1)S(1)}, bf16[1,64,1088]{2,1,0:T(8,128)(2,1)S(1)}, u32[]{:S(2)}, u32[]{:S(2)}) collective-permute-start(bf16[1,64,1088]{2,1,0:T(8,128)(2,1)S(1)} %collective-permute-done.below), channel_id=1, source_target_pairs={{256,384},{257,385},{258,386},{259,387},{260,388},{261,389},{262,3... | collective-permute-start | bytes 417800 | tf_op jit(solution)/shard_map/ppermute | solution.py:423
  16.2 0.0 collective-permute-done.2.lower
  16.2 0.0 collective-permute-done.3.near
  16.2 0.0 collective-permute-done.4.near_below
  16.2 1.7 %shard_map.79 = f32[16,128]{1,0:T(8,128)S(1)} custom-call(bf16[9,256,128]{2,1,0:T(8,128)(2,1)S(1)} %get-tuple-element.11.own_spec, f32[16,128]{1,0:T(8,128)S(1)} %get-tuple-element.12.own_energies, f32[1,128]{1,0:T(1,128)S(1)} %get-tuple-element.13.record, bf16[1,64,1088]{2,1,0:T(8,128)(2,1)S(1)} %collective-permute-done.2.lower, ...), custom_call_target="tpu_custom_call" | custom-call | tf_op jit(solution)/shard_map/pallas_call | solution.py:296
  17.9 11.6 %all_to_all.5 = f32[16,1,128]{2,1,0:T(1,128)S(1)} all-to-all(f32[16,1,128]{2,1,0:T(1,128)S(1)} %bitcast.8), channel_id=1, replica_groups={{0,1,2,3,128,129,130,131,256,257,258,259,384,385,386,387},{4,5,6,7,132,..., dimensions={0} | all-to-all | bytes 16384 | tf_op jit(solution)/shard_map/all_to_all | solution.py:428
  29.5 5.6 %collective-permute-start.5 = (f32[16,1,128]{2,0,1:T(8,128)S(1)}, f32[16,1,128]{2,0,1:T(8,128)S(1)}, u32[]{:S(2)}, u32[]{:S(2)}) collective-permute-start(f32[16,1,128]{2,0,1:T(8,128)S(1)} %bitcast.9), channel_id=1, source_target_pairs={{7,3},{0,4},{9,5},{10,6},{11,7},{4,8},{5,9},{6,10},{15,11},{8,12},... | collective-permute-start | bytes 24584 | tf_op jit(solution)/shard_map/ppermute | solution.py:429
  35.1 1.9 %collective-permute-start.6 = (f32[16,1,128]{2,0,1:T(8,128)S(1)}, f32[16,1,128]{2,0,1:T(8,128)S(1)}, u32[]{:S(2)}, u32[]{:S(2)}) collective-permute-start(f32[16,1,128]{2,0,1:T(8,128)S(1)} %bitcast.10), channel_id=1, source_target_pairs={{5,1},{6,2},{1,5},{2,6},{13,9},{14,10},{9,13},{10,14},{21,17},{22,... | collective-permute-start | bytes 24584 | tf_op jit(solution)/shard_map/ppermute | solution.py:429
  37.0 1.3 %collective-permute-done.5 = f32[16,1,128]{2,0,1:T(8,128)S(1)} collective-permute-done((f32[16,1,128]{2,0,1:T(8,128)S(1)}, f32[16,1,128]{2,0,1:T(8,128)S(1)}, u32[]{:S(2)}, u32[]{:S(2)}) %collective-permute-start.5) | collective-permute-done | bytes 8224 | tf_op jit(solution)/shard_map/ppermute | solution.py:429
  38.3 2.3 %collective-permute-done.6 = f32[16,1,128]{2,0,1:T(8,128)S(1)} collective-permute-done((f32[16,1,128]{2,0,1:T(8,128)S(1)}, f32[16,1,128]{2,0,1:T(8,128)S(1)}, u32[]{:S(2)}, u32[]{:S(2)}) %collective-permute-start.6) | collective-permute-done | bytes 8224 | tf_op jit(solution)/shard_map/ppermute | solution.py:429
  40.6 0.9 %shard_map.80 = (f32[1,2,1,16]{3,2,1,0:T(1,128)}, f32[1,2,1,16]{3,2,1,0:T(1,128)}) custom-call(f32[8,128]{1,0:T(8,128)S(1)} %shard_map.77.springs, f32[16,128]{1,0:T(8,128)S(1)} %bitcast.11, f32[16,128]{1,0:T(8,128)S(1)} %bitcast.12, f32[16,128]{1,0:T(8,128)S(1)} %bitcast.13), custom_call_target="tpu_custom_call" | custom-call | tf_op jit(solution)/shard_map/pallas_call | solution.py:380
  (5 shorter events, 0.0 us)
Async XLA Ops:
  0.6 13.0 %copy-start.2 = (f32[8,2]{0,1:T(2,128)S(1)}, f32[8,2]{0,1:T(2,128)}, u32[]{:S(2)}) copy-start(f32[8,2]{0,1:T(2,128)} %param.9) | copy-start | bytes 196
  0.6 13.0 %copy-start.4 = (s32[3]{0:T(128)S(1)}, s32[3]{0:T(128)}, u32[]{:S(2)}) copy-start(s32[3]{0:T(128)} %plan.1) | copy-start | bytes 40
  0.7 13.7 %collective-permute-start = (bf16[1,64,1088]{2,1,0:T(8,128)(2,1)}, bf16[1,64,1088]{2,1,0:T(8,128)(2,1)S(1)}, u32[]{:S(2)}, u32[]{:S(2)}) collective-permute-start(bf16[1,64,1088]{2,1,0:T(8,128)(2,1)} %own.1), channel_id=1, source_target_pairs={{129,128},{130,129},{131,130},{132,131},{133,132},{134,133},{135,1... | collective-permute-start | bytes 417800 | tf_op jit(solution)/shard_map/ppermute | solution.py:411
  1.5 14.7 %collective-permute-start.2 = (bf16[1,64,1088]{2,1,0:T(8,128)(2,1)}, bf16[1,64,1088]{2,1,0:T(8,128)(2,1)S(1)}, u32[]{:S(2)}, u32[]{:S(2)}) collective-permute-start(bf16[1,64,1088]{2,1,0:T(8,128)(2,1)} %own.1), channel_id=1, source_target_pairs={{1,128},{2,129},{3,130},{4,131},{5,132},{6,133},{7,134},{8,135},{9... | collective-permute-start | bytes 417800 | tf_op jit(solution)/shard_map/ppermute | solution.py:414
  9.7 6.5 %collective-permute-start.3 = (bf16[1,64,1088]{2,1,0:T(8,128)(2,1)}, bf16[1,64,1088]{2,1,0:T(8,128)(2,1)S(1)}, u32[]{:S(2)}, u32[]{:S(2)}) collective-permute-start(bf16[1,64,1088]{2,1,0:T(8,128)(2,1)} %own.1), channel_id=1, source_target_pairs={{0,128},{128,256},{256,384},{1,129},{129,257},{257,385},{2,130},{1... | collective-permute-start | bytes 417800 | tf_op jit(solution)/shard_map/ppermute | solution.py:392
  11.7 3.7 %collective-permute-start.1 = (s32[1,2,1,16]{3,2,1,0:T(1,128)}, s32[1,2,1,16]{3,2,1,0:T(1,128)S(1)}, u32[]{:S(2)}, u32[]{:S(2)}) collective-permute-start(s32[1,2,1,16]{3,2,1,0:T(1,128)} %param.8), channel_id=1, source_target_pairs={{0,128},{128,256},{256,384},{1,129},{129,257},{257,385},{2,130},{1... | collective-permute-start | bytes 392 | tf_op jit(solution)/shard_map/ppermute | solution.py:392
  13.7 1.1 %copy-start = (bf16[1344,256]{1,0:T(8,128)(2,1)S(1)}, bf16[1344,256]{1,0:T(8,128)(2,1)}, u32[]{:S(2)}) copy-start(bf16[1344,256]{1,0:T(8,128)(2,1)} %constant.2.clone.tables) | copy-start | bytes 2064388
  13.7 1.1 %copy-start.1 = (bf16[1,64,1088]{2,1,0:T(8,128)(2,1)S(1)}, bf16[1,64,1088]{2,1,0:T(8,128)(2,1)}, u32[]{:S(2)}) copy-start(bf16[1,64,1088]{2,1,0:T(8,128)(2,1)} %own.1) | copy-start | bytes 417796
  13.7 1.1 %copy-start.3 = (f32[1,2,1,16]{3,2,1,0:T(1,128)S(1)}, f32[1,2,1,16]{3,2,1,0:T(1,128)}, u32[]{:S(2)}) copy-start(f32[1,2,1,16]{3,2,1,0:T(1,128)} %initial.1) | copy-start | bytes 388
  15.5 0.7 %collective-permute-start.4 = (bf16[1,64,1088]{2,1,0:T(8,128)(2,1)S(1)}, bf16[1,64,1088]{2,1,0:T(8,128)(2,1)S(1)}, u32[]{:S(2)}, u32[]{:S(2)}) collective-permute-start(bf16[1,64,1088]{2,1,0:T(8,128)(2,1)S(1)} %collective-permute-done.below), channel_id=1, source_target_pairs={{256,384},{257,385},{258,386},{259,387},{260,388},{261,389},{262,3... | collective-permute-start | bytes 417800 | tf_op jit(solution)/shard_map/ppermute | solution.py:423
  29.5 8.9 %collective-permute-start.5 = (f32[16,1,128]{2,0,1:T(8,128)S(1)}, f32[16,1,128]{2,0,1:T(8,128)S(1)}, u32[]{:S(2)}, u32[]{:S(2)}) collective-permute-start(f32[16,1,128]{2,0,1:T(8,128)S(1)} %bitcast.9), channel_id=1, source_target_pairs={{7,3},{0,4},{9,5},{10,6},{11,7},{4,8},{5,9},{6,10},{15,11},{8,12},... | collective-permute-start | bytes 24584 | tf_op jit(solution)/shard_map/ppermute | solution.py:429
  35.1 5.5 %collective-permute-start.6 = (f32[16,1,128]{2,0,1:T(8,128)S(1)}, f32[16,1,128]{2,0,1:T(8,128)S(1)}, u32[]{:S(2)}, u32[]{:S(2)}) collective-permute-start(f32[16,1,128]{2,0,1:T(8,128)S(1)} %bitcast.10), channel_id=1, source_target_pairs={{5,1},{6,2},{1,5},{2,6},{13,9},{14,10},{9,13},{10,14},{21,17},{22,... | collective-permute-start | bytes 24584 | tf_op jit(solution)/shard_map/ppermute | solution.py:429
